TPU v7x, 32 devices: a whole 2x2x4 slice. The times are simulated.
32 devices in a mesh: parts: 2 (over y), freq: 4 (over z), state: 4 (over x, core).
Axes of the slice: x: 2, y: 2, z: 4, core: 2. Of those that a mesh axis runs over, the one named last changes fastest.
Arguments:
- gap_in: float32 [1024, 2048], P(('parts', 'freq'), 'state'), parts along dimension 0, may hold values from -10 to 10, as said below
- coupling: bfloat16 [32, 2, 9, 128, 128], P(('parts', 'state')), parts along dimension 0, may hold values from 0 to 0.0002593994
- pair_cols: int32 [32, 2], P(('parts', 'state')), parts along dimension 0, may hold values from 0 to 15, as said below
- pair_count: int32 [32], P(('parts', 'state')), parts along dimension 0, may hold values from 1 to 2, 24 in all
- block_order: int32 [32], P('parts'), parts along dimension 0, may hold values from 0 to 15, each once
- phonon: float32 [18], P('parts'), parts along dimension 0, may hold values from 0.015 to 0.5
Outputs:
- gap_out: float32 [1024, 2048], P(('parts', 'freq'), 'state'), parts along dimension 0
- renorm: float32 [1024, 2048], P(('parts', 'freq'), 'state'), parts along dimension 0
There are 2 independent parts, one for each index of `parts`. A program takes and returns all parts, laid end to end along the dimension named above; each array names one. Nothing has to cross between parts.
Inputs may be any that keep to these rules, and one draw needn't show every extreme that they name: gap_in[n] equals gap_in[511 - n] for every frequency row n. `pair_cols`: each row holds 2 different block numbers; every block number stands first in exactly one row. `pair_count`: the counts sum to 24. `block_order`: each block number once.
All inputs are finite; a program needn't handle non-finite values. No bound on the sum of `pair_count` on one device may be relied on, other than what follows from the above.
Results may differ from a plain program's by a relative error of at most 0.0003.
Values may be sent and summed in bfloat16 or wider, within the bound.
No kernel may reach another device: no remote copies, remote signals or barrier semaphores. Data moves between devices by JAX's collectives and lax.ppermute only.
A program may use at most 64 MiB of HBM per device.

v0:
```python
import jax
import jax.numpy as jnp
from jax import lax
from jax.sharding import PartitionSpec as P

ITERS = 2


CUTOFF = 4.0


def frequencies(total_rows):
    return (2.0 * jnp.arange(total_rows, dtype=jnp.float32) + 1.0 - total_rows) * (
        CUTOFF / total_rows
    )


def kernel(row_freq, col_freq, phonon):
    spacing = row_freq[:, None] - col_freq[None, :]
    return 2.0 * phonon[:, None, None] / (spacing[None, :, :] ** 2 + phonon[:, None, None] ** 2)


def on_device(gap_in, coupling, pair_cols, pair_count, block_order, phonon):
    own_rows, row_width = gap_in.shape
    blocks_here = coupling.shape[0]
    pair_slots = coupling.shape[1]
    block_size = coupling.shape[3]
    block_count = block_order.shape[0]
    freq_count = own_rows * lax.axis_size("freq")
    all_freq = frequencies(freq_count)
    own_freq = lax.dynamic_slice_in_dim(all_freq, lax.axis_index("freq") * own_rows, own_rows)
    numbers = jnp.arange(block_count, dtype=jnp.int32)
    position = jnp.sum(
        jnp.where(block_order[None, :] == numbers[:, None], numbers[None, :], 0), axis=1
    )
    column_place = jnp.sum(
        jnp.where(pair_cols[:, :, None] == numbers[None, None, :], position[None, None, :], 0),
        axis=2,
    )
    live_mask = (jnp.arange(pair_slots, dtype=jnp.int32)[None, :] < pair_count[:, None]).astype(
        jnp.bfloat16
    )
    gap_now = gap_in
    renorm = jnp.ones_like(gap_in)
    for iteration in range(ITERS):
        radius = jnp.sqrt(own_freq[:, None] ** 2 + gap_now**2)
        ratios = jnp.stack([gap_now / radius, own_freq[:, None] / radius]).astype(jnp.bfloat16)
        everyone = lax.all_gather(ratios, "state", axis=2, tiled=True)

        def columns_of(fetched, row_block):
            columns = [
                lax.dynamic_slice_in_dim(
                    fetched, column_place[row_block, pair_slot] * block_size, block_size, 2
                )
                for pair_slot in range(pair_slots)
            ]
            return jnp.stack(columns, axis=2) * live_mask[row_block][None, None, :, None]

        def row_terms(fetched):
            pieces = [
                jnp.einsum(
                    "jvst,qmjt->vqms",
                    coupling[row_block],
                    columns_of(fetched, row_block),
                    preferred_element_type=jnp.float32,
                )
                for row_block in range(blocks_here)
            ]
            return jnp.concatenate(pieces, axis=3)

        local_terms = row_terms(everyone)
        weights = kernel(all_freq, own_freq, phonon)
        summed = lax.psum_scatter(
            jnp.einsum("vnm,vqms->nqs", weights, local_terms, precision=lax.Precision.HIGHEST),
            "freq",
            scatter_dimension=0,
            tiled=True,
        )
        renorm = 1.0 + CUTOFF / freq_count * summed[:, 1, :] / own_freq[:, None]
        gap_now = CUTOFF / freq_count * summed[:, 0, :] / renorm
    return (gap_now, renorm)


def solution(mesh):
    return jax.shard_map(
        on_device,
        mesh=mesh,
        in_specs=(
            P(("parts", "freq"), "state"),
            P(("parts", "state"), None, None, None, None),
            P(("parts", "state"), None),
            P(("parts", "state")),
            P("parts"),
            P("parts"),
        ),
        out_specs=(P(("parts", "freq"), "state"), P(("parts", "freq"), "state")),
        check_vma=False,
    )
```

profile of v0, /device:TPU:0, one launch (start us, length us, event | category | flops | bytes accessed | tf_op | source)
XLA Modules:
  0.0 169.8 jit_solution(276781267479927741)
XLA Ops:
  7.3 1.1 fusion.67
  8.4 0.7 pad_maximum_fusion
  9.2 0.8 select_reduce_fusion
  10.0 0.9 select_reduce_fusion.1
  10.9 0.7 fusion.74
  16.6 0.7 fusion.69
  17.3 0.7 broadcast_multiply_fusion
  18.0 0.1 subtract_multiply_fusion
  18.1 1.8 %slice_bitcast_fusion.3 = (bf16[2,9,128,128,1]{3,2,1,0,4:T(8,128)(2,1)S(1)}, bf16[2,9,128,128,1]{3,2,1,0,4:T(8,128)(2,1)S(1)}, bf16[2,9,128,128,1]{3,2,1,0,4:T(8,128)(2,1)S(1)}, bf16[2,9,128,128,1]{3,2,1,0,4:T(8,128)(2,1)S(1)}) fusion(bf16[4,2,9,128,128]{4,3,2,1,0:T(8,128)(2,1)} %param.7), kind=kLoop, calls=%fused_computation.38 | loop fusion | bytes 4718592 | tf_op jit(solution)/shard_map/squeeze | solution.py:63
  20.0 9.6 %all-gather.3.cloned.1.call-done = bf16[2,128,2048]{2,1,0:T(8,128)(2,1)} async-done(((bf16[2,128,512]{2,1,0:T(8,128)(2,1)}), bf16[2,128,2048]{2,1,0:T(8,128)(2,1)}) %all-gather.3.cloned.1.call-update) | async-done | bytes 1048592 | tf_op jit(solution)/shard_map/all_gather | solution.py:48
  29.6 1.1 dynamic-slice_bitcast_fusion.15
  30.7 0.1 fusion.51
  30.8 0.4 convolution_bitcast_fusion.7
  31.2 0.4 convolution_bitcast_fusion.6
  31.5 0.1 fusion.53
  31.6 0.4 convolution_bitcast_fusion.4
  32.0 0.4 convolution_bitcast_fusion.5
  32.4 9.9 %fusion.23 = f32[512,2,512]{2,0,1:T(8,128)} fusion(f32[9,2,128,128]{3,2,0,1:T(8,128)S(1)} %convolution_bitcast_fusion.4, f32[9,2,128,128]{3,2,0,1:T(8,128)S(1)} %convolution_bitcast_fusion.5, f32[9,2,128,128]{3,2,0,1:T(8,128)S(1)} %convolution_bitcast_fusion.6, f32[9,2,128,128]{3,2,0,1:T(8,128)S(1)} %convolution_bitcast_fusion.7, ...), kind=kOutput, calls=%fused_computation.20 | convolution fusion | flops 7252475904 | bytes 7077960 | tf_op jit(solution)/shard_map/vnm,vqms->nqs/dot_general | solution.py:74
  42.4 44.0 %reduce-scatter.3.cloned.1.call-done = f32[128,2,512]{2,0,1:T(8,128)} async-done(((f32[512,2,512]{2,0,1:T(8,128)}), f32[128,2,512]{2,0,1:T(8,128)}) %reduce-scatter.3.cloned.1.call-update) | async-done | bytes 524304 | tf_op jit(solution)/shard_map/reduce_scatter | solution.py:73
  86.4 1.3 divide_convert_fusion
  87.6 0.1 multiply_convert_fusion
  87.7 0.7 pad_maximum_fusion.1
  88.5 0.2 reduce-scatter.5.cloned.1.call-start
  88.7 15.9 %all-gather.5.cloned.1.call-done = bf16[2,128,2048]{2,1,0:T(8,128)(2,1)} async-done(((bf16[2,128,512]{2,1,0:T(8,128)(2,1)}), bf16[2,128,2048]{2,1,0:T(8,128)(2,1)}) %all-gather.5.cloned.1.call-update) | async-done | bytes 1048592 | tf_op jit(solution)/shard_map/all_gather | solution.py:48
  104.7 1.1 dynamic-slice_bitcast_fusion.7
  105.8 0.4 convolution_bitcast_fusion.3
  106.2 0.4 convolution_bitcast_fusion
  106.5 0.4 convolution_bitcast_fusion.1
  106.9 0.4 convolution_bitcast_fusion.2
  107.3 9.9 %fusion.18 = f32[512,2,512]{2,0,1:T(8,128)} fusion(f32[9,2,128,128]{3,2,0,1:T(8,128)S(1)} %convolution_bitcast_fusion, f32[9,2,128,128]{3,2,0,1:T(8,128)S(1)} %convolution_bitcast_fusion.1, f32[9,2,128,128]{3,2,0,1:T(8,128)S(1)} %convolution_bitcast_fusion.2, f32[9,2,128,128]{3,2,0,1:T(8,128)S(1)} %convolution_bitcast_fusion.3, ...), kind=kOutput, calls=%fused_computation.19 | convolution fusion | flops 7252475904 | bytes 7077960 | tf_op jit(solution)/shard_map/vnm,vqms->nqs/dot_general | solution.py:74
  117.3 44.0 %reduce-scatter.5.cloned.1.call-done = f32[128,2,512]{2,0,1:T(8,128)} async-done(((f32[512,2,512]{2,0,1:T(8,128)}), f32[128,2,512]{2,0,1:T(8,128)}) %reduce-scatter.5.cloned.1.call-update) | async-done | bytes 524304 | tf_op jit(solution)/shard_map/reduce_scatter | solution.py:73
  161.3 1.9 %fusion.46 = (f32[128,512]{1,0:T(8,128)}, f32[128,512]{1,0:T(8,128)}) fusion(f32[128,2,512]{2,0,1:T(8,128)} %reduce-scatter.5.cloned.1.call-done, f32[128]{0:T(128)S(1)} %get-tuple-element.7), kind=kLoop, calls=%fused_computation.53 | loop fusion | flops 327680 | bytes 1049088 | tf_op jit(solution)/shard_map/div | solution.py:80
  (10 shorter events, 0.3 us)
Async XLA Ops:
  7.2 22.4 %all-gather.3.cloned.1.call-start = ((), (), s32[]{:S(2)}) async-start(), calls=%async_computation.2 | async-start | bytes 1310720 | tf_op jit(solution)/shard_map/all_gather | solution.py:48
  9.2 77.2 %reduce-scatter.3.cloned.1.call-start = ((), (), s32[]{:S(2)}) async-start(), calls=%async_computation.3 | async-start | bytes 2621440 | tf_op jit(solution)/shard_map/reduce_scatter | solution.py:73
  42.3 62.3 %all-gather.5.cloned.1.call-start = ((), (), s32[]{:S(2)}) async-start(), calls=%async_computation.4 | async-start | bytes 1310720 | tf_op jit(solution)/shard_map/all_gather | solution.py:48
  88.5 72.8 %reduce-scatter.5.cloned.1.call-start = ((), (), s32[]{:S(2)}) async-start(), calls=%async_computation.5 | async-start | bytes 2621440 | tf_op jit(solution)/shard_map/reduce_scatter | solution.py:73
Sparse Core Ops, SparseCore 0:
  10.1 19.4 all-gather.2
  42.4 43.8 reduce-scatter.2
  88.6 16.0 all-gather.4
  117.4 43.8 reduce-scatter.4
where the time goes:
time: 170 us
  waiting for transfers between devices  114 us (67%)
  matrix products  22.8 us (13%)
  between operations  18.9 us (11%)
  other arithmetic  9.32 us (5%)
  local copies, waits for them, and re-layouts  4.76 us (3%)
    reduce_scatter x2, waiting for transfers between devices, on_device(): lax.psum_scatter(jnp.einsum('vnm,vqms->nqs', weights, local_terms, precis...  88 us
    all_gather x2, waiting for transfers between devices, on_device(): everyone = lax.all_gather(ratios, 'state', axis=2, tiled=True)  25.6 us
    dot_general x2, matrix products, on_device(): jnp.einsum('vnm,vqms->nqs', weights, local_terms, precision=lax.Precision...  19.9 us
  transfers between devices with their start and end apart: 4, of which 4 were waited for; matrix products, arithmetic and copies ran while one was open for 3% of the time, Pallas kernels for 0%

commit v1 on v0

v1 whole, which is shorter than its diff:
```python
import functools

import jax
import jax.numpy as jnp
from jax import lax
from jax.experimental import pallas as pl
from jax.experimental.pallas import tpu as pltpu
from jax.sharding import PartitionSpec as P

ITERS = 2
CUTOFF = 4.0
LANES = 128


def omega_of(index, freq_count):
    return (2.0 * index.astype(jnp.float32) + 1.0 - freq_count) * (CUTOFF / freq_count)


def segment_omega(shape, axis, meta, segment_rows, freq_count):
    at = lax.broadcasted_iota(jnp.int32, shape, axis)
    index = at + meta[1]
    for number, start in enumerate(range(segment_rows, shape[axis], segment_rows), 1):
        index = jnp.where(at >= start, at - start + meta[1 + number], index)
    return omega_of(index, freq_count)


def tables_kernel(dims, meta, phonon, coupling, weights, table):
    freq_count, half_rows, segment_rows, padded_rows, modes = dims
    blocks, slots = coupling.shape[:2]
    size = coupling.shape[3]
    row = lax.broadcasted_iota(jnp.int32, (padded_rows, half_rows), 0) + meta[0]
    row_omega = omega_of(row, freq_count)
    col_omega = segment_omega(
        (padded_rows, half_rows), 1, meta, segment_rows, freq_count
    )
    near = (row_omega - col_omega) ** 2
    far = (row_omega + col_omega) ** 2
    for mode in range(modes):
        strength = phonon[mode]
        direct = 2.0 * strength / (near + strength * strength)
        mirrored = 2.0 * strength / (far + strength * strength)
        for part, value in enumerate((direct + mirrored, direct - mirrored)):
            high = value.astype(jnp.bfloat16)
            low = (value - high.astype(jnp.float32)).astype(jnp.bfloat16)
            columns = slice(mode * half_rows, (mode + 1) * half_rows)
            table[part, :padded_rows, columns] = high
            table[part, padded_rows:, columns] = low
    for block in range(blocks):
        for slot in range(slots):
            for mode in range(modes):
                weights[
                    block, slot * size : (slot + 1) * size, mode * size : (mode + 1) * size
                ] = coupling[block, slot, mode].T


def step_kernel(dims, groups, segments, meta, source, *refs):
    freq_count, half_rows, segment_rows, padded_rows, modes = dims
    pieces = refs[: groups * segments]
    weights, table, gap_out, renorm_out, fetched, ratios, high, low, sems = refs[
        groups * segments :
    ]
    own_rows = gap_out.shape[0]
    blocks = weights.shape[0]
    size = LANES
    slots = weights.shape[1] // size

    def copy(pair, group, segment):
        column = pl.multiple_of(source[1, pair] * size, size)
        return pltpu.make_async_copy(
            pieces[group * segments + segment].at[:, pl.ds(column, size)],
            fetched.at[pair, pl.ds(segment * segment_rows, segment_rows), :],
            sems.at[pair, segment],
        )

    for pair in range(blocks * slots):
        for group in range(groups):

            @pl.when(source[0, pair] == group)
            def _():
                for segment in range(segments):
                    copy(pair, group, segment).start()

    col_omega = segment_omega((half_rows, size), 0, meta, segment_rows, freq_count)
    square = col_omega * col_omega
    for block in range(blocks):
        for slot in range(slots):
            pair = block * slots + slot
            for segment in range(segments):
                copy(pair, 0, segment).wait()
            gap = fetched[pair]
            live = source[2, pair].astype(jnp.float32)
            inverse = lax.rsqrt(square + gap * gap) * live
            lanes = slice(slot * size, (slot + 1) * size)
            ratios[block, :half_rows, lanes] = (gap * inverse).astype(jnp.bfloat16)
            ratios[block, half_rows:, lanes] = (col_omega * inverse).astype(jnp.bfloat16)
        for part in range(2):
            for first in range(0, modes, 2):
                last = min(first + 2, modes)
                terms = jnp.dot(
                    ratios[block, part * half_rows : (part + 1) * half_rows, :],
                    weights[block, :, first * size : last * size],
                    preferred_element_type=jnp.float32,
                )
                upper = terms.astype(jnp.bfloat16)
                lower = (terms - upper.astype(jnp.float32)).astype(jnp.bfloat16)
                for mode in range(first, last):
                    rows = slice(mode * half_rows, (mode + 1) * half_rows)
                    taken = slice((mode - first) * size, (mode - first + 1) * size)
                    lanes = slice(block * size, (block + 1) * size)
                    high[part, rows, lanes] = upper[:, taken]
                    low[part, rows, lanes] = lower[:, taken]
    summed = []
    for part in range(2):
        both = jnp.dot(table[part], high[part], preferred_element_type=jnp.float32)
        rest = jnp.dot(
            table[part, :padded_rows], low[part], preferred_element_type=jnp.float32
        )
        summed.append((both[:padded_rows] + (both[padded_rows:] + rest))[:own_rows])
    row = lax.broadcasted_iota(jnp.int32, gap_out.shape, 0) + meta[0]
    temperature = CUTOFF / freq_count
    renorm = 1.0 + temperature * summed[1] / omega_of(row, freq_count)
    renorm_out[...] = renorm
    gap_out[...] = temperature * summed[0] / renorm


def swapped(axis_size, bit):
    return [(i, i ^ bit) for i in range(axis_size)]


def gather_pairwise(gap):
    core = lambda value: lax.ppermute(value, "state", swapped(4, 1))
    joint = [(4 * f + s, 4 * (f ^ 1) + (s ^ 2)) for f in range(4) for s in range(4)]
    along_x = lax.ppermute(gap, "state", swapped(4, 2))
    along_z = lax.ppermute(gap, "freq", swapped(4, 1))
    diagonal = lax.ppermute(gap, ("freq", "state"), joint)
    return [
        gap,
        along_z,
        core(gap),
        core(along_z),
        along_x,
        diagonal,
        core(along_x),
        core(diagonal),
    ]


def gather_general(gap, half_groups):
    groups = lax.axis_size("state")
    everyone = lax.all_gather(gap, "state", axis=0, tiled=False)
    rows = lax.all_gather(everyone, "freq", axis=1, tiled=True)
    own_rows = gap.shape[0]
    start = (lax.axis_index("freq") // half_groups) * (half_groups * own_rows)
    half = lax.dynamic_slice_in_dim(rows, start, half_groups * own_rows, 1)
    return [half[group] for group in range(groups)]


def on_device(gap_in, coupling, pair_cols, pair_count, block_order, phonon):
    own_rows, row_width = gap_in.shape
    blocks, slots, modes, size, _ = coupling.shape
    block_count = block_order.shape[0]
    freq_groups = lax.axis_size("freq")
    groups = lax.axis_size("state")
    freq_count = own_rows * freq_groups
    half_rows = freq_count // 2
    half_groups = freq_groups // 2
    pairwise = freq_groups == 4 and groups == 4
    padded_rows = -(-own_rows // 16) * 16
    freq_at = lax.axis_index("freq")
    state_at = lax.axis_index("state")

    numbers = jnp.arange(block_count, dtype=jnp.int32)
    position = jnp.sum(
        jnp.where(block_order[None, :] == numbers[:, None], numbers[None, :], 0), axis=1
    )
    column_place = jnp.sum(
        jnp.where(pair_cols[:, :, None] == numbers[None, None, :], position[None, None, :], 0),
        axis=2,
    )
    live = (jnp.arange(slots, dtype=jnp.int32)[None, :] < pair_count[:, None]).astype(jnp.int32)
    holder = column_place // blocks
    if pairwise:
        segments = 2
        holder = holder ^ state_at
        meta = jnp.stack([freq_at, freq_at, freq_at ^ 1]) * own_rows
    else:
        segments = 1
        first = (freq_at // half_groups) * half_rows
        meta = jnp.stack([freq_at * own_rows, first, first])
    meta = meta.astype(jnp.int32)
    source = jnp.stack(
        [holder.reshape(-1), (column_place % blocks).reshape(-1), live.reshape(-1)]
    ).astype(jnp.int32)

    segment_rows = half_rows // segments
    dims = (freq_count, half_rows, segment_rows, padded_rows, modes)
    smem = pl.BlockSpec(memory_space=pltpu.SMEM)
    vmem = pl.BlockSpec(memory_space=pltpu.VMEM)
    weights, table = pl.pallas_call(
        functools.partial(tables_kernel, dims),
        out_shape=(
            jax.ShapeDtypeStruct((blocks, slots * size, modes * size), jnp.bfloat16),
            jax.ShapeDtypeStruct((2, 2 * padded_rows, modes * half_rows), jnp.bfloat16),
        ),
        in_specs=[smem, smem, vmem],
        out_specs=(vmem, vmem),
        compiler_params=pltpu.CompilerParams(vmem_limit_bytes=32 << 20),
        cost_estimate=pl.CostEstimate(flops=10_000_000, bytes_accessed=8_000_000, transcendentals=0),
        name="tables",
    )(meta, phonon, coupling)
    step = pl.pallas_call(
        functools.partial(step_kernel, dims, groups, segments),
        out_shape=(jax.ShapeDtypeStruct(gap_in.shape, jnp.float32),) * 2,
        in_specs=[smem, smem]
        + [pl.BlockSpec(memory_space=pl.ANY)] * (groups * segments)
        + [vmem, vmem],
        out_specs=(vmem, vmem),
        scratch_shapes=[
            pltpu.VMEM((blocks * slots, half_rows, size), jnp.float32),
            pltpu.VMEM((blocks, 2 * half_rows, slots * size), jnp.bfloat16),
            pltpu.VMEM((2, modes * half_rows, row_width), jnp.bfloat16),
            pltpu.VMEM((2, modes * half_rows, row_width), jnp.bfloat16),
            pltpu.SemaphoreType.DMA((blocks * slots, segments)),
        ],
        compiler_params=pltpu.CompilerParams(vmem_limit_bytes=40 << 20),
        cost_estimate=pl.CostEstimate(
            flops=3_000_000_000, bytes_accessed=8_000_000, transcendentals=0
        ),
        name="step",
    )
    gap, renorm = gap_in, None
    for _ in range(ITERS):
        pieces = gather_pairwise(gap) if pairwise else gather_general(gap, half_groups)
        gap, renorm = step(meta, source, *pieces, weights, table)
    return (gap, renorm)


def solution(mesh):
    return jax.shard_map(
        on_device,
        mesh=mesh,
        in_specs=(
            P(("parts", "freq"), "state"),
            P(("parts", "state"), None, None, None, None),
            P(("parts", "state"), None),
            P(("parts", "state")),
            P("parts"),
            P("parts"),
        ),
        out_specs=(P(("parts", "freq"), "state"), P(("parts", "freq"), "state")),
        check_vma=False,
    )
```

time: 170 us -> 49.8 us (0.29)
  waiting for transfers between devices: 114 us -> 20 us
  matrix products: 22.8 us -> 0 us
  between operations: 18.9 us -> 0.86 us
  Pallas kernels: 0 us -> 14.9 us
  starting transfers between devices: 0.35 us -> 8.76 us
  other arithmetic: 9.32 us -> 2.49 us
  local copies, waits for them, and re-layouts: 4.76 us -> 2.59 us
    reduce_scatter x2 -> x0, waiting for transfers between devices: 88 us -> none  [on_device(): lax.psum_scatter(jnp.einsum('vnm,vqms->nqs', weights, local_terms, precis...]
    all_gather x2 -> x0, waiting for transfers between devices: 25.6 us -> none  [on_device(): everyone = lax.all_gather(ratios, 'state', axis=2, tiled=True)]
    dot_general x10 -> x0, matrix products: 22.8 us -> none  [the longest x2 19.9 us: on_device(): jnp.einsum('vnm,vqms->nqs', weights, local_terms, precision=lax.Precision...]
    ppermute x0 -> x14, waiting for transfers between devices: none -> 20 us  [the longest x2 11.6 us: gather_pairwise(): diagonal = lax.ppermute(gap, ('freq', 'state'), joint)]
    pallas_call x0 -> x3, Pallas kernels: none -> 14.9 us  [the longest x2 13 us: on_device(): gap, renorm = step(meta, source, *pieces, weights, table)]
    ppermute x0 -> x14, starting transfers between devices: none -> 8.76 us  [the longest x2 3.52 us: gather_pairwise(): along_x = lax.ppermute(gap, 'state', swapped(4, 2))]
    another operation x5 -> x1, other arithmetic: 3.94 us -> 0.01 us  [on_device(): jnp.stack([holder.reshape(-1), (column_place % blocks).reshape(-1), live....]
    unnamed x0 -> x6, local copies, waits for them, and re-layouts: none -> 2.33 us
  transfers between devices with their start and end apart: 4 -> 14, of which waited for: 4 -> 8; matrix products, arithmetic and copies ran while one was open for 3% -> 6% of each run, Pallas kernels for 0% -> 4%
where the time goes in v1:
time: 49.8 us; the launch traced here: 49.6 us
  waiting for transfers between devices  20 us (40%)
  Pallas kernels  14.9 us (30%)
  starting transfers between devices  8.76 us (18%)
  local copies, waits for them, and re-layouts  2.59 us (5%)
  other arithmetic  2.49 us (5%)
  between operations  0.86 us (2%)
    pallas_call x2, Pallas kernels, on_device(): gap, renorm = step(meta, source, *pieces, weights, table)  13 us
    ppermute x2, waiting for transfers between devices, gather_pairwise(): diagonal = lax.ppermute(gap, ('freq', 'state'), joint)  11.6 us
    ppermute x2, waiting for transfers between devices, gather_pairwise(): along_x = lax.ppermute(gap, 'state', swapped(4, 2))  4.79 us
    ppermute x2, starting transfers between devices, gather_pairwise(): along_x = lax.ppermute(gap, 'state', swapped(4, 2))  3.52 us
    ppermute x8, waiting for transfers between devices, gather_pairwise(): core = lambda value: lax.ppermute(value, 'state', swapped(4, 1))  2.87 us
    ppermute x2, starting transfers between devices, gather_pairwise(): diagonal = lax.ppermute(gap, ('freq', 'state'), joint)  2.78 us
    unnamed x6, local copies, waits for them, and re-layouts  2.33 us
    ppermute x2, starting transfers between devices, gather_pairwise(): along_z = lax.ppermute(gap, 'freq', swapped(4, 1))  1.87 us
  transfers between devices with their start and end apart: 14, of which 8 were waited for; matrix products, arithmetic and copies ran while one was open for 6% of the time, Pallas kernels for 4%

profile of v1, /device:TPU:0, one launch (start us, length us, event | category | flops | bytes accessed | tf_op | source)
XLA Modules:
  0.0 49.6 jit_solution(7631825399743232314)
XLA Ops:
  0.6 3.0 %collective-permute-start.3 = (f32[128,512]{1,0:T(8,128)}, f32[128,512]{1,0:T(8,128)S(1)}, u32[]{:S(2)}, u32[]{:S(2)}) collective-permute-start(f32[128,512]{1,0:T(8,128)} %refs_0_.1), channel_id=1, source_target_pairs={{0,2},{1,3},{2,0},{3,1},{4,6},{5,7},{6,4},{7,5},{8,10},{9,11},{10,... | collective-permute-start | bytes 786440 | tf_op jit(solution)/shard_map/ppermute | solution.py:133
  3.6 0.0 collective-permute-start.1
  3.6 1.6 %collective-permute-start = (f32[128,512]{1,0:T(8,128)}, f32[128,512]{1,0:T(8,128)S(1)}, u32[]{:S(2)}, u32[]{:S(2)}) collective-permute-start(f32[128,512]{1,0:T(8,128)} %refs_0_.1), channel_id=1, source_target_pairs={{0,4},{4,0},{8,12},{12,8},{1,5},{5,1},{9,13},{13,9},{2,6},{6,2},{1... | collective-permute-start | bytes 786440 | tf_op jit(solution)/shard_map/ppermute | solution.py:134
  5.2 0.0 collective-permute-start.4
  5.3 0.8 %select_reduce_fusion = s32[16]{0:T(128)S(1)} fusion(s32[16]{0:T(128)} %param.10), kind=kLoop, calls=%fused_computation | loop fusion | flops 752 | bytes 128 | tf_op jit(solution)/shard_map/reduce_sum | solution.py:173
  6.0 0.9 %select_reduce_fusion.1 = s32[4,2]{0,1:T(2,128)S(1)} fusion(s32[16]{0:T(128)S(1)} %select_reduce_fusion, s32[4,2]{0,1:T(2,128)} %param.8), kind=kLoop, calls=%fused_computation.2 | loop fusion | flops 376 | bytes 128 | tf_op jit(solution)/shard_map/reduce_sum | solution.py:176
  6.9 0.1 copy.10
  7.0 0.1 reduce_sum.22
  7.1 0.7 %fusion = s32[4,2]{1,0:T(4,128)S(1)} fusion(s32[4]{0:T(128)} %param.9), kind=kLoop, calls=%fused_computation.6 | loop fusion | flops 16 | bytes 48 | tf_op jit(solution)/shard_map/convert_element_type | solution.py:180
  7.8 0.1 reshape.140
  7.9 0.1 add_multiply_fusion.meta
  8.0 1.7 %copy-done = bf16[4,2,9,128,128]{4,3,2,1,0:T(8,128)(2,1)S(1)} copy-done((bf16[4,2,9,128,128]{4,3,2,1,0:T(8,128)(2,1)S(1)}, bf16[4,2,9,128,128]{4,3,2,1,0:T(8,128)(2,1)}, u32[]{:S(2)}) %copy-start) | copy-done | bytes 2359320
  9.7 0.7 %copy-done.1 = f32[9]{0:T(128)S(1)} copy-done((f32[9]{0:T(128)S(1)}, f32[9]{0:T(128)}, u32[]{:S(2)}) %copy-start.1) | copy-done | bytes 60
  10.3 1.9 %tables.1 = (bf16[4,256,1152]{2,1,0:T(8,128)(2,1)S(1)}, bf16[2,256,2304]{2,1,0:T(8,128)(2,1)S(1)}) custom-call(s32[3]{0:T(128)S(1)} %add_multiply_fusion.meta, f32[9]{0:T(128)S(1)} %copy-done.1, bf16[4,2,9,128,128]{4,3,2,1,0:T(8,128)(2,1)S(1)} %copy-done), custom_call_target="tpu_custom_call" | custom-call | flops 10000000 | bytes 8000000 | tf_op jit(solution)/shard_map/tables/pallas_call | solution.py:199
  12.2 0.3 collective-permute-start.5
  12.5 0.5 collective-permute-done.refs_1_
  12.9 0.0 collective-permute-start.2
  13.0 5.0 %collective-permute-done.4.refs_5_ = f32[128,512]{1,0:T(8,128)S(1)} collective-permute-done((f32[128,512]{1,0:T(8,128)}, f32[128,512]{1,0:T(8,128)S(1)}, u32[]{:S(2)}, u32[]{:S(2)}) %collective-permute-start.4) | collective-permute-done | bytes 262176 | tf_op jit(solution)/shard_map/ppermute | solution.py:135
  18.0 0.0 collective-permute-start.6
  18.1 1.5 %collective-permute-done.6.refs_7_ = f32[128,512]{1,0:T(8,128)S(1)} collective-permute-done((f32[128,512]{1,0:T(8,128)S(1)}, f32[128,512]{1,0:T(8,128)S(1)}, u32[]{:S(2)}, u32[]{:S(2)}) %collective-permute-start.6) | collective-permute-done | bytes 262176 | tf_op jit(solution)/shard_map/ppermute | solution.py:131
  19.5 6.4 %step.2 = (f32[128,512]{1,0:T(8,128)S(1)}, f32[128,512]{1,0:T(8,128)}) custom-call(s32[3]{0:T(128)S(1)} %add_multiply_fusion.meta, s32[3,8]{1,0:T(4,128)S(1)} %pad_add_fusion.source, f32[128,512]{1,0:T(8,128)S(1)} %copy-done.2, f32[128,512]{1,0:T(8,128)S(1)} %collective-permute-done.refs_1_, f32[128,512]{1,0:T(8,128)S(1)} %collective-permute-done.1.refs_2_, ...), custom_call_target="tpu_custom_call" | custom-call | flops 3000000000 | bytes 8000000 | tf_op jit(solution)/shard_map/step/pallas_call | solution.py:234
  25.9 2.7 %collective-permute-start.11 = (f32[128,512]{1,0:T(8,128)S(1)}, f32[128,512]{1,0:T(8,128)S(1)}, u32[]{:S(2)}, u32[]{:S(2)}) collective-permute-start(f32[128,512]{1,0:T(8,128)S(1)} %get-tuple-element.7.refs_0_), channel_id=1, source_target_pairs={{0,6},{1,7},{2,4},{3,5},{4,2},{5,3},{6,0},{7,1},{8,14},{9,15},{10,... | collective-permute-start | bytes 786440 | tf_op jit(solution)/shard_map/ppermute | solution.py:135
  28.7 0.5 %collective-permute-start.10 = (f32[128,512]{1,0:T(8,128)S(1)}, f32[128,512]{1,0:T(8,128)S(1)}, u32[]{:S(2)}, u32[]{:S(2)}) collective-permute-start(f32[128,512]{1,0:T(8,128)S(1)} %get-tuple-element.7.refs_0_), channel_id=1, source_target_pairs={{0,2},{1,3},{2,0},{3,1},{4,6},{5,7},{6,4},{7,5},{8,10},{9,11},{10,... | collective-permute-start | bytes 786440 | tf_op jit(solution)/shard_map/ppermute | solution.py:133
  29.2 0.3 collective-permute-start.7
  29.5 6.6 %collective-permute-done.11.refs_5_ = f32[128,512]{1,0:T(8,128)S(1)} collective-permute-done((f32[128,512]{1,0:T(8,128)S(1)}, f32[128,512]{1,0:T(8,128)S(1)}, u32[]{:S(2)}, u32[]{:S(2)}) %collective-permute-start.11) | collective-permute-done | bytes 262176 | tf_op jit(solution)/shard_map/ppermute | solution.py:135
  36.1 4.8 %collective-permute-done.10.refs_4_ = f32[128,512]{1,0:T(8,128)S(1)} collective-permute-done((f32[128,512]{1,0:T(8,128)S(1)}, f32[128,512]{1,0:T(8,128)S(1)}, u32[]{:S(2)}, u32[]{:S(2)}) %collective-permute-start.10) | collective-permute-done | bytes 262176 | tf_op jit(solution)/shard_map/ppermute | solution.py:133
  40.9 0.0 collective-permute-start.12
  40.9 0.2 collective-permute-done.7.refs_1_
  41.1 0.3 collective-permute-start.9
  41.4 1.0 %collective-permute-done.12.refs_6_ = f32[128,512]{1,0:T(8,128)S(1)} collective-permute-done((f32[128,512]{1,0:T(8,128)S(1)}, f32[128,512]{1,0:T(8,128)S(1)}, u32[]{:S(2)}, u32[]{:S(2)}) %collective-permute-start.12) | collective-permute-done | bytes 262176 | tf_op jit(solution)/shard_map/ppermute | solution.py:131
  42.4 0.4 collective-permute-done.9.refs_3_
  42.8 6.6 %step.3 = (f32[128,512]{1,0:T(8,128)}, f32[128,512]{1,0:T(8,128)}) custom-call(s32[3]{0:T(128)S(1)} %add_multiply_fusion.meta, s32[3,8]{1,0:T(4,128)S(1)} %pad_add_fusion.source, f32[128,512]{1,0:T(8,128)S(1)} %get-tuple-element.7.refs_0_, f32[128,512]{1,0:T(8,128)S(1)} %collective-permute-done.7.refs_1_, f32[128,512]{1,0:T(8,128)S(1)} %collective-permute-done.8.refs_2_, ...), custom_call_target="tpu_custom_call" | custom-call | flops 3000000000 | bytes 8000000 | tf_op jit(solution)/shard_map/step/pallas_call | solution.py:234
  (14 shorter events, 0.0 us)
Async XLA Ops:
  0.6 11.6 %collective-permute-start.3 = (f32[128,512]{1,0:T(8,128)}, f32[128,512]{1,0:T(8,128)S(1)}, u32[]{:S(2)}, u32[]{:S(2)}) collective-permute-start(f32[128,512]{1,0:T(8,128)} %refs_0_.1), channel_id=1, source_target_pairs={{0,2},{1,3},{2,0},{3,1},{4,6},{5,7},{6,4},{7,5},{8,10},{9,11},{10,... | collective-permute-start | bytes 786440 | tf_op jit(solution)/shard_map/ppermute | solution.py:133
  3.6 14.4 %collective-permute-start.1 = (f32[128,512]{1,0:T(8,128)}, f32[128,512]{1,0:T(8,128)S(1)}, u32[]{:S(2)}, u32[]{:S(2)}) collective-permute-start(f32[128,512]{1,0:T(8,128)} %refs_0_.1), channel_id=1, source_target_pairs={{0,1},{1,0},{2,3},{3,2},{4,5},{5,4},{6,7},{7,6},{8,9},{9,8},{10,11... | collective-permute-start | bytes 786440 | tf_op jit(solution)/shard_map/ppermute | solution.py:131
  3.6 9.3 %collective-permute-start = (f32[128,512]{1,0:T(8,128)}, f32[128,512]{1,0:T(8,128)S(1)}, u32[]{:S(2)}, u32[]{:S(2)}) collective-permute-start(f32[128,512]{1,0:T(8,128)} %refs_0_.1), channel_id=1, source_target_pairs={{0,4},{4,0},{8,12},{12,8},{1,5},{5,1},{9,13},{13,9},{2,6},{6,2},{1... | collective-permute-start | bytes 786440 | tf_op jit(solution)/shard_map/ppermute | solution.py:134
  5.2 12.8 %collective-permute-start.4 = (f32[128,512]{1,0:T(8,128)}, f32[128,512]{1,0:T(8,128)S(1)}, u32[]{:S(2)}, u32[]{:S(2)}) collective-permute-start(f32[128,512]{1,0:T(8,128)} %refs_0_.1), channel_id=1, source_target_pairs={{0,6},{1,7},{2,4},{3,5},{4,2},{5,3},{6,0},{7,1},{8,14},{9,15},{10,... | collective-permute-start | bytes 786440 | tf_op jit(solution)/shard_map/ppermute | solution.py:135
  8.0 1.7 %copy-start = (bf16[4,2,9,128,128]{4,3,2,1,0:T(8,128)(2,1)S(1)}, bf16[4,2,9,128,128]{4,3,2,1,0:T(8,128)(2,1)}, u32[]{:S(2)}) copy-start(bf16[4,2,9,128,128]{4,3,2,1,0:T(8,128)(2,1)} %coupling.1) | copy-start | bytes 7077892
  9.7 0.7 %copy-start.1 = (f32[9]{0:T(128)S(1)}, f32[9]{0:T(128)}, u32[]{:S(2)}) copy-start(f32[9]{0:T(128)} %phonon.1) | copy-start | bytes 112
  10.3 9.2 %copy-start.2 = (f32[128,512]{1,0:T(8,128)S(1)}, f32[128,512]{1,0:T(8,128)}, u32[]{:S(2)}) copy-start(f32[128,512]{1,0:T(8,128)} %refs_0_.1) | copy-start | bytes 786436
  12.2 5.8 %collective-permute-start.5 = (f32[128,512]{1,0:T(8,128)S(1)}, f32[128,512]{1,0:T(8,128)S(1)}, u32[]{:S(2)}, u32[]{:S(2)}) collective-permute-start(f32[128,512]{1,0:T(8,128)S(1)} %collective-permute-done.3.refs_4_), channel_id=1, source_target_pairs={{0,1},{1,0},{2,3},{3,2},{4,5},{5,4},{6,7},{7,6},{8,9},{9,8},{10,11... | collective-permute-start | bytes 786440 | tf_op jit(solution)/shard_map/ppermute | solution.py:131
  12.9 5.1 %collective-permute-start.2 = (f32[128,512]{1,0:T(8,128)S(1)}, f32[128,512]{1,0:T(8,128)S(1)}, u32[]{:S(2)}, u32[]{:S(2)}) collective-permute-start(f32[128,512]{1,0:T(8,128)S(1)} %collective-permute-done.refs_1_), channel_id=1, source_target_pairs={{0,1},{1,0},{2,3},{3,2},{4,5},{5,4},{6,7},{7,6},{8,9},{9,8},{10,11... | collective-permute-start | bytes 786440 | tf_op jit(solution)/shard_map/ppermute | solution.py:131
  18.0 1.5 %collective-permute-start.6 = (f32[128,512]{1,0:T(8,128)S(1)}, f32[128,512]{1,0:T(8,128)S(1)}, u32[]{:S(2)}, u32[]{:S(2)}) collective-permute-start(f32[128,512]{1,0:T(8,128)S(1)} %collective-permute-done.4.refs_5_), channel_id=1, source_target_pairs={{0,1},{1,0},{2,3},{3,2},{4,5},{5,4},{6,7},{7,6},{8,9},{9,8},{10,11... | collective-permute-start | bytes 786440 | tf_op jit(solution)/shard_map/ppermute | solution.py:131
  25.9 10.2 %collective-permute-start.11 = (f32[128,512]{1,0:T(8,128)S(1)}, f32[128,512]{1,0:T(8,128)S(1)}, u32[]{:S(2)}, u32[]{:S(2)}) collective-permute-start(f32[128,512]{1,0:T(8,128)S(1)} %get-tuple-element.7.refs_0_), channel_id=1, source_target_pairs={{0,6},{1,7},{2,4},{3,5},{4,2},{5,3},{6,0},{7,1},{8,14},{9,15},{10,... | collective-permute-start | bytes 786440 | tf_op jit(solution)/shard_map/ppermute | solution.py:135
  28.7 12.2 %collective-permute-start.10 = (f32[128,512]{1,0:T(8,128)S(1)}, f32[128,512]{1,0:T(8,128)S(1)}, u32[]{:S(2)}, u32[]{:S(2)}) collective-permute-start(f32[128,512]{1,0:T(8,128)S(1)} %get-tuple-element.7.refs_0_), channel_id=1, source_target_pairs={{0,2},{1,3},{2,0},{3,1},{4,6},{5,7},{6,4},{7,5},{8,10},{9,11},{10,... | collective-permute-start | bytes 786440 | tf_op jit(solution)/shard_map/ppermute | solution.py:133
  29.2 11.9 %collective-permute-start.7 = (f32[128,512]{1,0:T(8,128)S(1)}, f32[128,512]{1,0:T(8,128)S(1)}, u32[]{:S(2)}, u32[]{:S(2)}) collective-permute-start(f32[128,512]{1,0:T(8,128)S(1)} %get-tuple-element.7.refs_0_), channel_id=1, source_target_pairs={{0,4},{4,0},{8,12},{12,8},{1,5},{5,1},{9,13},{13,9},{2,6},{6,2},{1... | collective-permute-start | bytes 786440 | tf_op jit(solution)/shard_map/ppermute | solution.py:134
  29.5 11.9 %collective-permute-start.8 = (f32[128,512]{1,0:T(8,128)S(1)}, f32[128,512]{1,0:T(8,128)S(1)}, u32[]{:S(2)}, u32[]{:S(2)}) collective-permute-start(f32[128,512]{1,0:T(8,128)S(1)} %get-tuple-element.7.refs_0_), channel_id=1, source_target_pairs={{0,1},{1,0},{2,3},{3,2},{4,5},{5,4},{6,7},{7,6},{8,9},{9,8},{10,11... | collective-permute-start | bytes 786440 | tf_op jit(solution)/shard_map/ppermute | solution.py:131
  36.1 5.3 %collective-permute-start.13 = (f32[128,512]{1,0:T(8,128)S(1)}, f32[128,512]{1,0:T(8,128)S(1)}, u32[]{:S(2)}, u32[]{:S(2)}) collective-permute-start(f32[128,512]{1,0:T(8,128)S(1)} %collective-permute-done.11.refs_5_), channel_id=1, source_target_pairs={{0,1},{1,0},{2,3},{3,2},{4,5},{5,4},{6,7},{7,6},{8,9},{9,8},{10,11... | collective-permute-start | bytes 786440 | tf_op jit(solution)/shard_map/ppermute | solution.py:131
  40.9 1.5 %collective-permute-start.12 = (f32[128,512]{1,0:T(8,128)S(1)}, f32[128,512]{1,0:T(8,128)S(1)}, u32[]{:S(2)}, u32[]{:S(2)}) collective-permute-start(f32[128,512]{1,0:T(8,128)S(1)} %collective-permute-done.10.refs_4_), channel_id=1, source_target_pairs={{0,1},{1,0},{2,3},{3,2},{4,5},{5,4},{6,7},{7,6},{8,9},{9,8},{10,11... | collective-permute-start | bytes 786440 | tf_op jit(solution)/shard_map/ppermute | solution.py:131
  41.1 1.7 %collective-permute-start.9 = (f32[128,512]{1,0:T(8,128)S(1)}, f32[128,512]{1,0:T(8,128)S(1)}, u32[]{:S(2)}, u32[]{:S(2)}) collective-permute-start(f32[128,512]{1,0:T(8,128)S(1)} %collective-permute-done.7.refs_1_), channel_id=1, source_target_pairs={{0,1},{1,0},{2,3},{3,2},{4,5},{5,4},{6,7},{7,6},{8,9},{9,8},{10,11... | collective-permute-start | bytes 786440 | tf_op jit(solution)/shard_map/ppermute | solution.py:131

commit v2 on v1

--- a/solution.py
+++ b/solution.py
@@ -10,6 +10,9 @@
 ITERS = 2
 CUTOFF = 4.0
 LANES = 128
+GAP_LIMIT = 10.0
+CODE_LIMIT = 32767.0
+CODE_POWER = 5
 
 
 def omega_of(index, freq_count):
@@ -22,6 +25,23 @@
     for number, start in enumerate(range(segment_rows, shape[axis], segment_rows), 1):
         index = jnp.where(at >= start, at - start + meta[1 + number], index)
     return omega_of(index, freq_count)
+
+
+def encoded(gap):
+    share = jnp.minimum(jnp.abs(gap) * (1.0 / GAP_LIMIT), 1.0)
+    root = jnp.exp2(jnp.log2(jnp.maximum(share, 1e-37)) * (1.0 / CODE_POWER))
+    code = jnp.floor(root * CODE_LIMIT + 0.5)
+    return jnp.where(gap < 0, -code, code).astype(jnp.int32).astype(jnp.int16)
+
+
+def decoded(code):
+    root = code.astype(jnp.float32) * (1.0 / CODE_LIMIT)
+    square = root * root
+    return (root * GAP_LIMIT) * (square * square)
+
+
+def encode_kernel(gap, code):
+    code[...] = encoded(gap[...])
 
 
 def tables_kernel(dims, meta, phonon, coupling, weights, table):
@@ -53,12 +73,12 @@
                 ] = coupling[block, slot, mode].T
 
 
-def step_kernel(dims, groups, segments, meta, source, *refs):
+def step_kernel(dims, groups, segments, coded, final, meta, source, *refs):
     freq_count, half_rows, segment_rows, padded_rows, modes = dims
     pieces = refs[: groups * segments]
-    weights, table, gap_out, renorm_out, fetched, ratios, high, low, sems = refs[
-        groups * segments :
-    ]
+    refs = refs[groups * segments :]
+    weights, table, gap_out = refs[:3]
+    fetched, ratios, high, low, sems = refs[-5:]
     own_rows = gap_out.shape[0]
     blocks = weights.shape[0]
     size = LANES
@@ -87,7 +107,7 @@
             pair = block * slots + slot
             for segment in range(segments):
                 copy(pair, 0, segment).wait()
-            gap = fetched[pair]
+            gap = decoded(fetched[pair]) if coded else fetched[pair]
             live = source[2, pair].astype(jnp.float32)
             inverse = lax.rsqrt(square + gap * gap) * live
             lanes = slice(slot * size, (slot + 1) * size)
@@ -119,8 +139,12 @@
     row = lax.broadcasted_iota(jnp.int32, gap_out.shape, 0) + meta[0]
     temperature = CUTOFF / freq_count
     renorm = 1.0 + temperature * summed[1] / omega_of(row, freq_count)
-    renorm_out[...] = renorm
-    gap_out[...] = temperature * summed[0] / renorm
+    gap = temperature * summed[0] / renorm
+    if final:
+        refs[3][...] = renorm
+        gap_out[...] = gap
+    else:
+        gap_out[...] = encoded(gap) if coded else gap
 
 
 def swapped(axis_size, bit):
@@ -208,31 +232,47 @@
         cost_estimate=pl.CostEstimate(flops=10_000_000, bytes_accessed=8_000_000, transcendentals=0),
         name="tables",
     )(meta, phonon, coupling)
-    step = pl.pallas_call(
-        functools.partial(step_kernel, dims, groups, segments),
-        out_shape=(jax.ShapeDtypeStruct(gap_in.shape, jnp.float32),) * 2,
-        in_specs=[smem, smem]
-        + [pl.BlockSpec(memory_space=pl.ANY)] * (groups * segments)
-        + [vmem, vmem],
-        out_specs=(vmem, vmem),
-        scratch_shapes=[
-            pltpu.VMEM((blocks * slots, half_rows, size), jnp.float32),
-            pltpu.VMEM((blocks, 2 * half_rows, slots * size), jnp.bfloat16),
-            pltpu.VMEM((2, modes * half_rows, row_width), jnp.bfloat16),
-            pltpu.VMEM((2, modes * half_rows, row_width), jnp.bfloat16),
-            pltpu.SemaphoreType.DMA((blocks * slots, segments)),
-        ],
-        compiler_params=pltpu.CompilerParams(vmem_limit_bytes=40 << 20),
-        cost_estimate=pl.CostEstimate(
-            flops=3_000_000_000, bytes_accessed=8_000_000, transcendentals=0
-        ),
-        name="step",
-    )
-    gap, renorm = gap_in, None
-    for _ in range(ITERS):
-        pieces = gather_pairwise(gap) if pairwise else gather_general(gap, half_groups)
-        gap, renorm = step(meta, source, *pieces, weights, table)
-    return (gap, renorm)
+    coded = pairwise
+    link_type = jnp.int16 if coded else jnp.float32
+
+    def step(last, pieces):
+        full = jax.ShapeDtypeStruct(gap_in.shape, jnp.float32)
+        passed = jax.ShapeDtypeStruct(gap_in.shape, link_type)
+        return pl.pallas_call(
+            functools.partial(step_kernel, dims, groups, segments, coded, last),
+            out_shape=(full, full) if last else passed,
+            in_specs=[smem, smem]
+            + [pl.BlockSpec(memory_space=pl.ANY)] * (groups * segments)
+            + [vmem, vmem],
+            out_specs=(vmem, vmem) if last else vmem,
+            scratch_shapes=[
+                pltpu.VMEM((blocks * slots, half_rows, size), link_type),
+                pltpu.VMEM((blocks, 2 * half_rows, slots * size), jnp.bfloat16),
+                pltpu.VMEM((2, modes * half_rows, row_width), jnp.bfloat16),
+                pltpu.VMEM((2, modes * half_rows, row_width), jnp.bfloat16),
+                pltpu.SemaphoreType.DMA((blocks * slots, segments)),
+            ],
+            compiler_params=pltpu.CompilerParams(vmem_limit_bytes=40 << 20),
+            cost_estimate=pl.CostEstimate(
+                flops=3_000_000_000, bytes_accessed=8_000_000, transcendentals=0
+            ),
+            name="step",
+        )(meta, source, *pieces, weights, table)
+
+    passed = gap_in
+    if coded:
+        passed = pl.pallas_call(
+            encode_kernel,
+            out_shape=jax.ShapeDtypeStruct(gap_in.shape, link_type),
+            in_specs=[vmem],
+            out_specs=vmem,
+            name="encode",
+        )(gap_in)
+    for iteration in range(ITERS):
+        last = iteration == ITERS - 1
+        pieces = gather_pairwise(passed) if pairwise else gather_general(passed, half_groups)
+        passed = step(last, pieces)
+    return passed
 
 
 def solution(mesh):

time: 49.8 us -> 41.8 us (0.84)
  waiting for transfers between devices: 20 us -> 10.4 us
  Pallas kernels: 14.9 us -> 16.3 us
    ppermute x2, waiting for transfers between devices: 11.6 us -> 4.83 us  [gather_pairwise(): diagonal = lax.ppermute(gap, ('freq', 'state'), joint)]
    ppermute x2, starting transfers between devices: 2.78 us -> 5.76 us  [gather_pairwise(): diagonal = lax.ppermute(gap, ('freq', 'state'), joint)]
    ppermute x8, waiting for transfers between devices: 2.87 us -> 1.03 us  [gather_pairwise(): core = lambda value: lax.ppermute(value, 'state', swapped(4, 1))]
    ppermute x2, starting transfers between devices: 3.52 us -> 1.97 us  [gather_pairwise(): along_x = lax.ppermute(gap, 'state', swapped(4, 2))]
    ppermute x2, starting transfers between devices: 1.87 us -> 0.34 us  [gather_pairwise(): along_z = lax.ppermute(gap, 'freq', swapped(4, 1))]
    pallas_call x2 -> x3, Pallas kernels: 13 us -> 14.4 us  [the longest x2 12.7 us: step(): pl.pallas_call(functools.partial(step_kernel, dims, groups, segments, cod...]
  transfers between devices with their start and end apart: 14 -> 14, of which waited for: 8 -> 7; matrix products, arithmetic and copies ran while one was open for 6% -> 7% of each run, Pallas kernels for 4% -> 4%
where the time goes in v2:
time: 41.8 us; the launch traced here: 41.6 us
  Pallas kernels  16.3 us (39%)
  waiting for transfers between devices  10.4 us (25%)
  starting transfers between devices  8.91 us (21%)
  local copies, waits for them, and re-layouts  2.59 us (6%)
  other arithmetic  2.49 us (6%)
  between operations  0.87 us (2%)
    pallas_call x2, Pallas kernels, step(): pl.pallas_call(functools.partial(step_kernel, dims, groups, segments, cod...  12.7 us
    ppermute x2, starting transfers between devices, gather_pairwise(): diagonal = lax.ppermute(gap, ('freq', 'state'), joint)  5.76 us
    ppermute x2, waiting for transfers between devices, gather_pairwise(): diagonal = lax.ppermute(gap, ('freq', 'state'), joint)  4.83 us
    ppermute x2, waiting for transfers between devices, gather_pairwise(): along_x = lax.ppermute(gap, 'state', swapped(4, 2))  4.34 us
    unnamed x6, local copies, waits for them, and re-layouts  2.33 us
    ppermute x2, starting transfers between devices, gather_pairwise(): along_x = lax.ppermute(gap, 'state', swapped(4, 2))  1.97 us
    pallas_call x1, Pallas kernels, on_device(): pl.pallas_call(functools.partial(tables_kernel, dims), out_shape=(jax.Sha...  1.87 us
    pallas_call x1, Pallas kernels, on_device(): pl.pallas_call(encode_kernel, out_shape=jax.ShapeDtypeStruct(gap_in.shape...  1.75 us
  transfers between devices with their start and end apart: 14, of which 7 were waited for; matrix products, arithmetic and copies ran while one was open for 7% of the time, Pallas kernels for 4%

profile of v2, /device:TPU:0, one launch (start us, length us, event | category | flops | bytes accessed | tf_op | source)
XLA Modules:
  0.0 41.6 jit_solution(3969834412527273398)
XLA Ops:
  0.6 1.7 %encode.1.refs_0_ = s16[128,512]{1,0:T(8,128)(2,1)} custom-call(f32[128,512]{1,0:T(8,128)} %gap.1), custom_call_target="tpu_custom_call" | custom-call | tf_op jit(solution)/shard_map/encode/pallas_call | solution.py:264
  2.4 4.0 %collective-permute-start.4 = (s16[128,512]{1,0:T(8,128)(2,1)}, s16[128,512]{1,0:T(8,128)(2,1)S(1)}, u32[]{:S(2)}, u32[]{:S(2)}) collective-permute-start(s16[128,512]{1,0:T(8,128)(2,1)} %encode.1.refs_0_), channel_id=1, source_target_pairs={{0,6},{1,7},{2,4},{3,5},{4,2},{5,3},{6,0},{7,1},{8,14},{9,15},{10,... | collective-permute-start | bytes 393224 | tf_op jit(solution)/shard_map/ppermute | solution.py:159
  6.3 0.5 %collective-permute-start.3 = (s16[128,512]{1,0:T(8,128)(2,1)}, s16[128,512]{1,0:T(8,128)(2,1)S(1)}, u32[]{:S(2)}, u32[]{:S(2)}) collective-permute-start(s16[128,512]{1,0:T(8,128)(2,1)} %encode.1.refs_0_), channel_id=1, source_target_pairs={{0,2},{1,3},{2,0},{3,1},{4,6},{5,7},{6,4},{7,5},{8,10},{9,11},{10,... | collective-permute-start | bytes 393224 | tf_op jit(solution)/shard_map/ppermute | solution.py:157
  6.9 0.0 collective-permute-start.1
  6.9 0.0 collective-permute-start
  6.9 0.8 %select_reduce_fusion = s32[16]{0:T(128)S(1)} fusion(s32[16]{0:T(128)} %param.10), kind=kLoop, calls=%fused_computation | loop fusion | flops 752 | bytes 128 | tf_op jit(solution)/shard_map/reduce_sum | solution.py:197
  7.7 0.9 %select_reduce_fusion.1 = s32[4,2]{0,1:T(2,128)S(1)} fusion(s32[16]{0:T(128)S(1)} %select_reduce_fusion, s32[4,2]{0,1:T(2,128)} %param.8), kind=kLoop, calls=%fused_computation.2 | loop fusion | flops 376 | bytes 128 | tf_op jit(solution)/shard_map/reduce_sum | solution.py:200
  8.6 0.1 copy.10
  8.7 0.1 reduce_sum.22
  8.7 0.7 %fusion = s32[4,2]{1,0:T(4,128)S(1)} fusion(s32[4]{0:T(128)} %param.9), kind=kLoop, calls=%fused_computation.6 | loop fusion | flops 16 | bytes 48 | tf_op jit(solution)/shard_map/convert_element_type | solution.py:204
  9.5 1.1 %collective-permute-done.4.refs_5_ = s16[128,512]{1,0:T(8,128)(2,1)S(1)} collective-permute-done((s16[128,512]{1,0:T(8,128)(2,1)}, s16[128,512]{1,0:T(8,128)(2,1)S(1)}, u32[]{:S(2)}, u32[]{:S(2)}) %collective-permute-start.4) | collective-permute-done | bytes 131104 | tf_op jit(solution)/shard_map/ppermute | solution.py:159
  10.6 2.3 %collective-permute-done.3.refs_4_ = s16[128,512]{1,0:T(8,128)(2,1)S(1)} collective-permute-done((s16[128,512]{1,0:T(8,128)(2,1)}, s16[128,512]{1,0:T(8,128)(2,1)S(1)}, u32[]{:S(2)}, u32[]{:S(2)}) %collective-permute-start.3) | collective-permute-done | bytes 131104 | tf_op jit(solution)/shard_map/ppermute | solution.py:157
  12.8 0.0 collective-permute-start.5
  12.9 0.2 collective-permute-done.refs_1_
  13.1 0.3 collective-permute-start.2
  13.4 0.1 add_multiply_fusion.meta
  13.4 0.1 reshape.140
  13.5 1.7 %copy-done = bf16[4,2,9,128,128]{4,3,2,1,0:T(8,128)(2,1)S(1)} copy-done((bf16[4,2,9,128,128]{4,3,2,1,0:T(8,128)(2,1)S(1)}, bf16[4,2,9,128,128]{4,3,2,1,0:T(8,128)(2,1)}, u32[]{:S(2)}) %copy-start) | copy-done | bytes 2359320
  15.2 0.7 %copy-done.2 = f32[9]{0:T(128)S(1)} copy-done((f32[9]{0:T(128)S(1)}, f32[9]{0:T(128)}, u32[]{:S(2)}) %copy-start.2) | copy-done | bytes 60
  15.8 1.9 %tables.1 = (bf16[4,256,1152]{2,1,0:T(8,128)(2,1)S(1)}, bf16[2,256,2304]{2,1,0:T(8,128)(2,1)S(1)}) custom-call(s32[3]{0:T(128)S(1)} %add_multiply_fusion.meta, f32[9]{0:T(128)S(1)} %copy-done.2, bf16[4,2,9,128,128]{4,3,2,1,0:T(8,128)(2,1)S(1)} %copy-done), custom_call_target="tpu_custom_call" | custom-call | flops 10000000 | bytes 8000000 | tf_op jit(solution)/shard_map/tables/pallas_call | solution.py:223
  17.7 0.0 collective-permute-done.1.refs_2_
  17.8 5.9 %step.2.refs_0_ = s16[128,512]{1,0:T(8,128)(2,1)S(1)} custom-call(s32[3]{0:T(128)S(1)} %add_multiply_fusion.meta, s32[3,8]{1,0:T(4,128)S(1)} %pad_add_fusion.source, s16[128,512]{1,0:T(8,128)(2,1)S(1)} %copy-done.1, s16[128,512]{1,0:T(8,128)(2,1)S(1)} %collective-permute-done.refs_1_, s16[128,512]{1,0:T(8,128)(2,1)S(1)} %collective-permute-done.1.refs_2_, ...), custom_call_target="tpu_custom_call" | custom-call | flops 3000000000 | bytes 8000000 | tf_op jit(solution)/shard_map/step/pallas_call | solution.py:241
  23.7 1.8 %collective-permute-start.11 = (s16[128,512]{1,0:T(8,128)(2,1)S(1)}, s16[128,512]{1,0:T(8,128)(2,1)S(1)}, u32[]{:S(2)}, u32[]{:S(2)}) collective-permute-start(s16[128,512]{1,0:T(8,128)(2,1)S(1)} %step.2.refs_0_), channel_id=1, source_target_pairs={{0,6},{1,7},{2,4},{3,5},{4,2},{5,3},{6,0},{7,1},{8,14},{9,15},{10,... | collective-permute-start | bytes 393224 | tf_op jit(solution)/shard_map/ppermute | solution.py:159
  25.5 1.4 %collective-permute-start.10 = (s16[128,512]{1,0:T(8,128)(2,1)S(1)}, s16[128,512]{1,0:T(8,128)(2,1)S(1)}, u32[]{:S(2)}, u32[]{:S(2)}) collective-permute-start(s16[128,512]{1,0:T(8,128)(2,1)S(1)} %step.2.refs_0_), channel_id=1, source_target_pairs={{0,2},{1,3},{2,0},{3,1},{4,6},{5,7},{6,4},{7,5},{8,10},{9,11},{10,... | collective-permute-start | bytes 393224 | tf_op jit(solution)/shard_map/ppermute | solution.py:157
  27.0 0.3 collective-permute-start.7
  27.3 3.8 %collective-permute-done.11.refs_5_ = s16[128,512]{1,0:T(8,128)(2,1)S(1)} collective-permute-done((s16[128,512]{1,0:T(8,128)(2,1)S(1)}, s16[128,512]{1,0:T(8,128)(2,1)S(1)}, u32[]{:S(2)}, u32[]{:S(2)}) %collective-permute-start.11) | collective-permute-done | bytes 131104 | tf_op jit(solution)/shard_map/ppermute | solution.py:159
  31.1 2.1 %collective-permute-done.10.refs_4_ = s16[128,512]{1,0:T(8,128)(2,1)S(1)} collective-permute-done((s16[128,512]{1,0:T(8,128)(2,1)S(1)}, s16[128,512]{1,0:T(8,128)(2,1)S(1)}, u32[]{:S(2)}, u32[]{:S(2)}) %collective-permute-start.10) | collective-permute-done | bytes 131104 | tf_op jit(solution)/shard_map/ppermute | solution.py:157
  33.1 0.0 collective-permute-start.12
  33.1 0.5 %collective-permute-start.9 = (s16[128,512]{1,0:T(8,128)(2,1)S(1)}, s16[128,512]{1,0:T(8,128)(2,1)S(1)}, u32[]{:S(2)}, u32[]{:S(2)}) collective-permute-start(s16[128,512]{1,0:T(8,128)(2,1)S(1)} %collective-permute-done.7.refs_1_), channel_id=1, source_target_pairs={{0,1},{1,0},{2,3},{3,2},{4,5},{5,4},{6,7},{7,6},{8,9},{9,8},{10,11... | collective-permute-start | bytes 393224 | tf_op jit(solution)/shard_map/ppermute | solution.py:155
  33.6 0.8 %collective-permute-done.12.refs_6_ = s16[128,512]{1,0:T(8,128)(2,1)S(1)} collective-permute-done((s16[128,512]{1,0:T(8,128)(2,1)S(1)}, s16[128,512]{1,0:T(8,128)(2,1)S(1)}, u32[]{:S(2)}, u32[]{:S(2)}) %collective-permute-start.12) | collective-permute-done | bytes 131104 | tf_op jit(solution)/shard_map/ppermute | solution.py:155
  34.5 0.2 collective-permute-done.9.refs_3_
  34.7 6.8 %step.3 = (f32[128,512]{1,0:T(8,128)}, f32[128,512]{1,0:T(8,128)}) custom-call(s32[3]{0:T(128)S(1)} %add_multiply_fusion.meta, s32[3,8]{1,0:T(4,128)S(1)} %pad_add_fusion.source, s16[128,512]{1,0:T(8,128)(2,1)S(1)} %step.2.refs_0_, s16[128,512]{1,0:T(8,128)(2,1)S(1)} %collective-permute-done.7.refs_1_, s16[128,512]{1,0:T(8,128)(2,1)S(1)} %collective-permute-done.8.refs_2_, ...), custom_call_target="tpu_custom_call" | custom-call | flops 3000000000 | bytes 8000000 | tf_op jit(solution)/shard_map/step/pallas_call | solution.py:241
  (15 shorter events, 0.1 us)
Async XLA Ops:
  2.4 8.2 %collective-permute-start.4 = (s16[128,512]{1,0:T(8,128)(2,1)}, s16[128,512]{1,0:T(8,128)(2,1)S(1)}, u32[]{:S(2)}, u32[]{:S(2)}) collective-permute-start(s16[128,512]{1,0:T(8,128)(2,1)} %encode.1.refs_0_), channel_id=1, source_target_pairs={{0,6},{1,7},{2,4},{3,5},{4,2},{5,3},{6,0},{7,1},{8,14},{9,15},{10,... | collective-permute-start | bytes 393224 | tf_op jit(solution)/shard_map/ppermute | solution.py:159
  6.3 6.5 %collective-permute-start.3 = (s16[128,512]{1,0:T(8,128)(2,1)}, s16[128,512]{1,0:T(8,128)(2,1)S(1)}, u32[]{:S(2)}, u32[]{:S(2)}) collective-permute-start(s16[128,512]{1,0:T(8,128)(2,1)} %encode.1.refs_0_), channel_id=1, source_target_pairs={{0,2},{1,3},{2,0},{3,1},{4,6},{5,7},{6,4},{7,5},{8,10},{9,11},{10,... | collective-permute-start | bytes 393224 | tf_op jit(solution)/shard_map/ppermute | solution.py:157
  6.9 10.9 %collective-permute-start.1 = (s16[128,512]{1,0:T(8,128)(2,1)}, s16[128,512]{1,0:T(8,128)(2,1)S(1)}, u32[]{:S(2)}, u32[]{:S(2)}) collective-permute-start(s16[128,512]{1,0:T(8,128)(2,1)} %encode.1.refs_0_), channel_id=1, source_target_pairs={{0,1},{1,0},{2,3},{3,2},{4,5},{5,4},{6,7},{7,6},{8,9},{9,8},{10,11... | collective-permute-start | bytes 393224 | tf_op jit(solution)/shard_map/ppermute | solution.py:155
  6.9 6.2 %collective-permute-start = (s16[128,512]{1,0:T(8,128)(2,1)}, s16[128,512]{1,0:T(8,128)(2,1)S(1)}, u32[]{:S(2)}, u32[]{:S(2)}) collective-permute-start(s16[128,512]{1,0:T(8,128)(2,1)} %encode.1.refs_0_), channel_id=1, source_target_pairs={{0,4},{4,0},{8,12},{12,8},{1,5},{5,1},{9,13},{13,9},{2,6},{6,2},{1... | collective-permute-start | bytes 393224 | tf_op jit(solution)/shard_map/ppermute | solution.py:158
  10.5 7.2 %collective-permute-start.6 = (s16[128,512]{1,0:T(8,128)(2,1)S(1)}, s16[128,512]{1,0:T(8,128)(2,1)S(1)}, u32[]{:S(2)}, u32[]{:S(2)}) collective-permute-start(s16[128,512]{1,0:T(8,128)(2,1)S(1)} %collective-permute-done.4.refs_5_), channel_id=1, source_target_pairs={{0,1},{1,0},{2,3},{3,2},{4,5},{5,4},{6,7},{7,6},{8,9},{9,8},{10,11... | collective-permute-start | bytes 393224 | tf_op jit(solution)/shard_map/ppermute | solution.py:155
  12.8 4.9 %collective-permute-start.5 = (s16[128,512]{1,0:T(8,128)(2,1)S(1)}, s16[128,512]{1,0:T(8,128)(2,1)S(1)}, u32[]{:S(2)}, u32[]{:S(2)}) collective-permute-start(s16[128,512]{1,0:T(8,128)(2,1)S(1)} %collective-permute-done.3.refs_4_), channel_id=1, source_target_pairs={{0,1},{1,0},{2,3},{3,2},{4,5},{5,4},{6,7},{7,6},{8,9},{9,8},{10,11... | collective-permute-start | bytes 393224 | tf_op jit(solution)/shard_map/ppermute | solution.py:155
  13.1 4.7 %collective-permute-start.2 = (s16[128,512]{1,0:T(8,128)(2,1)S(1)}, s16[128,512]{1,0:T(8,128)(2,1)S(1)}, u32[]{:S(2)}, u32[]{:S(2)}) collective-permute-start(s16[128,512]{1,0:T(8,128)(2,1)S(1)} %collective-permute-done.refs_1_), channel_id=1, source_target_pairs={{0,1},{1,0},{2,3},{3,2},{4,5},{5,4},{6,7},{7,6},{8,9},{9,8},{10,11... | collective-permute-start | bytes 393224 | tf_op jit(solution)/shard_map/ppermute | solution.py:155
  13.5 1.7 %copy-start = (bf16[4,2,9,128,128]{4,3,2,1,0:T(8,128)(2,1)S(1)}, bf16[4,2,9,128,128]{4,3,2,1,0:T(8,128)(2,1)}, u32[]{:S(2)}) copy-start(bf16[4,2,9,128,128]{4,3,2,1,0:T(8,128)(2,1)} %coupling.1) | copy-start | bytes 7077892
  15.2 0.7 %copy-start.2 = (f32[9]{0:T(128)S(1)}, f32[9]{0:T(128)}, u32[]{:S(2)}) copy-start(f32[9]{0:T(128)} %phonon.1) | copy-start | bytes 112
  15.8 1.9 %copy-start.1 = (s16[128,512]{1,0:T(8,128)(2,1)S(1)}, s16[128,512]{1,0:T(8,128)(2,1)}, u32[]{:S(2)}) copy-start(s16[128,512]{1,0:T(8,128)(2,1)} %encode.1.refs_0_) | copy-start | bytes 393220
  23.7 7.3 %collective-permute-start.11 = (s16[128,512]{1,0:T(8,128)(2,1)S(1)}, s16[128,512]{1,0:T(8,128)(2,1)S(1)}, u32[]{:S(2)}, u32[]{:S(2)}) collective-permute-start(s16[128,512]{1,0:T(8,128)(2,1)S(1)} %step.2.refs_0_), channel_id=1, source_target_pairs={{0,6},{1,7},{2,4},{3,5},{4,2},{5,3},{6,0},{7,1},{8,14},{9,15},{10,... | collective-permute-start | bytes 393224 | tf_op jit(solution)/shard_map/ppermute | solution.py:159
  25.5 7.6 %collective-permute-start.10 = (s16[128,512]{1,0:T(8,128)(2,1)S(1)}, s16[128,512]{1,0:T(8,128)(2,1)S(1)}, u32[]{:S(2)}, u32[]{:S(2)}) collective-permute-start(s16[128,512]{1,0:T(8,128)(2,1)S(1)} %step.2.refs_0_), channel_id=1, source_target_pairs={{0,2},{1,3},{2,0},{3,1},{4,6},{5,7},{6,4},{7,5},{8,10},{9,11},{10,... | collective-permute-start | bytes 393224 | tf_op jit(solution)/shard_map/ppermute | solution.py:157
  27.0 6.2 %collective-permute-start.7 = (s16[128,512]{1,0:T(8,128)(2,1)S(1)}, s16[128,512]{1,0:T(8,128)(2,1)S(1)}, u32[]{:S(2)}, u32[]{:S(2)}) collective-permute-start(s16[128,512]{1,0:T(8,128)(2,1)S(1)} %step.2.refs_0_), channel_id=1, source_target_pairs={{0,4},{4,0},{8,12},{12,8},{1,5},{5,1},{9,13},{13,9},{2,6},{6,2},{1... | collective-permute-start | bytes 393224 | tf_op jit(solution)/shard_map/ppermute | solution.py:158
  27.3 6.3 %collective-permute-start.8 = (s16[128,512]{1,0:T(8,128)(2,1)S(1)}, s16[128,512]{1,0:T(8,128)(2,1)S(1)}, u32[]{:S(2)}, u32[]{:S(2)}) collective-permute-start(s16[128,512]{1,0:T(8,128)(2,1)S(1)} %step.2.refs_0_), channel_id=1, source_target_pairs={{0,1},{1,0},{2,3},{3,2},{4,5},{5,4},{6,7},{7,6},{8,9},{9,8},{10,11... | collective-permute-start | bytes 393224 | tf_op jit(solution)/shard_map/ppermute | solution.py:155
  31.1 2.6 %collective-permute-start.13 = (s16[128,512]{1,0:T(8,128)(2,1)S(1)}, s16[128,512]{1,0:T(8,128)(2,1)S(1)}, u32[]{:S(2)}, u32[]{:S(2)}) collective-permute-start(s16[128,512]{1,0:T(8,128)(2,1)S(1)} %collective-permute-done.11.refs_5_), channel_id=1, source_target_pairs={{0,1},{1,0},{2,3},{3,2},{4,5},{5,4},{6,7},{7,6},{8,9},{9,8},{10,11... | collective-permute-start | bytes 393224 | tf_op jit(solution)/shard_map/ppermute | solution.py:155
  33.1 1.3 %collective-permute-start.12 = (s16[128,512]{1,0:T(8,128)(2,1)S(1)}, s16[128,512]{1,0:T(8,128)(2,1)S(1)}, u32[]{:S(2)}, u32[]{:S(2)}) collective-permute-start(s16[128,512]{1,0:T(8,128)(2,1)S(1)} %collective-permute-done.10.refs_4_), channel_id=1, source_target_pairs={{0,1},{1,0},{2,3},{3,2},{4,5},{5,4},{6,7},{7,6},{8,9},{9,8},{10,11... | collective-permute-start | bytes 393224 | tf_op jit(solution)/shard_map/ppermute | solution.py:155
  33.1 1.5 %collective-permute-start.9 = (s16[128,512]{1,0:T(8,128)(2,1)S(1)}, s16[128,512]{1,0:T(8,128)(2,1)S(1)}, u32[]{:S(2)}, u32[]{:S(2)}) collective-permute-start(s16[128,512]{1,0:T(8,128)(2,1)S(1)} %collective-permute-done.7.refs_1_), channel_id=1, source_target_pairs={{0,1},{1,0},{2,3},{3,2},{4,5},{5,4},{6,7},{7,6},{8,9},{9,8},{10,11... | collective-permute-start | bytes 393224 | tf_op jit(solution)/shard_map/ppermute | solution.py:155

commit v3 on v0

v3 whole, which is shorter than its diff:
```python
import functools

import jax
import jax.numpy as jnp
from jax import lax
from jax.experimental import pallas as pl
from jax.experimental.pallas import tpu as pltpu
from jax.sharding import PartitionSpec as P

ITERS = 2
CUTOFF = 4.0
LANES = 128
GAP_LIMIT = 10.0
CODE_LIMIT = 32767.0
CODE_POWER = 5
HOLDER, PLACE, LIVE, ROWS = 0, 1, 2, 3


def omega_of(index, freq_count):
    return (2.0 * index.astype(jnp.float32) + 1.0 - freq_count) * (CUTOFF / freq_count)


def encoded(gap):
    share = jnp.minimum(jnp.abs(gap) * (1.0 / GAP_LIMIT), 1.0)
    root = jnp.exp2(jnp.log2(jnp.maximum(share, 1e-37)) * (1.0 / CODE_POWER))
    code = jnp.floor(root * CODE_LIMIT + 0.5)
    return jnp.where(gap < 0, -code, code).astype(jnp.int32).astype(jnp.int16)


def decoded(code):
    root = code.astype(jnp.float32) * (1.0 / CODE_LIMIT)
    square = root * root
    return (root * GAP_LIMIT) * (square * square)


def encode_kernel(gap, code):
    code[...] = encoded(gap[...])


def split(value):
    high = value.astype(jnp.bfloat16)
    return high, (value - high.astype(jnp.float32)).astype(jnp.bfloat16)


def tables_kernel(
    dims, paired, meta, phonon, pair_cols, pair_count, block_order, coupling, plan, weights, *refs
):
    freq_count, segments, segment_rows, padded_rows, modes = dims
    tables, (held, sems) = refs[:segments], refs[segments:]
    blocks, slots = coupling.shape[:2]
    size = coupling.shape[3]

    def fetch(block):
        return pltpu.make_async_copy(coupling.at[block], held.at[block], sems.at[block])

    for block in range(blocks):
        fetch(block).start()
    for at in range(1 + segments):
        plan[ROWS, at] = meta[at]
    for block in range(blocks):
        for slot in range(slots):
            wanted = pair_cols[block, slot]
            position = jnp.int32(0)
            for at in range(block_order.shape[0]):
                position = jnp.where(block_order[at] == wanted, at, position)
            pair = block * slots + slot
            holder = position // blocks
            if paired:
                apart = holder ^ meta[1 + segments]
                holder = (apart % 2) * 2 + apart // 2
            plan[HOLDER, pair] = holder
            plan[PLACE, pair] = position % blocks
            plan[LIVE, pair] = (pair_count[block] > slot).astype(jnp.int32)
    shape = (padded_rows, segment_rows)
    row_omega = omega_of(lax.broadcasted_iota(jnp.int32, shape, 0) + meta[0], freq_count)
    for segment in range(segments):
        col = lax.broadcasted_iota(jnp.int32, shape, 1) + meta[1 + segment]
        col_omega = omega_of(col, freq_count)
        near = (row_omega - col_omega) ** 2
        far = (row_omega + col_omega) ** 2
        cross = 4.0 * (row_omega * col_omega)
        for mode in range(modes):
            strength = phonon[mode]
            below = near + strength * strength
            above = far + strength * strength
            common = (2.0 * strength) / (below * above)
            columns = slice(mode * segment_rows, (mode + 1) * segment_rows)
            for part, value in enumerate((common * (below + above), common * cross)):
                high, low = split(value)
                tables[segment][part, :padded_rows, columns] = high
                tables[segment][part, padded_rows:, columns] = low
    for block in range(blocks):
        fetch(block).wait()
        for slot in range(slots):
            for mode in range(modes):
                weights[
                    block, slot * size : (slot + 1) * size, mode * size : (mode + 1) * size
                ] = held[block, slot, mode].T


def step_kernel(dims, segment, coded, final, plan, *refs):
    freq_count, segments, segment_rows, padded_rows, modes = dims
    first, last = segment == 0, segment == segments - 1
    refs = list(refs)
    fetched, ratios, high, low = refs[-4:]
    del refs[-4:]
    outs = [refs.pop() for _ in range(2 if last and final else 1)][::-1]
    before = None if first else refs.pop()
    weights, table = refs[-2:]
    pieces = refs[:-2]
    blocks = weights.shape[0]
    size = LANES
    slots = weights.shape[1] // size
    pieces = [
        piece.at[part]
        for piece in pieces
        for part in range(piece.shape[0])
    ] if len(pieces[0].shape) == 3 else pieces
    for pair in range(blocks * slots):
        column = pl.multiple_of(plan[PLACE, pair] * size, size)
        for group, piece in enumerate(pieces):

            @pl.when(plan[HOLDER, pair] == group)
            def _():
                fetched[pair] = piece[:, pl.ds(column, size)]

    shape = (segment_rows, size)
    col = lax.broadcasted_iota(jnp.int32, shape, 0) + plan[ROWS, 1 + segment]
    col_omega = omega_of(col, freq_count)
    square = col_omega * col_omega
    for block in range(blocks):
        for slot in range(slots):
            pair = block * slots + slot
            gap = decoded(fetched[pair]) if coded else fetched[pair]
            live = plan[LIVE, pair].astype(jnp.float32)
            inverse = lax.rsqrt(square + gap * gap) * live
            lanes = slice(slot * size, (slot + 1) * size)
            ratios[block, :segment_rows, lanes] = (gap * inverse).astype(jnp.bfloat16)
            ratios[block, segment_rows:, lanes] = (col_omega * inverse).astype(jnp.bfloat16)
        lanes = slice(block * size, (block + 1) * size)
        for start in range(0, modes, 2):
            stop = min(start + 2, modes)
            terms = jnp.dot(
                ratios[block],
                weights[block, :, start * size : stop * size],
                preferred_element_type=jnp.float32,
            )
            upper, lower = split(terms)
            for mode in range(start, stop):
                rows = slice(mode * segment_rows, (mode + 1) * segment_rows)
                taken = slice((mode - start) * size, (mode - start + 1) * size)
                for part in range(2):
                    source = slice(part * segment_rows, (part + 1) * segment_rows)
                    high[part, rows, lanes] = upper[source, taken]
                    low[part, rows, lanes] = lower[source, taken]
    summed = []
    for part in range(2):
        both = jnp.dot(table[part], high[part], preferred_element_type=jnp.float32)
        rest = jnp.dot(
            table[part, :padded_rows], low[part], preferred_element_type=jnp.float32
        )
        total = both[:padded_rows] + (both[padded_rows:] + rest)
        summed.append(total if first else total + before[part])
    if not last:
        for part in range(2):
            outs[0][part] = summed[part]
        return
    own_rows = outs[0].shape[0]
    row = lax.broadcasted_iota(jnp.int32, outs[0].shape, 0) + plan[ROWS, 0]
    temperature = CUTOFF / freq_count
    renorm = 1.0 + temperature * summed[1][:own_rows] / omega_of(row, freq_count)
    gap = temperature * summed[0][:own_rows] / renorm
    if final:
        outs[1][...] = renorm
        outs[0][...] = gap
    else:
        outs[0][...] = encoded(gap) if coded else gap


def join_kernel(first, second, after, joined):
    joined[0] = first[...]
    joined[1] = second[...]


def swapped(axis_size, bit):
    return [(i, i ^ bit) for i in range(axis_size)]


def gather_pairwise(gap):
    joint = [(4 * f + s, 4 * (f ^ 1) + (s ^ 2)) for f in range(4) for s in range(4)]
    along_x = lax.ppermute(gap, "state", swapped(4, 2))
    along_z = lax.ppermute(gap, "freq", swapped(4, 1))
    diagonal = lax.ppermute(gap, ("freq", "state"), joint)
    return [[gap, along_x], [along_z, diagonal]]


def from_other_core(value):
    return lax.ppermute(value, "state", swapped(4, 1))


def gather_general(gap, half_groups):
    groups = lax.axis_size("state")
    everyone = lax.all_gather(gap, "state", axis=0, tiled=False)
    rows = lax.all_gather(everyone, "freq", axis=1, tiled=True)
    own_rows = gap.shape[0]
    start = (lax.axis_index("freq") // half_groups) * (half_groups * own_rows)
    half = lax.dynamic_slice_in_dim(rows, start, half_groups * own_rows, 1)
    return [[half[group] for group in range(groups)]]


def on_device(gap_in, coupling, pair_cols, pair_count, block_order, phonon):
    own_rows, row_width = gap_in.shape
    blocks, slots, modes, size, _ = coupling.shape
    freq_groups = lax.axis_size("freq")
    groups = lax.axis_size("state")
    freq_count = own_rows * freq_groups
    half_rows = freq_count // 2
    half_groups = freq_groups // 2
    pairwise = freq_groups == 4 and groups == 4
    padded_rows = -(-own_rows // 16) * 16
    freq_at = lax.axis_index("freq")
    if pairwise:
        segments = 2
        own = freq_at * own_rows
        meta = [own, own, (freq_at ^ 1) * own_rows, lax.axis_index("state")]
    else:
        segments = 1
        own = freq_at * own_rows
        meta = [own, (freq_at // half_groups) * half_rows]
    meta = jnp.stack([jnp.asarray(value, jnp.int32) for value in meta])
    segment_rows = half_rows // segments
    dims = (freq_count, segments, segment_rows, padded_rows, modes)
    smem = pl.BlockSpec(memory_space=pltpu.SMEM)
    vmem = pl.BlockSpec(memory_space=pltpu.VMEM)
    link_type = jnp.int16 if pairwise else jnp.float32

    passed = gap_in
    if pairwise:
        passed = pl.pallas_call(
            encode_kernel,
            out_shape=jax.ShapeDtypeStruct(gap_in.shape, link_type),
            in_specs=[vmem],
            out_specs=vmem,
            cost_estimate=pl.CostEstimate(
                flops=10_000_000_000, bytes_accessed=40_000_000, transcendentals=0
            ),
            name="encode",
        )(gap_in)

    plan, weights, *tables = pl.pallas_call(
        functools.partial(tables_kernel, dims, pairwise),
        out_shape=[
            jax.ShapeDtypeStruct((4, max(blocks * slots, 1 + segments)), jnp.int32),
            jax.ShapeDtypeStruct((blocks, slots * size, modes * size), jnp.bfloat16),
        ]
        + [jax.ShapeDtypeStruct((2, 2 * padded_rows, modes * segment_rows), jnp.bfloat16)]
        * segments,
        in_specs=[smem] * 5 + [pl.BlockSpec(memory_space=pltpu.HBM)],
        out_specs=[smem] + [vmem] * (1 + segments),
        scratch_shapes=[
            pltpu.VMEM(coupling.shape, jnp.bfloat16),
            pltpu.SemaphoreType.DMA((blocks,)),
        ],
        compiler_params=pltpu.CompilerParams(vmem_limit_bytes=32 << 20),
        cost_estimate=pl.CostEstimate(
            flops=10_000_000, bytes_accessed=8_000_000, transcendentals=0
        ),
        name="tables",
    )(meta, phonon, pair_cols, pair_count, block_order, coupling)

    def step(segment, final, pieces, before):
        full = jax.ShapeDtypeStruct(gap_in.shape, jnp.float32)
        if segment < segments - 1:
            outs = [jax.ShapeDtypeStruct((2, padded_rows, row_width), jnp.float32)]
        elif final:
            outs = [full, full]
        else:
            outs = [jax.ShapeDtypeStruct(gap_in.shape, link_type)]
        inputs = [*pieces, weights, tables[segment], *before]
        return pl.pallas_call(
            functools.partial(step_kernel, dims, segment, pairwise, final),
            out_shape=outs,
            in_specs=[smem] + [vmem] * len(inputs),
            out_specs=[vmem] * len(outs),
            scratch_shapes=[
                pltpu.VMEM((blocks * slots, segment_rows, size), link_type),
                pltpu.VMEM((blocks, 2 * segment_rows, slots * size), jnp.bfloat16),
                pltpu.VMEM((2, modes * segment_rows, row_width), jnp.bfloat16),
                pltpu.VMEM((2, modes * segment_rows, row_width), jnp.bfloat16),
            ],
            compiler_params=pltpu.CompilerParams(vmem_limit_bytes=32 << 20),
            cost_estimate=pl.CostEstimate(
                flops=1_000_000, bytes_accessed=100_000, transcendentals=0
            ),
            name="step",
        )(plan, *inputs)

    def join(near, across, after):
        return pl.pallas_call(
            join_kernel,
            out_shape=jax.ShapeDtypeStruct((2, *near.shape), near.dtype),
            in_specs=[vmem, vmem, pl.BlockSpec(memory_space=pl.ANY)],
            out_specs=vmem,
            name="join",
        )(near, across, after)

    for iteration in range(ITERS):
        final = iteration == ITERS - 1
        if pairwise:
            gathered = gather_pairwise(passed)
        else:
            gathered = gather_general(passed, half_groups)
        results = []
        for segment, pieces in enumerate(gathered):
            if pairwise and segment == 0:
                near, across = pieces
                pieces = [near, across, from_other_core(near), from_other_core(across)]
            elif pairwise:
                both = join(*pieces, *results)
                pieces = [both, from_other_core(both)]
            results = step(segment, final, pieces, results)
        passed = results[0]
    return tuple(results)


def solution(mesh):
    return jax.shard_map(
        on_device,
        mesh=mesh,
        in_specs=(
            P(("parts", "freq"), "state"),
            P(("parts", "state"), None, None, None, None),
            P(("parts", "state"), None),
            P(("parts", "state")),
            P("parts"),
            P("parts"),
        ),
        out_specs=(P(("parts", "freq"), "state"), P(("parts", "freq"), "state")),
        check_vma=False,
    )
```

time: 170 us -> 56.4 us (0.33)
  waiting for transfers between devices: 114 us -> 14.8 us
  matrix products: 22.8 us -> 0 us
  Pallas kernels: 0 us -> 22.4 us
  between operations: 18.9 us -> 0.76 us
  other arithmetic: 9.32 us -> 0.08 us
  starting transfers between devices: 0.35 us -> 8.23 us
  local copies, waits for them, and re-layouts: 4.76 us -> 9.7 us
    reduce_scatter x2 -> x0, waiting for transfers between devices: 88 us -> none  [on_device(): lax.psum_scatter(jnp.einsum('vnm,vqms->nqs', weights, local_terms, precis...]
    all_gather x2 -> x0, waiting for transfers between devices: 25.6 us -> none  [on_device(): everyone = lax.all_gather(ratios, 'state', axis=2, tiled=True)]
    dot_general x10 -> x0, matrix products: 22.8 us -> none  [the longest x2 19.9 us: on_device(): jnp.einsum('vnm,vqms->nqs', weights, local_terms, precision=lax.Precision...]
    pallas_call x0 -> x8, Pallas kernels: none -> 22.4 us  [the longest x4 14 us: step(): pl.pallas_call(functools.partial(step_kernel, dims, segment, pairwise, fi...]
    ppermute x0 -> x12, waiting for transfers between devices: none -> 14.8 us  [the longest x2 9.07 us: gather_pairwise(): along_x = lax.ppermute(gap, 'state', swapped(4, 2))]
    unnamed x0 -> x31, local copies, waits for them, and re-layouts: none -> 9.7 us
    ppermute x0 -> x12, starting transfers between devices: none -> 8.23 us  [the longest x2 3.41 us: gather_pairwise(): along_z = lax.ppermute(gap, 'freq', swapped(4, 1))]
    another operation x5 -> x1, other arithmetic: 3.94 us -> 0.08 us  [on_device(): meta = jnp.stack([jnp.asarray(value, jnp.int32) for value in meta])]
  transfers between devices with their start and end apart: 4 -> 12, of which waited for: 4 -> 6; matrix products, arithmetic and copies ran while one was open for 3% -> 0% of each run, Pallas kernels for 0% -> 18%
where the time goes in v3:
time: 56.4 us; the launch traced here: 56 us
  Pallas kernels  22.4 us (40%)
  waiting for transfers between devices  14.8 us (26%)
  local copies, waits for them, and re-layouts  9.7 us (17%)
  starting transfers between devices  8.23 us (15%)
  between operations  0.76 us (1%)
    pallas_call x4, Pallas kernels, step(): pl.pallas_call(functools.partial(step_kernel, dims, segment, pairwise, fi...  14 us
    unnamed x31, local copies, waits for them, and re-layouts  9.7 us
    ppermute x2, waiting for transfers between devices, gather_pairwise(): along_x = lax.ppermute(gap, 'state', swapped(4, 2))  9.07 us
    ppermute x6, waiting for transfers between devices, from_other_core(): return lax.ppermute(value, 'state', swapped(4, 1))  3.5 us
    ppermute x2, starting transfers between devices, gather_pairwise(): along_z = lax.ppermute(gap, 'freq', swapped(4, 1))  3.41 us
    pallas_call x2, Pallas kernels, join(): pl.pallas_call(join_kernel, out_shape=jax.ShapeDtypeStruct((2, *near.shap...  3.38 us
    pallas_call x1, Pallas kernels, on_device(): pl.pallas_call(functools.partial(tables_kernel, dims, pairwise), out_shap...  3.26 us
    ppermute x2, starting transfers between devices, gather_pairwise(): along_x = lax.ppermute(gap, 'state', swapped(4, 2))  3.26 us
  transfers between devices with their start and end apart: 12, of which 6 were waited for; matrix products, arithmetic and copies ran while one was open for 0% of the time, Pallas kernels for 18%

profile of v3, /device:TPU:0, one launch (start us, length us, event | category | flops | bytes accessed | tf_op | source)
XLA Modules:
  0.0 56.0 jit_solution(1675348385518923959)
XLA Ops:
  0.7 1.8 %encode.1.refs_0_ = s16[128,512]{1,0:T(8,128)(2,1)} custom-call(f32[128,512]{1,0:T(8,128)} %gap.1), custom_call_target="tpu_custom_call" | custom-call | flops 10000000000 | bytes 40000000 | tf_op jit(solution)/shard_map/encode/pallas_call | solution.py:239
  2.4 2.9 %collective-permute-start.2 = (s16[128,512]{1,0:T(8,128)(2,1)}, s16[128,512]{1,0:T(8,128)(2,1)}, u32[]{:S(2)}, u32[]{:S(2)}) collective-permute-start(s16[128,512]{1,0:T(8,128)(2,1)} %encode.1.refs_0_), channel_id=1, source_target_pairs={{0,2},{1,3},{2,0},{3,1},{4,6},{5,7},{6,4},{7,5},{8,10},{9,11},{10,... | collective-permute-start | bytes 393224 | tf_op jit(solution)/shard_map/ppermute | solution.py:191
  5.4 3.8 %collective-permute-done.2.refs_1_ = s16[128,512]{1,0:T(8,128)(2,1)} collective-permute-done((s16[128,512]{1,0:T(8,128)(2,1)}, s16[128,512]{1,0:T(8,128)(2,1)}, u32[]{:S(2)}, u32[]{:S(2)}) %collective-permute-start.2) | collective-permute-done | bytes 131104 | tf_op jit(solution)/shard_map/ppermute | solution.py:191
  9.2 1.8 %collective-permute-start = (s16[128,512]{1,0:T(8,128)(2,1)}, s16[128,512]{1,0:T(8,128)(2,1)}, u32[]{:S(2)}, u32[]{:S(2)}) collective-permute-start(s16[128,512]{1,0:T(8,128)(2,1)} %encode.1.refs_0_), channel_id=1, source_target_pairs={{0,4},{4,0},{8,12},{12,8},{1,5},{5,1},{9,13},{13,9},{2,6},{6,2},{1... | collective-permute-start | bytes 393224 | tf_op jit(solution)/shard_map/ppermute | solution.py:192
  11.0 1.4 %collective-permute-start.1 = (s16[128,512]{1,0:T(8,128)(2,1)}, s16[128,512]{1,0:T(8,128)(2,1)}, u32[]{:S(2)}, u32[]{:S(2)}) collective-permute-start(s16[128,512]{1,0:T(8,128)(2,1)} %encode.1.refs_0_), channel_id=1, source_target_pairs={{0,6},{1,7},{2,4},{3,5},{4,2},{5,3},{6,0},{7,1},{8,14},{9,15},{10,... | collective-permute-start | bytes 393224 | tf_op jit(solution)/shard_map/ppermute | solution.py:193
  12.4 0.1 copy.8.pair_cols
  12.5 0.1 pad_add_fusion.meta
  12.6 1.7 %copy-done.6 = bf16[4,2,9,128,128]{4,3,2,1,0:T(8,128)(2,1)S(1)} copy-done((bf16[4,2,9,128,128]{4,3,2,1,0:T(8,128)(2,1)S(1)}, bf16[4,2,9,128,128]{4,3,2,1,0:T(8,128)(2,1)}, u32[]{:S(2)}) %copy-start.6) | copy-done | bytes 2359320
  14.2 0.7 %copy-done.12 = s32[16]{0:T(128)S(1)} copy-done((s32[16]{0:T(128)S(1)}, s32[16]{0:T(128)}, u32[]{:S(2)}) %copy-start.12) | copy-done | bytes 88
  14.9 3.3 %tables.1 = (s32[4,8]{1,0:T(4,128)S(1)}, bf16[4,256,1152]{2,1,0:T(8,128)(2,1)S(1)}, bf16[2,256,1152]{2,1,0:T(8,128)(2,1)S(1)}, bf16[2,256,1152]{2,1,0:T(8,128)(2,1)S(1)}) custom-call(s32[4]{0:T(128)S(1)} %pad_add_fusion.meta, f32[9]{0:T(128)S(1)} %copy-done.10, s32[4,2]{1,0:T(4,128)S(1)} %copy.8.pair_cols, s32[4]{0:T(128)S(1)} %copy-done.11, ...), custom_call_target="tpu_custom_call" | custom-call | flops 10000000 | bytes 8000000 | tf_op jit(solution)/shard_map/tables/pallas_call | solution.py:250
  18.2 3.6 %step.4.after.refs_4_ = f32[2,128,512]{2,1,0:T(8,128)S(1)} custom-call(s32[4,8]{1,0:T(4,128)S(1)} %get-tuple-element.6.plan, s16[128,512]{1,0:T(8,128)(2,1)S(1)} %copy-done.9, s16[128,512]{1,0:T(8,128)(2,1)} %collective-permute-done.2.refs_1_, s16[128,512]{1,0:T(8,128)(2,1)} %collective-permute-done.3.refs_2_, ...), custom_call_target="tpu_custom_call" | custom-call | flops 1000000 | bytes 100000 | tf_op jit(solution)/shard_map/step/pallas_call | solution.py:280
  21.8 1.0 %copy-done = bf16[2,256,1152]{2,1,0:T(8,128)(2,1)} copy-done((bf16[2,256,1152]{2,1,0:T(8,128)(2,1)}, bf16[2,256,1152]{2,1,0:T(8,128)(2,1)S(1)}, u32[]{:S(2)}) %copy-start) | copy-done | bytes 1179672
  22.9 0.8 %copy-done.2 = f32[2,128,512]{2,1,0:T(8,128)} copy-done((f32[2,128,512]{2,1,0:T(8,128)}, f32[2,128,512]{2,1,0:T(8,128)S(1)}, u32[]{:S(2)}) %copy-start.2) | copy-done | bytes 524312
  23.7 1.7 %join.2.refs_0_ = s16[2,128,512]{2,1,0:T(8,128)(2,1)} custom-call(s16[128,512]{1,0:T(8,128)(2,1)} %collective-permute-done.first, s16[128,512]{1,0:T(8,128)(2,1)} %collective-permute-done.1.second, f32[2,128,512]{2,1,0:T(8,128)} %copy-done.2), custom_call_target="tpu_custom_call" | custom-call | tf_op jit(solution)/shard_map/join/pallas_call | solution.py:299
  25.3 1.7 %collective-permute-done.5.refs_1_ = s16[2,128,512]{2,1,0:T(8,128)(2,1)S(1)} collective-permute-done((s16[2,128,512]{2,1,0:T(8,128)(2,1)}, s16[2,128,512]{2,1,0:T(8,128)(2,1)S(1)}, u32[]{:S(2)}, u32[]{:S(2)}) %collective-permute-start.5) | collective-permute-done | bytes 262176 | tf_op jit(solution)/shard_map/ppermute | solution.py:198
  27.1 1.0 %copy-done.3 = f32[2,128,512]{2,1,0:T(8,128)S(1)} copy-done((f32[2,128,512]{2,1,0:T(8,128)S(1)}, f32[2,128,512]{2,1,0:T(8,128)}, u32[]{:S(2)}) %copy-start.3) | copy-done | bytes 524312
  28.1 0.9 %copy-done.8 = s16[2,128,512]{2,1,0:T(8,128)(2,1)S(1)} copy-done((s16[2,128,512]{2,1,0:T(8,128)(2,1)S(1)}, s16[2,128,512]{2,1,0:T(8,128)(2,1)}, u32[]{:S(2)}) %copy-start.8) | copy-done | bytes 262168
  29.1 3.3 %step.5.refs_0_ = s16[128,512]{1,0:T(8,128)(2,1)S(1)} custom-call(s32[4,8]{1,0:T(4,128)S(1)} %get-tuple-element.6.plan, s16[2,128,512]{2,1,0:T(8,128)(2,1)S(1)} %copy-done.8, s16[2,128,512]{2,1,0:T(8,128)(2,1)S(1)} %collective-permute-done.5.refs_1_, bf16[4,256,1152]{2,1,0:T(8,128)(2,1)S(1)} %get-tuple-element.7.refs_4_.refs_2_, ...), custom_call_target="tpu_custom_call" | custom-call | flops 1000000 | bytes 100000 | tf_op jit(solution)/shard_map/step/pallas_call | solution.py:280
  32.4 0.3 collective-permute-start.8
  32.7 5.3 %collective-permute-done.8.refs_1_ = s16[128,512]{1,0:T(8,128)(2,1)S(1)} collective-permute-done((s16[128,512]{1,0:T(8,128)(2,1)S(1)}, s16[128,512]{1,0:T(8,128)(2,1)S(1)}, u32[]{:S(2)}, u32[]{:S(2)}) %collective-permute-start.8) | collective-permute-done | bytes 131104 | tf_op jit(solution)/shard_map/ppermute | solution.py:191
  38.0 1.6 %collective-permute-start.6 = (s16[128,512]{1,0:T(8,128)(2,1)S(1)}, s16[128,512]{1,0:T(8,128)(2,1)S(1)}, u32[]{:S(2)}, u32[]{:S(2)}) collective-permute-start(s16[128,512]{1,0:T(8,128)(2,1)S(1)} %step.5.refs_0_), channel_id=1, source_target_pairs={{0,4},{4,0},{8,12},{12,8},{1,5},{5,1},{9,13},{13,9},{2,6},{6,2},{1... | collective-permute-start | bytes 393224 | tf_op jit(solution)/shard_map/ppermute | solution.py:192
  39.6 0.2 collective-permute-start.7
  39.8 3.1 %step.6.after.refs_4_ = f32[2,128,512]{2,1,0:T(8,128)S(1)} custom-call(s32[4,8]{1,0:T(4,128)S(1)} %get-tuple-element.6.plan, s16[128,512]{1,0:T(8,128)(2,1)S(1)} %step.5.refs_0_, s16[128,512]{1,0:T(8,128)(2,1)S(1)} %collective-permute-done.8.refs_1_, s16[128,512]{1,0:T(8,128)(2,1)S(1)} %collective-permute-done.9.refs_2_, ...), custom_call_target="tpu_custom_call" | custom-call | flops 1000000 | bytes 100000 | tf_op jit(solution)/shard_map/step/pallas_call | solution.py:280
  42.9 0.8 %copy-done.4 = f32[2,128,512]{2,1,0:T(8,128)} copy-done((f32[2,128,512]{2,1,0:T(8,128)}, f32[2,128,512]{2,1,0:T(8,128)S(1)}, u32[]{:S(2)}) %copy-start.4) | copy-done | bytes 524312
  43.7 0.6 %collective-permute-done.6.first = s16[128,512]{1,0:T(8,128)(2,1)S(1)} collective-permute-done((s16[128,512]{1,0:T(8,128)(2,1)S(1)}, s16[128,512]{1,0:T(8,128)(2,1)S(1)}, u32[]{:S(2)}, u32[]{:S(2)}) %collective-permute-start.6) | collective-permute-done | bytes 131104 | tf_op jit(solution)/shard_map/ppermute | solution.py:192
  44.3 0.7 %copy-done.13 = s16[128,512]{1,0:T(8,128)(2,1)} copy-done((s16[128,512]{1,0:T(8,128)(2,1)}, s16[128,512]{1,0:T(8,128)(2,1)S(1)}, u32[]{:S(2)}) %copy-start.13) | copy-done | bytes 131096
  44.9 1.7 %collective-permute-done.7.second = s16[128,512]{1,0:T(8,128)(2,1)} collective-permute-done((s16[128,512]{1,0:T(8,128)(2,1)S(1)}, s16[128,512]{1,0:T(8,128)(2,1)}, u32[]{:S(2)}, u32[]{:S(2)}) %collective-permute-start.7) | collective-permute-done | bytes 131104 | tf_op jit(solution)/shard_map/ppermute | solution.py:193
  46.6 1.7 %join.3.refs_0_ = s16[2,128,512]{2,1,0:T(8,128)(2,1)} custom-call(s16[128,512]{1,0:T(8,128)(2,1)} %copy-done.13, s16[128,512]{1,0:T(8,128)(2,1)} %collective-permute-done.7.second, f32[2,128,512]{2,1,0:T(8,128)} %copy-done.4), custom_call_target="tpu_custom_call" | custom-call | tf_op jit(solution)/shard_map/join/pallas_call | solution.py:299
  48.3 1.7 %collective-permute-done.11.refs_1_ = s16[2,128,512]{2,1,0:T(8,128)(2,1)S(1)} collective-permute-done((s16[2,128,512]{2,1,0:T(8,128)(2,1)}, s16[2,128,512]{2,1,0:T(8,128)(2,1)S(1)}, u32[]{:S(2)}, u32[]{:S(2)}) %collective-permute-start.11) | collective-permute-done | bytes 262176 | tf_op jit(solution)/shard_map/ppermute | solution.py:198
  50.1 1.0 %copy-done.5 = f32[2,128,512]{2,1,0:T(8,128)S(1)} copy-done((f32[2,128,512]{2,1,0:T(8,128)S(1)}, f32[2,128,512]{2,1,0:T(8,128)}, u32[]{:S(2)}) %copy-start.5) | copy-done | bytes 524312
  51.1 0.9 %copy-done.7 = s16[2,128,512]{2,1,0:T(8,128)(2,1)S(1)} copy-done((s16[2,128,512]{2,1,0:T(8,128)(2,1)S(1)}, s16[2,128,512]{2,1,0:T(8,128)(2,1)}, u32[]{:S(2)}) %copy-start.7) | copy-done | bytes 262168
  52.0 3.9 %step.7 = (f32[128,512]{1,0:T(8,128)}, f32[128,512]{1,0:T(8,128)}) custom-call(s32[4,8]{1,0:T(4,128)S(1)} %get-tuple-element.6.plan, s16[2,128,512]{2,1,0:T(8,128)(2,1)S(1)} %copy-done.7, s16[2,128,512]{2,1,0:T(8,128)(2,1)S(1)} %collective-permute-done.11.refs_1_, bf16[4,256,1152]{2,1,0:T(8,128)(2,1)S(1)} %get-tuple-element.7.refs_4_.refs_2_, ...), custom_call_target="tpu_custom_call" | custom-call | flops 1000000 | bytes 100000 | tf_op jit(solution)/shard_map/step/pallas_call | solution.py:280
  (32 shorter events, 0.1 us)
Async XLA Ops:
  0.6 11.8 %copy-start.14 = (s32[4,2]{0,1:T(2,128)S(1)}, s32[4,2]{0,1:T(2,128)}, u32[]{:S(2)}) copy-start(s32[4,2]{0,1:T(2,128)} %param.8) | copy-start | bytes 100
  0.6 11.9 %copy-start.10 = (f32[9]{0:T(128)S(1)}, f32[9]{0:T(128)}, u32[]{:S(2)}) copy-start(f32[9]{0:T(128)} %phonon.1) | copy-start | bytes 112
  0.7 11.9 %copy-start.11 = (s32[4]{0:T(128)S(1)}, s32[4]{0:T(128)}, u32[]{:S(2)}) copy-start(s32[4]{0:T(128)} %pair_count.1) | copy-start | bytes 52
  2.4 6.7 %collective-permute-start.2 = (s16[128,512]{1,0:T(8,128)(2,1)}, s16[128,512]{1,0:T(8,128)(2,1)}, u32[]{:S(2)}, u32[]{:S(2)}) collective-permute-start(s16[128,512]{1,0:T(8,128)(2,1)} %encode.1.refs_0_), channel_id=1, source_target_pairs={{0,2},{1,3},{2,0},{3,1},{4,6},{5,7},{6,4},{7,5},{8,10},{9,11},{10,... | collective-permute-start | bytes 393224 | tf_op jit(solution)/shard_map/ppermute | solution.py:191
  5.4 12.8 %collective-permute-start.3 = (s16[128,512]{1,0:T(8,128)(2,1)}, s16[128,512]{1,0:T(8,128)(2,1)}, u32[]{:S(2)}, u32[]{:S(2)}) collective-permute-start(s16[128,512]{1,0:T(8,128)(2,1)} %encode.1.refs_0_), channel_id=1, source_target_pairs={{0,1},{1,0},{2,3},{3,2},{4,5},{5,4},{6,7},{7,6},{8,9},{9,8},{10,11... | collective-permute-start | bytes 393224 | tf_op jit(solution)/shard_map/ppermute | solution.py:198
  9.2 9.0 %collective-permute-start.4 = (s16[128,512]{1,0:T(8,128)(2,1)}, s16[128,512]{1,0:T(8,128)(2,1)}, u32[]{:S(2)}, u32[]{:S(2)}) collective-permute-start(s16[128,512]{1,0:T(8,128)(2,1)} %collective-permute-done.2.refs_1_), channel_id=1, source_target_pairs={{0,1},{1,0},{2,3},{3,2},{4,5},{5,4},{6,7},{7,6},{8,9},{9,8},{10,11... | collective-permute-start | bytes 393224 | tf_op jit(solution)/shard_map/ppermute | solution.py:198
  9.2 14.5 %collective-permute-start = (s16[128,512]{1,0:T(8,128)(2,1)}, s16[128,512]{1,0:T(8,128)(2,1)}, u32[]{:S(2)}, u32[]{:S(2)}) collective-permute-start(s16[128,512]{1,0:T(8,128)(2,1)} %encode.1.refs_0_), channel_id=1, source_target_pairs={{0,4},{4,0},{8,12},{12,8},{1,5},{5,1},{9,13},{13,9},{2,6},{6,2},{1... | collective-permute-start | bytes 393224 | tf_op jit(solution)/shard_map/ppermute | solution.py:192
  11.0 12.6 %collective-permute-start.1 = (s16[128,512]{1,0:T(8,128)(2,1)}, s16[128,512]{1,0:T(8,128)(2,1)}, u32[]{:S(2)}, u32[]{:S(2)}) collective-permute-start(s16[128,512]{1,0:T(8,128)(2,1)} %encode.1.refs_0_), channel_id=1, source_target_pairs={{0,6},{1,7},{2,4},{3,5},{4,2},{5,3},{6,0},{7,1},{8,14},{9,15},{10,... | collective-permute-start | bytes 393224 | tf_op jit(solution)/shard_map/ppermute | solution.py:193
  12.6 1.7 %copy-start.6 = (bf16[4,2,9,128,128]{4,3,2,1,0:T(8,128)(2,1)S(1)}, bf16[4,2,9,128,128]{4,3,2,1,0:T(8,128)(2,1)}, u32[]{:S(2)}) copy-start(bf16[4,2,9,128,128]{4,3,2,1,0:T(8,128)(2,1)} %coupling.1) | copy-start | bytes 7077892
  14.2 0.7 %copy-start.12 = (s32[16]{0:T(128)S(1)}, s32[16]{0:T(128)}, u32[]{:S(2)}) copy-start(s32[16]{0:T(128)} %block_order.1) | copy-start | bytes 196
  14.9 3.3 %copy-start.9 = (s16[128,512]{1,0:T(8,128)(2,1)S(1)}, s16[128,512]{1,0:T(8,128)(2,1)}, u32[]{:S(2)}) copy-start(s16[128,512]{1,0:T(8,128)(2,1)} %encode.1.refs_0_) | copy-start | bytes 393220
  21.8 1.1 %copy-start = (bf16[2,256,1152]{2,1,0:T(8,128)(2,1)}, bf16[2,256,1152]{2,1,0:T(8,128)(2,1)S(1)}, u32[]{:S(2)}) copy-start(bf16[2,256,1152]{2,1,0:T(8,128)(2,1)S(1)} %get-tuple-element.8.refs_5_) | copy-start | bytes 3538948
  22.9 0.8 %copy-start.2 = (f32[2,128,512]{2,1,0:T(8,128)}, f32[2,128,512]{2,1,0:T(8,128)S(1)}, u32[]{:S(2)}) copy-start(f32[2,128,512]{2,1,0:T(8,128)S(1)} %step.4.after.refs_4_) | copy-start | bytes 1572868
  25.3 1.7 %collective-permute-start.5 = (s16[2,128,512]{2,1,0:T(8,128)(2,1)}, s16[2,128,512]{2,1,0:T(8,128)(2,1)S(1)}, u32[]{:S(2)}, u32[]{:S(2)}) collective-permute-start(s16[2,128,512]{2,1,0:T(8,128)(2,1)} %join.2.refs_0_), channel_id=1, source_target_pairs={{0,1},{1,0},{2,3},{3,2},{4,5},{5,4},{6,7},{7,6},{8,9},{9,8},{10,11... | collective-permute-start | bytes 786440 | tf_op jit(solution)/shard_map/ppermute | solution.py:198
  27.1 1.0 %copy-start.3 = (f32[2,128,512]{2,1,0:T(8,128)S(1)}, f32[2,128,512]{2,1,0:T(8,128)}, u32[]{:S(2)}) copy-start(f32[2,128,512]{2,1,0:T(8,128)} %copy-done.2) | copy-start | bytes 1572868
  28.1 0.9 %copy-start.8 = (s16[2,128,512]{2,1,0:T(8,128)(2,1)S(1)}, s16[2,128,512]{2,1,0:T(8,128)(2,1)}, u32[]{:S(2)}) copy-start(s16[2,128,512]{2,1,0:T(8,128)(2,1)} %join.2.refs_0_) | copy-start | bytes 786436
  29.1 10.7 %copy-start.1 = (bf16[2,256,1152]{2,1,0:T(8,128)(2,1)S(1)}, bf16[2,256,1152]{2,1,0:T(8,128)(2,1)}, u32[]{:S(2)}) copy-start(bf16[2,256,1152]{2,1,0:T(8,128)(2,1)} %copy-done) | copy-start | bytes 3538948
  32.4 5.6 %collective-permute-start.8 = (s16[128,512]{1,0:T(8,128)(2,1)S(1)}, s16[128,512]{1,0:T(8,128)(2,1)S(1)}, u32[]{:S(2)}, u32[]{:S(2)}) collective-permute-start(s16[128,512]{1,0:T(8,128)(2,1)S(1)} %step.5.refs_0_), channel_id=1, source_target_pairs={{0,2},{1,3},{2,0},{3,1},{4,6},{5,7},{6,4},{7,5},{8,10},{9,11},{10,... | collective-permute-start | bytes 393224 | tf_op jit(solution)/shard_map/ppermute | solution.py:191
  32.7 7.0 %collective-permute-start.9 = (s16[128,512]{1,0:T(8,128)(2,1)S(1)}, s16[128,512]{1,0:T(8,128)(2,1)S(1)}, u32[]{:S(2)}, u32[]{:S(2)}) collective-permute-start(s16[128,512]{1,0:T(8,128)(2,1)S(1)} %step.5.refs_0_), channel_id=1, source_target_pairs={{0,1},{1,0},{2,3},{3,2},{4,5},{5,4},{6,7},{7,6},{8,9},{9,8},{10,11... | collective-permute-start | bytes 393224 | tf_op jit(solution)/shard_map/ppermute | solution.py:198
  38.0 1.8 %collective-permute-start.10 = (s16[128,512]{1,0:T(8,128)(2,1)S(1)}, s16[128,512]{1,0:T(8,128)(2,1)S(1)}, u32[]{:S(2)}, u32[]{:S(2)}) collective-permute-start(s16[128,512]{1,0:T(8,128)(2,1)S(1)} %collective-permute-done.8.refs_1_), channel_id=1, source_target_pairs={{0,1},{1,0},{2,3},{3,2},{4,5},{5,4},{6,7},{7,6},{8,9},{9,8},{10,11... | collective-permute-start | bytes 393224 | tf_op jit(solution)/shard_map/ppermute | solution.py:198
  38.0 6.3 %collective-permute-start.6 = (s16[128,512]{1,0:T(8,128)(2,1)S(1)}, s16[128,512]{1,0:T(8,128)(2,1)S(1)}, u32[]{:S(2)}, u32[]{:S(2)}) collective-permute-start(s16[128,512]{1,0:T(8,128)(2,1)S(1)} %step.5.refs_0_), channel_id=1, source_target_pairs={{0,4},{4,0},{8,12},{12,8},{1,5},{5,1},{9,13},{13,9},{2,6},{6,2},{1... | collective-permute-start | bytes 393224 | tf_op jit(solution)/shard_map/ppermute | solution.py:192
  39.6 7.1 %collective-permute-start.7 = (s16[128,512]{1,0:T(8,128)(2,1)S(1)}, s16[128,512]{1,0:T(8,128)(2,1)}, u32[]{:S(2)}, u32[]{:S(2)}) collective-permute-start(s16[128,512]{1,0:T(8,128)(2,1)S(1)} %step.5.refs_0_), channel_id=1, source_target_pairs={{0,6},{1,7},{2,4},{3,5},{4,2},{5,3},{6,0},{7,1},{8,14},{9,15},{10,... | collective-permute-start | bytes 393224 | tf_op jit(solution)/shard_map/ppermute | solution.py:193
  42.9 0.8 %copy-start.4 = (f32[2,128,512]{2,1,0:T(8,128)}, f32[2,128,512]{2,1,0:T(8,128)S(1)}, u32[]{:S(2)}) copy-start(f32[2,128,512]{2,1,0:T(8,128)S(1)} %step.6.after.refs_4_) | copy-start | bytes 1572868
  44.3 0.7 %copy-start.13 = (s16[128,512]{1,0:T(8,128)(2,1)}, s16[128,512]{1,0:T(8,128)(2,1)S(1)}, u32[]{:S(2)}) copy-start(s16[128,512]{1,0:T(8,128)(2,1)S(1)} %collective-permute-done.6.first) | copy-start | bytes 393220
  48.3 1.7 %collective-permute-start.11 = (s16[2,128,512]{2,1,0:T(8,128)(2,1)}, s16[2,128,512]{2,1,0:T(8,128)(2,1)S(1)}, u32[]{:S(2)}, u32[]{:S(2)}) collective-permute-start(s16[2,128,512]{2,1,0:T(8,128)(2,1)} %join.3.refs_0_), channel_id=1, source_target_pairs={{0,1},{1,0},{2,3},{3,2},{4,5},{5,4},{6,7},{7,6},{8,9},{9,8},{10,11... | collective-permute-start | bytes 786440 | tf_op jit(solution)/shard_map/ppermute | solution.py:198
  50.1 1.0 %copy-start.5 = (f32[2,128,512]{2,1,0:T(8,128)S(1)}, f32[2,128,512]{2,1,0:T(8,128)}, u32[]{:S(2)}) copy-start(f32[2,128,512]{2,1,0:T(8,128)} %copy-done.4) | copy-start | bytes 1572868
  51.1 0.9 %copy-start.7 = (s16[2,128,512]{2,1,0:T(8,128)(2,1)S(1)}, s16[2,128,512]{2,1,0:T(8,128)(2,1)}, u32[]{:S(2)}) copy-start(s16[2,128,512]{2,1,0:T(8,128)(2,1)} %join.3.refs_0_) | copy-start | bytes 786436

commit v4 on v3

v4 whole, which is shorter than its diff:
```python
import functools

import jax
import jax.numpy as jnp
from jax import lax
from jax.experimental import pallas as pl
from jax.experimental.pallas import tpu as pltpu
from jax.sharding import PartitionSpec as P

ITERS = 2
CUTOFF = 4.0
LANES = 128
GAP_LIMIT = 10.0
CODE_LIMIT = 32767.0
CODE_POWER = 5
HOLDER, PLACE, LIVE, SIDE, ROWS = 0, 1, 2, 3, 4


def omega_of(index, freq_count):
    return (2.0 * index.astype(jnp.float32) + 1.0 - freq_count) * (CUTOFF / freq_count)


def encoded(gap):
    share = jnp.minimum(jnp.abs(gap) * (1.0 / GAP_LIMIT), 1.0)
    root = jnp.exp2(jnp.log2(jnp.maximum(share, 1e-37)) * (1.0 / CODE_POWER))
    code = jnp.floor(root * CODE_LIMIT + 0.5)
    return jnp.where(gap < 0, -code, code).astype(jnp.int32).astype(jnp.int16)


def decoded(code):
    root = code.astype(jnp.float32) * (1.0 / CODE_LIMIT)
    square = root * root
    return (root * GAP_LIMIT) * (square * square)


def encode_kernel(gap, codes):
    code = encoded(gap[...])
    for copy in range(codes.shape[0]):
        codes[copy] = code


def split(value):
    high = value.astype(jnp.bfloat16)
    return high, (value - high.astype(jnp.float32)).astype(jnp.bfloat16)


def tables_kernel(
    dims, meta, phonon, pair_cols, pair_count, block_order, coupling, plan, weights, table, held, sems
):
    freq_count, segments, segment_rows, padded_rows, modes, sides = dims
    blocks, slots = coupling.shape[:2]
    size = coupling.shape[3]
    half_rows = segments * segment_rows

    def fetch(block):
        return pltpu.make_async_copy(coupling.at[block], held.at[block], sems.at[block])

    for block in range(blocks):
        fetch(block).start()
    for at in range(1 + segments):
        plan[ROWS, at] = meta[at]
    for block in range(blocks):
        for slot in range(slots):
            wanted = pair_cols[block, slot]
            position = jnp.int32(0)
            for at in range(block_order.shape[0]):
                position = jnp.where(block_order[at] == wanted, at, position)
            pair = block * slots + slot
            holder = position // blocks
            plan[HOLDER, pair] = holder // sides
            plan[SIDE, pair] = (holder % sides) ^ meta[1 + segments]
            plan[PLACE, pair] = position % blocks
            plan[LIVE, pair] = (pair_count[block] > slot).astype(jnp.int32)
    shape = (padded_rows, segment_rows)
    row_omega = omega_of(lax.broadcasted_iota(jnp.int32, shape, 0) + meta[0], freq_count)
    for segment in range(segments):
        col = lax.broadcasted_iota(jnp.int32, shape, 1) + meta[1 + segment]
        col_omega = omega_of(col, freq_count)
        near = (row_omega - col_omega) ** 2
        far = (row_omega + col_omega) ** 2
        cross = 4.0 * (row_omega * col_omega)
        for mode in range(modes):
            strength = phonon[mode]
            below = near + strength * strength
            above = far + strength * strength
            common = (2.0 * strength) / (below * above)
            first = mode * half_rows + segment * segment_rows
            columns = slice(first, first + segment_rows)
            for part, value in enumerate((common * (below + above), common * cross)):
                high, low = split(value)
                table[part, :padded_rows, columns] = high
                table[part, padded_rows:, columns] = low
    for block in range(blocks):
        fetch(block).wait()
        for slot in range(slots):
            for mode in range(modes):
                weights[
                    block, slot * size : (slot + 1) * size, mode * size : (mode + 1) * size
                ] = held[block, slot, mode].T


def step_kernel(dims, coded, final, plan, *refs):
    freq_count, segments, segment_rows, padded_rows, modes, sides = dims
    pieces, (weights, table, gap_out), refs = refs[:sides], refs[sides : sides + 3], refs[sides + 3 :]
    fetched, ratios, high, low = refs[-4:]
    half_rows = segments * segment_rows
    blocks = weights.shape[0]
    size = LANES
    slots = weights.shape[1] // size
    holders = pieces[0].shape[0] // segments
    for pair in range(blocks * slots):
        column = pl.multiple_of(plan[PLACE, pair] * size, size)
        holder = plan[HOLDER, pair]
        for side, piece in enumerate(pieces):

            @pl.when(plan[SIDE, pair] == side)
            def _():
                for segment in range(segments):
                    rows = slice(segment * segment_rows, (segment + 1) * segment_rows)
                    fetched[pair, rows] = piece[
                        segment * holders + holder, :, pl.ds(column, size)
                    ]

    shape = (segment_rows, size)
    omegas = []
    for segment in range(segments):
        col = lax.broadcasted_iota(jnp.int32, shape, 0) + plan[ROWS, 1 + segment]
        omegas.append(omega_of(col, freq_count))
    col_omega = jnp.concatenate(omegas, axis=0)
    square = col_omega * col_omega
    for block in range(blocks):
        for slot in range(slots):
            pair = block * slots + slot
            gap = decoded(fetched[pair]) if coded else fetched[pair]
            live = plan[LIVE, pair].astype(jnp.float32)
            inverse = lax.rsqrt(square + gap * gap) * live
            lanes = slice(slot * size, (slot + 1) * size)
            ratios[block, :half_rows, lanes] = (gap * inverse).astype(jnp.bfloat16)
            ratios[block, half_rows:, lanes] = (col_omega * inverse).astype(jnp.bfloat16)
        lanes = slice(block * size, (block + 1) * size)
        for part in range(2):
            for start in range(0, modes, 2):
                stop = min(start + 2, modes)
                terms = jnp.dot(
                    ratios[block, part * half_rows : (part + 1) * half_rows, :],
                    weights[block, :, start * size : stop * size],
                    preferred_element_type=jnp.float32,
                )
                upper, lower = split(terms)
                for mode in range(start, stop):
                    rows = slice(mode * half_rows, (mode + 1) * half_rows)
                    taken = slice((mode - start) * size, (mode - start + 1) * size)
                    high[part, rows, lanes] = upper[:, taken]
                    low[part, rows, lanes] = lower[:, taken]
    summed = []
    for part in range(2):
        both = jnp.dot(table[part], high[part], preferred_element_type=jnp.float32)
        rest = jnp.dot(
            table[part, :padded_rows], low[part], preferred_element_type=jnp.float32
        )
        summed.append(both[:padded_rows] + (both[padded_rows:] + rest))
    own_rows, width = gap_out.shape[-2:]
    row = lax.broadcasted_iota(jnp.int32, (own_rows, width), 0) + plan[ROWS, 0]
    temperature = CUTOFF / freq_count
    renorm = 1.0 + temperature * summed[1][:own_rows] / omega_of(row, freq_count)
    gap = temperature * summed[0][:own_rows] / renorm
    if final:
        refs[0][...] = renorm
        gap_out[...] = gap
    elif coded:
        code = encoded(gap)
        for copy in range(gap_out.shape[0]):
            gap_out[copy] = code
    else:
        gap_out[...] = gap


def gather_pairwise(codes):
    chips = lax.all_to_all(codes, ("zlo", "x"), 0, 0, tiled=True)
    return [chips, lax.ppermute(chips, "core", [(0, 1), (1, 0)])]


def gather_general(gap, half_groups):
    everyone = lax.all_gather(gap, "state", axis=0, tiled=False)
    rows = lax.all_gather(everyone, "freq", axis=1, tiled=True)
    own_rows = gap.shape[0]
    start = (lax.axis_index("freq") // half_groups) * (half_groups * own_rows)
    return [lax.dynamic_slice_in_dim(rows, start, half_groups * own_rows, 1)]


def on_device(pairwise, freq_groups, gap_in, coupling, pair_cols, pair_count, block_order, phonon):
    own_rows, row_width = gap_in.shape
    blocks, slots, modes, size, _ = coupling.shape
    freq_count = own_rows * freq_groups
    half_rows = freq_count // 2
    half_groups = freq_groups // 2
    padded_rows = -(-own_rows // 16) * 16
    if pairwise:
        segments, sides = 2, 2
        half = lax.axis_index("zhi") * half_rows
        own = half + lax.axis_index("zlo") * own_rows
        meta = [own, half, half + own_rows, lax.axis_index("core")]
    else:
        segments, sides = 1, 1
        freq_at = lax.axis_index("freq")
        meta = [freq_at * own_rows, (freq_at // half_groups) * half_rows, 0]
    meta = jnp.stack([jnp.asarray(value, jnp.int32) for value in meta])
    segment_rows = half_rows // segments
    dims = (freq_count, segments, segment_rows, padded_rows, modes, sides)
    smem = pl.BlockSpec(memory_space=pltpu.SMEM)
    vmem = pl.BlockSpec(memory_space=pltpu.VMEM)
    link_type = jnp.int16 if pairwise else jnp.float32
    passed_shape = ((4,) if pairwise else ()) + gap_in.shape

    passed = gap_in
    if pairwise:
        passed = pl.pallas_call(
            encode_kernel,
            out_shape=jax.ShapeDtypeStruct(passed_shape, link_type),
            in_specs=[vmem],
            out_specs=vmem,
            compiler_params=pltpu.CompilerParams(vmem_limit_bytes=8 << 20),
            cost_estimate=pl.CostEstimate(
                flops=10_000_000_000, bytes_accessed=40_000_000, transcendentals=0
            ),
            name="encode",
        )(gap_in)

    plan, weights, table = pl.pallas_call(
        functools.partial(tables_kernel, dims),
        out_shape=[
            jax.ShapeDtypeStruct((5, max(blocks * slots, 1 + segments)), jnp.int32),
            jax.ShapeDtypeStruct((blocks, slots * size, modes * size), jnp.bfloat16),
            jax.ShapeDtypeStruct((2, 2 * padded_rows, modes * half_rows), jnp.bfloat16),
        ],
        in_specs=[smem] * 5 + [pl.BlockSpec(memory_space=pltpu.HBM)],
        out_specs=[smem, vmem, vmem],
        scratch_shapes=[
            pltpu.VMEM(coupling.shape, jnp.bfloat16),
            pltpu.SemaphoreType.DMA((blocks,)),
        ],
        compiler_params=pltpu.CompilerParams(vmem_limit_bytes=32 << 20),
        cost_estimate=pl.CostEstimate(
            flops=10_000_000, bytes_accessed=8_000_000, transcendentals=0
        ),
        name="tables",
    )(meta, phonon, pair_cols, pair_count, block_order, coupling)

    def step(final, pieces):
        full = jax.ShapeDtypeStruct(gap_in.shape, jnp.float32)
        outs = [full, full] if final else [jax.ShapeDtypeStruct(passed_shape, link_type)]
        inputs = [*pieces, weights, table]
        return pl.pallas_call(
            functools.partial(step_kernel, dims, pairwise, final),
            out_shape=outs,
            in_specs=[smem] + [vmem] * len(inputs),
            out_specs=[vmem] * len(outs),
            scratch_shapes=[
                pltpu.VMEM((blocks * slots, half_rows, size), link_type),
                pltpu.VMEM((blocks, 2 * half_rows, slots * size), jnp.bfloat16),
                pltpu.VMEM((2, modes * half_rows, row_width), jnp.bfloat16),
                pltpu.VMEM((2, modes * half_rows, row_width), jnp.bfloat16),
            ],
            compiler_params=pltpu.CompilerParams(vmem_limit_bytes=32 << 20),
            cost_estimate=pl.CostEstimate(
                flops=3_000_000_000, bytes_accessed=8_000_000, transcendentals=0
            ),
            name="step",
        )(plan, *inputs)

    for iteration in range(ITERS):
        if pairwise:
            pieces = gather_pairwise(passed)
        else:
            pieces = gather_general(passed, half_groups)
        results = step(iteration == ITERS - 1, pieces)
        passed = results[0]
    return tuple(results)


def solution(mesh):
    shape = tuple(mesh.shape[axis] for axis in ("parts", "freq", "state"))
    pairwise = shape[1:] == (4, 4)
    parts, freq, state = "parts", "freq", "state"
    if pairwise:
        names = ("parts", "zhi", "zlo", "x", "core")
        mesh = jax.sharding.Mesh(mesh.devices.reshape(shape[0], 2, 2, 2, 2), names)
        freq, state = ("zhi", "zlo"), ("x", "core")
    rows = ("parts", *freq) if pairwise else ("parts", freq)
    groups = ("parts", *state) if pairwise else ("parts", state)
    return jax.shard_map(
        functools.partial(on_device, pairwise, shape[1]),
        mesh=mesh,
        in_specs=(
            P(rows, state),
            P(groups, None, None, None, None),
            P(groups, None),
            P(groups),
            P(parts),
            P(parts),
        ),
        out_specs=(P(rows, state), P(rows, state)),
        check_vma=False,
    )
```

time: 56.4 us -> 44.3 us (0.79)
  blocking collectives: 0 us -> 25.5 us
  waiting for transfers between devices: 14.8 us -> 1.91 us
  local copies, waits for them, and re-layouts: 9.7 us -> 1.07 us
  starting transfers between devices: 8.23 us -> 0.01 us
  Pallas kernels: 22.4 us -> 14.7 us
    all_to_all x0 -> x2, blocking collectives: none -> 25.5 us  [gather_pairwise(): chips = lax.all_to_all(codes, ('zlo', 'x'), 0, 0, tiled=True)]
    ppermute x12 -> x2, waiting for transfers between devices: 14.8 us -> 1.91 us  [gather_pairwise(): return [chips, lax.ppermute(chips, 'core', [(0, 1), (1, 0)])]]
    unnamed x31 -> x13, local copies, waits for them, and re-layouts: 9.7 us -> 1.07 us
    ppermute x12 -> x2, starting transfers between devices: 8.23 us -> 0.01 us  [gather_pairwise(): return [chips, lax.ppermute(chips, 'core', [(0, 1), (1, 0)])]]
    pallas_call x8 -> x4, Pallas kernels: 22.4 us -> 14.7 us  [the longest x2 11.3 us: step(): pl.pallas_call(functools.partial(step_kernel, dims, pairwise, final), out...]
  transfers between devices with their start and end apart: 12 -> 2, of which waited for: 6 -> 1; matrix products, arithmetic and copies ran while one was open for 0% -> 0% of each run, Pallas kernels for 18% -> 7%
where the time goes in v4:
time: 44.3 us; the launch traced here: 44.1 us
  blocking collectives  25.5 us (58%)
  Pallas kernels  14.7 us (33%)
  waiting for transfers between devices  1.91 us (4%)
  local copies, waits for them, and re-layouts  1.07 us (2%)
  between operations  0.71 us (2%)
    all_to_all x2, blocking collectives, gather_pairwise(): chips = lax.all_to_all(codes, ('zlo', 'x'), 0, 0, tiled=True)  25.5 us
    pallas_call x2, Pallas kernels, step(): pl.pallas_call(functools.partial(step_kernel, dims, pairwise, final), out...  11.3 us
    pallas_call x1, Pallas kernels, on_device(): pl.pallas_call(functools.partial(tables_kernel, dims), out_shape=[jax.Sha...  3.3 us
    ppermute x2, waiting for transfers between devices, gather_pairwise(): return [chips, lax.ppermute(chips, 'core', [(0, 1), (1, 0)])]  1.91 us
    unnamed x13, local copies, waits for them, and re-layouts  1.07 us
  transfers between devices with their start and end apart: 2, of which 1 were waited for; matrix products, arithmetic and copies ran while one was open for 0% of the time, Pallas kernels for 7%

profile of v4, /device:TPU:0, one launch (start us, length us, event | category | flops | bytes accessed | tf_op | source)
XLA Modules:
  0.0 44.1 jit_solution(1683346135809312749)
XLA Ops:
  0.6 0.0 copy-start.1
  0.6 0.0 copy-start.3
  0.7 0.0 copy-start.2
  0.7 0.0 copy-start.4
  0.7 1.0 %copy-done.4 = f32[128,512]{1,0:T(8,128)S(1)} copy-done((f32[128,512]{1,0:T(8,128)S(1)}, f32[128,512]{1,0:T(8,128)}, u32[]{:S(2)}) %copy-start.4) | copy-done | bytes 262168
  1.6 0.0 copy-start.5
  1.6 0.0 copy-start
  1.6 0.1 encode.1
  1.8 13.7 %all_to_all.10.refs_0_ = s16[4,128,512]{2,1,0:T(8,128)(2,1)S(1)} all-to-all(s16[4,128,512]{2,1,0:T(8,128)(2,1)S(1)} %encode.1), channel_id=1, replica_groups=mesh['parts'=2,'zhi'=2,'zlo'=2,'x'=2,'core'=2] {'zlo','x'}, dimensions={0} | all-to-all | bytes 1048576 | tf_op jit(solution)/shard_map/all_to_all | solution.py:179
  15.5 0.0 collective-permute-start
  15.5 0.0 copy-done.5
  15.5 0.1 copy.8.pair_cols
  15.6 0.1 pad_add_fusion.meta
  15.6 0.0 copy-done.1
  15.6 0.0 copy-done.3
  15.6 0.0 copy-done.2
  15.6 0.0 copy-done
  15.7 3.3 %tables.1 = (s32[5,8]{1,0:T(8,128)S(1)}, bf16[4,256,1152]{2,1,0:T(8,128)(2,1)S(1)}, bf16[2,256,2304]{2,1,0:T(8,128)(2,1)S(1)}) custom-call(s32[4]{0:T(128)S(1)} %pad_add_fusion.meta, f32[9]{0:T(128)S(1)} %copy-done.1, s32[4,2]{1,0:T(4,128)S(1)} %copy.8.pair_cols, s32[4]{0:T(128)S(1)} %copy-done.2, s32[16]{0:T(128)S(1)} %copy-done.3, ...), custom_call_target="tpu_custom_call" | custom-call | flops 10000000 | bytes 8000000 | tf_op jit(solution)/shard_map/tables/pallas_call | solution.py:229
  19.0 0.0 collective-permute-done.refs_1_
  19.0 5.3 %step.2 = s16[4,128,512]{2,1,0:T(8,128)(2,1)S(1)} custom-call(s32[5,8]{1,0:T(8,128)S(1)} %get-tuple-element.5.plan, s16[4,128,512]{2,1,0:T(8,128)(2,1)S(1)} %all_to_all.10.refs_0_, s16[4,128,512]{2,1,0:T(8,128)(2,1)S(1)} %collective-permute-done.refs_1_, bf16[4,256,1152]{2,1,0:T(8,128)(2,1)S(1)} %get-tuple-element.6.refs_2_, ...), custom_call_target="tpu_custom_call" | custom-call | flops 3000000000 | bytes 8000000 | tf_op jit(solution)/shard_map/step/pallas_call | solution.py:253
  24.3 11.9 %all_to_all.11.refs_0_ = s16[4,128,512]{2,1,0:T(8,128)(2,1)S(1)} all-to-all(s16[4,128,512]{2,1,0:T(8,128)(2,1)S(1)} %step.2), channel_id=1, replica_groups=mesh['parts'=2,'zhi'=2,'zlo'=2,'x'=2,'core'=2] {'zlo','x'}, dimensions={0} | all-to-all | bytes 1048576 | tf_op jit(solution)/shard_map/all_to_all | solution.py:179
  36.2 0.0 collective-permute-start.1
  36.2 1.9 %collective-permute-done.1.refs_1_ = s16[4,128,512]{2,1,0:T(8,128)(2,1)S(1)} collective-permute-done((s16[4,128,512]{2,1,0:T(8,128)(2,1)S(1)}, s16[4,128,512]{2,1,0:T(8,128)(2,1)S(1)}, u32[]{:S(2)}, u32[]{:S(2)}) %collective-permute-start.1) | collective-permute-done | bytes 524320 | tf_op jit(solution)/shard_map/ppermute | solution.py:180
  38.1 6.0 %step.3 = (f32[128,512]{1,0:T(8,128)}, f32[128,512]{1,0:T(8,128)}) custom-call(s32[5,8]{1,0:T(8,128)S(1)} %get-tuple-element.5.plan, s16[4,128,512]{2,1,0:T(8,128)(2,1)S(1)} %all_to_all.11.refs_0_, s16[4,128,512]{2,1,0:T(8,128)(2,1)S(1)} %collective-permute-done.1.refs_1_, bf16[4,256,1152]{2,1,0:T(8,128)(2,1)S(1)} %get-tuple-element.6.refs_2_, ...), custom_call_target="tpu_custom_call" | custom-call | flops 3000000000 | bytes 8000000 | tf_op jit(solution)/shard_map/step/pallas_call | solution.py:253
Async XLA Ops:
  0.6 15.0 %copy-start.1 = (f32[9]{0:T(128)S(1)}, f32[9]{0:T(128)}, u32[]{:S(2)}) copy-start(f32[9]{0:T(128)} %phonon.1) | copy-start | bytes 112
  0.6 15.0 %copy-start.3 = (s32[16]{0:T(128)S(1)}, s32[16]{0:T(128)}, u32[]{:S(2)}) copy-start(s32[16]{0:T(128)} %block_order.1) | copy-start | bytes 196
  0.7 15.0 %copy-start.2 = (s32[4]{0:T(128)S(1)}, s32[4]{0:T(128)}, u32[]{:S(2)}) copy-start(s32[4]{0:T(128)} %pair_count.1) | copy-start | bytes 52
  0.7 1.0 %copy-start.4 = (f32[128,512]{1,0:T(8,128)S(1)}, f32[128,512]{1,0:T(8,128)}, u32[]{:S(2)}) copy-start(f32[128,512]{1,0:T(8,128)} %gap.1) | copy-start | bytes 786436
  1.6 13.8 %copy-start.5 = (s32[4,2]{0,1:T(2,128)S(1)}, s32[4,2]{0,1:T(2,128)}, u32[]{:S(2)}) copy-start(s32[4,2]{0,1:T(2,128)} %param.8) | copy-start | bytes 100
  1.6 14.0 %copy-start = (bf16[4,2,9,128,128]{4,3,2,1,0:T(8,128)(2,1)S(1)}, bf16[4,2,9,128,128]{4,3,2,1,0:T(8,128)(2,1)}, u32[]{:S(2)}) copy-start(bf16[4,2,9,128,128]{4,3,2,1,0:T(8,128)(2,1)} %coupling.1) | copy-start | bytes 7077892
  15.5 3.5 %collective-permute-start = (s16[4,128,512]{2,1,0:T(8,128)(2,1)S(1)}, s16[4,128,512]{2,1,0:T(8,128)(2,1)S(1)}, u32[]{:S(2)}, u32[]{:S(2)}) collective-permute-start(s16[4,128,512]{2,1,0:T(8,128)(2,1)S(1)} %all_to_all.10.refs_0_), channel_id=1, source_target_pairs={{0,1},{1,0},{2,3},{3,2},{4,5},{5,4},{6,7},{7,6},{8,9},{9,8},{10,11... | collective-permute-start | bytes 1572872 | tf_op jit(solution)/shard_map/ppermute | solution.py:180
  36.2 1.9 %collective-permute-start.1 = (s16[4,128,512]{2,1,0:T(8,128)(2,1)S(1)}, s16[4,128,512]{2,1,0:T(8,128)(2,1)S(1)}, u32[]{:S(2)}, u32[]{:S(2)}) collective-permute-start(s16[4,128,512]{2,1,0:T(8,128)(2,1)S(1)} %all_to_all.11.refs_0_), channel_id=1, source_target_pairs={{0,1},{1,0},{2,3},{3,2},{4,5},{5,4},{6,7},{7,6},{8,9},{9,8},{10,11... | collective-permute-start | bytes 1572872 | tf_op jit(solution)/shard_map/ppermute | solution.py:180

commit v5 on v3

v5 whole, which is shorter than its diff:
```python
import functools

import jax
import jax.numpy as jnp
from jax import lax
from jax.experimental import pallas as pl
from jax.experimental.pallas import tpu as pltpu
from jax.sharding import PartitionSpec as P

ITERS = 2
CUTOFF = 4.0
LANES = 128
GAP_LIMIT = 10.0
CODE_LIMIT = 32767.0
CODE_POWER = 5
STEP_FLOPS = 1_000_000
HOLDER, PLACE, LIVE, SIDE, ROWS = 0, 1, 2, 3, 4


def omega_of(index, freq_count):
    return (2.0 * index.astype(jnp.float32) + 1.0 - freq_count) * (CUTOFF / freq_count)


def encoded(gap):
    share = jnp.minimum(jnp.abs(gap) * (1.0 / GAP_LIMIT), 1.0)
    root = jnp.exp2(jnp.log2(jnp.maximum(share, 1e-37)) * (1.0 / CODE_POWER))
    code = jnp.floor(root * CODE_LIMIT + 0.5)
    return jnp.where(gap < 0, -code, code).astype(jnp.int32).astype(jnp.int16)


def decoded(code):
    root = code.astype(jnp.float32) * (1.0 / CODE_LIMIT)
    square = root * root
    return (root * GAP_LIMIT) * (square * square)


def encode_kernel(gap, code):
    code[...] = encoded(gap[...])


def join_kernel(first, second, after, joined):
    joined[0] = first[...]
    joined[1] = second[...]


def split(value):
    high = value.astype(jnp.bfloat16)
    return high, (value - high.astype(jnp.float32)).astype(jnp.bfloat16)


def tables_kernel(
    dims, sides, meta, phonon, pair_cols, pair_count, block_order, coupling, plan, weights, *tables
):
    freq_count, segments, segment_rows, padded_rows, modes = dims
    blocks, slots = coupling.shape[:2]
    size = coupling.shape[3]
    for at in range(1 + segments):
        plan[ROWS, at] = meta[at]
    for block in range(blocks):
        for slot in range(slots):
            wanted = pair_cols[block, slot]
            position = jnp.int32(0)
            for at in range(block_order.shape[0]):
                position = jnp.where(block_order[at] == wanted, at, position)
            pair = block * slots + slot
            holder = position // blocks
            plan[HOLDER, pair] = (holder // sides) ^ meta[1 + segments]
            plan[SIDE, pair] = (holder % sides) ^ meta[2 + segments]
            plan[PLACE, pair] = position % blocks
            plan[LIVE, pair] = (pair_count[block] > slot).astype(jnp.int32)
    shape = (padded_rows, segment_rows)
    row_omega = omega_of(lax.broadcasted_iota(jnp.int32, shape, 0) + meta[0], freq_count)
    for segment in range(segments):
        col = lax.broadcasted_iota(jnp.int32, shape, 1) + meta[1 + segment]
        col_omega = omega_of(col, freq_count)
        near = (row_omega - col_omega) ** 2
        far = (row_omega + col_omega) ** 2
        cross = 4.0 * (row_omega * col_omega)
        for mode in range(modes):
            strength = phonon[mode]
            below = near + strength * strength
            above = far + strength * strength
            common = (2.0 * strength) / (below * above)
            columns = slice(mode * segment_rows, (mode + 1) * segment_rows)
            for part, value in enumerate((common * (below + above), common * cross)):
                high, low = split(value)
                tables[segment][part, :padded_rows, columns] = high
                tables[segment][part, padded_rows:, columns] = low
    for block in range(blocks):
        for slot in range(slots):
            for mode in range(modes):
                weights[
                    block, slot * size : (slot + 1) * size, mode * size : (mode + 1) * size
                ] = coupling[block, slot, mode].T


def step_kernel(dims, segment, sides, coded, final, plan, *refs):
    freq_count, segments, segment_rows, padded_rows, modes = dims
    refs = list(refs)
    ratios, high, low = refs[-3:]
    first, last = segment == 0, segment == segments - 1
    outs = refs[-5:-3] if last and final else refs[-4:-3]
    inputs = refs[: -3 - len(outs)]
    before = None if first else inputs.pop()
    weights, table = inputs[-2:]
    pieces = []
    for piece in inputs[:-2]:
        if len(piece.shape) == 3:
            pieces += [piece.at[at] for at in range(piece.shape[0])]
        else:
            pieces.append(piece)
    holders = len(pieces) // sides
    blocks = weights.shape[0]
    size = LANES
    slots = weights.shape[1] // size
    shape = (segment_rows, size)
    col = lax.broadcasted_iota(jnp.int32, shape, 0) + plan[ROWS, 1 + segment]
    col_omega = omega_of(col, freq_count)
    square = col_omega * col_omega

    def fetch(pair):
        column = pl.multiple_of(plan[PLACE, pair] * size, size)
        wanted = plan[SIDE, pair] * holders + plan[HOLDER, pair]
        value = pieces[0][:, pl.ds(column, size)]
        for at in range(1, len(pieces)):
            value = lax.select(wanted == at, pieces[at][:, pl.ds(column, size)], value)
        return decoded(value) if coded else value

    def find_ratios(block):
        for slot in range(slots):
            pair = block * slots + slot
            gap = fetch(pair)
            live = plan[LIVE, pair].astype(jnp.float32)
            inverse = lax.rsqrt(square + gap * gap) * live
            lanes = slice(slot * size, (slot + 1) * size)
            ratios[block, :segment_rows, lanes] = (gap * inverse).astype(jnp.bfloat16)
            ratios[block, segment_rows:, lanes] = (col_omega * inverse).astype(jnp.bfloat16)

    def find_terms(block):
        lanes = slice(block * size, (block + 1) * size)
        for start in range(0, modes, 2):
            stop = min(start + 2, modes)
            terms = jnp.dot(
                ratios[block],
                weights[block, :, start * size : stop * size],
                preferred_element_type=jnp.float32,
            )
            upper, lower = split(terms)
            for mode in range(start, stop):
                rows = slice(mode * segment_rows, (mode + 1) * segment_rows)
                taken = slice((mode - start) * size, (mode - start + 1) * size)
                for part in range(2):
                    source = slice(part * segment_rows, (part + 1) * segment_rows)
                    high[part, rows, lanes] = upper[source, taken]
                    low[part, rows, lanes] = lower[source, taken]

    def find_sums(lanes):
        sums = []
        for part in range(2):
            both = jnp.dot(
                table[part], high[part, :, lanes], preferred_element_type=jnp.float32
            )
            rest = jnp.dot(
                table[part, :padded_rows],
                low[part, :, lanes],
                preferred_element_type=jnp.float32,
            )
            total = both[:padded_rows] + (both[padded_rows:] + rest)
            sums.append(total if first else total + before[part, :, lanes])
        if not last:
            for part in range(2):
                outs[0][part, :, lanes] = sums[part]
            return
        own_rows = outs[0].shape[0]
        width = lanes.stop - lanes.start
        row = lax.broadcasted_iota(jnp.int32, (own_rows, width), 0) + plan[ROWS, 0]
        temperature = CUTOFF / freq_count
        renorm = 1.0 + temperature * sums[1][:own_rows] / omega_of(row, freq_count)
        gap = temperature * sums[0][:own_rows] / renorm
        if final:
            outs[1][:, lanes] = renorm
            outs[0][:, lanes] = gap
        else:
            outs[0][:, lanes] = encoded(gap) if coded else gap

    for block in range(blocks):
        find_ratios(block)
    for block in range(blocks):
        find_terms(block)
        if block % 2 == 1 and block > 1:
            find_sums(slice((block - 3) * size, (block - 1) * size))
    find_sums(slice((blocks - 2) * size, blocks * size))


SWAP = [(0, 1), (1, 0)]


def gather_general(gap, half_groups):
    everyone = lax.all_gather(gap, "state", axis=0, tiled=False)
    rows = lax.all_gather(everyone, "freq", axis=1, tiled=True)
    own_rows = gap.shape[0]
    start = (lax.axis_index("freq") // half_groups) * (half_groups * own_rows)
    return [lax.dynamic_slice_in_dim(rows, start, half_groups * own_rows, 1)]


def on_device(pairwise, freq_groups, gap_in, coupling, pair_cols, pair_count, block_order, phonon):
    own_rows, row_width = gap_in.shape
    blocks, slots, modes, size, _ = coupling.shape
    freq_count = own_rows * freq_groups
    half_rows = freq_count // 2
    half_groups = freq_groups // 2
    padded_rows = -(-own_rows // 16) * 16
    if pairwise:
        segments, sides = 2, 2
        half = lax.axis_index("zhi") * half_rows
        own = half + lax.axis_index("zlo") * own_rows
        other = half + (1 - lax.axis_index("zlo")) * own_rows
        meta = [own, own, other, lax.axis_index("x"), lax.axis_index("core")]
    else:
        segments, sides = 1, 1
        freq_at = lax.axis_index("freq")
        meta = [freq_at * own_rows, (freq_at // half_groups) * half_rows, 0, 0]
    meta = jnp.stack([jnp.asarray(value, jnp.int32) for value in meta])
    segment_rows = half_rows // segments
    dims = (freq_count, segments, segment_rows, padded_rows, modes)
    smem = pl.BlockSpec(memory_space=pltpu.SMEM)
    vmem = pl.BlockSpec(memory_space=pltpu.VMEM)
    link_type = jnp.int16 if pairwise else jnp.float32

    passed = gap_in
    if pairwise:
        passed = pl.pallas_call(
            encode_kernel,
            out_shape=jax.ShapeDtypeStruct(gap_in.shape, link_type),
            in_specs=[vmem],
            out_specs=vmem,
            compiler_params=pltpu.CompilerParams(vmem_limit_bytes=8 << 20),
            cost_estimate=pl.CostEstimate(
                flops=10_000_000_000, bytes_accessed=40_000_000, transcendentals=0
            ),
            name="encode",
        )(gap_in)

    plan, weights, *tables = pl.pallas_call(
        functools.partial(tables_kernel, dims, sides),
        out_shape=[
            jax.ShapeDtypeStruct((5, max(blocks * slots, 1 + segments)), jnp.int32),
            jax.ShapeDtypeStruct((blocks, slots * size, modes * size), jnp.bfloat16),
        ]
        + [jax.ShapeDtypeStruct((2, 2 * padded_rows, modes * segment_rows), jnp.bfloat16)]
        * segments,
        in_specs=[smem] * 5 + [vmem],
        out_specs=[smem] + [vmem] * (1 + segments),
        compiler_params=pltpu.CompilerParams(vmem_limit_bytes=24 << 20),
        cost_estimate=pl.CostEstimate(
            flops=10_000_000, bytes_accessed=8_000_000, transcendentals=0
        ),
        name="tables",
    )(meta, phonon, pair_cols, pair_count, block_order, coupling)

    def step(plan, segment, final, pieces, before):
        full = jax.ShapeDtypeStruct(gap_in.shape, jnp.float32)
        if segment < segments - 1:
            outs = [jax.ShapeDtypeStruct((2, padded_rows, row_width), jnp.float32)]
        elif final:
            outs = [full, full]
        else:
            outs = [jax.ShapeDtypeStruct(gap_in.shape, link_type)]
        inputs = [*pieces, weights, tables[segment], *before]
        return pl.pallas_call(
            functools.partial(step_kernel, dims, segment, sides, pairwise, final),
            out_shape=outs,
            in_specs=[smem] + [vmem] * len(inputs),
            out_specs=[vmem] * len(outs),
            scratch_shapes=[
                pltpu.VMEM((blocks, 2 * segment_rows, slots * size), jnp.bfloat16),
                pltpu.VMEM((2, modes * segment_rows, row_width), jnp.bfloat16),
                pltpu.VMEM((2, modes * segment_rows, row_width), jnp.bfloat16),
            ],
            compiler_params=pltpu.CompilerParams(vmem_limit_bytes=24 << 20),
            cost_estimate=pl.CostEstimate(
                flops=STEP_FLOPS, bytes_accessed=100_000, transcendentals=0
            ),
            name="step",
        )(plan, *inputs)

    def join(near, across, after):
        return pl.pallas_call(
            join_kernel,
            out_shape=jax.ShapeDtypeStruct((2, *near.shape), near.dtype),
            in_specs=[vmem, vmem, pl.BlockSpec(memory_space=pl.ANY)],
            out_specs=vmem,
            compiler_params=pltpu.CompilerParams(vmem_limit_bytes=4 << 20),
            cost_estimate=pl.CostEstimate(flops=1000, bytes_accessed=1000, transcendentals=0),
            name="join",
        )(near, across, after)

    for iteration in range(ITERS):
        final = iteration == ITERS - 1
        if not pairwise:
            results = step(plan, 0, final, gather_general(passed, half_groups), [])
        else:
            along_x = lax.ppermute(passed, "x", SWAP)
            along_z = lax.ppermute(passed, "zlo", SWAP)
            if iteration == 0:
                along_x, plan = lax.optimization_barrier((along_x, plan))
            relayed = lax.ppermute(along_z, "x", SWAP)
            near = [passed, along_x]
            pieces = near + [lax.ppermute(piece, "core", SWAP) for piece in near]
            results = step(plan, 0, final, pieces, [])
            far = join(along_z, relayed, *results)
            results = step(plan, 1, final, [far, lax.ppermute(far, "core", SWAP)], results)
        passed = results[0]
    return tuple(results)


def solution(mesh):
    shape = tuple(mesh.shape[axis] for axis in ("parts", "freq", "state"))
    pairwise = shape[1:] == (4, 4)
    parts, freq, state = "parts", "freq", "state"
    if pairwise:
        names = ("parts", "zhi", "zlo", "x", "core")
        mesh = jax.sharding.Mesh(mesh.devices.reshape(shape[0], 2, 2, 2, 2), names)
        freq, state = ("zhi", "zlo"), ("x", "core")
    rows = ("parts", *freq) if pairwise else ("parts", freq)
    groups = ("parts", *state) if pairwise else ("parts", state)
    return jax.shard_map(
        functools.partial(on_device, pairwise, shape[1]),
        mesh=mesh,
        in_specs=(
            P(rows, state),
            P(groups, None, None, None, None),
            P(groups, None),
            P(groups),
            P(parts),
            P(parts),
        ),
        out_specs=(P(rows, state), P(rows, state)),
        check_vma=False,
    )
```

time: 56.4 us -> 36.9 us (0.65)
  local copies, waits for them, and re-layouts: 9.7 us -> 1.29 us
  Pallas kernels: 22.4 us -> 15.4 us
  waiting for transfers between devices: 14.8 us -> 9.92 us
  starting transfers between devices: 8.23 us -> 9.31 us
    unnamed x31 -> x13, local copies, waits for them, and re-layouts: 9.7 us -> 1.21 us
    ppermute x12, waiting for transfers between devices: 14.8 us -> 9.92 us  [the longest x2 3.04 us: on_device(): lax.ppermute(far, 'core', SWAP)]
    pallas_call x2, Pallas kernels: 3.38 us -> 0.04 us  [join(): pl.pallas_call(join_kernel, out_shape=jax.ShapeDtypeStruct((2, *near.shap...]
    pallas_call x5, Pallas kernels: 17.2 us -> 15.3 us  [the longest x4 13 us: step(): pl.pallas_call(functools.partial(step_kernel, dims, segment, sides, pairw...]
    pallas_call x1, Pallas kernels: 1.76 us -> 0.14 us  [on_device(): pl.pallas_call(encode_kernel, out_shape=jax.ShapeDtypeStruct(gap_in.shape...]
    ppermute x12, starting transfers between devices: 8.23 us -> 9.31 us  [the longest x2 4.13 us: on_device(): along_x = lax.ppermute(passed, 'x', SWAP)]
  transfers between devices with their start and end apart: 12 -> 12, of which waited for: 6 -> 8; matrix products, arithmetic and copies ran while one was open for 0% -> 0% of each run, Pallas kernels for 18% -> 23%
where the time goes in v5:
time: 36.9 us; the launch traced here: 36.7 us
  Pallas kernels  15.4 us (42%)
  waiting for transfers between devices  9.92 us (27%)
  starting transfers between devices  9.31 us (25%)
  local copies, waits for them, and re-layouts  1.29 us (3%)
  between operations  0.75 us (2%)
    pallas_call x4, Pallas kernels, step(): pl.pallas_call(functools.partial(step_kernel, dims, segment, sides, pairw...  13 us
    ppermute x2, starting transfers between devices, on_device(): along_x = lax.ppermute(passed, 'x', SWAP)  4.13 us
    ppermute x2, starting transfers between devices, on_device(): along_z = lax.ppermute(passed, 'zlo', SWAP)  3.14 us
    ppermute x2, waiting for transfers between devices, on_device(): lax.ppermute(far, 'core', SWAP)  3.04 us
    ppermute x2, waiting for transfers between devices, on_device(): along_x = lax.ppermute(passed, 'x', SWAP)  2.92 us
    ppermute x2, waiting for transfers between devices, on_device(): relayed = lax.ppermute(along_z, 'x', SWAP)  2.54 us
    pallas_call x1, Pallas kernels, on_device(): pl.pallas_call(functools.partial(tables_kernel, dims, sides), out_shape=[...  2.25 us
    ppermute x2, starting transfers between devices, on_device(): relayed = lax.ppermute(along_z, 'x', SWAP)  1.32 us
  transfers between devices with their start and end apart: 12, of which 8 were waited for; matrix products, arithmetic and copies ran while one was open for 0% of the time, Pallas kernels for 23%

profile of v5, /device:TPU:0, one launch (start us, length us, event | category | flops | bytes accessed | tf_op | source)
XLA Modules:
  0.0 36.7 jit_solution(13264820391725350879)
XLA Ops:
  0.7 1.1 %copy-done.4 = f32[128,512]{1,0:T(8,128)S(1)} copy-done((f32[128,512]{1,0:T(8,128)S(1)}, f32[128,512]{1,0:T(8,128)}, u32[]{:S(2)}) %copy-start.4) | copy-done | bytes 262168
  1.8 0.1 encode.1.refs_0_
  1.9 3.0 %collective-permute-start = (s16[128,512]{1,0:T(8,128)(2,1)S(1)}, s16[128,512]{1,0:T(8,128)(2,1)S(1)}, u32[]{:S(2)}, u32[]{:S(2)}) collective-permute-start(s16[128,512]{1,0:T(8,128)(2,1)S(1)} %encode.1.refs_0_), channel_id=1, source_target_pairs={{0,2},{2,0},{1,3},{3,1},{4,6},{6,4},{5,7},{7,5},{8,10},{10,8},{9,1... | collective-permute-start | bytes 393224 | tf_op jit(solution)/shard_map/ppermute | solution.py:303
  4.9 1.6 %collective-permute-start.1 = (s16[128,512]{1,0:T(8,128)(2,1)S(1)}, s16[128,512]{1,0:T(8,128)(2,1)S(1)}, u32[]{:S(2)}, u32[]{:S(2)}) collective-permute-start(s16[128,512]{1,0:T(8,128)(2,1)S(1)} %encode.1.refs_0_), channel_id=1, source_target_pairs={{0,4},{4,0},{1,5},{5,1},{2,6},{6,2},{3,7},{7,3},{8,12},{12,8},{9,1... | collective-permute-start | bytes 393224 | tf_op jit(solution)/shard_map/ppermute | solution.py:304
  6.5 0.0 collective-permute-start.3
  6.5 0.1 copy.8.pair_cols
  6.6 0.1 stack.20.meta
  6.7 2.3 %tables.1 = (s32[5,8]{1,0:T(8,128)S(1)}, bf16[4,256,1152]{2,1,0:T(8,128)(2,1)S(1)}, bf16[2,256,1152]{2,1,0:T(8,128)(2,1)S(1)}, bf16[2,256,1152]{2,1,0:T(8,128)(2,1)S(1)}) custom-call(s32[5]{0:T(128)S(1)} %stack.20.meta, f32[9]{0:T(128)S(1)} %copy-done.1, s32[4,2]{1,0:T(4,128)S(1)} %copy.8.pair_cols, s32[4]{0:T(128)S(1)} %copy-done.2, s32[16]{0:T(128)S(1)} %copy-done.3, ...), custom_call_target="tpu_custom_call" | custom-call | flops 10000000 | bytes 8000000 | tf_op jit(solution)/shard_map/tables/pallas_call | solution.py:244
  9.0 0.0 collective-permute-done.refs_1_
  9.0 0.6 %collective-permute-start.4 = (s16[128,512]{1,0:T(8,128)(2,1)S(1)}, s16[128,512]{1,0:T(8,128)(2,1)S(1)}, u32[]{:S(2)}, u32[]{:S(2)}) collective-permute-start(s16[128,512]{1,0:T(8,128)(2,1)S(1)} %collective-permute-done.refs_1_), channel_id=1, source_target_pairs={{0,1},{1,0},{2,3},{3,2},{4,5},{5,4},{6,7},{7,6},{8,9},{9,8},{10,11... | collective-permute-start | bytes 393224 | tf_op jit(solution)/shard_map/ppermute | solution.py:309
  9.5 0.3 collective-permute-done.1.first
  9.9 0.4 collective-permute-start.2
  10.2 0.3 collective-permute-done.4.refs_3_
  10.5 3.1 %step.4.after.refs_4_ = f32[2,128,512]{2,1,0:T(8,128)S(1)} custom-call(s32[5,8]{1,0:T(8,128)S(1)} %get-tuple-element.9.plan, s16[128,512]{1,0:T(8,128)(2,1)S(1)} %encode.1.refs_0_, s16[128,512]{1,0:T(8,128)(2,1)S(1)} %collective-permute-done.refs_1_, s16[128,512]{1,0:T(8,128)(2,1)S(1)} %collective-permute-done.3.refs_2_, ...), custom_call_target="tpu_custom_call" | custom-call | flops 1000000 | bytes 100000 | tf_op jit(solution)/shard_map/step/pallas_call | solution.py:270
  13.6 1.4 %collective-permute-done.2.second = s16[128,512]{1,0:T(8,128)(2,1)S(1)} collective-permute-done((s16[128,512]{1,0:T(8,128)(2,1)S(1)}, s16[128,512]{1,0:T(8,128)(2,1)S(1)}, u32[]{:S(2)}, u32[]{:S(2)}) %collective-permute-start.2) | collective-permute-done | bytes 131104 | tf_op jit(solution)/shard_map/ppermute | solution.py:307
  15.0 0.1 collective-permute-start.5
  15.1 1.5 %collective-permute-done.5.refs_1_ = s16[2,128,512]{2,1,0:T(8,128)(2,1)S(1)} collective-permute-done((s16[2,128,512]{2,1,0:T(8,128)(2,1)S(1)}, s16[2,128,512]{2,1,0:T(8,128)(2,1)S(1)}, u32[]{:S(2)}, u32[]{:S(2)}) %collective-permute-start.5) | collective-permute-done | bytes 262176 | tf_op jit(solution)/shard_map/ppermute | solution.py:312
  16.6 3.1 %step.5.refs_0_ = s16[128,512]{1,0:T(8,128)(2,1)S(1)} custom-call(s32[5,8]{1,0:T(8,128)S(1)} %get-tuple-element.9.plan, s16[2,128,512]{2,1,0:T(8,128)(2,1)S(1)} %join.2.refs_0_, s16[2,128,512]{2,1,0:T(8,128)(2,1)S(1)} %collective-permute-done.5.refs_1_, bf16[4,256,1152]{2,1,0:T(8,128)(2,1)S(1)} %get-tuple-element.11.refs_4_.refs_2_, ...), custom_call_target="tpu_custom_call" | custom-call | flops 1000000 | bytes 100000 | tf_op jit(solution)/shard_map/step/pallas_call | solution.py:270
  19.8 1.1 %collective-permute-start.8 = (s16[128,512]{1,0:T(8,128)(2,1)S(1)}, s16[128,512]{1,0:T(8,128)(2,1)S(1)}, u32[]{:S(2)}, u32[]{:S(2)}) collective-permute-start(s16[128,512]{1,0:T(8,128)(2,1)S(1)} %step.5.refs_0_), channel_id=1, source_target_pairs={{0,2},{2,0},{1,3},{3,1},{4,6},{6,4},{5,7},{7,5},{8,10},{10,8},{9,1... | collective-permute-start | bytes 393224 | tf_op jit(solution)/shard_map/ppermute | solution.py:303
  20.9 1.6 %collective-permute-start.6 = (s16[128,512]{1,0:T(8,128)(2,1)S(1)}, s16[128,512]{1,0:T(8,128)(2,1)S(1)}, u32[]{:S(2)}, u32[]{:S(2)}) collective-permute-start(s16[128,512]{1,0:T(8,128)(2,1)S(1)} %step.5.refs_0_), channel_id=1, source_target_pairs={{0,4},{4,0},{1,5},{5,1},{2,6},{6,2},{3,7},{7,3},{8,12},{12,8},{9,1... | collective-permute-start | bytes 393224 | tf_op jit(solution)/shard_map/ppermute | solution.py:304
  22.4 0.0 collective-permute-start.9
  22.4 2.9 %collective-permute-done.8.refs_1_ = s16[128,512]{1,0:T(8,128)(2,1)S(1)} collective-permute-done((s16[128,512]{1,0:T(8,128)(2,1)S(1)}, s16[128,512]{1,0:T(8,128)(2,1)S(1)}, u32[]{:S(2)}, u32[]{:S(2)}) %collective-permute-start.8) | collective-permute-done | bytes 131104 | tf_op jit(solution)/shard_map/ppermute | solution.py:303
  25.4 0.0 collective-permute-start.10
  25.4 0.8 %collective-permute-done.6.first = s16[128,512]{1,0:T(8,128)(2,1)S(1)} collective-permute-done((s16[128,512]{1,0:T(8,128)(2,1)S(1)}, s16[128,512]{1,0:T(8,128)(2,1)S(1)}, u32[]{:S(2)}, u32[]{:S(2)}) %collective-permute-start.6) | collective-permute-done | bytes 131104 | tf_op jit(solution)/shard_map/ppermute | solution.py:304
  26.1 1.0 %collective-permute-start.7 = (s16[128,512]{1,0:T(8,128)(2,1)S(1)}, s16[128,512]{1,0:T(8,128)(2,1)S(1)}, u32[]{:S(2)}, u32[]{:S(2)}) collective-permute-start(s16[128,512]{1,0:T(8,128)(2,1)S(1)} %collective-permute-done.6.first), channel_id=1, source_target_pairs={{0,2},{2,0},{1,3},{3,1},{4,6},{6,4},{5,7},{7,5},{8,10},{10,8},{9,1... | collective-permute-start | bytes 393224 | tf_op jit(solution)/shard_map/ppermute | solution.py:307
  27.1 0.0 collective-permute-done.9.refs_2_
  27.1 0.0 collective-permute-done.10.refs_3_
  27.1 3.1 %step.6.after.refs_4_ = f32[2,128,512]{2,1,0:T(8,128)S(1)} custom-call(s32[5,8]{1,0:T(8,128)S(1)} %get-tuple-element.9.plan, s16[128,512]{1,0:T(8,128)(2,1)S(1)} %step.5.refs_0_, s16[128,512]{1,0:T(8,128)(2,1)S(1)} %collective-permute-done.8.refs_1_, s16[128,512]{1,0:T(8,128)(2,1)S(1)} %collective-permute-done.9.refs_2_, ...), custom_call_target="tpu_custom_call" | custom-call | flops 1000000 | bytes 100000 | tf_op jit(solution)/shard_map/step/pallas_call | solution.py:270
  30.2 1.1 %collective-permute-done.7.second = s16[128,512]{1,0:T(8,128)(2,1)S(1)} collective-permute-done((s16[128,512]{1,0:T(8,128)(2,1)S(1)}, s16[128,512]{1,0:T(8,128)(2,1)S(1)}, u32[]{:S(2)}, u32[]{:S(2)}) %collective-permute-start.7) | collective-permute-done | bytes 131104 | tf_op jit(solution)/shard_map/ppermute | solution.py:307
  31.3 0.1 collective-permute-start.11
  31.4 1.5 %collective-permute-done.11.refs_1_ = s16[2,128,512]{2,1,0:T(8,128)(2,1)S(1)} collective-permute-done((s16[2,128,512]{2,1,0:T(8,128)(2,1)S(1)}, s16[2,128,512]{2,1,0:T(8,128)(2,1)S(1)}, u32[]{:S(2)}, u32[]{:S(2)}) %collective-permute-start.11) | collective-permute-done | bytes 262176 | tf_op jit(solution)/shard_map/ppermute | solution.py:312
  32.9 3.8 %step.7 = (f32[128,512]{1,0:T(8,128)}, f32[128,512]{1,0:T(8,128)}) custom-call(s32[5,8]{1,0:T(8,128)S(1)} %get-tuple-element.9.plan, s16[2,128,512]{2,1,0:T(8,128)(2,1)S(1)} %join.3.refs_0_, s16[2,128,512]{2,1,0:T(8,128)(2,1)S(1)} %collective-permute-done.11.refs_1_, bf16[4,256,1152]{2,1,0:T(8,128)(2,1)S(1)} %get-tuple-element.11.refs_4_.refs_2_, ...), custom_call_target="tpu_custom_call" | custom-call | flops 1000000 | bytes 100000 | tf_op jit(solution)/shard_map/step/pallas_call | solution.py:270
  (14 shorter events, 0.1 us)
Async XLA Ops:
  0.6 6.0 %copy-start.3 = (s32[16]{0:T(128)S(1)}, s32[16]{0:T(128)}, u32[]{:S(2)}) copy-start(s32[16]{0:T(128)} %block_order.1) | copy-start | bytes 196
  0.6 6.0 %copy-start.1 = (f32[9]{0:T(128)S(1)}, f32[9]{0:T(128)}, u32[]{:S(2)}) copy-start(f32[9]{0:T(128)} %phonon.1) | copy-start | bytes 112
  0.7 6.0 %copy-start = (bf16[4,2,9,128,128]{4,3,2,1,0:T(8,128)(2,1)S(1)}, bf16[4,2,9,128,128]{4,3,2,1,0:T(8,128)(2,1)}, u32[]{:S(2)}) copy-start(bf16[4,2,9,128,128]{4,3,2,1,0:T(8,128)(2,1)} %coupling.1) | copy-start | bytes 7077892
  0.7 1.1 %copy-start.4 = (f32[128,512]{1,0:T(8,128)S(1)}, f32[128,512]{1,0:T(8,128)}, u32[]{:S(2)}) copy-start(f32[128,512]{1,0:T(8,128)} %gap.1) | copy-start | bytes 786436
  1.8 4.7 %copy-start.5 = (s32[4,2]{0,1:T(2,128)S(1)}, s32[4,2]{0,1:T(2,128)}, u32[]{:S(2)}) copy-start(s32[4,2]{0,1:T(2,128)} %param.8) | copy-start | bytes 100
  1.8 4.9 %copy-start.2 = (s32[4]{0:T(128)S(1)}, s32[4]{0:T(128)}, u32[]{:S(2)}) copy-start(s32[4]{0:T(128)} %pair_count.1) | copy-start | bytes 52
  1.9 7.0 %collective-permute-start = (s16[128,512]{1,0:T(8,128)(2,1)S(1)}, s16[128,512]{1,0:T(8,128)(2,1)S(1)}, u32[]{:S(2)}, u32[]{:S(2)}) collective-permute-start(s16[128,512]{1,0:T(8,128)(2,1)S(1)} %encode.1.refs_0_), channel_id=1, source_target_pairs={{0,2},{2,0},{1,3},{3,1},{4,6},{6,4},{5,7},{7,5},{8,10},{10,8},{9,1... | collective-permute-start | bytes 393224 | tf_op jit(solution)/shard_map/ppermute | solution.py:303
  4.9 5.0 %collective-permute-start.1 = (s16[128,512]{1,0:T(8,128)(2,1)S(1)}, s16[128,512]{1,0:T(8,128)(2,1)S(1)}, u32[]{:S(2)}, u32[]{:S(2)}) collective-permute-start(s16[128,512]{1,0:T(8,128)(2,1)S(1)} %encode.1.refs_0_), channel_id=1, source_target_pairs={{0,4},{4,0},{1,5},{5,1},{2,6},{6,2},{3,7},{7,3},{8,12},{12,8},{9,1... | collective-permute-start | bytes 393224 | tf_op jit(solution)/shard_map/ppermute | solution.py:304
  6.5 3.8 %collective-permute-start.3 = (s16[128,512]{1,0:T(8,128)(2,1)S(1)}, s16[128,512]{1,0:T(8,128)(2,1)S(1)}, u32[]{:S(2)}, u32[]{:S(2)}) collective-permute-start(s16[128,512]{1,0:T(8,128)(2,1)S(1)} %encode.1.refs_0_), channel_id=1, source_target_pairs={{0,1},{1,0},{2,3},{3,2},{4,5},{5,4},{6,7},{7,6},{8,9},{9,8},{10,11... | collective-permute-start | bytes 393224 | tf_op jit(solution)/shard_map/ppermute | solution.py:309
  9.0 1.6 %collective-permute-start.4 = (s16[128,512]{1,0:T(8,128)(2,1)S(1)}, s16[128,512]{1,0:T(8,128)(2,1)S(1)}, u32[]{:S(2)}, u32[]{:S(2)}) collective-permute-start(s16[128,512]{1,0:T(8,128)(2,1)S(1)} %collective-permute-done.refs_1_), channel_id=1, source_target_pairs={{0,1},{1,0},{2,3},{3,2},{4,5},{5,4},{6,7},{7,6},{8,9},{9,8},{10,11... | collective-permute-start | bytes 393224 | tf_op jit(solution)/shard_map/ppermute | solution.py:309
  9.9 5.1 %collective-permute-start.2 = (s16[128,512]{1,0:T(8,128)(2,1)S(1)}, s16[128,512]{1,0:T(8,128)(2,1)S(1)}, u32[]{:S(2)}, u32[]{:S(2)}) collective-permute-start(s16[128,512]{1,0:T(8,128)(2,1)S(1)} %collective-permute-done.1.first), channel_id=1, source_target_pairs={{0,2},{2,0},{1,3},{3,1},{4,6},{6,4},{5,7},{7,5},{8,10},{10,8},{9,1... | collective-permute-start | bytes 393224 | tf_op jit(solution)/shard_map/ppermute | solution.py:307
  15.0 1.6 %collective-permute-start.5 = (s16[2,128,512]{2,1,0:T(8,128)(2,1)S(1)}, s16[2,128,512]{2,1,0:T(8,128)(2,1)S(1)}, u32[]{:S(2)}, u32[]{:S(2)}) collective-permute-start(s16[2,128,512]{2,1,0:T(8,128)(2,1)S(1)} %join.2.refs_0_), channel_id=1, source_target_pairs={{0,1},{1,0},{2,3},{3,2},{4,5},{5,4},{6,7},{7,6},{8,9},{9,8},{10,11... | collective-permute-start | bytes 786440 | tf_op jit(solution)/shard_map/ppermute | solution.py:312
  19.8 5.6 %collective-permute-start.8 = (s16[128,512]{1,0:T(8,128)(2,1)S(1)}, s16[128,512]{1,0:T(8,128)(2,1)S(1)}, u32[]{:S(2)}, u32[]{:S(2)}) collective-permute-start(s16[128,512]{1,0:T(8,128)(2,1)S(1)} %step.5.refs_0_), channel_id=1, source_target_pairs={{0,2},{2,0},{1,3},{3,1},{4,6},{6,4},{5,7},{7,5},{8,10},{10,8},{9,1... | collective-permute-start | bytes 393224 | tf_op jit(solution)/shard_map/ppermute | solution.py:303
  20.9 5.3 %collective-permute-start.6 = (s16[128,512]{1,0:T(8,128)(2,1)S(1)}, s16[128,512]{1,0:T(8,128)(2,1)S(1)}, u32[]{:S(2)}, u32[]{:S(2)}) collective-permute-start(s16[128,512]{1,0:T(8,128)(2,1)S(1)} %step.5.refs_0_), channel_id=1, source_target_pairs={{0,4},{4,0},{1,5},{5,1},{2,6},{6,2},{3,7},{7,3},{8,12},{12,8},{9,1... | collective-permute-start | bytes 393224 | tf_op jit(solution)/shard_map/ppermute | solution.py:304
  22.4 4.7 %collective-permute-start.9 = (s16[128,512]{1,0:T(8,128)(2,1)S(1)}, s16[128,512]{1,0:T(8,128)(2,1)S(1)}, u32[]{:S(2)}, u32[]{:S(2)}) collective-permute-start(s16[128,512]{1,0:T(8,128)(2,1)S(1)} %step.5.refs_0_), channel_id=1, source_target_pairs={{0,1},{1,0},{2,3},{3,2},{4,5},{5,4},{6,7},{7,6},{8,9},{9,8},{10,11... | collective-permute-start | bytes 393224 | tf_op jit(solution)/shard_map/ppermute | solution.py:309
  25.4 1.8 %collective-permute-start.10 = (s16[128,512]{1,0:T(8,128)(2,1)S(1)}, s16[128,512]{1,0:T(8,128)(2,1)S(1)}, u32[]{:S(2)}, u32[]{:S(2)}) collective-permute-start(s16[128,512]{1,0:T(8,128)(2,1)S(1)} %collective-permute-done.8.refs_1_), channel_id=1, source_target_pairs={{0,1},{1,0},{2,3},{3,2},{4,5},{5,4},{6,7},{7,6},{8,9},{9,8},{10,11... | collective-permute-start | bytes 393224 | tf_op jit(solution)/shard_map/ppermute | solution.py:309
  26.1 5.1 %collective-permute-start.7 = (s16[128,512]{1,0:T(8,128)(2,1)S(1)}, s16[128,512]{1,0:T(8,128)(2,1)S(1)}, u32[]{:S(2)}, u32[]{:S(2)}) collective-permute-start(s16[128,512]{1,0:T(8,128)(2,1)S(1)} %collective-permute-done.6.first), channel_id=1, source_target_pairs={{0,2},{2,0},{1,3},{3,1},{4,6},{6,4},{5,7},{7,5},{8,10},{10,8},{9,1... | collective-permute-start | bytes 393224 | tf_op jit(solution)/shard_map/ppermute | solution.py:307
  31.3 1.6 %collective-permute-start.11 = (s16[2,128,512]{2,1,0:T(8,128)(2,1)S(1)}, s16[2,128,512]{2,1,0:T(8,128)(2,1)S(1)}, u32[]{:S(2)}, u32[]{:S(2)}) collective-permute-start(s16[2,128,512]{2,1,0:T(8,128)(2,1)S(1)} %join.3.refs_0_), channel_id=1, source_target_pairs={{0,1},{1,0},{2,3},{3,2},{4,5},{5,4},{6,7},{7,6},{8,9},{9,8},{10,11... | collective-permute-start | bytes 786440 | tf_op jit(solution)/shard_map/ppermute | solution.py:312

commit v6 on v5

--- a/solution.py
+++ b/solution.py
@@ -46,6 +46,32 @@
 def split(value):
     high = value.astype(jnp.bfloat16)
     return high, (value - high.astype(jnp.float32)).astype(jnp.bfloat16)
+
+
+def fill_tables(dims, meta, row_from, phonon, tables):
+    freq_count, segments, segment_rows, padded_rows, modes = dims
+    shape = (padded_rows, segment_rows)
+    row_omega = omega_of(lax.broadcasted_iota(jnp.int32, shape, 0) + meta[row_from], freq_count)
+    for segment in range(len(tables)):
+        col = lax.broadcasted_iota(jnp.int32, shape, 1) + meta[1 + segment]
+        col_omega = omega_of(col, freq_count)
+        near = (row_omega - col_omega) ** 2
+        far = (row_omega + col_omega) ** 2
+        cross = 4.0 * (row_omega * col_omega)
+        for mode in range(modes):
+            strength = phonon[mode]
+            below = near + strength * strength
+            above = far + strength * strength
+            common = (2.0 * strength) / (below * above)
+            columns = slice(mode * segment_rows, (mode + 1) * segment_rows)
+            for part, value in enumerate((common * (below + above), common * cross)):
+                high, low = split(value)
+                tables[segment][part, :padded_rows, columns] = high
+                tables[segment][part, padded_rows:, columns] = low
+
+
+def other_tables_kernel(dims, meta, phonon, *tables):
+    fill_tables(dims, meta, 2, phonon, tables)
 
 
 def tables_kernel(
@@ -68,24 +94,7 @@
             plan[SIDE, pair] = (holder % sides) ^ meta[2 + segments]
             plan[PLACE, pair] = position % blocks
             plan[LIVE, pair] = (pair_count[block] > slot).astype(jnp.int32)
-    shape = (padded_rows, segment_rows)
-    row_omega = omega_of(lax.broadcasted_iota(jnp.int32, shape, 0) + meta[0], freq_count)
-    for segment in range(segments):
-        col = lax.broadcasted_iota(jnp.int32, shape, 1) + meta[1 + segment]
-        col_omega = omega_of(col, freq_count)
-        near = (row_omega - col_omega) ** 2
-        far = (row_omega + col_omega) ** 2
-        cross = 4.0 * (row_omega * col_omega)
-        for mode in range(modes):
-            strength = phonon[mode]
-            below = near + strength * strength
-            above = far + strength * strength
-            common = (2.0 * strength) / (below * above)
-            columns = slice(mode * segment_rows, (mode + 1) * segment_rows)
-            for part, value in enumerate((common * (below + above), common * cross)):
-                high, low = split(value)
-                tables[segment][part, :padded_rows, columns] = high
-                tables[segment][part, padded_rows:, columns] = low
+    fill_tables(dims, meta, 0, phonon, tables)
     for block in range(blocks):
         for slot in range(slots):
             for mode in range(modes):
@@ -94,14 +103,21 @@
                 ] = coupling[block, slot, mode].T
 
 
-def step_kernel(dims, segment, sides, coded, final, plan, *refs):
+def step_kernel(dims, segment, span, sides, coded, final, keep, parted, plan, *refs):
     freq_count, segments, segment_rows, padded_rows, modes = dims
     refs = list(refs)
-    ratios, high, low = refs[-3:]
     first, last = segment == 0, segment == segments - 1
-    outs = refs[-5:-3] if last and final else refs[-4:-3]
-    inputs = refs[: -3 - len(outs)]
-    before = None if first else inputs.pop()
+    take = lambda count: [refs.pop() for _ in range(count)][::-1]
+    copied = last and final
+    if copied:
+        *held, sems = take(3)
+    high, low = (None, None) if keep else take(2)
+    ratios = refs.pop()
+    if keep:
+        high, low = take(2)
+    outs = take(2 if copied else 1)
+    inputs = refs
+    before = [inputs.pop() for _ in range(0 if first else parted)][::-1]
     weights, table = inputs[-2:]
     pieces = []
     for piece in inputs[:-2]:
@@ -110,7 +126,7 @@
         else:
             pieces.append(piece)
     holders = len(pieces) // sides
-    blocks = weights.shape[0]
+    blocks = span[1] - span[0]
     size = LANES
     slots = weights.shape[1] // size
     shape = (segment_rows, size)
@@ -128,7 +144,7 @@
 
     def find_ratios(block):
         for slot in range(slots):
-            pair = block * slots + slot
+            pair = (span[0] + block) * slots + slot
             gap = fetch(pair)
             live = plan[LIVE, pair].astype(jnp.float32)
             inverse = lax.rsqrt(square + gap * gap) * live
@@ -142,7 +158,7 @@
             stop = min(start + 2, modes)
             terms = jnp.dot(
                 ratios[block],
-                weights[block, :, start * size : stop * size],
+                weights[span[0] + block, :, start * size : stop * size],
                 preferred_element_type=jnp.float32,
             )
             upper, lower = split(terms)
@@ -153,6 +169,11 @@
                     source = slice(part * segment_rows, (part + 1) * segment_rows)
                     high[part, rows, lanes] = upper[source, taken]
                     low[part, rows, lanes] = lower[source, taken]
+
+    def earlier(part, lanes):
+        width = before[0].shape[-1]
+        start = lanes.start % width
+        return before[lanes.start // width][part, :, start : start + lanes.stop - lanes.start]
 
     def find_sums(lanes):
         sums = []
@@ -166,7 +187,7 @@
                 preferred_element_type=jnp.float32,
             )
             total = both[:padded_rows] + (both[padded_rows:] + rest)
-            sums.append(total if first else total + before[part, :, lanes])
+            sums.append(total if first else total + earlier(part, lanes))
         if not last:
             for part in range(2):
                 outs[0][part, :, lanes] = sums[part]
@@ -177,19 +198,54 @@
         temperature = CUTOFF / freq_count
         renorm = 1.0 + temperature * sums[1][:own_rows] / omega_of(row, freq_count)
         gap = temperature * sums[0][:own_rows] / renorm
-        if final:
-            outs[1][:, lanes] = renorm
-            outs[0][:, lanes] = gap
-        else:
+        if not final:
             outs[0][:, lanes] = encoded(gap) if coded else gap
-
+            return
+        for at, value in enumerate((gap, renorm)):
+            held[at][:, lanes] = value
+            copy_out(at, lanes).start()
+
+    def copy_out(at, lanes):
+        width = lanes.stop - lanes.start
+        return pltpu.make_async_copy(
+            held[at].at[:, pl.ds(lanes.start, width)],
+            outs[at].at[:, pl.ds(lanes.start, width)],
+            sems.at[at, lanes.start // width],
+        )
+
+    halves = [slice(start * size, (start + 2) * size) for start in range(0, blocks, 2)]
     for block in range(blocks):
         find_ratios(block)
     for block in range(blocks):
         find_terms(block)
         if block % 2 == 1 and block > 1:
-            find_sums(slice((block - 3) * size, (block - 1) * size))
-    find_sums(slice((blocks - 2) * size, blocks * size))
+            find_sums(halves[block // 2 - 1])
+    find_sums(halves[-1])
+    if copied:
+        for lanes in halves:
+            for at in range(2):
+                copy_out(at, lanes).wait()
+
+
+def other_rows_kernel(dims, plan, *refs):
+    freq_count, segments, segment_rows, padded_rows, modes = dims
+    tables, terms, code = refs[:segments], refs[segments:-1], refs[-1]
+    sums = []
+    for part in range(2):
+        total = None
+        for segment in range(segments):
+            table, high, low = tables[segment], terms[2 * segment], terms[2 * segment + 1]
+            both = jnp.dot(table[part], high[part], preferred_element_type=jnp.float32)
+            rest = jnp.dot(
+                table[part, :padded_rows], low[part], preferred_element_type=jnp.float32
+            )
+            piece = both[:padded_rows] + (both[padded_rows:] + rest)
+            total = piece if total is None else total + piece
+        sums.append(total)
+    row = lax.broadcasted_iota(jnp.int32, code.shape, 0) + plan[ROWS, 2]
+    temperature = CUTOFF / freq_count
+    renorm = 1.0 + temperature * sums[1] / omega_of(row, freq_count)
+    code[...] = encoded(temperature * sums[0] / renorm)
 
 
 SWAP = [(0, 1), (1, 0)]
@@ -241,14 +297,16 @@
             name="encode",
         )(gap_in)
 
+    table_shape = jax.ShapeDtypeStruct(
+        (2, 2 * padded_rows, modes * segment_rows), jnp.bfloat16
+    )
     plan, weights, *tables = pl.pallas_call(
         functools.partial(tables_kernel, dims, sides),
         out_shape=[
             jax.ShapeDtypeStruct((5, max(blocks * slots, 1 + segments)), jnp.int32),
             jax.ShapeDtypeStruct((blocks, slots * size, modes * size), jnp.bfloat16),
         ]
-        + [jax.ShapeDtypeStruct((2, 2 * padded_rows, modes * segment_rows), jnp.bfloat16)]
-        * segments,
+        + [table_shape] * segments,
         in_specs=[smem] * 5 + [vmem],
         out_specs=[smem] + [vmem] * (1 + segments),
         compiler_params=pltpu.CompilerParams(vmem_limit_bytes=24 << 20),
@@ -258,31 +316,52 @@
         name="tables",
     )(meta, phonon, pair_cols, pair_count, block_order, coupling)
 
-    def step(plan, segment, final, pieces, before):
-        full = jax.ShapeDtypeStruct(gap_in.shape, jnp.float32)
+    full = jax.ShapeDtypeStruct(gap_in.shape, jnp.float32)
+    passed_out = jax.ShapeDtypeStruct(gap_in.shape, link_type)
+    step_params = dict(
+        compiler_params=pltpu.CompilerParams(vmem_limit_bytes=24 << 20),
+        cost_estimate=pl.CostEstimate(
+            flops=STEP_FLOPS, bytes_accessed=100_000, transcendentals=0
+        ),
+    )
+
+    def step(plan, segment, final, pieces, before, keep=False, span=(0, blocks)):
+        copied = final and segment == segments - 1
+        width = (span[1] - span[0]) * size
+        terms_shape = (2, modes * segment_rows, width)
         if segment < segments - 1:
-            outs = [jax.ShapeDtypeStruct((2, padded_rows, row_width), jnp.float32)]
-        elif final:
-            outs = [full, full]
+            outs = [jax.ShapeDtypeStruct((2, padded_rows, width), jnp.float32)]
         else:
-            outs = [jax.ShapeDtypeStruct(gap_in.shape, link_type)]
+            outs = [full, full] if final else [passed_out]
+        out_specs = [pl.BlockSpec(memory_space=pl.ANY) if copied else vmem] * len(outs)
+        scratch = [pltpu.VMEM((span[1] - span[0], 2 * segment_rows, slots * size), jnp.bfloat16)]
+        if keep:
+            outs += [jax.ShapeDtypeStruct(terms_shape, jnp.bfloat16)] * 2
+            out_specs += [vmem] * 2
+        else:
+            scratch += [pltpu.VMEM(terms_shape, jnp.bfloat16)] * 2
+        if copied:
+            scratch += [pltpu.VMEM(gap_in.shape, jnp.float32)] * 2
+            scratch += [pltpu.SemaphoreType.DMA((2, blocks // 2))]
         inputs = [*pieces, weights, tables[segment], *before]
         return pl.pallas_call(
-            functools.partial(step_kernel, dims, segment, sides, pairwise, final),
+            functools.partial(
+                step_kernel, dims, segment, span, sides, pairwise, final, keep, len(before)
+            ),
             out_shape=outs,
             in_specs=[smem] + [vmem] * len(inputs),
-            out_specs=[vmem] * len(outs),
-            scratch_shapes=[
-                pltpu.VMEM((blocks, 2 * segment_rows, slots * size), jnp.bfloat16),
-                pltpu.VMEM((2, modes * segment_rows, row_width), jnp.bfloat16),
-                pltpu.VMEM((2, modes * segment_rows, row_width), jnp.bfloat16),
-            ],
-            compiler_params=pltpu.CompilerParams(vmem_limit_bytes=24 << 20),
-            cost_estimate=pl.CostEstimate(
-                flops=STEP_FLOPS, bytes_accessed=100_000, transcendentals=0
-            ),
+            out_specs=out_specs,
+            scratch_shapes=scratch,
             name="step",
+            **step_params,
         )(plan, *inputs)
+
+    if not pairwise:
+        for iteration in range(ITERS):
+            final = iteration == ITERS - 1
+            results = step(plan, 0, final, gather_general(passed, half_groups), [])
+            passed = results[0]
+        return tuple(results)
 
     def join(near, across, after):
         return pl.pallas_call(
@@ -295,23 +374,45 @@
             name="join",
         )(near, across, after)
 
-    for iteration in range(ITERS):
-        final = iteration == ITERS - 1
-        if not pairwise:
-            results = step(plan, 0, final, gather_general(passed, half_groups), [])
-        else:
-            along_x = lax.ppermute(passed, "x", SWAP)
-            along_z = lax.ppermute(passed, "zlo", SWAP)
-            if iteration == 0:
-                along_x, plan = lax.optimization_barrier((along_x, plan))
-            relayed = lax.ppermute(along_z, "x", SWAP)
-            near = [passed, along_x]
-            pieces = near + [lax.ppermute(piece, "core", SWAP) for piece in near]
-            results = step(plan, 0, final, pieces, [])
-            far = join(along_z, relayed, *results)
-            results = step(plan, 1, final, [far, lax.ppermute(far, "core", SWAP)], results)
-        passed = results[0]
-    return tuple(results)
+    def with_core(near):
+        return near + [lax.ppermute(piece, "core", SWAP) for piece in near]
+
+    other_tables = pl.pallas_call(
+        functools.partial(other_tables_kernel, dims),
+        out_shape=[table_shape] * segments,
+        in_specs=[smem, smem],
+        out_specs=[vmem] * segments,
+        compiler_params=pltpu.CompilerParams(vmem_limit_bytes=12 << 20),
+        cost_estimate=pl.CostEstimate(
+            flops=10_000_000, bytes_accessed=3_000_000, transcendentals=0
+        ),
+        name="other_tables",
+    )(meta, phonon)
+    along_x = lax.ppermute(passed, "x", SWAP)
+    along_z = lax.ppermute(passed, "zlo", SWAP)
+    along_x, plan = lax.optimization_barrier((along_x, plan))
+    relayed = lax.ppermute(along_z, "x", SWAP)
+    partial, *near_terms = step(plan, 0, False, with_core([passed, along_x]), [], keep=True)
+    far = join(along_z, relayed, partial)
+    pieces = [far, lax.ppermute(far, "core", SWAP)]
+    plan, *other_tables = lax.optimization_barrier((plan, *other_tables))
+    own, *far_terms = step(plan, 1, False, pieces, [partial], keep=True)
+    inputs = [*other_tables, *near_terms, *far_terms]
+    other = pl.pallas_call(
+        functools.partial(other_rows_kernel, dims),
+        out_shape=passed_out,
+        in_specs=[smem] + [vmem] * len(inputs),
+        out_specs=vmem,
+        name="other_rows",
+        **step_params,
+    )(plan, *inputs)
+    along_x, other = lax.optimization_barrier((lax.ppermute(own, "x", SWAP), other))
+    near = with_core([own, along_x])
+    middle = blocks // 2
+    partial = step(plan, 0, True, near, [], span=(0, middle))
+    far = join(other, lax.ppermute(other, "x", SWAP), *partial)
+    partial += step(plan, 0, True, near, [], span=(middle, blocks))
+    return tuple(step(plan, 1, True, [far, lax.ppermute(far, "core", SWAP)], partial))
 
 
 def solution(mesh):

time: 36.9 us -> 37.3 us (1.011)
  Pallas kernels: 15.4 us -> 20.3 us
  waiting for transfers between devices: 9.92 us -> 7.01 us
  starting transfers between devices: 9.31 us -> 7.86 us
    ppermute x4 -> x7, waiting for transfers between devices: 0.28 us -> 5.14 us  [the longest x1 2.7 us: on_device(): far = join(other, lax.ppermute(other, 'x', SWAP), *partial)]
    pallas_call x4 -> x7, Pallas kernels: 13 us -> 17.9 us  [the longest x5 13.6 us: step(): pl.pallas_call(functools.partial(step_kernel, dims, segment, span, sides,...]
    ppermute x2 -> x1, waiting for transfers between devices: 3.04 us -> 0.01 us  [on_device(): lax.ppermute(far, 'core', SWAP)]
    ppermute x2 -> x1, waiting for transfers between devices: 2.92 us -> 0.01 us  [on_device(): along_x = lax.ppermute(passed, 'x', SWAP)]
    ppermute x4 -> x7, starting transfers between devices: 0.58 us -> 2.85 us  [the longest x1 1.14 us: on_device(): lax.ppermute(own, 'x', SWAP)]
    ppermute x2 -> x1, starting transfers between devices: 3.14 us -> 1.58 us  [on_device(): along_z = lax.ppermute(passed, 'zlo', SWAP)]
    ppermute x2 -> x1, starting transfers between devices: 4.13 us -> 3 us  [on_device(): along_x = lax.ppermute(passed, 'x', SWAP)]
    ppermute x2 -> x1, waiting for transfers between devices: 2.54 us -> 1.52 us  [on_device(): relayed = lax.ppermute(along_z, 'x', SWAP)]
  transfers between devices with their start and end apart: 12 -> 11, of which waited for: 8 -> 7; matrix products, arithmetic and copies ran while one was open for 0% -> 0% of each run, Pallas kernels for 23% -> 36%
where the time goes in v6:
time: 37.3 us; the launch traced here: 37.1 us
  Pallas kernels  20.3 us (54%)
  starting transfers between devices  7.86 us (21%)
  waiting for transfers between devices  7.01 us (19%)
  local copies, waits for them, and re-layouts  1.16 us (3%)
  between operations  0.77 us (2%)
    pallas_call x5, Pallas kernels, step(): pl.pallas_call(functools.partial(step_kernel, dims, segment, span, sides,...  13.6 us
    ppermute x1, starting transfers between devices, on_device(): along_x = lax.ppermute(passed, 'x', SWAP)  3 us
    pallas_call x1, Pallas kernels, on_device(): pl.pallas_call(functools.partial(other_rows_kernel, dims), out_shape=pass...  2.96 us
    ppermute x1, waiting for transfers between devices, on_device(): far = join(other, lax.ppermute(other, 'x', SWAP), *partial)  2.7 us
    pallas_call x1, Pallas kernels, on_device(): pl.pallas_call(functools.partial(tables_kernel, dims, sides), out_shape=[...  2.25 us
    ppermute x1, waiting for transfers between devices, on_device(): lax.ppermute(own, 'x', SWAP)  1.66 us
    ppermute x1, starting transfers between devices, on_device(): along_z = lax.ppermute(passed, 'zlo', SWAP)  1.58 us
    ppermute x1, waiting for transfers between devices, on_device(): relayed = lax.ppermute(along_z, 'x', SWAP)  1.52 us
  transfers between devices with their start and end apart: 11, of which 7 were waited for; matrix products, arithmetic and copies ran while one was open for 0% of the time, Pallas kernels for 36%

profile of v6, /device:TPU:0, one launch (start us, length us, event | category | flops | bytes accessed | tf_op | source)
XLA Modules:
  0.0 37.1 jit_solution(13507621593227825166)
XLA Ops:
  0.7 1.0 %copy-done.4 = f32[128,512]{1,0:T(8,128)S(1)} copy-done((f32[128,512]{1,0:T(8,128)S(1)}, f32[128,512]{1,0:T(8,128)}, u32[]{:S(2)}) %copy-start.4) | copy-done | bytes 262168
  1.6 0.1 encode.1.refs_0_
  1.8 3.0 %collective-permute-start = (s16[128,512]{1,0:T(8,128)(2,1)S(1)}, s16[128,512]{1,0:T(8,128)(2,1)S(1)}, u32[]{:S(2)}, u32[]{:S(2)}) collective-permute-start(s16[128,512]{1,0:T(8,128)(2,1)S(1)} %encode.1.refs_0_), channel_id=1, source_target_pairs={{0,2},{2,0},{1,3},{3,1},{4,6},{6,4},{5,7},{7,5},{8,10},{10,8},{9,1... | collective-permute-start | bytes 393224 | tf_op jit(solution)/shard_map/ppermute | solution.py:391
  4.8 1.6 %collective-permute-start.1 = (s16[128,512]{1,0:T(8,128)(2,1)S(1)}, s16[128,512]{1,0:T(8,128)(2,1)S(1)}, u32[]{:S(2)}, u32[]{:S(2)}) collective-permute-start(s16[128,512]{1,0:T(8,128)(2,1)S(1)} %encode.1.refs_0_), channel_id=1, source_target_pairs={{0,4},{4,0},{1,5},{5,1},{2,6},{6,2},{3,7},{7,3},{8,12},{12,8},{9,1... | collective-permute-start | bytes 393224 | tf_op jit(solution)/shard_map/ppermute | solution.py:392
  6.4 0.0 collective-permute-start.3
  6.4 0.1 copy.8.pair_cols
  6.5 0.1 stack.20.meta
  6.6 2.3 %tables.1 = (s32[5,8]{1,0:T(8,128)S(1)}, bf16[4,256,1152]{2,1,0:T(8,128)(2,1)S(1)}, bf16[2,256,1152]{2,1,0:T(8,128)(2,1)S(1)}, bf16[2,256,1152]{2,1,0:T(8,128)(2,1)S(1)}) custom-call(s32[5]{0:T(128)S(1)} %stack.20.meta, f32[9]{0:T(128)S(1)} %copy-done.3, s32[4,2]{1,0:T(4,128)S(1)} %copy.8.pair_cols, s32[4]{0:T(128)S(1)} %copy-done.1, s32[16]{0:T(128)S(1)} %copy-done.2, ...), custom_call_target="tpu_custom_call" | custom-call | flops 10000000 | bytes 8000000 | tf_op jit(solution)/shard_map/tables/pallas_call | solution.py:303
  8.8 0.0 collective-permute-done.refs_1_
  8.8 0.6 %collective-permute-start.4 = (s16[128,512]{1,0:T(8,128)(2,1)S(1)}, s16[128,512]{1,0:T(8,128)(2,1)S(1)}, u32[]{:S(2)}, u32[]{:S(2)}) collective-permute-start(s16[128,512]{1,0:T(8,128)(2,1)S(1)} %collective-permute-done.refs_1_), channel_id=1, source_target_pairs={{0,1},{1,0},{2,3},{3,2},{4,5},{5,4},{6,7},{7,6},{8,9},{9,8},{10,11... | collective-permute-start | bytes 393224 | tf_op jit(solution)/shard_map/ppermute | solution.py:378
  9.4 0.3 collective-permute-done.1.first
  9.8 0.4 collective-permute-start.2
  10.1 0.0 collective-permute-done.3.refs_2_
  10.1 0.3 collective-permute-done.4.refs_3_
  10.4 3.0 %step.5 = (f32[2,128,512]{2,1,0:T(8,128)S(1)}, bf16[2,1152,512]{2,1,0:T(8,128)(2,1)S(1)}, bf16[2,1152,512]{2,1,0:T(8,128)(2,1)S(1)}) custom-call(s32[5,8]{1,0:T(8,128)S(1)} %get-tuple-element.25.plan, s16[128,512]{1,0:T(8,128)(2,1)S(1)} %encode.1.refs_0_, s16[128,512]{1,0:T(8,128)(2,1)S(1)} %collective-permute-done.refs_1_, ...), custom_call_target="tpu_custom_call" | custom-call | flops 1000000 | bytes 100000 | tf_op jit(solution)/shard_map/step/pallas_call | solution.py:347
  13.4 1.5 %collective-permute-done.2.second = s16[128,512]{1,0:T(8,128)(2,1)S(1)} collective-permute-done((s16[128,512]{1,0:T(8,128)(2,1)S(1)}, s16[128,512]{1,0:T(8,128)(2,1)S(1)}, u32[]{:S(2)}, u32[]{:S(2)}) %collective-permute-start.2) | collective-permute-done | bytes 131104 | tf_op jit(solution)/shard_map/ppermute | solution.py:394
  14.9 0.1 collective-permute-start.5
  15.0 1.3 %other_tables.1 = (bf16[2,256,1152]{2,1,0:T(8,128)(2,1)S(1)}, bf16[2,256,1152]{2,1,0:T(8,128)(2,1)S(1)}) custom-call(s32[5]{0:T(128)S(1)} %stack.20.meta, f32[9]{0:T(128)S(1)} %copy-done.3), custom_call_target="tpu_custom_call" | custom-call | flops 10000000 | bytes 3000000 | tf_op jit(solution)/shard_map/other_tables/pallas_call | solution.py:380
  16.3 0.2 collective-permute-done.5.refs_1_
  16.5 3.1 %step.6 = (s16[128,512]{1,0:T(8,128)(2,1)S(1)}, bf16[2,1152,512]{2,1,0:T(8,128)(2,1)S(1)}, bf16[2,1152,512]{2,1,0:T(8,128)(2,1)S(1)}) custom-call(s32[5,8]{1,0:T(8,128)S(1)} %get-tuple-element.25.plan, s16[2,128,512]{2,1,0:T(8,128)(2,1)S(1)} %join.2.refs_0_, s16[2,128,512]{2,1,0:T(8,128)(2,1)S(1)} %collective-permute-done.5.refs_1_, ...), custom_call_target="tpu_custom_call" | custom-call | flops 1000000 | bytes 100000 | tf_op jit(solution)/shard_map/step/pallas_call | solution.py:347
  19.6 1.1 %collective-permute-start.6 = (s16[128,512]{1,0:T(8,128)(2,1)S(1)}, s16[128,512]{1,0:T(8,128)(2,1)S(1)}, u32[]{:S(2)}, u32[]{:S(2)}) collective-permute-start(s16[128,512]{1,0:T(8,128)(2,1)S(1)} %get-tuple-element.31.refs_0_), channel_id=1, source_target_pairs={{0,2},{2,0},{1,3},{3,1},{4,6},{6,4},{5,7},{7,5},{8,10},{10,8},{9,1... | collective-permute-start | bytes 393224 | tf_op jit(solution)/shard_map/ppermute | solution.py:409
  20.8 0.0 collective-permute-start.8
  20.8 3.0 %other_rows.1.first = s16[128,512]{1,0:T(8,128)(2,1)S(1)} custom-call(s32[5,8]{1,0:T(8,128)S(1)} %get-tuple-element.25.plan, bf16[2,256,1152]{2,1,0:T(8,128)(2,1)S(1)} %get-tuple-element.32.refs_0_, bf16[2,256,1152]{2,1,0:T(8,128)(2,1)S(1)} %get-tuple-element.33.refs_1_, bf16[2,1152,512]{2,1,0:T(8,128)(2,1)S(1)} %get-tuple-element.34.refs_2_, ...), custom_call_target="tpu_custom_call" | custom-call | flops 1000000 | bytes 100000 | tf_op jit(solution)/shard_map/other_rows/pallas_call | solution.py:401
  23.7 1.7 %collective-permute-done.6.refs_1_ = s16[128,512]{1,0:T(8,128)(2,1)S(1)} collective-permute-done((s16[128,512]{1,0:T(8,128)(2,1)S(1)}, s16[128,512]{1,0:T(8,128)(2,1)S(1)}, u32[]{:S(2)}, u32[]{:S(2)}) %collective-permute-start.6) | collective-permute-done | bytes 131104 | tf_op jit(solution)/shard_map/ppermute | solution.py:409
  25.4 1.1 %collective-permute-start.7 = (s16[128,512]{1,0:T(8,128)(2,1)S(1)}, s16[128,512]{1,0:T(8,128)(2,1)S(1)}, u32[]{:S(2)}, u32[]{:S(2)}) collective-permute-start(s16[128,512]{1,0:T(8,128)(2,1)S(1)} %other_rows.1.first), channel_id=1, source_target_pairs={{0,2},{2,0},{1,3},{3,1},{4,6},{6,4},{5,7},{7,5},{8,10},{10,8},{9,1... | collective-permute-start | bytes 393224 | tf_op jit(solution)/shard_map/ppermute | solution.py:413
  26.5 0.3 collective-permute-done.9.refs_3_
  26.7 1.9 %step.7.after.refs_4_ = f32[2,128,256]{2,1,0:T(8,128)S(1)} custom-call(s32[5,8]{1,0:T(8,128)S(1)} %get-tuple-element.25.plan, s16[128,512]{1,0:T(8,128)(2,1)S(1)} %get-tuple-element.31.refs_0_, s16[128,512]{1,0:T(8,128)(2,1)S(1)} %collective-permute-done.6.refs_1_, s16[128,512]{1,0:T(8,128)(2,1)S(1)} %collective-permute-done.8.refs_2_, ...), custom_call_target="tpu_custom_call" | custom-call | flops 1000000 | bytes 100000 | tf_op jit(solution)/shard_map/step/pallas_call | solution.py:347
  28.6 2.7 %collective-permute-done.7.second = s16[128,512]{1,0:T(8,128)(2,1)S(1)} collective-permute-done((s16[128,512]{1,0:T(8,128)(2,1)S(1)}, s16[128,512]{1,0:T(8,128)(2,1)S(1)}, u32[]{:S(2)}, u32[]{:S(2)}) %collective-permute-start.7) | collective-permute-done | bytes 131104 | tf_op jit(solution)/shard_map/ppermute | solution.py:413
  31.3 0.1 collective-permute-start.10
  31.4 1.8 %step.8.refs_5_ = f32[2,128,256]{2,1,0:T(8,128)S(1)} custom-call(s32[5,8]{1,0:T(8,128)S(1)} %get-tuple-element.25.plan, s16[128,512]{1,0:T(8,128)(2,1)S(1)} %get-tuple-element.31.refs_0_, s16[128,512]{1,0:T(8,128)(2,1)S(1)} %collective-permute-done.6.refs_1_, s16[128,512]{1,0:T(8,128)(2,1)S(1)} %collective-permute-done.8.refs_2_, ...), custom_call_target="tpu_custom_call" | custom-call | flops 1000000 | bytes 100000 | tf_op jit(solution)/shard_map/step/pallas_call | solution.py:347
  33.3 0.0 collective-permute-done.10.refs_1_
  33.3 3.8 %step.9 = (f32[128,512]{1,0:T(8,128)}, f32[128,512]{1,0:T(8,128)}) custom-call(s32[5,8]{1,0:T(8,128)S(1)} %get-tuple-element.25.plan, s16[2,128,512]{2,1,0:T(8,128)(2,1)S(1)} %join.3.refs_0_, s16[2,128,512]{2,1,0:T(8,128)(2,1)S(1)} %collective-permute-done.10.refs_1_, bf16[4,256,1152]{2,1,0:T(8,128)(2,1)S(1)} %get-tuple-element.27.refs_4_.refs_2_, ...), custom_call_target="tpu_custom_call" | custom-call | flops 1000000 | bytes 100000 | tf_op jit(solution)/shard_map/step/pallas_call | solution.py:347
  (15 shorter events, 0.1 us)
Async XLA Ops:
  0.6 5.9 %copy-start.3 = (f32[9]{0:T(128)S(1)}, f32[9]{0:T(128)}, u32[]{:S(2)}) copy-start(f32[9]{0:T(128)} %phonon.3) | copy-start | bytes 112
  0.6 5.9 %copy-start.2 = (s32[16]{0:T(128)S(1)}, s32[16]{0:T(128)}, u32[]{:S(2)}) copy-start(s32[16]{0:T(128)} %block_order.1) | copy-start | bytes 196
  0.7 5.9 %copy-start.1 = (s32[4]{0:T(128)S(1)}, s32[4]{0:T(128)}, u32[]{:S(2)}) copy-start(s32[4]{0:T(128)} %pair_count.1) | copy-start | bytes 52
  0.7 1.0 %copy-start.4 = (f32[128,512]{1,0:T(8,128)S(1)}, f32[128,512]{1,0:T(8,128)}, u32[]{:S(2)}) copy-start(f32[128,512]{1,0:T(8,128)} %gap.1) | copy-start | bytes 786436
  1.6 4.7 %copy-start.5 = (s32[4,2]{0,1:T(2,128)S(1)}, s32[4,2]{0,1:T(2,128)}, u32[]{:S(2)}) copy-start(s32[4,2]{0,1:T(2,128)} %param.8) | copy-start | bytes 100
  1.6 4.9 %copy-start = (bf16[4,2,9,128,128]{4,3,2,1,0:T(8,128)(2,1)S(1)}, bf16[4,2,9,128,128]{4,3,2,1,0:T(8,128)(2,1)}, u32[]{:S(2)}) copy-start(bf16[4,2,9,128,128]{4,3,2,1,0:T(8,128)(2,1)} %coupling.1) | copy-start | bytes 7077892
  1.8 7.0 %collective-permute-start = (s16[128,512]{1,0:T(8,128)(2,1)S(1)}, s16[128,512]{1,0:T(8,128)(2,1)S(1)}, u32[]{:S(2)}, u32[]{:S(2)}) collective-permute-start(s16[128,512]{1,0:T(8,128)(2,1)S(1)} %encode.1.refs_0_), channel_id=1, source_target_pairs={{0,2},{2,0},{1,3},{3,1},{4,6},{6,4},{5,7},{7,5},{8,10},{10,8},{9,1... | collective-permute-start | bytes 393224 | tf_op jit(solution)/shard_map/ppermute | solution.py:391
  4.8 5.0 %collective-permute-start.1 = (s16[128,512]{1,0:T(8,128)(2,1)S(1)}, s16[128,512]{1,0:T(8,128)(2,1)S(1)}, u32[]{:S(2)}, u32[]{:S(2)}) collective-permute-start(s16[128,512]{1,0:T(8,128)(2,1)S(1)} %encode.1.refs_0_), channel_id=1, source_target_pairs={{0,4},{4,0},{1,5},{5,1},{2,6},{6,2},{3,7},{7,3},{8,12},{12,8},{9,1... | collective-permute-start | bytes 393224 | tf_op jit(solution)/shard_map/ppermute | solution.py:392
  6.4 3.8 %collective-permute-start.3 = (s16[128,512]{1,0:T(8,128)(2,1)S(1)}, s16[128,512]{1,0:T(8,128)(2,1)S(1)}, u32[]{:S(2)}, u32[]{:S(2)}) collective-permute-start(s16[128,512]{1,0:T(8,128)(2,1)S(1)} %encode.1.refs_0_), channel_id=1, source_target_pairs={{0,1},{1,0},{2,3},{3,2},{4,5},{5,4},{6,7},{7,6},{8,9},{9,8},{10,11... | collective-permute-start | bytes 393224 | tf_op jit(solution)/shard_map/ppermute | solution.py:378
  8.8 1.6 %collective-permute-start.4 = (s16[128,512]{1,0:T(8,128)(2,1)S(1)}, s16[128,512]{1,0:T(8,128)(2,1)S(1)}, u32[]{:S(2)}, u32[]{:S(2)}) collective-permute-start(s16[128,512]{1,0:T(8,128)(2,1)S(1)} %collective-permute-done.refs_1_), channel_id=1, source_target_pairs={{0,1},{1,0},{2,3},{3,2},{4,5},{5,4},{6,7},{7,6},{8,9},{9,8},{10,11... | collective-permute-start | bytes 393224 | tf_op jit(solution)/shard_map/ppermute | solution.py:378
  9.8 5.1 %collective-permute-start.2 = (s16[128,512]{1,0:T(8,128)(2,1)S(1)}, s16[128,512]{1,0:T(8,128)(2,1)S(1)}, u32[]{:S(2)}, u32[]{:S(2)}) collective-permute-start(s16[128,512]{1,0:T(8,128)(2,1)S(1)} %collective-permute-done.1.first), channel_id=1, source_target_pairs={{0,2},{2,0},{1,3},{3,1},{4,6},{6,4},{5,7},{7,5},{8,10},{10,8},{9,1... | collective-permute-start | bytes 393224 | tf_op jit(solution)/shard_map/ppermute | solution.py:394
  14.9 1.6 %collective-permute-start.5 = (s16[2,128,512]{2,1,0:T(8,128)(2,1)S(1)}, s16[2,128,512]{2,1,0:T(8,128)(2,1)S(1)}, u32[]{:S(2)}, u32[]{:S(2)}) collective-permute-start(s16[2,128,512]{2,1,0:T(8,128)(2,1)S(1)} %join.2.refs_0_), channel_id=1, source_target_pairs={{0,1},{1,0},{2,3},{3,2},{4,5},{5,4},{6,7},{7,6},{8,9},{9,8},{10,11... | collective-permute-start | bytes 786440 | tf_op jit(solution)/shard_map/ppermute | solution.py:397
  19.6 5.8 %collective-permute-start.6 = (s16[128,512]{1,0:T(8,128)(2,1)S(1)}, s16[128,512]{1,0:T(8,128)(2,1)S(1)}, u32[]{:S(2)}, u32[]{:S(2)}) collective-permute-start(s16[128,512]{1,0:T(8,128)(2,1)S(1)} %get-tuple-element.31.refs_0_), channel_id=1, source_target_pairs={{0,2},{2,0},{1,3},{3,1},{4,6},{6,4},{5,7},{7,5},{8,10},{10,8},{9,1... | collective-permute-start | bytes 393224 | tf_op jit(solution)/shard_map/ppermute | solution.py:409
  20.8 5.7 %collective-permute-start.8 = (s16[128,512]{1,0:T(8,128)(2,1)S(1)}, s16[128,512]{1,0:T(8,128)(2,1)S(1)}, u32[]{:S(2)}, u32[]{:S(2)}) collective-permute-start(s16[128,512]{1,0:T(8,128)(2,1)S(1)} %get-tuple-element.31.refs_0_), channel_id=1, source_target_pairs={{0,1},{1,0},{2,3},{3,2},{4,5},{5,4},{6,7},{7,6},{8,9},{9,8},{10,11... | collective-permute-start | bytes 393224 | tf_op jit(solution)/shard_map/ppermute | solution.py:378
  25.4 1.3 %collective-permute-start.9 = (s16[128,512]{1,0:T(8,128)(2,1)S(1)}, s16[128,512]{1,0:T(8,128)(2,1)S(1)}, u32[]{:S(2)}, u32[]{:S(2)}) collective-permute-start(s16[128,512]{1,0:T(8,128)(2,1)S(1)} %collective-permute-done.6.refs_1_), channel_id=1, source_target_pairs={{0,1},{1,0},{2,3},{3,2},{4,5},{5,4},{6,7},{7,6},{8,9},{9,8},{10,11... | collective-permute-start | bytes 393224 | tf_op jit(solution)/shard_map/ppermute | solution.py:378
  25.4 5.9 %collective-permute-start.7 = (s16[128,512]{1,0:T(8,128)(2,1)S(1)}, s16[128,512]{1,0:T(8,128)(2,1)S(1)}, u32[]{:S(2)}, u32[]{:S(2)}) collective-permute-start(s16[128,512]{1,0:T(8,128)(2,1)S(1)} %other_rows.1.first), channel_id=1, source_target_pairs={{0,2},{2,0},{1,3},{3,1},{4,6},{6,4},{5,7},{7,5},{8,10},{10,8},{9,1... | collective-permute-start | bytes 393224 | tf_op jit(solution)/shard_map/ppermute | solution.py:413
  31.3 1.9 %collective-permute-start.10 = (s16[2,128,512]{2,1,0:T(8,128)(2,1)S(1)}, s16[2,128,512]{2,1,0:T(8,128)(2,1)S(1)}, u32[]{:S(2)}, u32[]{:S(2)}) collective-permute-start(s16[2,128,512]{2,1,0:T(8,128)(2,1)S(1)} %join.3.refs_0_), channel_id=1, source_target_pairs={{0,1},{1,0},{2,3},{3,2},{4,5},{5,4},{6,7},{7,6},{8,9},{9,8},{10,11... | collective-permute-start | bytes 786440 | tf_op jit(solution)/shard_map/ppermute | solution.py:415

commit v7 on v6

--- a/solution.py
+++ b/solution.py
@@ -14,6 +14,7 @@
 CODE_LIMIT = 32767.0
 CODE_POWER = 5
 STEP_FLOPS = 1_000_000
+SPARE_ROWS = 16
 HOLDER, PLACE, LIVE, SIDE, ROWS = 0, 1, 2, 3, 4
 
 
@@ -34,13 +35,17 @@
     return (root * GAP_LIMIT) * (square * square)
 
 
-def encode_kernel(gap, code):
+def encode_kernel(gap, code, *longer):
     code[...] = encoded(gap[...])
+    for other in longer:
+        other[: code.shape[0]] = code[...]
+        other[code.shape[0] :] = jnp.zeros((SPARE_ROWS, code.shape[1]), code.dtype)
 
 
 def join_kernel(first, second, after, joined):
-    joined[0] = first[...]
-    joined[1] = second[...]
+    rows = joined.shape[1]
+    joined[0] = first[:rows]
+    joined[1] = second[:rows]
 
 
 def split(value):
@@ -242,10 +247,11 @@
             piece = both[:padded_rows] + (both[padded_rows:] + rest)
             total = piece if total is None else total + piece
         sums.append(total)
-    row = lax.broadcasted_iota(jnp.int32, code.shape, 0) + plan[ROWS, 2]
+    row = lax.broadcasted_iota(jnp.int32, (padded_rows, code.shape[1]), 0) + plan[ROWS, 2]
     temperature = CUTOFF / freq_count
     renorm = 1.0 + temperature * sums[1] / omega_of(row, freq_count)
-    code[...] = encoded(temperature * sums[0] / renorm)
+    code[:padded_rows] = encoded(temperature * sums[0] / renorm)
+    code[padded_rows:] = jnp.zeros((SPARE_ROWS, code.shape[1]), code.dtype)
 
 
 SWAP = [(0, 1), (1, 0)]
@@ -285,11 +291,14 @@
 
     passed = gap_in
     if pairwise:
-        passed = pl.pallas_call(
+        passed, longer = pl.pallas_call(
             encode_kernel,
-            out_shape=jax.ShapeDtypeStruct(gap_in.shape, link_type),
+            out_shape=[
+                jax.ShapeDtypeStruct(gap_in.shape, link_type),
+                jax.ShapeDtypeStruct((own_rows + SPARE_ROWS, row_width), link_type),
+            ],
             in_specs=[vmem],
-            out_specs=vmem,
+            out_specs=[vmem, vmem],
             compiler_params=pltpu.CompilerParams(vmem_limit_bytes=8 << 20),
             cost_estimate=pl.CostEstimate(
                 flops=10_000_000_000, bytes_accessed=40_000_000, transcendentals=0
@@ -366,7 +375,7 @@
     def join(near, across, after):
         return pl.pallas_call(
             join_kernel,
-            out_shape=jax.ShapeDtypeStruct((2, *near.shape), near.dtype),
+            out_shape=jax.ShapeDtypeStruct((2, *gap_in.shape), near.dtype),
             in_specs=[vmem, vmem, pl.BlockSpec(memory_space=pl.ANY)],
             out_specs=vmem,
             compiler_params=pltpu.CompilerParams(vmem_limit_bytes=4 << 20),
@@ -389,24 +398,24 @@
         name="other_tables",
     )(meta, phonon)
     along_x = lax.ppermute(passed, "x", SWAP)
-    along_z = lax.ppermute(passed, "zlo", SWAP)
+    along_z = lax.ppermute(longer, "zlo", SWAP)
+    diagonal = lax.ppermute(longer, ("zlo", "x"), [(at, 3 - at) for at in range(4)])
     along_x, plan = lax.optimization_barrier((along_x, plan))
-    relayed = lax.ppermute(along_z, "x", SWAP)
     partial, *near_terms = step(plan, 0, False, with_core([passed, along_x]), [], keep=True)
-    far = join(along_z, relayed, partial)
+    far = join(along_z, diagonal, partial)
     pieces = [far, lax.ppermute(far, "core", SWAP)]
     plan, *other_tables = lax.optimization_barrier((plan, *other_tables))
     own, *far_terms = step(plan, 1, False, pieces, [partial], keep=True)
     inputs = [*other_tables, *near_terms, *far_terms]
     other = pl.pallas_call(
         functools.partial(other_rows_kernel, dims),
-        out_shape=passed_out,
+        out_shape=jax.ShapeDtypeStruct((own_rows + SPARE_ROWS, row_width), link_type),
         in_specs=[smem] + [vmem] * len(inputs),
         out_specs=vmem,
         name="other_rows",
         **step_params,
     )(plan, *inputs)
-    along_x, other = lax.optimization_barrier((lax.ppermute(own, "x", SWAP), other))
+    along_x = lax.ppermute(own, "x", SWAP)
     near = with_core([own, along_x])
     middle = blocks // 2
     partial = step(plan, 0, True, near, [], span=(0, middle))

time: 37.3 us -> 37.2 us (level)
    ppermute x3, waiting for transfers between devices: 3.53 us -> 0.83 us  [the longest x1 0.83 us: on_device(): along_x = lax.ppermute(own, 'x', SWAP)]
    ppermute x4, waiting for transfers between devices: 0.57 us -> 2.69 us  [with_core(): return near + [lax.ppermute(piece, 'core', SWAP) for piece in near]]
    ppermute x1, waiting for transfers between devices: 0.01 us -> 1.88 us  [on_device(): along_x = lax.ppermute(passed, 'x', SWAP)]
    ppermute x3, starting transfers between devices: 3.07 us -> 4.13 us  [the longest x1 2.55 us: on_device(): along_x = lax.ppermute(own, 'x', SWAP)]
    ppermute x1, waiting for transfers between devices: 2.7 us -> 1.64 us  [on_device(): far = join(other, lax.ppermute(other, 'x', SWAP), *partial)]
    ppermute x1, starting transfers between devices: 1.05 us -> 0.08 us  [on_device(): far = join(other, lax.ppermute(other, 'x', SWAP), *partial)]
    ppermute x4, starting transfers between devices: 0.59 us -> 0.08 us  [with_core(): return near + [lax.ppermute(piece, 'core', SWAP) for piece in near]]
where the time goes in v7:
time: 37.2 us; the launch traced here: 37 us
  Pallas kernels  20.3 us (55%)
  starting transfers between devices  7.59 us (20%)
  waiting for transfers between devices  7.11 us (19%)
  local copies, waits for them, and re-layouts  1.16 us (3%)
  between operations  0.77 us (2%)
    pallas_call x5, Pallas kernels, step(): pl.pallas_call(functools.partial(step_kernel, dims, segment, span, sides,...  13.6 us
    ppermute x1, starting transfers between devices, on_device(): along_x = lax.ppermute(passed, 'x', SWAP)  3 us
    pallas_call x1, Pallas kernels, on_device(): pl.pallas_call(functools.partial(other_rows_kernel, dims), out_shape=jax....  2.96 us
    ppermute x4, waiting for transfers between devices, with_core(): return near + [lax.ppermute(piece, 'core', SWAP) for piece in near]  2.69 us
    ppermute x1, starting transfers between devices, on_device(): along_x = lax.ppermute(own, 'x', SWAP)  2.55 us
    pallas_call x1, Pallas kernels, on_device(): pl.pallas_call(functools.partial(tables_kernel, dims, sides), out_shape=[...  2.25 us
    ppermute x1, waiting for transfers between devices, on_device(): along_x = lax.ppermute(passed, 'x', SWAP)  1.88 us
    ppermute x1, waiting for transfers between devices, on_device(): far = join(other, lax.ppermute(other, 'x', SWAP), *partial)  1.64 us
  transfers between devices with their start and end apart: 11, of which 7 were waited for; matrix products, arithmetic and copies ran while one was open for 0% of the time, Pallas kernels for 36%

profile of v7, /device:TPU:0, one launch (start us, length us, event | category | flops | bytes accessed | tf_op | source)
XLA Modules:
  0.0 37.0 jit_solution(8383617104838183665)
XLA Ops:
  0.7 1.0 %copy-done.4 = f32[128,512]{1,0:T(8,128)S(1)} copy-done((f32[128,512]{1,0:T(8,128)S(1)}, f32[128,512]{1,0:T(8,128)}, u32[]{:S(2)}) %copy-start.4) | copy-done | bytes 262168
  1.6 0.2 encode.1
  1.8 3.0 %collective-permute-start = (s16[128,512]{1,0:T(8,128)(2,1)S(1)}, s16[128,512]{1,0:T(8,128)(2,1)S(1)}, u32[]{:S(2)}, u32[]{:S(2)}) collective-permute-start(s16[128,512]{1,0:T(8,128)(2,1)S(1)} %get-tuple-element.21.refs_0_), channel_id=1, source_target_pairs={{0,2},{2,0},{1,3},{3,1},{4,6},{6,4},{5,7},{7,5},{8,10},{10,8},{9,1... | collective-permute-start | bytes 393224 | tf_op jit(solution)/shard_map/ppermute | solution.py:400
  4.8 1.5 %collective-permute-start.4 = (s16[144,512]{1,0:T(8,128)(2,1)S(1)}, s16[144,512]{1,0:T(8,128)(2,1)S(1)}, u32[]{:S(2)}, u32[]{:S(2)}) collective-permute-start(s16[144,512]{1,0:T(8,128)(2,1)S(1)} %get-tuple-element.34), channel_id=1, source_target_pairs={{0,6},{2,4},{4,2},{6,0},{1,7},{3,5},{5,3},{7,1},{8,14},{10,12},{12... | collective-permute-start | bytes 442376 | tf_op jit(solution)/shard_map/ppermute | solution.py:402
  6.4 0.0 collective-permute-start.3
  6.4 0.1 copy.8.pair_cols
  6.5 0.1 stack.20.meta
  6.6 2.3 %tables.1 = (s32[5,8]{1,0:T(8,128)S(1)}, bf16[4,256,1152]{2,1,0:T(8,128)(2,1)S(1)}, bf16[2,256,1152]{2,1,0:T(8,128)(2,1)S(1)}, bf16[2,256,1152]{2,1,0:T(8,128)(2,1)S(1)}) custom-call(s32[5]{0:T(128)S(1)} %stack.20.meta, f32[9]{0:T(128)S(1)} %copy-done.3, s32[4,2]{1,0:T(4,128)S(1)} %copy.8.pair_cols, s32[4]{0:T(128)S(1)} %copy-done.1, s32[16]{0:T(128)S(1)} %copy-done.2, ...), custom_call_target="tpu_custom_call" | custom-call | flops 10000000 | bytes 8000000 | tf_op jit(solution)/shard_map/tables/pallas_call | solution.py:312
  8.9 1.9 %collective-permute-done.refs_1_ = s16[128,512]{1,0:T(8,128)(2,1)S(1)} collective-permute-done((s16[128,512]{1,0:T(8,128)(2,1)S(1)}, s16[128,512]{1,0:T(8,128)(2,1)S(1)}, u32[]{:S(2)}, u32[]{:S(2)}) %collective-permute-start) | collective-permute-done | bytes 131104 | tf_op jit(solution)/shard_map/ppermute | solution.py:400
  10.7 0.0 collective-permute-start.2
  10.7 0.0 collective-permute-done.1.refs_2_
  10.7 1.3 %collective-permute-done.2.refs_3_ = s16[128,512]{1,0:T(8,128)(2,1)S(1)} collective-permute-done((s16[128,512]{1,0:T(8,128)(2,1)S(1)}, s16[128,512]{1,0:T(8,128)(2,1)S(1)}, u32[]{:S(2)}, u32[]{:S(2)}) %collective-permute-start.2) | collective-permute-done | bytes 131104 | tf_op jit(solution)/shard_map/ppermute | solution.py:387
  12.1 3.0 %step.5 = (f32[2,128,512]{2,1,0:T(8,128)S(1)}, bf16[2,1152,512]{2,1,0:T(8,128)(2,1)S(1)}, bf16[2,1152,512]{2,1,0:T(8,128)(2,1)S(1)}) custom-call(s32[5,8]{1,0:T(8,128)S(1)} %get-tuple-element.26.plan, s16[128,512]{1,0:T(8,128)(2,1)S(1)} %get-tuple-element.21.refs_0_, s16[128,512]{1,0:T(8,128)(2,1)S(1)} %collective-permute-done.refs_1_, ...), custom_call_target="tpu_custom_call" | custom-call | flops 1000000 | bytes 100000 | tf_op jit(solution)/shard_map/step/pallas_call | solution.py:356
  15.1 0.0 collective-permute-done.4.second
  15.1 0.0 collective-permute-done.3.first
  15.1 0.2 collective-permute-start.5
  15.3 1.3 %other_tables.1 = (bf16[2,256,1152]{2,1,0:T(8,128)(2,1)S(1)}, bf16[2,256,1152]{2,1,0:T(8,128)(2,1)S(1)}) custom-call(s32[5]{0:T(128)S(1)} %stack.20.meta, f32[9]{0:T(128)S(1)} %copy-done.3), custom_call_target="tpu_custom_call" | custom-call | flops 10000000 | bytes 3000000 | tf_op jit(solution)/shard_map/other_tables/pallas_call | solution.py:389
  16.7 0.1 collective-permute-done.5.refs_1_
  16.7 3.1 %step.6 = (s16[128,512]{1,0:T(8,128)(2,1)S(1)}, bf16[2,1152,512]{2,1,0:T(8,128)(2,1)S(1)}, bf16[2,1152,512]{2,1,0:T(8,128)(2,1)S(1)}) custom-call(s32[5,8]{1,0:T(8,128)S(1)} %get-tuple-element.26.plan, s16[2,128,512]{2,1,0:T(8,128)(2,1)S(1)} %join.2.refs_0_, s16[2,128,512]{2,1,0:T(8,128)(2,1)S(1)} %collective-permute-done.5.refs_1_, ...), custom_call_target="tpu_custom_call" | custom-call | flops 1000000 | bytes 100000 | tf_op jit(solution)/shard_map/step/pallas_call | solution.py:356
  19.8 2.6 %collective-permute-start.7 = (s16[128,512]{1,0:T(8,128)(2,1)S(1)}, s16[128,512]{1,0:T(8,128)(2,1)S(1)}, u32[]{:S(2)}, u32[]{:S(2)}) collective-permute-start(s16[128,512]{1,0:T(8,128)(2,1)S(1)} %get-tuple-element.39.refs_0_), channel_id=1, source_target_pairs={{0,2},{2,0},{1,3},{3,1},{4,6},{6,4},{5,7},{7,5},{8,10},{10,8},{9,1... | collective-permute-start | bytes 393224 | tf_op jit(solution)/shard_map/ppermute | solution.py:418
  22.4 3.0 %other_rows.1.first = s16[144,512]{1,0:T(8,128)(2,1)S(1)} custom-call(s32[5,8]{1,0:T(8,128)S(1)} %get-tuple-element.26.plan, bf16[2,256,1152]{2,1,0:T(8,128)(2,1)S(1)} %get-tuple-element.27.refs_0_, bf16[2,256,1152]{2,1,0:T(8,128)(2,1)S(1)} %get-tuple-element.28.refs_1_, bf16[2,1152,512]{2,1,0:T(8,128)(2,1)S(1)} %get-tuple-element.32.refs_2_, ...), custom_call_target="tpu_custom_call" | custom-call | flops 1000000 | bytes 100000 | tf_op jit(solution)/shard_map/other_rows/pallas_call | solution.py:410
  25.3 0.1 collective-permute-start.6
  25.4 0.1 collective-permute-start.8
  25.5 0.8 %collective-permute-done.7.refs_1_ = s16[128,512]{1,0:T(8,128)(2,1)S(1)} collective-permute-done((s16[128,512]{1,0:T(8,128)(2,1)S(1)}, s16[128,512]{1,0:T(8,128)(2,1)S(1)}, u32[]{:S(2)}, u32[]{:S(2)}) %collective-permute-start.7) | collective-permute-done | bytes 131104 | tf_op jit(solution)/shard_map/ppermute | solution.py:418
  26.3 0.0 collective-permute-start.9
  26.3 0.5 %collective-permute-done.8.refs_2_ = s16[128,512]{1,0:T(8,128)(2,1)S(1)} collective-permute-done((s16[128,512]{1,0:T(8,128)(2,1)S(1)}, s16[128,512]{1,0:T(8,128)(2,1)S(1)}, u32[]{:S(2)}, u32[]{:S(2)}) %collective-permute-start.8) | collective-permute-done | bytes 131104 | tf_op jit(solution)/shard_map/ppermute | solution.py:387
  26.8 0.8 %collective-permute-done.9.refs_3_ = s16[128,512]{1,0:T(8,128)(2,1)S(1)} collective-permute-done((s16[128,512]{1,0:T(8,128)(2,1)S(1)}, s16[128,512]{1,0:T(8,128)(2,1)S(1)}, u32[]{:S(2)}, u32[]{:S(2)}) %collective-permute-start.9) | collective-permute-done | bytes 131104 | tf_op jit(solution)/shard_map/ppermute | solution.py:387
  27.7 1.9 %step.7.after.refs_4_ = f32[2,128,256]{2,1,0:T(8,128)S(1)} custom-call(s32[5,8]{1,0:T(8,128)S(1)} %get-tuple-element.26.plan, s16[128,512]{1,0:T(8,128)(2,1)S(1)} %get-tuple-element.39.refs_0_, s16[128,512]{1,0:T(8,128)(2,1)S(1)} %collective-permute-done.7.refs_1_, s16[128,512]{1,0:T(8,128)(2,1)S(1)} %collective-permute-done.8.refs_2_, ...), custom_call_target="tpu_custom_call" | custom-call | flops 1000000 | bytes 100000 | tf_op jit(solution)/shard_map/step/pallas_call | solution.py:356
  29.5 1.6 %collective-permute-done.6.second = s16[144,512]{1,0:T(8,128)(2,1)S(1)} collective-permute-done((s16[144,512]{1,0:T(8,128)(2,1)S(1)}, s16[144,512]{1,0:T(8,128)(2,1)S(1)}, u32[]{:S(2)}, u32[]{:S(2)}) %collective-permute-start.6) | collective-permute-done | bytes 147488 | tf_op jit(solution)/shard_map/ppermute | solution.py:422
  31.2 0.1 collective-permute-start.10
  31.3 1.9 %step.8.refs_5_ = f32[2,128,256]{2,1,0:T(8,128)S(1)} custom-call(s32[5,8]{1,0:T(8,128)S(1)} %get-tuple-element.26.plan, s16[128,512]{1,0:T(8,128)(2,1)S(1)} %get-tuple-element.39.refs_0_, s16[128,512]{1,0:T(8,128)(2,1)S(1)} %collective-permute-done.7.refs_1_, s16[128,512]{1,0:T(8,128)(2,1)S(1)} %collective-permute-done.8.refs_2_, ...), custom_call_target="tpu_custom_call" | custom-call | flops 1000000 | bytes 100000 | tf_op jit(solution)/shard_map/step/pallas_call | solution.py:356
  33.1 3.8 %step.9 = (f32[128,512]{1,0:T(8,128)}, f32[128,512]{1,0:T(8,128)}) custom-call(s32[5,8]{1,0:T(8,128)S(1)} %get-tuple-element.26.plan, s16[2,128,512]{2,1,0:T(8,128)(2,1)S(1)} %join.3.refs_0_, s16[2,128,512]{2,1,0:T(8,128)(2,1)S(1)} %collective-permute-done.10.refs_1_, bf16[4,256,1152]{2,1,0:T(8,128)(2,1)S(1)} %get-tuple-element.30.refs_4_.refs_2_, ...), custom_call_target="tpu_custom_call" | custom-call | flops 1000000 | bytes 100000 | tf_op jit(solution)/shard_map/step/pallas_call | solution.py:356
  (15 shorter events, 0.1 us)
Async XLA Ops:
  0.6 6.0 %copy-start.3 = (f32[9]{0:T(128)S(1)}, f32[9]{0:T(128)}, u32[]{:S(2)}) copy-start(f32[9]{0:T(128)} %phonon.3) | copy-start | bytes 112
  0.6 6.0 %copy-start.2 = (s32[16]{0:T(128)S(1)}, s32[16]{0:T(128)}, u32[]{:S(2)}) copy-start(s32[16]{0:T(128)} %block_order.1) | copy-start | bytes 196
  0.7 5.9 %copy-start.1 = (s32[4]{0:T(128)S(1)}, s32[4]{0:T(128)}, u32[]{:S(2)}) copy-start(s32[4]{0:T(128)} %pair_count.1) | copy-start | bytes 52
  0.7 1.0 %copy-start.4 = (f32[128,512]{1,0:T(8,128)S(1)}, f32[128,512]{1,0:T(8,128)}, u32[]{:S(2)}) copy-start(f32[128,512]{1,0:T(8,128)} %gap.1) | copy-start | bytes 786436
  1.6 4.8 %copy-start.5 = (s32[4,2]{0,1:T(2,128)S(1)}, s32[4,2]{0,1:T(2,128)}, u32[]{:S(2)}) copy-start(s32[4,2]{0,1:T(2,128)} %param.8) | copy-start | bytes 100
  1.6 5.0 %copy-start = (bf16[4,2,9,128,128]{4,3,2,1,0:T(8,128)(2,1)S(1)}, bf16[4,2,9,128,128]{4,3,2,1,0:T(8,128)(2,1)}, u32[]{:S(2)}) copy-start(bf16[4,2,9,128,128]{4,3,2,1,0:T(8,128)(2,1)} %coupling.1) | copy-start | bytes 7077892
  1.8 8.9 %collective-permute-start = (s16[128,512]{1,0:T(8,128)(2,1)S(1)}, s16[128,512]{1,0:T(8,128)(2,1)S(1)}, u32[]{:S(2)}, u32[]{:S(2)}) collective-permute-start(s16[128,512]{1,0:T(8,128)(2,1)S(1)} %get-tuple-element.21.refs_0_), channel_id=1, source_target_pairs={{0,2},{2,0},{1,3},{3,1},{4,6},{6,4},{5,7},{7,5},{8,10},{10,8},{9,1... | collective-permute-start | bytes 393224 | tf_op jit(solution)/shard_map/ppermute | solution.py:400
  4.8 10.3 %collective-permute-start.4 = (s16[144,512]{1,0:T(8,128)(2,1)S(1)}, s16[144,512]{1,0:T(8,128)(2,1)S(1)}, u32[]{:S(2)}, u32[]{:S(2)}) collective-permute-start(s16[144,512]{1,0:T(8,128)(2,1)S(1)} %get-tuple-element.34), channel_id=1, source_target_pairs={{0,6},{2,4},{4,2},{6,0},{1,7},{3,5},{5,3},{7,1},{8,14},{10,12},{12... | collective-permute-start | bytes 442376 | tf_op jit(solution)/shard_map/ppermute | solution.py:402
  6.4 8.7 %collective-permute-start.3 = (s16[144,512]{1,0:T(8,128)(2,1)S(1)}, s16[144,512]{1,0:T(8,128)(2,1)S(1)}, u32[]{:S(2)}, u32[]{:S(2)}) collective-permute-start(s16[144,512]{1,0:T(8,128)(2,1)S(1)} %get-tuple-element.34), channel_id=1, source_target_pairs={{0,4},{4,0},{1,5},{5,1},{2,6},{6,2},{3,7},{7,3},{8,12},{12,8},{9,1... | collective-permute-start | bytes 442376 | tf_op jit(solution)/shard_map/ppermute | solution.py:401
  6.4 4.3 %collective-permute-start.1 = (s16[128,512]{1,0:T(8,128)(2,1)S(1)}, s16[128,512]{1,0:T(8,128)(2,1)S(1)}, u32[]{:S(2)}, u32[]{:S(2)}) collective-permute-start(s16[128,512]{1,0:T(8,128)(2,1)S(1)} %get-tuple-element.21.refs_0_), channel_id=1, source_target_pairs={{0,1},{1,0},{2,3},{3,2},{4,5},{5,4},{6,7},{7,6},{8,9},{9,8},{10,11... | collective-permute-start | bytes 393224 | tf_op jit(solution)/shard_map/ppermute | solution.py:387
  10.7 1.3 %collective-permute-start.2 = (s16[128,512]{1,0:T(8,128)(2,1)S(1)}, s16[128,512]{1,0:T(8,128)(2,1)S(1)}, u32[]{:S(2)}, u32[]{:S(2)}) collective-permute-start(s16[128,512]{1,0:T(8,128)(2,1)S(1)} %collective-permute-done.refs_1_), channel_id=1, source_target_pairs={{0,1},{1,0},{2,3},{3,2},{4,5},{5,4},{6,7},{7,6},{8,9},{9,8},{10,11... | collective-permute-start | bytes 393224 | tf_op jit(solution)/shard_map/ppermute | solution.py:387
  15.1 1.6 %collective-permute-start.5 = (s16[2,128,512]{2,1,0:T(8,128)(2,1)S(1)}, s16[2,128,512]{2,1,0:T(8,128)(2,1)S(1)}, u32[]{:S(2)}, u32[]{:S(2)}) collective-permute-start(s16[2,128,512]{2,1,0:T(8,128)(2,1)S(1)} %join.2.refs_0_), channel_id=1, source_target_pairs={{0,1},{1,0},{2,3},{3,2},{4,5},{5,4},{6,7},{7,6},{8,9},{9,8},{10,11... | collective-permute-start | bytes 786440 | tf_op jit(solution)/shard_map/ppermute | solution.py:406
  19.8 6.5 %collective-permute-start.7 = (s16[128,512]{1,0:T(8,128)(2,1)S(1)}, s16[128,512]{1,0:T(8,128)(2,1)S(1)}, u32[]{:S(2)}, u32[]{:S(2)}) collective-permute-start(s16[128,512]{1,0:T(8,128)(2,1)S(1)} %get-tuple-element.39.refs_0_), channel_id=1, source_target_pairs={{0,2},{2,0},{1,3},{3,1},{4,6},{6,4},{5,7},{7,5},{8,10},{10,8},{9,1... | collective-permute-start | bytes 393224 | tf_op jit(solution)/shard_map/ppermute | solution.py:418
  25.3 5.8 %collective-permute-start.6 = (s16[144,512]{1,0:T(8,128)(2,1)S(1)}, s16[144,512]{1,0:T(8,128)(2,1)S(1)}, u32[]{:S(2)}, u32[]{:S(2)}) collective-permute-start(s16[144,512]{1,0:T(8,128)(2,1)S(1)} %other_rows.1.first), channel_id=1, source_target_pairs={{0,2},{2,0},{1,3},{3,1},{4,6},{6,4},{5,7},{7,5},{8,10},{10,8},{9,1... | collective-permute-start | bytes 442376 | tf_op jit(solution)/shard_map/ppermute | solution.py:422
  25.4 1.4 %collective-permute-start.8 = (s16[128,512]{1,0:T(8,128)(2,1)S(1)}, s16[128,512]{1,0:T(8,128)(2,1)S(1)}, u32[]{:S(2)}, u32[]{:S(2)}) collective-permute-start(s16[128,512]{1,0:T(8,128)(2,1)S(1)} %get-tuple-element.39.refs_0_), channel_id=1, source_target_pairs={{0,1},{1,0},{2,3},{3,2},{4,5},{5,4},{6,7},{7,6},{8,9},{9,8},{10,11... | collective-permute-start | bytes 393224 | tf_op jit(solution)/shard_map/ppermute | solution.py:387
  26.3 1.3 %collective-permute-start.9 = (s16[128,512]{1,0:T(8,128)(2,1)S(1)}, s16[128,512]{1,0:T(8,128)(2,1)S(1)}, u32[]{:S(2)}, u32[]{:S(2)}) collective-permute-start(s16[128,512]{1,0:T(8,128)(2,1)S(1)} %collective-permute-done.7.refs_1_), channel_id=1, source_target_pairs={{0,1},{1,0},{2,3},{3,2},{4,5},{5,4},{6,7},{7,6},{8,9},{9,8},{10,11... | collective-permute-start | bytes 393224 | tf_op jit(solution)/shard_map/ppermute | solution.py:387
  31.2 1.9 %collective-permute-start.10 = (s16[2,128,512]{2,1,0:T(8,128)(2,1)S(1)}, s16[2,128,512]{2,1,0:T(8,128)(2,1)S(1)}, u32[]{:S(2)}, u32[]{:S(2)}) collective-permute-start(s16[2,128,512]{2,1,0:T(8,128)(2,1)S(1)} %join.3.refs_0_), channel_id=1, source_target_pairs={{0,1},{1,0},{2,3},{3,2},{4,5},{5,4},{6,7},{7,6},{8,9},{9,8},{10,11... | collective-permute-start | bytes 786440 | tf_op jit(solution)/shard_map/ppermute | solution.py:424

commit v8 on v6

--- a/solution.py
+++ b/solution.py
@@ -14,6 +14,7 @@
 CODE_LIMIT = 32767.0
 CODE_POWER = 5
 STEP_FLOPS = 1_000_000
+SPARE_ROWS = 16
 HOLDER, PLACE, LIVE, SIDE, ROWS = 0, 1, 2, 3, 4
 
 
@@ -39,8 +40,9 @@
 
 
 def join_kernel(first, second, after, joined):
-    joined[0] = first[...]
-    joined[1] = second[...]
+    rows = joined.shape[1]
+    joined[0] = first[:rows]
+    joined[1] = second[:rows]
 
 
 def split(value):
@@ -242,10 +244,11 @@
             piece = both[:padded_rows] + (both[padded_rows:] + rest)
             total = piece if total is None else total + piece
         sums.append(total)
-    row = lax.broadcasted_iota(jnp.int32, code.shape, 0) + plan[ROWS, 2]
+    row = lax.broadcasted_iota(jnp.int32, (padded_rows, code.shape[1]), 0) + plan[ROWS, 2]
     temperature = CUTOFF / freq_count
     renorm = 1.0 + temperature * sums[1] / omega_of(row, freq_count)
-    code[...] = encoded(temperature * sums[0] / renorm)
+    code[:padded_rows] = encoded(temperature * sums[0] / renorm)
+    code[padded_rows:] = jnp.zeros((SPARE_ROWS, code.shape[1]), code.dtype)
 
 
 SWAP = [(0, 1), (1, 0)]
@@ -366,7 +369,7 @@
     def join(near, across, after):
         return pl.pallas_call(
             join_kernel,
-            out_shape=jax.ShapeDtypeStruct((2, *near.shape), near.dtype),
+            out_shape=jax.ShapeDtypeStruct((2, *gap_in.shape), near.dtype),
             in_specs=[vmem, vmem, pl.BlockSpec(memory_space=pl.ANY)],
             out_specs=vmem,
             compiler_params=pltpu.CompilerParams(vmem_limit_bytes=4 << 20),
@@ -400,13 +403,13 @@
     inputs = [*other_tables, *near_terms, *far_terms]
     other = pl.pallas_call(
         functools.partial(other_rows_kernel, dims),
-        out_shape=passed_out,
+        out_shape=jax.ShapeDtypeStruct((own_rows + SPARE_ROWS, row_width), link_type),
         in_specs=[smem] + [vmem] * len(inputs),
         out_specs=vmem,
         name="other_rows",
         **step_params,
     )(plan, *inputs)
-    along_x, other = lax.optimization_barrier((lax.ppermute(own, "x", SWAP), other))
+    along_x = lax.ppermute(own, "x", SWAP)
     near = with_core([own, along_x])
     middle = blocks // 2
     partial = step(plan, 0, True, near, [], span=(0, middle))

time: 37.3 us -> 35.5 us (0.952)
  waiting for transfers between devices: 7.01 us -> 5.29 us
    ppermute x1, waiting for transfers between devices: 2.7 us -> 0.96 us  [on_device(): far = join(other, lax.ppermute(other, 'x', SWAP), *partial)]
    ppermute x4, waiting for transfers between devices: 0.57 us -> 1.62 us  [with_core(): return near + [lax.ppermute(piece, 'core', SWAP) for piece in near]]
    ppermute x1, waiting for transfers between devices: 1.66 us -> 0.63 us  [on_device(): along_x = lax.ppermute(own, 'x', SWAP)]
  transfers between devices with their start and end apart: 11 -> 11, of which waited for: 7 -> 8; matrix products, arithmetic and copies ran while one was open for 0% -> 0% of each run, Pallas kernels for 36% -> 37%
where the time goes in v8:
time: 35.5 us; the launch traced here: 35.3 us
  Pallas kernels  20.3 us (57%)
  starting transfers between devices  7.81 us (22%)
  waiting for transfers between devices  5.29 us (15%)
  local copies, waits for them, and re-layouts  1.16 us (3%)
  between operations  0.77 us (2%)
    pallas_call x5, Pallas kernels, step(): pl.pallas_call(functools.partial(step_kernel, dims, segment, span, sides,...  13.6 us
    ppermute x1, starting transfers between devices, on_device(): along_x = lax.ppermute(passed, 'x', SWAP)  3 us
    pallas_call x1, Pallas kernels, on_device(): pl.pallas_call(functools.partial(other_rows_kernel, dims), out_shape=jax....  2.96 us
    pallas_call x1, Pallas kernels, on_device(): pl.pallas_call(functools.partial(tables_kernel, dims, sides), out_shape=[...  2.25 us
    ppermute x4, waiting for transfers between devices, with_core(): return near + [lax.ppermute(piece, 'core', SWAP) for piece in near]  1.62 us
    ppermute x1, starting transfers between devices, on_device(): along_z = lax.ppermute(passed, 'zlo', SWAP)  1.58 us
    ppermute x1, waiting for transfers between devices, on_device(): relayed = lax.ppermute(along_z, 'x', SWAP)  1.52 us
    pallas_call x1, Pallas kernels, on_device(): pl.pallas_call(functools.partial(other_tables_kernel, dims), out_shape=[t...  1.3 us
  transfers between devices with their start and end apart: 11, of which 8 were waited for; matrix products, arithmetic and copies ran while one was open for 0% of the time, Pallas kernels for 37%

profile of v8, /device:TPU:0, one launch (start us, length us, event | category | flops | bytes accessed | tf_op | source)
XLA Modules:
  0.0 35.3 jit_solution(5663060925320604357)
XLA Ops:
  0.7 1.0 %copy-done.4 = f32[128,512]{1,0:T(8,128)S(1)} copy-done((f32[128,512]{1,0:T(8,128)S(1)}, f32[128,512]{1,0:T(8,128)}, u32[]{:S(2)}) %copy-start.4) | copy-done | bytes 262168
  1.6 0.1 encode.1.refs_0_
  1.8 3.0 %collective-permute-start = (s16[128,512]{1,0:T(8,128)(2,1)S(1)}, s16[128,512]{1,0:T(8,128)(2,1)S(1)}, u32[]{:S(2)}, u32[]{:S(2)}) collective-permute-start(s16[128,512]{1,0:T(8,128)(2,1)S(1)} %encode.1.refs_0_), channel_id=1, source_target_pairs={{0,2},{2,0},{1,3},{3,1},{4,6},{6,4},{5,7},{7,5},{8,10},{10,8},{9,1... | collective-permute-start | bytes 393224 | tf_op jit(solution)/shard_map/ppermute | solution.py:394
  4.8 1.6 %collective-permute-start.3 = (s16[128,512]{1,0:T(8,128)(2,1)S(1)}, s16[128,512]{1,0:T(8,128)(2,1)S(1)}, u32[]{:S(2)}, u32[]{:S(2)}) collective-permute-start(s16[128,512]{1,0:T(8,128)(2,1)S(1)} %encode.1.refs_0_), channel_id=1, source_target_pairs={{0,4},{4,0},{1,5},{5,1},{2,6},{6,2},{3,7},{7,3},{8,12},{12,8},{9,1... | collective-permute-start | bytes 393224 | tf_op jit(solution)/shard_map/ppermute | solution.py:395
  6.4 0.0 collective-permute-start.1
  6.4 0.1 copy.8.pair_cols
  6.5 0.1 stack.20.meta
  6.6 2.3 %tables.1 = (s32[5,8]{1,0:T(8,128)S(1)}, bf16[4,256,1152]{2,1,0:T(8,128)(2,1)S(1)}, bf16[2,256,1152]{2,1,0:T(8,128)(2,1)S(1)}, bf16[2,256,1152]{2,1,0:T(8,128)(2,1)S(1)}) custom-call(s32[5]{0:T(128)S(1)} %stack.20.meta, f32[9]{0:T(128)S(1)} %copy-done.3, s32[4,2]{1,0:T(4,128)S(1)} %copy.8.pair_cols, s32[4]{0:T(128)S(1)} %copy-done.1, s32[16]{0:T(128)S(1)} %copy-done.2, ...), custom_call_target="tpu_custom_call" | custom-call | flops 10000000 | bytes 8000000 | tf_op jit(solution)/shard_map/tables/pallas_call | solution.py:306
  8.8 0.0 collective-permute-done.refs_1_
  8.8 0.6 %collective-permute-start.2 = (s16[128,512]{1,0:T(8,128)(2,1)S(1)}, s16[128,512]{1,0:T(8,128)(2,1)S(1)}, u32[]{:S(2)}, u32[]{:S(2)}) collective-permute-start(s16[128,512]{1,0:T(8,128)(2,1)S(1)} %collective-permute-done.refs_1_), channel_id=1, source_target_pairs={{0,1},{1,0},{2,3},{3,2},{4,5},{5,4},{6,7},{7,6},{8,9},{9,8},{10,11... | collective-permute-start | bytes 393224 | tf_op jit(solution)/shard_map/ppermute | solution.py:381
  9.4 0.3 collective-permute-done.3.first
  9.8 0.4 %collective-permute-start.4 = (s16[128,512]{1,0:T(8,128)(2,1)S(1)}, s16[128,512]{1,0:T(8,128)(2,1)S(1)}, u32[]{:S(2)}, u32[]{:S(2)}) collective-permute-start(s16[128,512]{1,0:T(8,128)(2,1)S(1)} %collective-permute-done.3.first), channel_id=1, source_target_pairs={{0,2},{2,0},{1,3},{3,1},{4,6},{6,4},{5,7},{7,5},{8,10},{10,8},{9,1... | collective-permute-start | bytes 393224 | tf_op jit(solution)/shard_map/ppermute | solution.py:397
  10.1 0.3 collective-permute-done.2.refs_3_
  10.4 3.0 %step.5 = (f32[2,128,512]{2,1,0:T(8,128)S(1)}, bf16[2,1152,512]{2,1,0:T(8,128)(2,1)S(1)}, bf16[2,1152,512]{2,1,0:T(8,128)(2,1)S(1)}) custom-call(s32[5,8]{1,0:T(8,128)S(1)} %get-tuple-element.23.plan, s16[128,512]{1,0:T(8,128)(2,1)S(1)} %encode.1.refs_0_, s16[128,512]{1,0:T(8,128)(2,1)S(1)} %collective-permute-done.refs_1_, ...), custom_call_target="tpu_custom_call" | custom-call | flops 1000000 | bytes 100000 | tf_op jit(solution)/shard_map/step/pallas_call | solution.py:350
  13.4 1.5 %collective-permute-done.4.second = s16[128,512]{1,0:T(8,128)(2,1)S(1)} collective-permute-done((s16[128,512]{1,0:T(8,128)(2,1)S(1)}, s16[128,512]{1,0:T(8,128)(2,1)S(1)}, u32[]{:S(2)}, u32[]{:S(2)}) %collective-permute-start.4) | collective-permute-done | bytes 131104 | tf_op jit(solution)/shard_map/ppermute | solution.py:397
  14.9 0.1 collective-permute-start.5
  15.0 1.3 %other_tables.1 = (bf16[2,256,1152]{2,1,0:T(8,128)(2,1)S(1)}, bf16[2,256,1152]{2,1,0:T(8,128)(2,1)S(1)}) custom-call(s32[5]{0:T(128)S(1)} %stack.20.meta, f32[9]{0:T(128)S(1)} %copy-done.3), custom_call_target="tpu_custom_call" | custom-call | flops 10000000 | bytes 3000000 | tf_op jit(solution)/shard_map/other_tables/pallas_call | solution.py:383
  16.3 0.2 collective-permute-done.5.refs_1_
  16.5 3.1 %step.6 = (s16[128,512]{1,0:T(8,128)(2,1)S(1)}, bf16[2,1152,512]{2,1,0:T(8,128)(2,1)S(1)}, bf16[2,1152,512]{2,1,0:T(8,128)(2,1)S(1)}) custom-call(s32[5,8]{1,0:T(8,128)S(1)} %get-tuple-element.23.plan, s16[2,128,512]{2,1,0:T(8,128)(2,1)S(1)} %join.2.refs_0_, s16[2,128,512]{2,1,0:T(8,128)(2,1)S(1)} %collective-permute-done.5.refs_1_, ...), custom_call_target="tpu_custom_call" | custom-call | flops 1000000 | bytes 100000 | tf_op jit(solution)/shard_map/step/pallas_call | solution.py:350
  19.6 1.1 %collective-permute-start.7 = (s16[128,512]{1,0:T(8,128)(2,1)S(1)}, s16[128,512]{1,0:T(8,128)(2,1)S(1)}, u32[]{:S(2)}, u32[]{:S(2)}) collective-permute-start(s16[128,512]{1,0:T(8,128)(2,1)S(1)} %get-tuple-element.35.refs_0_), channel_id=1, source_target_pairs={{0,2},{2,0},{1,3},{3,1},{4,6},{6,4},{5,7},{7,5},{8,10},{10,8},{9,1... | collective-permute-start | bytes 393224 | tf_op jit(solution)/shard_map/ppermute | solution.py:412
  20.7 3.0 %other_rows.1.first = s16[144,512]{1,0:T(8,128)(2,1)S(1)} custom-call(s32[5,8]{1,0:T(8,128)S(1)} %get-tuple-element.23.plan, bf16[2,256,1152]{2,1,0:T(8,128)(2,1)S(1)} %get-tuple-element.24.refs_0_, bf16[2,256,1152]{2,1,0:T(8,128)(2,1)S(1)} %get-tuple-element.25.refs_1_, bf16[2,1152,512]{2,1,0:T(8,128)(2,1)S(1)} %get-tuple-element.29.refs_2_, ...), custom_call_target="tpu_custom_call" | custom-call | flops 1000000 | bytes 100000 | tf_op jit(solution)/shard_map/other_rows/pallas_call | solution.py:404
  23.7 1.0 %collective-permute-start.6 = (s16[144,512]{1,0:T(8,128)(2,1)S(1)}, s16[144,512]{1,0:T(8,128)(2,1)S(1)}, u32[]{:S(2)}, u32[]{:S(2)}) collective-permute-start(s16[144,512]{1,0:T(8,128)(2,1)S(1)} %other_rows.1.first), channel_id=1, source_target_pairs={{0,2},{2,0},{1,3},{3,1},{4,6},{6,4},{5,7},{7,5},{8,10},{10,8},{9,1... | collective-permute-start | bytes 442376 | tf_op jit(solution)/shard_map/ppermute | solution.py:416
  24.8 0.0 collective-permute-start.8
  24.8 0.6 %collective-permute-done.7.refs_1_ = s16[128,512]{1,0:T(8,128)(2,1)S(1)} collective-permute-done((s16[128,512]{1,0:T(8,128)(2,1)S(1)}, s16[128,512]{1,0:T(8,128)(2,1)S(1)}, u32[]{:S(2)}, u32[]{:S(2)}) %collective-permute-start.7) | collective-permute-done | bytes 131104 | tf_op jit(solution)/shard_map/ppermute | solution.py:412
  25.4 0.0 collective-permute-start.9
  25.4 0.7 %collective-permute-done.8.refs_2_ = s16[128,512]{1,0:T(8,128)(2,1)S(1)} collective-permute-done((s16[128,512]{1,0:T(8,128)(2,1)S(1)}, s16[128,512]{1,0:T(8,128)(2,1)S(1)}, u32[]{:S(2)}, u32[]{:S(2)}) %collective-permute-start.8) | collective-permute-done | bytes 131104 | tf_op jit(solution)/shard_map/ppermute | solution.py:381
  26.1 0.6 %collective-permute-done.9.refs_3_ = s16[128,512]{1,0:T(8,128)(2,1)S(1)} collective-permute-done((s16[128,512]{1,0:T(8,128)(2,1)S(1)}, s16[128,512]{1,0:T(8,128)(2,1)S(1)}, u32[]{:S(2)}, u32[]{:S(2)}) %collective-permute-start.9) | collective-permute-done | bytes 131104 | tf_op jit(solution)/shard_map/ppermute | solution.py:381
  26.7 1.9 %step.7.after.refs_4_ = f32[2,128,256]{2,1,0:T(8,128)S(1)} custom-call(s32[5,8]{1,0:T(8,128)S(1)} %get-tuple-element.23.plan, s16[128,512]{1,0:T(8,128)(2,1)S(1)} %get-tuple-element.35.refs_0_, s16[128,512]{1,0:T(8,128)(2,1)S(1)} %collective-permute-done.7.refs_1_, s16[128,512]{1,0:T(8,128)(2,1)S(1)} %collective-permute-done.8.refs_2_, ...), custom_call_target="tpu_custom_call" | custom-call | flops 1000000 | bytes 100000 | tf_op jit(solution)/shard_map/step/pallas_call | solution.py:350
  28.6 1.0 %collective-permute-done.6.second = s16[144,512]{1,0:T(8,128)(2,1)S(1)} collective-permute-done((s16[144,512]{1,0:T(8,128)(2,1)S(1)}, s16[144,512]{1,0:T(8,128)(2,1)S(1)}, u32[]{:S(2)}, u32[]{:S(2)}) %collective-permute-start.6) | collective-permute-done | bytes 147488 | tf_op jit(solution)/shard_map/ppermute | solution.py:416
  29.6 0.1 collective-permute-start.10
  29.6 1.9 %step.8.refs_5_ = f32[2,128,256]{2,1,0:T(8,128)S(1)} custom-call(s32[5,8]{1,0:T(8,128)S(1)} %get-tuple-element.23.plan, s16[128,512]{1,0:T(8,128)(2,1)S(1)} %get-tuple-element.35.refs_0_, s16[128,512]{1,0:T(8,128)(2,1)S(1)} %collective-permute-done.7.refs_1_, s16[128,512]{1,0:T(8,128)(2,1)S(1)} %collective-permute-done.8.refs_2_, ...), custom_call_target="tpu_custom_call" | custom-call | flops 1000000 | bytes 100000 | tf_op jit(solution)/shard_map/step/pallas_call | solution.py:350
  31.5 3.8 %step.9 = (f32[128,512]{1,0:T(8,128)}, f32[128,512]{1,0:T(8,128)}) custom-call(s32[5,8]{1,0:T(8,128)S(1)} %get-tuple-element.23.plan, s16[2,128,512]{2,1,0:T(8,128)(2,1)S(1)} %join.3.refs_0_, s16[2,128,512]{2,1,0:T(8,128)(2,1)S(1)} %collective-permute-done.10.refs_1_, bf16[4,256,1152]{2,1,0:T(8,128)(2,1)S(1)} %get-tuple-element.27.refs_4_.refs_2_, ...), custom_call_target="tpu_custom_call" | custom-call | flops 1000000 | bytes 100000 | tf_op jit(solution)/shard_map/step/pallas_call | solution.py:350
  (15 shorter events, 0.1 us)
Async XLA Ops:
  0.6 5.9 %copy-start.3 = (f32[9]{0:T(128)S(1)}, f32[9]{0:T(128)}, u32[]{:S(2)}) copy-start(f32[9]{0:T(128)} %phonon.3) | copy-start | bytes 112
  0.6 5.9 %copy-start.2 = (s32[16]{0:T(128)S(1)}, s32[16]{0:T(128)}, u32[]{:S(2)}) copy-start(s32[16]{0:T(128)} %block_order.1) | copy-start | bytes 196
  0.7 5.9 %copy-start.1 = (s32[4]{0:T(128)S(1)}, s32[4]{0:T(128)}, u32[]{:S(2)}) copy-start(s32[4]{0:T(128)} %pair_count.1) | copy-start | bytes 52
  0.7 1.0 %copy-start.4 = (f32[128,512]{1,0:T(8,128)S(1)}, f32[128,512]{1,0:T(8,128)}, u32[]{:S(2)}) copy-start(f32[128,512]{1,0:T(8,128)} %gap.1) | copy-start | bytes 786436
  1.6 4.7 %copy-start.5 = (s32[4,2]{0,1:T(2,128)S(1)}, s32[4,2]{0,1:T(2,128)}, u32[]{:S(2)}) copy-start(s32[4,2]{0,1:T(2,128)} %param.8) | copy-start | bytes 100
  1.6 4.9 %copy-start = (bf16[4,2,9,128,128]{4,3,2,1,0:T(8,128)(2,1)S(1)}, bf16[4,2,9,128,128]{4,3,2,1,0:T(8,128)(2,1)}, u32[]{:S(2)}) copy-start(bf16[4,2,9,128,128]{4,3,2,1,0:T(8,128)(2,1)} %coupling.1) | copy-start | bytes 7077892
  1.8 7.0 %collective-permute-start = (s16[128,512]{1,0:T(8,128)(2,1)S(1)}, s16[128,512]{1,0:T(8,128)(2,1)S(1)}, u32[]{:S(2)}, u32[]{:S(2)}) collective-permute-start(s16[128,512]{1,0:T(8,128)(2,1)S(1)} %encode.1.refs_0_), channel_id=1, source_target_pairs={{0,2},{2,0},{1,3},{3,1},{4,6},{6,4},{5,7},{7,5},{8,10},{10,8},{9,1... | collective-permute-start | bytes 393224 | tf_op jit(solution)/shard_map/ppermute | solution.py:394
  4.8 5.0 %collective-permute-start.3 = (s16[128,512]{1,0:T(8,128)(2,1)S(1)}, s16[128,512]{1,0:T(8,128)(2,1)S(1)}, u32[]{:S(2)}, u32[]{:S(2)}) collective-permute-start(s16[128,512]{1,0:T(8,128)(2,1)S(1)} %encode.1.refs_0_), channel_id=1, source_target_pairs={{0,4},{4,0},{1,5},{5,1},{2,6},{6,2},{3,7},{7,3},{8,12},{12,8},{9,1... | collective-permute-start | bytes 393224 | tf_op jit(solution)/shard_map/ppermute | solution.py:395
  6.4 3.8 %collective-permute-start.1 = (s16[128,512]{1,0:T(8,128)(2,1)S(1)}, s16[128,512]{1,0:T(8,128)(2,1)S(1)}, u32[]{:S(2)}, u32[]{:S(2)}) collective-permute-start(s16[128,512]{1,0:T(8,128)(2,1)S(1)} %encode.1.refs_0_), channel_id=1, source_target_pairs={{0,1},{1,0},{2,3},{3,2},{4,5},{5,4},{6,7},{7,6},{8,9},{9,8},{10,11... | collective-permute-start | bytes 393224 | tf_op jit(solution)/shard_map/ppermute | solution.py:381
  8.8 1.6 %collective-permute-start.2 = (s16[128,512]{1,0:T(8,128)(2,1)S(1)}, s16[128,512]{1,0:T(8,128)(2,1)S(1)}, u32[]{:S(2)}, u32[]{:S(2)}) collective-permute-start(s16[128,512]{1,0:T(8,128)(2,1)S(1)} %collective-permute-done.refs_1_), channel_id=1, source_target_pairs={{0,1},{1,0},{2,3},{3,2},{4,5},{5,4},{6,7},{7,6},{8,9},{9,8},{10,11... | collective-permute-start | bytes 393224 | tf_op jit(solution)/shard_map/ppermute | solution.py:381
  9.8 5.1 %collective-permute-start.4 = (s16[128,512]{1,0:T(8,128)(2,1)S(1)}, s16[128,512]{1,0:T(8,128)(2,1)S(1)}, u32[]{:S(2)}, u32[]{:S(2)}) collective-permute-start(s16[128,512]{1,0:T(8,128)(2,1)S(1)} %collective-permute-done.3.first), channel_id=1, source_target_pairs={{0,2},{2,0},{1,3},{3,1},{4,6},{6,4},{5,7},{7,5},{8,10},{10,8},{9,1... | collective-permute-start | bytes 393224 | tf_op jit(solution)/shard_map/ppermute | solution.py:397
  14.9 1.6 %collective-permute-start.5 = (s16[2,128,512]{2,1,0:T(8,128)(2,1)S(1)}, s16[2,128,512]{2,1,0:T(8,128)(2,1)S(1)}, u32[]{:S(2)}, u32[]{:S(2)}) collective-permute-start(s16[2,128,512]{2,1,0:T(8,128)(2,1)S(1)} %join.2.refs_0_), channel_id=1, source_target_pairs={{0,1},{1,0},{2,3},{3,2},{4,5},{5,4},{6,7},{7,6},{8,9},{9,8},{10,11... | collective-permute-start | bytes 786440 | tf_op jit(solution)/shard_map/ppermute | solution.py:400
  19.6 5.8 %collective-permute-start.7 = (s16[128,512]{1,0:T(8,128)(2,1)S(1)}, s16[128,512]{1,0:T(8,128)(2,1)S(1)}, u32[]{:S(2)}, u32[]{:S(2)}) collective-permute-start(s16[128,512]{1,0:T(8,128)(2,1)S(1)} %get-tuple-element.35.refs_0_), channel_id=1, source_target_pairs={{0,2},{2,0},{1,3},{3,1},{4,6},{6,4},{5,7},{7,5},{8,10},{10,8},{9,1... | collective-permute-start | bytes 393224 | tf_op jit(solution)/shard_map/ppermute | solution.py:412
  23.7 5.8 %collective-permute-start.6 = (s16[144,512]{1,0:T(8,128)(2,1)S(1)}, s16[144,512]{1,0:T(8,128)(2,1)S(1)}, u32[]{:S(2)}, u32[]{:S(2)}) collective-permute-start(s16[144,512]{1,0:T(8,128)(2,1)S(1)} %other_rows.1.first), channel_id=1, source_target_pairs={{0,2},{2,0},{1,3},{3,1},{4,6},{6,4},{5,7},{7,5},{8,10},{10,8},{9,1... | collective-permute-start | bytes 442376 | tf_op jit(solution)/shard_map/ppermute | solution.py:416
  24.8 1.3 %collective-permute-start.8 = (s16[128,512]{1,0:T(8,128)(2,1)S(1)}, s16[128,512]{1,0:T(8,128)(2,1)S(1)}, u32[]{:S(2)}, u32[]{:S(2)}) collective-permute-start(s16[128,512]{1,0:T(8,128)(2,1)S(1)} %get-tuple-element.35.refs_0_), channel_id=1, source_target_pairs={{0,1},{1,0},{2,3},{3,2},{4,5},{5,4},{6,7},{7,6},{8,9},{9,8},{10,11... | collective-permute-start | bytes 393224 | tf_op jit(solution)/shard_map/ppermute | solution.py:381
  25.4 1.3 %collective-permute-start.9 = (s16[128,512]{1,0:T(8,128)(2,1)S(1)}, s16[128,512]{1,0:T(8,128)(2,1)S(1)}, u32[]{:S(2)}, u32[]{:S(2)}) collective-permute-start(s16[128,512]{1,0:T(8,128)(2,1)S(1)} %collective-permute-done.7.refs_1_), channel_id=1, source_target_pairs={{0,1},{1,0},{2,3},{3,2},{4,5},{5,4},{6,7},{7,6},{8,9},{9,8},{10,11... | collective-permute-start | bytes 393224 | tf_op jit(solution)/shard_map/ppermute | solution.py:381
  29.6 1.9 %collective-permute-start.10 = (s16[2,128,512]{2,1,0:T(8,128)(2,1)S(1)}, s16[2,128,512]{2,1,0:T(8,128)(2,1)S(1)}, u32[]{:S(2)}, u32[]{:S(2)}) collective-permute-start(s16[2,128,512]{2,1,0:T(8,128)(2,1)S(1)} %join.3.refs_0_), channel_id=1, source_target_pairs={{0,1},{1,0},{2,3},{3,2},{4,5},{5,4},{6,7},{7,6},{8,9},{9,8},{10,11... | collective-permute-start | bytes 786440 | tf_op jit(solution)/shard_map/ppermute | solution.py:418

commit v9 on v8

--- a/solution.py
+++ b/solution.py
@@ -14,7 +14,7 @@
 CODE_LIMIT = 32767.0
 CODE_POWER = 5
 STEP_FLOPS = 1_000_000
-SPARE_ROWS = 16
+SPARE_ROWS = 32
 HOLDER, PLACE, LIVE, SIDE, ROWS = 0, 1, 2, 3, 4
 
 
@@ -36,7 +36,7 @@
 
 
 def encode_kernel(gap, code):
-    code[...] = encoded(gap[...])
+    code[...] = encoded(gap[...].T)
 
 
 def join_kernel(first, second, after, joined):
@@ -52,10 +52,11 @@
 
 def fill_tables(dims, meta, row_from, phonon, tables):
     freq_count, segments, segment_rows, padded_rows, modes = dims
-    shape = (padded_rows, segment_rows)
-    row_omega = omega_of(lax.broadcasted_iota(jnp.int32, shape, 0) + meta[row_from], freq_count)
-    for segment in range(len(tables)):
-        col = lax.broadcasted_iota(jnp.int32, shape, 1) + meta[1 + segment]
+    shape = (segment_rows, padded_rows)
+    row = lax.broadcasted_iota(jnp.int32, shape, 1) + meta[row_from]
+    row_omega = omega_of(row, freq_count)
+    for segment in range(segments):
+        col = lax.broadcasted_iota(jnp.int32, shape, 0) + meta[1 + segment]
         col_omega = omega_of(col, freq_count)
         near = (row_omega - col_omega) ** 2
         far = (row_omega + col_omega) ** 2
@@ -65,11 +66,11 @@
             below = near + strength * strength
             above = far + strength * strength
             common = (2.0 * strength) / (below * above)
-            columns = slice(mode * segment_rows, (mode + 1) * segment_rows)
+            rows = slice(mode * segment_rows, (mode + 1) * segment_rows)
             for part, value in enumerate((common * (below + above), common * cross)):
                 high, low = split(value)
-                tables[segment][part, :padded_rows, columns] = high
-                tables[segment][part, padded_rows:, columns] = low
+                tables[segment][part, rows, :padded_rows] = high
+                tables[segment][part, rows, padded_rows:] = low
 
 
 def other_tables_kernel(dims, meta, phonon, *tables):
@@ -101,8 +102,8 @@
         for slot in range(slots):
             for mode in range(modes):
                 weights[
-                    block, slot * size : (slot + 1) * size, mode * size : (mode + 1) * size
-                ] = coupling[block, slot, mode].T
+                    block, mode * size : (mode + 1) * size, slot * size : (slot + 1) * size
+                ] = coupling[block, slot, mode]
 
 
 def step_kernel(dims, segment, span, sides, coded, final, keep, parted, plan, *refs):
@@ -130,18 +131,18 @@
     holders = len(pieces) // sides
     blocks = span[1] - span[0]
     size = LANES
-    slots = weights.shape[1] // size
-    shape = (segment_rows, size)
-    col = lax.broadcasted_iota(jnp.int32, shape, 0) + plan[ROWS, 1 + segment]
+    slots = weights.shape[2] // size
+    shape = (size, segment_rows)
+    col = lax.broadcasted_iota(jnp.int32, shape, 1) + plan[ROWS, 1 + segment]
     col_omega = omega_of(col, freq_count)
     square = col_omega * col_omega
 
     def fetch(pair):
-        column = pl.multiple_of(plan[PLACE, pair] * size, size)
+        start = pl.multiple_of(plan[PLACE, pair] * size, size)
         wanted = plan[SIDE, pair] * holders + plan[HOLDER, pair]
-        value = pieces[0][:, pl.ds(column, size)]
+        value = pieces[0][pl.ds(start, size), :]
         for at in range(1, len(pieces)):
-            value = lax.select(wanted == at, pieces[at][:, pl.ds(column, size)], value)
+            value = lax.select(wanted == at, pieces[at][pl.ds(start, size), :], value)
         return decoded(value) if coded else value
 
     def find_ratios(block):
@@ -150,69 +151,63 @@
             gap = fetch(pair)
             live = plan[LIVE, pair].astype(jnp.float32)
             inverse = lax.rsqrt(square + gap * gap) * live
-            lanes = slice(slot * size, (slot + 1) * size)
-            ratios[block, :segment_rows, lanes] = (gap * inverse).astype(jnp.bfloat16)
-            ratios[block, segment_rows:, lanes] = (col_omega * inverse).astype(jnp.bfloat16)
+            rows = slice(slot * size, (slot + 1) * size)
+            ratios[block, rows, :segment_rows] = (gap * inverse).astype(jnp.bfloat16)
+            ratios[block, rows, segment_rows:] = (col_omega * inverse).astype(jnp.bfloat16)
 
     def find_terms(block):
-        lanes = slice(block * size, (block + 1) * size)
+        rows = slice(block * size, (block + 1) * size)
         for start in range(0, modes, 2):
             stop = min(start + 2, modes)
             terms = jnp.dot(
+                weights[span[0] + block, start * size : stop * size, :],
                 ratios[block],
-                weights[span[0] + block, :, start * size : stop * size],
                 preferred_element_type=jnp.float32,
             )
             upper, lower = split(terms)
             for mode in range(start, stop):
-                rows = slice(mode * segment_rows, (mode + 1) * segment_rows)
+                lanes = slice(mode * segment_rows, (mode + 1) * segment_rows)
                 taken = slice((mode - start) * size, (mode - start + 1) * size)
                 for part in range(2):
                     source = slice(part * segment_rows, (part + 1) * segment_rows)
-                    high[part, rows, lanes] = upper[source, taken]
-                    low[part, rows, lanes] = lower[source, taken]
-
-    def earlier(part, lanes):
-        width = before[0].shape[-1]
-        start = lanes.start % width
-        return before[lanes.start // width][part, :, start : start + lanes.stop - lanes.start]
-
-    def find_sums(lanes):
+                    high[part, rows, lanes] = upper[taken, source]
+                    low[part, rows, lanes] = lower[taken, source]
+
+    def earlier(part, rows):
+        height = before[0].shape[1]
+        start = rows.start % height
+        return before[rows.start // height][part, start : start + rows.stop - rows.start, :]
+
+    def find_sums(rows):
         sums = []
         for part in range(2):
-            both = jnp.dot(
-                table[part], high[part, :, lanes], preferred_element_type=jnp.float32
-            )
-            rest = jnp.dot(
-                table[part, :padded_rows],
-                low[part, :, lanes],
-                preferred_element_type=jnp.float32,
-            )
-            total = both[:padded_rows] + (both[padded_rows:] + rest)
-            sums.append(total if first else total + earlier(part, lanes))
+            total = table_sums(padded_rows, table, high, low, part, rows)
+            sums.append(total if first else total + earlier(part, rows))
         if not last:
             for part in range(2):
-                outs[0][part, :, lanes] = sums[part]
+                outs[0][part, rows, :] = sums[part]
             return
-        own_rows = outs[0].shape[0]
-        width = lanes.stop - lanes.start
-        row = lax.broadcasted_iota(jnp.int32, (own_rows, width), 0) + plan[ROWS, 0]
-        temperature = CUTOFF / freq_count
-        renorm = 1.0 + temperature * sums[1][:own_rows] / omega_of(row, freq_count)
-        gap = temperature * sums[0][:own_rows] / renorm
-        if not final:
-            outs[0][:, lanes] = encoded(gap) if coded else gap
+        gap, renorm = finished(freq_count, plan[ROWS, 0], sums)
+        if coded and not final:
+            outs[0][rows, :] = encoded(gap)
             return
-        for at, value in enumerate((gap, renorm)):
-            held[at][:, lanes] = value
-            copy_out(at, lanes).start()
-
-    def copy_out(at, lanes):
-        width = lanes.stop - lanes.start
+        for at, value in enumerate((gap, renorm)[: len(outs)]):
+            for start in range(0, rows.stop - rows.start, size):
+                turned = value[start : start + size].T
+                lanes = slice(rows.start + start, rows.start + start + size)
+                if copied:
+                    held[at][:, lanes] = turned[: held[at].shape[0]]
+                else:
+                    outs[at][:, lanes] = turned[: outs[at].shape[0]]
+            if copied:
+                copy_out(at, rows).start()
+
+    def copy_out(at, rows):
+        width = rows.stop - rows.start
         return pltpu.make_async_copy(
-            held[at].at[:, pl.ds(lanes.start, width)],
-            outs[at].at[:, pl.ds(lanes.start, width)],
-            sems.at[at, lanes.start // width],
+            held[at].at[:, pl.ds(rows.start, width)],
+            outs[at].at[:, pl.ds(rows.start, width)],
+            sems.at[at, rows.start // width],
         )
 
     halves = [slice(start * size, (start + 2) * size) for start in range(0, blocks, 2)]
@@ -224,31 +219,41 @@
             find_sums(halves[block // 2 - 1])
     find_sums(halves[-1])
     if copied:
-        for lanes in halves:
+        for rows in halves:
             for at in range(2):
-                copy_out(at, lanes).wait()
+                copy_out(at, rows).wait()
+
+
+def table_sums(padded_rows, table, high, low, part, rows):
+    both = jnp.dot(high[part, rows, :], table[part], preferred_element_type=jnp.float32)
+    rest = jnp.dot(
+        low[part, rows, :], table[part, :, :padded_rows], preferred_element_type=jnp.float32
+    )
+    return both[:, :padded_rows] + (both[:, padded_rows:] + rest)
+
+
+def finished(freq_count, first_row, sums):
+    row = lax.broadcasted_iota(jnp.int32, sums[0].shape, 1) + first_row
+    temperature = CUTOFF / freq_count
+    renorm = 1.0 + temperature * sums[1] / omega_of(row, freq_count)
+    return temperature * sums[0] / renorm, renorm
 
 
 def other_rows_kernel(dims, plan, *refs):
     freq_count, segments, segment_rows, padded_rows, modes = dims
     tables, terms, code = refs[:segments], refs[segments:-1], refs[-1]
+    states = terms[0].shape[1]
     sums = []
     for part in range(2):
         total = None
         for segment in range(segments):
-            table, high, low = tables[segment], terms[2 * segment], terms[2 * segment + 1]
-            both = jnp.dot(table[part], high[part], preferred_element_type=jnp.float32)
-            rest = jnp.dot(
-                table[part, :padded_rows], low[part], preferred_element_type=jnp.float32
-            )
-            piece = both[:padded_rows] + (both[padded_rows:] + rest)
+            high, low = terms[2 * segment], terms[2 * segment + 1]
+            piece = table_sums(padded_rows, tables[segment], high, low, part, slice(0, states))
             total = piece if total is None else total + piece
         sums.append(total)
-    row = lax.broadcasted_iota(jnp.int32, (padded_rows, code.shape[1]), 0) + plan[ROWS, 2]
-    temperature = CUTOFF / freq_count
-    renorm = 1.0 + temperature * sums[1] / omega_of(row, freq_count)
-    code[:padded_rows] = encoded(temperature * sums[0] / renorm)
-    code[padded_rows:] = jnp.zeros((SPARE_ROWS, code.shape[1]), code.dtype)
+    gap, _ = finished(freq_count, plan[ROWS, 2], sums)
+    code[:states] = encoded(gap)
+    code[states:] = jnp.zeros((SPARE_ROWS, code.shape[1]), code.dtype)
 
 
 SWAP = [(0, 1), (1, 0)]
@@ -259,7 +264,8 @@
     rows = lax.all_gather(everyone, "freq", axis=1, tiled=True)
     own_rows = gap.shape[0]
     start = (lax.axis_index("freq") // half_groups) * (half_groups * own_rows)
-    return [lax.dynamic_slice_in_dim(rows, start, half_groups * own_rows, 1)]
+    half = lax.dynamic_slice_in_dim(rows, start, half_groups * own_rows, 1)
+    return [jnp.swapaxes(half, 1, 2)]
 
 
 def on_device(pairwise, freq_groups, gap_in, coupling, pair_cols, pair_count, block_order, phonon):
@@ -268,7 +274,7 @@
     freq_count = own_rows * freq_groups
     half_rows = freq_count // 2
     half_groups = freq_groups // 2
-    padded_rows = -(-own_rows // 16) * 16
+    padded_rows = -(-own_rows // LANES) * LANES
     if pairwise:
         segments, sides = 2, 2
         half = lax.axis_index("zhi") * half_rows
@@ -290,7 +296,7 @@
     if pairwise:
         passed = pl.pallas_call(
             encode_kernel,
-            out_shape=jax.ShapeDtypeStruct(gap_in.shape, link_type),
+            out_shape=jax.ShapeDtypeStruct((row_width, own_rows), link_type),
             in_specs=[vmem],
             out_specs=vmem,
             compiler_params=pltpu.CompilerParams(vmem_limit_bytes=8 << 20),
@@ -301,13 +307,13 @@
         )(gap_in)
 
     table_shape = jax.ShapeDtypeStruct(
-        (2, 2 * padded_rows, modes * segment_rows), jnp.bfloat16
+        (2, modes * segment_rows, 2 * padded_rows), jnp.bfloat16
     )
     plan, weights, *tables = pl.pallas_call(
         functools.partial(tables_kernel, dims, sides),
         out_shape=[
             jax.ShapeDtypeStruct((5, max(blocks * slots, 1 + segments)), jnp.int32),
-            jax.ShapeDtypeStruct((blocks, slots * size, modes * size), jnp.bfloat16),
+            jax.ShapeDtypeStruct((blocks, modes * size, slots * size), jnp.bfloat16),
         ]
         + [table_shape] * segments,
         in_specs=[smem] * 5 + [vmem],
@@ -320,7 +326,8 @@
     )(meta, phonon, pair_cols, pair_count, block_order, coupling)
 
     full = jax.ShapeDtypeStruct(gap_in.shape, jnp.float32)
-    passed_out = jax.ShapeDtypeStruct(gap_in.shape, link_type)
+    passed_shape = (row_width, own_rows) if pairwise else gap_in.shape
+    passed_out = jax.ShapeDtypeStruct(passed_shape, link_type)
     step_params = dict(
         compiler_params=pltpu.CompilerParams(vmem_limit_bytes=24 << 20),
         cost_estimate=pl.CostEstimate(
@@ -331,13 +338,13 @@
     def step(plan, segment, final, pieces, before, keep=False, span=(0, blocks)):
         copied = final and segment == segments - 1
         width = (span[1] - span[0]) * size
-        terms_shape = (2, modes * segment_rows, width)
+        terms_shape = (2, width, modes * segment_rows)
         if segment < segments - 1:
-            outs = [jax.ShapeDtypeStruct((2, padded_rows, width), jnp.float32)]
+            outs = [jax.ShapeDtypeStruct((2, width, padded_rows), jnp.float32)]
         else:
             outs = [full, full] if final else [passed_out]
         out_specs = [pl.BlockSpec(memory_space=pl.ANY) if copied else vmem] * len(outs)
-        scratch = [pltpu.VMEM((span[1] - span[0], 2 * segment_rows, slots * size), jnp.bfloat16)]
+        scratch = [pltpu.VMEM((span[1] - span[0], slots * size, 2 * segment_rows), jnp.bfloat16)]
         if keep:
             outs += [jax.ShapeDtypeStruct(terms_shape, jnp.bfloat16)] * 2
             out_specs += [vmem] * 2
@@ -369,7 +376,7 @@
     def join(near, across, after):
         return pl.pallas_call(
             join_kernel,
-            out_shape=jax.ShapeDtypeStruct((2, *gap_in.shape), near.dtype),
+            out_shape=jax.ShapeDtypeStruct((2, *passed_shape), near.dtype),
             in_specs=[vmem, vmem, pl.BlockSpec(memory_space=pl.ANY)],
             out_specs=vmem,
             compiler_params=pltpu.CompilerParams(vmem_limit_bytes=4 << 20),
@@ -403,7 +410,7 @@
     inputs = [*other_tables, *near_terms, *far_terms]
     other = pl.pallas_call(
         functools.partial(other_rows_kernel, dims),
-        out_shape=jax.ShapeDtypeStruct((own_rows + SPARE_ROWS, row_width), link_type),
+        out_shape=jax.ShapeDtypeStruct((row_width + SPARE_ROWS, own_rows), link_type),
         in_specs=[smem] + [vmem] * len(inputs),
         out_specs=vmem,
         name="other_rows",

time: 35.5 us -> 37 us (1.042)
  Pallas kernels: 20.3 us -> 22.4 us
  waiting for transfers between devices: 5.29 us -> 3.95 us
  starting transfers between devices: 7.81 us -> 8.38 us
    pallas_call x5, Pallas kernels: 13.6 us -> 14.8 us  [step(): pl.pallas_call(functools.partial(step_kernel, dims, segment, span, sides,...]
    pallas_call x1, Pallas kernels: 2.96 us -> 3.54 us  [on_device(): pl.pallas_call(functools.partial(other_rows_kernel, dims), out_shape=jax....]
    ppermute x1, waiting for transfers between devices: 0.63 us -> 0.06 us  [on_device(): along_x = lax.ppermute(own, 'x', SWAP)]
    ppermute x4, starting transfers between devices: 0.58 us -> 1.03 us  [with_core(): return near + [lax.ppermute(piece, 'core', SWAP) for piece in near]]
  transfers between devices with their start and end apart: 11 -> 11, of which waited for: 8 -> 8; matrix products, arithmetic and copies ran while one was open for 0% -> 0% of each run, Pallas kernels for 37% -> 40%
where the time goes in v9:
time: 37 us; the launch traced here: 36.8 us
  Pallas kernels  22.4 us (61%)
  starting transfers between devices  8.38 us (23%)
  waiting for transfers between devices  3.95 us (11%)
  local copies, waits for them, and re-layouts  1.16 us (3%)
  between operations  0.94 us (3%)
    pallas_call x5, Pallas kernels, step(): pl.pallas_call(functools.partial(step_kernel, dims, segment, span, sides,...  14.8 us
    pallas_call x1, Pallas kernels, on_device(): pl.pallas_call(functools.partial(other_rows_kernel, dims), out_shape=jax....  3.54 us
    ppermute x1, starting transfers between devices, on_device(): along_x = lax.ppermute(passed, 'x', SWAP)  3 us
    pallas_call x1, Pallas kernels, on_device(): pl.pallas_call(functools.partial(tables_kernel, dims, sides), out_shape=[...  2.53 us
    ppermute x1, starting transfers between devices, on_device(): along_z = lax.ppermute(passed, 'zlo', SWAP)  1.58 us
    ppermute x4, waiting for transfers between devices, with_core(): return near + [lax.ppermute(piece, 'core', SWAP) for piece in near]  1.47 us
    ppermute x1, starting transfers between devices, on_device(): far = join(other, lax.ppermute(other, 'x', SWAP), *partial)  1.33 us
    pallas_call x1, Pallas kernels, on_device(): pl.pallas_call(functools.partial(other_tables_kernel, dims), out_shape=[t...  1.31 us
  transfers between devices with their start and end apart: 11, of which 8 were waited for; matrix products, arithmetic and copies ran while one was open for 0% of the time, Pallas kernels for 40%

profile of v9, /device:TPU:0, one launch (start us, length us, event | category | flops | bytes accessed | tf_op | source)
XLA Modules:
  0.0 36.8 jit_solution(6602652131743846712)
XLA Ops:
  0.7 1.0 %copy-done.4 = f32[128,512]{1,0:T(8,128)S(1)} copy-done((f32[128,512]{1,0:T(8,128)S(1)}, f32[128,512]{1,0:T(8,128)}, u32[]{:S(2)}) %copy-start.4) | copy-done | bytes 262168
  1.6 0.2 encode.1.refs_0_
  1.9 3.0 %collective-permute-start = (s16[512,128]{1,0:T(8,128)(2,1)S(1)}, s16[512,128]{1,0:T(8,128)(2,1)S(1)}, u32[]{:S(2)}, u32[]{:S(2)}) collective-permute-start(s16[512,128]{1,0:T(8,128)(2,1)S(1)} %encode.1.refs_0_), channel_id=1, source_target_pairs={{0,2},{2,0},{1,3},{3,1},{4,6},{6,4},{5,7},{7,5},{8,10},{10,8},{9,1... | collective-permute-start | bytes 393224 | tf_op jit(solution)/shard_map/ppermute | solution.py:401
  4.9 1.6 %collective-permute-start.3 = (s16[512,128]{1,0:T(8,128)(2,1)S(1)}, s16[512,128]{1,0:T(8,128)(2,1)S(1)}, u32[]{:S(2)}, u32[]{:S(2)}) collective-permute-start(s16[512,128]{1,0:T(8,128)(2,1)S(1)} %encode.1.refs_0_), channel_id=1, source_target_pairs={{0,4},{4,0},{1,5},{5,1},{2,6},{6,2},{3,7},{7,3},{8,12},{12,8},{9,1... | collective-permute-start | bytes 393224 | tf_op jit(solution)/shard_map/ppermute | solution.py:402
  6.4 0.0 collective-permute-start.1
  6.4 0.1 copy.8.pair_cols
  6.5 0.1 stack.20.meta
  6.6 2.5 %tables.1 = (s32[5,8]{1,0:T(8,128)S(1)}, bf16[4,1152,256]{2,1,0:T(8,128)(2,1)S(1)}, bf16[2,1152,256]{2,1,0:T(8,128)(2,1)S(1)}, bf16[2,1152,256]{2,1,0:T(8,128)(2,1)S(1)}) custom-call(s32[5]{0:T(128)S(1)} %stack.20.meta, f32[9]{0:T(128)S(1)} %copy-done.3, s32[4,2]{1,0:T(4,128)S(1)} %copy.8.pair_cols, s32[4]{0:T(128)S(1)} %copy-done.1, s32[16]{0:T(128)S(1)} %copy-done.2, ...), custom_call_target="tpu_custom_call" | custom-call | flops 10000000 | bytes 8000000 | tf_op jit(solution)/shard_map/tables/pallas_call | solution.py:312
  9.2 0.0 collective-permute-done.refs_1_
  9.2 0.6 %collective-permute-start.2 = (s16[512,128]{1,0:T(8,128)(2,1)S(1)}, s16[512,128]{1,0:T(8,128)(2,1)S(1)}, u32[]{:S(2)}, u32[]{:S(2)}) collective-permute-start(s16[512,128]{1,0:T(8,128)(2,1)S(1)} %collective-permute-done.refs_1_), channel_id=1, source_target_pairs={{0,1},{1,0},{2,3},{3,2},{4,5},{5,4},{6,7},{7,6},{8,9},{9,8},{10,11... | collective-permute-start | bytes 393224 | tf_op jit(solution)/shard_map/ppermute | solution.py:388
  9.8 0.1 collective-permute-done.3.first
  9.8 0.5 %collective-permute-start.4 = (s16[512,128]{1,0:T(8,128)(2,1)S(1)}, s16[512,128]{1,0:T(8,128)(2,1)S(1)}, u32[]{:S(2)}, u32[]{:S(2)}) collective-permute-start(s16[512,128]{1,0:T(8,128)(2,1)S(1)} %collective-permute-done.3.first), channel_id=1, source_target_pairs={{0,2},{2,0},{1,3},{3,1},{4,6},{6,4},{5,7},{7,5},{8,10},{10,8},{9,1... | collective-permute-start | bytes 393224 | tf_op jit(solution)/shard_map/ppermute | solution.py:404
  10.3 0.0 collective-permute-done.1.refs_2_
  10.3 0.4 %collective-permute-done.2.refs_3_ = s16[512,128]{1,0:T(8,128)(2,1)S(1)} collective-permute-done((s16[512,128]{1,0:T(8,128)(2,1)S(1)}, s16[512,128]{1,0:T(8,128)(2,1)S(1)}, u32[]{:S(2)}, u32[]{:S(2)}) %collective-permute-start.2) | collective-permute-done | bytes 131104 | tf_op jit(solution)/shard_map/ppermute | solution.py:388
  10.7 3.2 %step.5 = (f32[2,512,128]{2,1,0:T(8,128)S(1)}, bf16[2,512,1152]{2,1,0:T(8,128)(2,1)S(1)}, bf16[2,512,1152]{2,1,0:T(8,128)(2,1)S(1)}) custom-call(s32[5,8]{1,0:T(8,128)S(1)} %get-tuple-element.23.plan, s16[512,128]{1,0:T(8,128)(2,1)S(1)} %encode.1.refs_0_, s16[512,128]{1,0:T(8,128)(2,1)S(1)} %collective-permute-done.refs_1_, ...), custom_call_target="tpu_custom_call" | custom-call | flops 1000000 | bytes 100000 | tf_op jit(solution)/shard_map/step/pallas_call | solution.py:357
  14.0 1.3 %collective-permute-done.4.second = s16[512,128]{1,0:T(8,128)(2,1)S(1)} collective-permute-done((s16[512,128]{1,0:T(8,128)(2,1)S(1)}, s16[512,128]{1,0:T(8,128)(2,1)S(1)}, u32[]{:S(2)}, u32[]{:S(2)}) %collective-permute-start.4) | collective-permute-done | bytes 131104 | tf_op jit(solution)/shard_map/ppermute | solution.py:404
  15.3 0.1 collective-permute-start.5
  15.4 1.3 %other_tables.1 = (bf16[2,1152,256]{2,1,0:T(8,128)(2,1)S(1)}, bf16[2,1152,256]{2,1,0:T(8,128)(2,1)S(1)}) custom-call(s32[5]{0:T(128)S(1)} %stack.20.meta, f32[9]{0:T(128)S(1)} %copy-done.3), custom_call_target="tpu_custom_call" | custom-call | flops 10000000 | bytes 3000000 | tf_op jit(solution)/shard_map/other_tables/pallas_call | solution.py:390
  16.7 0.2 collective-permute-done.5.refs_1_
  16.9 3.4 %step.6 = (s16[512,128]{1,0:T(8,128)(2,1)S(1)}, bf16[2,512,1152]{2,1,0:T(8,128)(2,1)S(1)}, bf16[2,512,1152]{2,1,0:T(8,128)(2,1)S(1)}) custom-call(s32[5,8]{1,0:T(8,128)S(1)} %get-tuple-element.23.plan, s16[2,512,128]{2,1,0:T(8,128)(2,1)S(1)} %join.2.refs_0_, s16[2,512,128]{2,1,0:T(8,128)(2,1)S(1)} %collective-permute-done.5.refs_1_, ...), custom_call_target="tpu_custom_call" | custom-call | flops 1000000 | bytes 100000 | tf_op jit(solution)/shard_map/step/pallas_call | solution.py:357
  20.3 0.8 %collective-permute-start.7 = (s16[512,128]{1,0:T(8,128)(2,1)S(1)}, s16[512,128]{1,0:T(8,128)(2,1)S(1)}, u32[]{:S(2)}, u32[]{:S(2)}) collective-permute-start(s16[512,128]{1,0:T(8,128)(2,1)S(1)} %get-tuple-element.35.refs_0_), channel_id=1, source_target_pairs={{0,2},{2,0},{1,3},{3,1},{4,6},{6,4},{5,7},{7,5},{8,10},{10,8},{9,1... | collective-permute-start | bytes 393224 | tf_op jit(solution)/shard_map/ppermute | solution.py:419
  21.1 3.5 %other_rows.1.first = s16[544,128]{1,0:T(8,128)(2,1)S(1)} custom-call(s32[5,8]{1,0:T(8,128)S(1)} %get-tuple-element.23.plan, bf16[2,1152,256]{2,1,0:T(8,128)(2,1)S(1)} %get-tuple-element.24.refs_0_, bf16[2,1152,256]{2,1,0:T(8,128)(2,1)S(1)} %get-tuple-element.25.refs_1_, bf16[2,512,1152]{2,1,0:T(8,128)(2,1)S(1)} %get-tuple-element.29.refs_2_, ...), custom_call_target="tpu_custom_call" | custom-call | flops 1000000 | bytes 100000 | tf_op jit(solution)/shard_map/other_rows/pallas_call | solution.py:411
  24.7 1.3 %collective-permute-start.6 = (s16[544,128]{1,0:T(8,128)(2,1)S(1)}, s16[544,128]{1,0:T(8,128)(2,1)S(1)}, u32[]{:S(2)}, u32[]{:S(2)}) collective-permute-start(s16[544,128]{1,0:T(8,128)(2,1)S(1)} %other_rows.1.first), channel_id=1, source_target_pairs={{0,2},{2,0},{1,3},{3,1},{4,6},{6,4},{5,7},{7,5},{8,10},{10,8},{9,1... | collective-permute-start | bytes 417800 | tf_op jit(solution)/shard_map/ppermute | solution.py:423
  26.0 0.1 collective-permute-done.7.refs_1_
  26.1 0.4 %collective-permute-start.9 = (s16[512,128]{1,0:T(8,128)(2,1)S(1)}, s16[512,128]{1,0:T(8,128)(2,1)S(1)}, u32[]{:S(2)}, u32[]{:S(2)}) collective-permute-start(s16[512,128]{1,0:T(8,128)(2,1)S(1)} %collective-permute-done.7.refs_1_), channel_id=1, source_target_pairs={{0,1},{1,0},{2,3},{3,2},{4,5},{5,4},{6,7},{7,6},{8,9},{9,8},{10,11... | collective-permute-start | bytes 393224 | tf_op jit(solution)/shard_map/ppermute | solution.py:388
  26.5 0.8 %collective-permute-done.8.refs_2_ = s16[512,128]{1,0:T(8,128)(2,1)S(1)} collective-permute-done((s16[512,128]{1,0:T(8,128)(2,1)S(1)}, s16[512,128]{1,0:T(8,128)(2,1)S(1)}, u32[]{:S(2)}, u32[]{:S(2)}) %collective-permute-start.8) | collective-permute-done | bytes 131104 | tf_op jit(solution)/shard_map/ppermute | solution.py:388
  27.4 0.2 collective-permute-done.9.refs_3_
  27.6 1.9 %step.7.after.refs_4_ = f32[2,256,128]{2,1,0:T(8,128)S(1)} custom-call(s32[5,8]{1,0:T(8,128)S(1)} %get-tuple-element.23.plan, s16[512,128]{1,0:T(8,128)(2,1)S(1)} %get-tuple-element.35.refs_0_, s16[512,128]{1,0:T(8,128)(2,1)S(1)} %collective-permute-done.7.refs_1_, s16[512,128]{1,0:T(8,128)(2,1)S(1)} %collective-permute-done.8.refs_2_, ...), custom_call_target="tpu_custom_call" | custom-call | flops 1000000 | bytes 100000 | tf_op jit(solution)/shard_map/step/pallas_call | solution.py:357
  29.5 0.9 %collective-permute-done.6.second = s16[544,128]{1,0:T(8,128)(2,1)S(1)} collective-permute-done((s16[544,128]{1,0:T(8,128)(2,1)S(1)}, s16[544,128]{1,0:T(8,128)(2,1)S(1)}, u32[]{:S(2)}, u32[]{:S(2)}) %collective-permute-start.6) | collective-permute-done | bytes 139296 | tf_op jit(solution)/shard_map/ppermute | solution.py:423
  30.4 0.1 collective-permute-start.10
  30.5 2.1 %step.8.refs_5_ = f32[2,256,128]{2,1,0:T(8,128)S(1)} custom-call(s32[5,8]{1,0:T(8,128)S(1)} %get-tuple-element.23.plan, s16[512,128]{1,0:T(8,128)(2,1)S(1)} %get-tuple-element.35.refs_0_, s16[512,128]{1,0:T(8,128)(2,1)S(1)} %collective-permute-done.7.refs_1_, s16[512,128]{1,0:T(8,128)(2,1)S(1)} %collective-permute-done.8.refs_2_, ...), custom_call_target="tpu_custom_call" | custom-call | flops 1000000 | bytes 100000 | tf_op jit(solution)/shard_map/step/pallas_call | solution.py:357
  32.6 4.1 %step.9 = (f32[128,512]{1,0:T(8,128)}, f32[128,512]{1,0:T(8,128)}) custom-call(s32[5,8]{1,0:T(8,128)S(1)} %get-tuple-element.23.plan, s16[2,512,128]{2,1,0:T(8,128)(2,1)S(1)} %join.3.refs_0_, s16[2,512,128]{2,1,0:T(8,128)(2,1)S(1)} %collective-permute-done.10.refs_1_, bf16[4,1152,256]{2,1,0:T(8,128)(2,1)S(1)} %get-tuple-element.27.refs_4_.refs_2_, ...), custom_call_target="tpu_custom_call" | custom-call | flops 1000000 | bytes 100000 | tf_op jit(solution)/shard_map/step/pallas_call | solution.py:357
  (15 shorter events, 0.1 us)
Async XLA Ops:
  0.6 6.0 %copy-start.3 = (f32[9]{0:T(128)S(1)}, f32[9]{0:T(128)}, u32[]{:S(2)}) copy-start(f32[9]{0:T(128)} %phonon.3) | copy-start | bytes 112
  0.6 6.0 %copy-start.2 = (s32[16]{0:T(128)S(1)}, s32[16]{0:T(128)}, u32[]{:S(2)}) copy-start(s32[16]{0:T(128)} %block_order.1) | copy-start | bytes 196
  0.7 6.0 %copy-start.1 = (s32[4]{0:T(128)S(1)}, s32[4]{0:T(128)}, u32[]{:S(2)}) copy-start(s32[4]{0:T(128)} %pair_count.1) | copy-start | bytes 52
  0.7 1.0 %copy-start.4 = (f32[128,512]{1,0:T(8,128)S(1)}, f32[128,512]{1,0:T(8,128)}, u32[]{:S(2)}) copy-start(f32[128,512]{1,0:T(8,128)} %gap.1) | copy-start | bytes 786436
  1.6 4.8 %copy-start.5 = (s32[4,2]{0,1:T(2,128)S(1)}, s32[4,2]{0,1:T(2,128)}, u32[]{:S(2)}) copy-start(s32[4,2]{0,1:T(2,128)} %param.8) | copy-start | bytes 100
  1.6 5.0 %copy-start = (bf16[4,2,9,128,128]{4,3,2,1,0:T(8,128)(2,1)S(1)}, bf16[4,2,9,128,128]{4,3,2,1,0:T(8,128)(2,1)}, u32[]{:S(2)}) copy-start(bf16[4,2,9,128,128]{4,3,2,1,0:T(8,128)(2,1)} %coupling.1) | copy-start | bytes 7077892
  1.9 7.3 %collective-permute-start = (s16[512,128]{1,0:T(8,128)(2,1)S(1)}, s16[512,128]{1,0:T(8,128)(2,1)S(1)}, u32[]{:S(2)}, u32[]{:S(2)}) collective-permute-start(s16[512,128]{1,0:T(8,128)(2,1)S(1)} %encode.1.refs_0_), channel_id=1, source_target_pairs={{0,2},{2,0},{1,3},{3,1},{4,6},{6,4},{5,7},{7,5},{8,10},{10,8},{9,1... | collective-permute-start | bytes 393224 | tf_op jit(solution)/shard_map/ppermute | solution.py:401
  4.9 5.0 %collective-permute-start.3 = (s16[512,128]{1,0:T(8,128)(2,1)S(1)}, s16[512,128]{1,0:T(8,128)(2,1)S(1)}, u32[]{:S(2)}, u32[]{:S(2)}) collective-permute-start(s16[512,128]{1,0:T(8,128)(2,1)S(1)} %encode.1.refs_0_), channel_id=1, source_target_pairs={{0,4},{4,0},{1,5},{5,1},{2,6},{6,2},{3,7},{7,3},{8,12},{12,8},{9,1... | collective-permute-start | bytes 393224 | tf_op jit(solution)/shard_map/ppermute | solution.py:402
  6.4 3.9 %collective-permute-start.1 = (s16[512,128]{1,0:T(8,128)(2,1)S(1)}, s16[512,128]{1,0:T(8,128)(2,1)S(1)}, u32[]{:S(2)}, u32[]{:S(2)}) collective-permute-start(s16[512,128]{1,0:T(8,128)(2,1)S(1)} %encode.1.refs_0_), channel_id=1, source_target_pairs={{0,1},{1,0},{2,3},{3,2},{4,5},{5,4},{6,7},{7,6},{8,9},{9,8},{10,11... | collective-permute-start | bytes 393224 | tf_op jit(solution)/shard_map/ppermute | solution.py:388
  9.2 1.6 %collective-permute-start.2 = (s16[512,128]{1,0:T(8,128)(2,1)S(1)}, s16[512,128]{1,0:T(8,128)(2,1)S(1)}, u32[]{:S(2)}, u32[]{:S(2)}) collective-permute-start(s16[512,128]{1,0:T(8,128)(2,1)S(1)} %collective-permute-done.refs_1_), channel_id=1, source_target_pairs={{0,1},{1,0},{2,3},{3,2},{4,5},{5,4},{6,7},{7,6},{8,9},{9,8},{10,11... | collective-permute-start | bytes 393224 | tf_op jit(solution)/shard_map/ppermute | solution.py:388
  9.8 5.4 %collective-permute-start.4 = (s16[512,128]{1,0:T(8,128)(2,1)S(1)}, s16[512,128]{1,0:T(8,128)(2,1)S(1)}, u32[]{:S(2)}, u32[]{:S(2)}) collective-permute-start(s16[512,128]{1,0:T(8,128)(2,1)S(1)} %collective-permute-done.3.first), channel_id=1, source_target_pairs={{0,2},{2,0},{1,3},{3,1},{4,6},{6,4},{5,7},{7,5},{8,10},{10,8},{9,1... | collective-permute-start | bytes 393224 | tf_op jit(solution)/shard_map/ppermute | solution.py:404
  15.3 1.6 %collective-permute-start.5 = (s16[2,512,128]{2,1,0:T(8,128)(2,1)S(1)}, s16[2,512,128]{2,1,0:T(8,128)(2,1)S(1)}, u32[]{:S(2)}, u32[]{:S(2)}) collective-permute-start(s16[2,512,128]{2,1,0:T(8,128)(2,1)S(1)} %join.2.refs_0_), channel_id=1, source_target_pairs={{0,1},{1,0},{2,3},{3,2},{4,5},{5,4},{6,7},{7,6},{8,9},{9,8},{10,11... | collective-permute-start | bytes 786440 | tf_op jit(solution)/shard_map/ppermute | solution.py:407
  20.3 5.8 %collective-permute-start.7 = (s16[512,128]{1,0:T(8,128)(2,1)S(1)}, s16[512,128]{1,0:T(8,128)(2,1)S(1)}, u32[]{:S(2)}, u32[]{:S(2)}) collective-permute-start(s16[512,128]{1,0:T(8,128)(2,1)S(1)} %get-tuple-element.35.refs_0_), channel_id=1, source_target_pairs={{0,2},{2,0},{1,3},{3,1},{4,6},{6,4},{5,7},{7,5},{8,10},{10,8},{9,1... | collective-permute-start | bytes 393224 | tf_op jit(solution)/shard_map/ppermute | solution.py:419
  24.7 5.7 %collective-permute-start.6 = (s16[544,128]{1,0:T(8,128)(2,1)S(1)}, s16[544,128]{1,0:T(8,128)(2,1)S(1)}, u32[]{:S(2)}, u32[]{:S(2)}) collective-permute-start(s16[544,128]{1,0:T(8,128)(2,1)S(1)} %other_rows.1.first), channel_id=1, source_target_pairs={{0,2},{2,0},{1,3},{3,1},{4,6},{6,4},{5,7},{7,5},{8,10},{10,8},{9,1... | collective-permute-start | bytes 417800 | tf_op jit(solution)/shard_map/ppermute | solution.py:423
  26.0 1.3 %collective-permute-start.8 = (s16[512,128]{1,0:T(8,128)(2,1)S(1)}, s16[512,128]{1,0:T(8,128)(2,1)S(1)}, u32[]{:S(2)}, u32[]{:S(2)}) collective-permute-start(s16[512,128]{1,0:T(8,128)(2,1)S(1)} %get-tuple-element.35.refs_0_), channel_id=1, source_target_pairs={{0,1},{1,0},{2,3},{3,2},{4,5},{5,4},{6,7},{7,6},{8,9},{9,8},{10,11... | collective-permute-start | bytes 393224 | tf_op jit(solution)/shard_map/ppermute | solution.py:388
  26.1 1.5 %collective-permute-start.9 = (s16[512,128]{1,0:T(8,128)(2,1)S(1)}, s16[512,128]{1,0:T(8,128)(2,1)S(1)}, u32[]{:S(2)}, u32[]{:S(2)}) collective-permute-start(s16[512,128]{1,0:T(8,128)(2,1)S(1)} %collective-permute-done.7.refs_1_), channel_id=1, source_target_pairs={{0,1},{1,0},{2,3},{3,2},{4,5},{5,4},{6,7},{7,6},{8,9},{9,8},{10,11... | collective-permute-start | bytes 393224 | tf_op jit(solution)/shard_map/ppermute | solution.py:388
  30.4 2.2 %collective-permute-start.10 = (s16[2,512,128]{2,1,0:T(8,128)(2,1)S(1)}, s16[2,512,128]{2,1,0:T(8,128)(2,1)S(1)}, u32[]{:S(2)}, u32[]{:S(2)}) collective-permute-start(s16[2,512,128]{2,1,0:T(8,128)(2,1)S(1)} %join.3.refs_0_), channel_id=1, source_target_pairs={{0,1},{1,0},{2,3},{3,2},{4,5},{5,4},{6,7},{7,6},{8,9},{9,8},{10,11... | collective-permute-start | bytes 786440 | tf_op jit(solution)/shard_map/ppermute | solution.py:425

commit v10 on v8

--- a/solution.py
+++ b/solution.py
@@ -69,7 +69,8 @@
             for part, value in enumerate((common * (below + above), common * cross)):
                 high, low = split(value)
                 tables[segment][part, :padded_rows, columns] = high
-                tables[segment][part, padded_rows:, columns] = low
+                if tables[segment].shape[1] > padded_rows:
+                    tables[segment][part, padded_rows:, columns] = low
 
 
 def other_tables_kernel(dims, meta, phonon, *tables):
@@ -113,10 +114,9 @@
     copied = last and final
     if copied:
         *held, sems = take(3)
-    high, low = (None, None) if keep else take(2)
+    terms = [] if keep else take(2 if first else 1)
     ratios = refs.pop()
-    if keep:
-        high, low = take(2)
+    terms = terms or take(2)
     outs = take(2 if copied else 1)
     inputs = refs
     before = [inputs.pop() for _ in range(0 if first else parted)][::-1]
@@ -158,19 +158,19 @@
         lanes = slice(block * size, (block + 1) * size)
         for start in range(0, modes, 2):
             stop = min(start + 2, modes)
-            terms = jnp.dot(
+            found = jnp.dot(
                 ratios[block],
                 weights[span[0] + block, :, start * size : stop * size],
                 preferred_element_type=jnp.float32,
             )
-            upper, lower = split(terms)
+            pieces_of = split(found) if len(terms) > 1 else [found.astype(jnp.bfloat16)]
             for mode in range(start, stop):
                 rows = slice(mode * segment_rows, (mode + 1) * segment_rows)
                 taken = slice((mode - start) * size, (mode - start + 1) * size)
                 for part in range(2):
                     source = slice(part * segment_rows, (part + 1) * segment_rows)
-                    high[part, rows, lanes] = upper[source, taken]
-                    low[part, rows, lanes] = lower[source, taken]
+                    for held_terms, value in zip(terms, pieces_of):
+                        held_terms[part, rows, lanes] = value[source, taken]
 
     def earlier(part, lanes):
         width = before[0].shape[-1]
@@ -180,15 +180,8 @@
     def find_sums(lanes):
         sums = []
         for part in range(2):
-            both = jnp.dot(
-                table[part], high[part, :, lanes], preferred_element_type=jnp.float32
-            )
-            rest = jnp.dot(
-                table[part, :padded_rows],
-                low[part, :, lanes],
-                preferred_element_type=jnp.float32,
-            )
-            total = both[:padded_rows] + (both[padded_rows:] + rest)
+            views = [held_terms.at[part, :, lanes] for held_terms in terms]
+            total = table_sums(padded_rows, table.at[part], *views)
             sums.append(total if first else total + earlier(part, lanes))
         if not last:
             for part in range(2):
@@ -229,6 +222,14 @@
                 copy_out(at, lanes).wait()
 
 
+def table_sums(padded_rows, table, high, low=None):
+    both = jnp.dot(table[...], high[...], preferred_element_type=jnp.float32)
+    if table.shape[0] == padded_rows:
+        return both
+    rest = jnp.dot(table[:padded_rows], low[...], preferred_element_type=jnp.float32)
+    return both[:padded_rows] + (both[padded_rows:] + rest)
+
+
 def other_rows_kernel(dims, plan, *refs):
     freq_count, segments, segment_rows, padded_rows, modes = dims
     tables, terms, code = refs[:segments], refs[segments:-1], refs[-1]
@@ -236,12 +237,8 @@
     for part in range(2):
         total = None
         for segment in range(segments):
-            table, high, low = tables[segment], terms[2 * segment], terms[2 * segment + 1]
-            both = jnp.dot(table[part], high[part], preferred_element_type=jnp.float32)
-            rest = jnp.dot(
-                table[part, :padded_rows], low[part], preferred_element_type=jnp.float32
-            )
-            piece = both[:padded_rows] + (both[padded_rows:] + rest)
+            views = [terms[2 * segment + at].at[part] for at in range(2)]
+            piece = table_sums(padded_rows, tables[segment].at[part], *views)
             total = piece if total is None else total + piece
         sums.append(total)
     row = lax.broadcasted_iota(jnp.int32, (padded_rows, code.shape[1]), 0) + plan[ROWS, 2]
@@ -300,16 +297,17 @@
             name="encode",
         )(gap_in)
 
-    table_shape = jax.ShapeDtypeStruct(
-        (2, 2 * padded_rows, modes * segment_rows), jnp.bfloat16
-    )
+    near_table, far_table = [
+        jax.ShapeDtypeStruct((2, count * padded_rows, modes * segment_rows), jnp.bfloat16)
+        for count in (2, 1)
+    ]
     plan, weights, *tables = pl.pallas_call(
         functools.partial(tables_kernel, dims, sides),
         out_shape=[
             jax.ShapeDtypeStruct((5, max(blocks * slots, 1 + segments)), jnp.int32),
             jax.ShapeDtypeStruct((blocks, slots * size, modes * size), jnp.bfloat16),
         ]
-        + [table_shape] * segments,
+        + [near_table, far_table][:segments],
         in_specs=[smem] * 5 + [vmem],
         out_specs=[smem] + [vmem] * (1 + segments),
         compiler_params=pltpu.CompilerParams(vmem_limit_bytes=24 << 20),
@@ -342,7 +340,7 @@
             outs += [jax.ShapeDtypeStruct(terms_shape, jnp.bfloat16)] * 2
             out_specs += [vmem] * 2
         else:
-            scratch += [pltpu.VMEM(terms_shape, jnp.bfloat16)] * 2
+            scratch += [pltpu.VMEM(terms_shape, jnp.bfloat16)] * (2 if segment == 0 else 1)
         if copied:
             scratch += [pltpu.VMEM(gap_in.shape, jnp.float32)] * 2
             scratch += [pltpu.SemaphoreType.DMA((2, blocks // 2))]
@@ -382,7 +380,7 @@
 
     other_tables = pl.pallas_call(
         functools.partial(other_tables_kernel, dims),
-        out_shape=[table_shape] * segments,
+        out_shape=[far_table, near_table],
         in_specs=[smem, smem],
         out_specs=[vmem] * segments,
         compiler_params=pltpu.CompilerParams(vmem_limit_bytes=12 << 20),

time: 35.5 us -> 33 us (0.930)
  Pallas kernels: 20.3 us -> 17.7 us
    pallas_call x5, Pallas kernels: 13.6 us -> 11.9 us  [step(): pl.pallas_call(functools.partial(step_kernel, dims, segment, span, sides,...]
    pallas_call x1, Pallas kernels: 2.96 us -> 2.29 us  [on_device(): pl.pallas_call(functools.partial(other_rows_kernel, dims), out_shape=jax....]
    ppermute x1, waiting for transfers between devices: 0.96 us -> 0.29 us  [on_device(): far = join(other, lax.ppermute(other, 'x', SWAP), *partial)]
    ppermute x1, waiting for transfers between devices: 0.63 us -> 1.18 us  [on_device(): along_x = lax.ppermute(own, 'x', SWAP)]
  transfers between devices with their start and end apart: 11 -> 11, of which waited for: 8 -> 8; matrix products, arithmetic and copies ran while one was open for 0% -> 1% of each run, Pallas kernels for 37% -> 38%
where the time goes in v10:
time: 33 us; the launch traced here: 32.8 us
  Pallas kernels  17.7 us (54%)
  starting transfers between devices  7.82 us (24%)
  waiting for transfers between devices  5.32 us (16%)
  local copies, waits for them, and re-layouts  1.16 us (4%)
  between operations  0.77 us (2%)
    pallas_call x5, Pallas kernels, step(): pl.pallas_call(functools.partial(step_kernel, dims, segment, span, sides,...  11.9 us
    ppermute x1, starting transfers between devices, on_device(): along_x = lax.ppermute(passed, 'x', SWAP)  3 us
    pallas_call x1, Pallas kernels, on_device(): pl.pallas_call(functools.partial(other_rows_kernel, dims), out_shape=jax....  2.29 us
    pallas_call x1, Pallas kernels, on_device(): pl.pallas_call(functools.partial(tables_kernel, dims, sides), out_shape=[...  2.25 us
    ppermute x4, waiting for transfers between devices, with_core(): return near + [lax.ppermute(piece, 'core', SWAP) for piece in near]  1.62 us
    ppermute x1, starting transfers between devices, on_device(): along_z = lax.ppermute(passed, 'zlo', SWAP)  1.58 us
    ppermute x1, waiting for transfers between devices, on_device(): relayed = lax.ppermute(along_z, 'x', SWAP)  1.52 us
    ppermute x1, waiting for transfers between devices, on_device(): along_x = lax.ppermute(own, 'x', SWAP)  1.18 us
  transfers between devices with their start and end apart: 11, of which 8 were waited for; matrix products, arithmetic and copies ran while one was open for 1% of the time, Pallas kernels for 38%

profile of v10, /device:TPU:0, one launch (start us, length us, event | category | flops | bytes accessed | tf_op | source)
XLA Modules:
  0.0 32.8 jit_solution(189837586414399979)
XLA Ops:
  0.7 1.0 %copy-done.4 = f32[128,512]{1,0:T(8,128)S(1)} copy-done((f32[128,512]{1,0:T(8,128)S(1)}, f32[128,512]{1,0:T(8,128)}, u32[]{:S(2)}) %copy-start.4) | copy-done | bytes 262168
  1.6 0.1 encode.1.refs_0_
  1.8 3.0 %collective-permute-start = (s16[128,512]{1,0:T(8,128)(2,1)S(1)}, s16[128,512]{1,0:T(8,128)(2,1)S(1)}, u32[]{:S(2)}, u32[]{:S(2)}) collective-permute-start(s16[128,512]{1,0:T(8,128)(2,1)S(1)} %encode.1.refs_0_), channel_id=1, source_target_pairs={{0,2},{2,0},{1,3},{3,1},{4,6},{6,4},{5,7},{7,5},{8,10},{10,8},{9,1... | collective-permute-start | bytes 393224 | tf_op jit(solution)/shard_map/ppermute | solution.py:392
  4.8 1.6 %collective-permute-start.3 = (s16[128,512]{1,0:T(8,128)(2,1)S(1)}, s16[128,512]{1,0:T(8,128)(2,1)S(1)}, u32[]{:S(2)}, u32[]{:S(2)}) collective-permute-start(s16[128,512]{1,0:T(8,128)(2,1)S(1)} %encode.1.refs_0_), channel_id=1, source_target_pairs={{0,4},{4,0},{1,5},{5,1},{2,6},{6,2},{3,7},{7,3},{8,12},{12,8},{9,1... | collective-permute-start | bytes 393224 | tf_op jit(solution)/shard_map/ppermute | solution.py:393
  6.4 0.0 collective-permute-start.1
  6.4 0.1 copy.8.pair_cols
  6.5 0.1 stack.20.meta
  6.6 2.2 %tables.1 = (s32[5,8]{1,0:T(8,128)S(1)}, bf16[4,256,1152]{2,1,0:T(8,128)(2,1)S(1)}, bf16[2,256,1152]{2,1,0:T(8,128)(2,1)S(1)}, bf16[2,128,1152]{2,1,0:T(8,128)(2,1)S(1)}) custom-call(s32[5]{0:T(128)S(1)} %stack.20.meta, f32[9]{0:T(128)S(1)} %copy-done.3, s32[4,2]{1,0:T(4,128)S(1)} %copy.8.pair_cols, s32[4]{0:T(128)S(1)} %copy-done.1, s32[16]{0:T(128)S(1)} %copy-done.2, ...), custom_call_target="tpu_custom_call" | custom-call | flops 10000000 | bytes 8000000 | tf_op jit(solution)/shard_map/tables/pallas_call | solution.py:304
  8.8 0.0 collective-permute-done.refs_1_
  8.8 0.6 %collective-permute-start.2 = (s16[128,512]{1,0:T(8,128)(2,1)S(1)}, s16[128,512]{1,0:T(8,128)(2,1)S(1)}, u32[]{:S(2)}, u32[]{:S(2)}) collective-permute-start(s16[128,512]{1,0:T(8,128)(2,1)S(1)} %collective-permute-done.refs_1_), channel_id=1, source_target_pairs={{0,1},{1,0},{2,3},{3,2},{4,5},{5,4},{6,7},{7,6},{8,9},{9,8},{10,11... | collective-permute-start | bytes 393224 | tf_op jit(solution)/shard_map/ppermute | solution.py:379
  9.4 0.4 %collective-permute-done.3.first = s16[128,512]{1,0:T(8,128)(2,1)S(1)} collective-permute-done((s16[128,512]{1,0:T(8,128)(2,1)S(1)}, s16[128,512]{1,0:T(8,128)(2,1)S(1)}, u32[]{:S(2)}, u32[]{:S(2)}) %collective-permute-start.3) | collective-permute-done | bytes 131104 | tf_op jit(solution)/shard_map/ppermute | solution.py:393
  9.8 0.4 %collective-permute-start.4 = (s16[128,512]{1,0:T(8,128)(2,1)S(1)}, s16[128,512]{1,0:T(8,128)(2,1)S(1)}, u32[]{:S(2)}, u32[]{:S(2)}) collective-permute-start(s16[128,512]{1,0:T(8,128)(2,1)S(1)} %collective-permute-done.3.first), channel_id=1, source_target_pairs={{0,2},{2,0},{1,3},{3,1},{4,6},{6,4},{5,7},{7,5},{8,10},{10,8},{9,1... | collective-permute-start | bytes 393224 | tf_op jit(solution)/shard_map/ppermute | solution.py:395
  10.1 0.0 collective-permute-done.1.refs_2_
  10.1 0.3 collective-permute-done.2.refs_3_
  10.4 3.0 %step.5 = (f32[2,128,512]{2,1,0:T(8,128)S(1)}, bf16[2,1152,512]{2,1,0:T(8,128)(2,1)S(1)}, bf16[2,1152,512]{2,1,0:T(8,128)(2,1)S(1)}) custom-call(s32[5,8]{1,0:T(8,128)S(1)} %get-tuple-element.23.plan, s16[128,512]{1,0:T(8,128)(2,1)S(1)} %encode.1.refs_0_, s16[128,512]{1,0:T(8,128)(2,1)S(1)} %collective-permute-done.refs_1_, ...), custom_call_target="tpu_custom_call" | custom-call | flops 1000000 | bytes 100000 | tf_op jit(solution)/shard_map/step/pallas_call | solution.py:348
  13.4 1.5 %collective-permute-done.4.second = s16[128,512]{1,0:T(8,128)(2,1)S(1)} collective-permute-done((s16[128,512]{1,0:T(8,128)(2,1)S(1)}, s16[128,512]{1,0:T(8,128)(2,1)S(1)}, u32[]{:S(2)}, u32[]{:S(2)}) %collective-permute-start.4) | collective-permute-done | bytes 131104 | tf_op jit(solution)/shard_map/ppermute | solution.py:395
  14.9 0.1 collective-permute-start.5
  15.0 1.2 %other_tables.1 = (bf16[2,128,1152]{2,1,0:T(8,128)(2,1)S(1)}, bf16[2,256,1152]{2,1,0:T(8,128)(2,1)S(1)}) custom-call(s32[5]{0:T(128)S(1)} %stack.20.meta, f32[9]{0:T(128)S(1)} %copy-done.3), custom_call_target="tpu_custom_call" | custom-call | flops 10000000 | bytes 3000000 | tf_op jit(solution)/shard_map/other_tables/pallas_call | solution.py:381
  16.2 0.3 %collective-permute-done.5.refs_1_ = s16[2,128,512]{2,1,0:T(8,128)(2,1)S(1)} collective-permute-done((s16[2,128,512]{2,1,0:T(8,128)(2,1)S(1)}, s16[2,128,512]{2,1,0:T(8,128)(2,1)S(1)}, u32[]{:S(2)}, u32[]{:S(2)}) %collective-permute-start.5) | collective-permute-done | bytes 262176 | tf_op jit(solution)/shard_map/ppermute | solution.py:398
  16.5 2.4 %step.6 = (s16[128,512]{1,0:T(8,128)(2,1)S(1)}, bf16[2,1152,512]{2,1,0:T(8,128)(2,1)S(1)}, bf16[2,1152,512]{2,1,0:T(8,128)(2,1)S(1)}) custom-call(s32[5,8]{1,0:T(8,128)S(1)} %get-tuple-element.23.plan, s16[2,128,512]{2,1,0:T(8,128)(2,1)S(1)} %join.2.refs_0_, s16[2,128,512]{2,1,0:T(8,128)(2,1)S(1)} %collective-permute-done.5.refs_1_, ...), custom_call_target="tpu_custom_call" | custom-call | flops 1000000 | bytes 100000 | tf_op jit(solution)/shard_map/step/pallas_call | solution.py:348
  19.0 1.1 %collective-permute-start.7 = (s16[128,512]{1,0:T(8,128)(2,1)S(1)}, s16[128,512]{1,0:T(8,128)(2,1)S(1)}, u32[]{:S(2)}, u32[]{:S(2)}) collective-permute-start(s16[128,512]{1,0:T(8,128)(2,1)S(1)} %get-tuple-element.35.refs_0_), channel_id=1, source_target_pairs={{0,2},{2,0},{1,3},{3,1},{4,6},{6,4},{5,7},{7,5},{8,10},{10,8},{9,1... | collective-permute-start | bytes 393224 | tf_op jit(solution)/shard_map/ppermute | solution.py:410
  20.1 2.3 %other_rows.1.first = s16[144,512]{1,0:T(8,128)(2,1)S(1)} custom-call(s32[5,8]{1,0:T(8,128)S(1)} %get-tuple-element.23.plan, bf16[2,128,1152]{2,1,0:T(8,128)(2,1)S(1)} %get-tuple-element.24.refs_0_, bf16[2,256,1152]{2,1,0:T(8,128)(2,1)S(1)} %get-tuple-element.25.refs_1_, bf16[2,1152,512]{2,1,0:T(8,128)(2,1)S(1)} %get-tuple-element.29.refs_2_, ...), custom_call_target="tpu_custom_call" | custom-call | flops 1000000 | bytes 100000 | tf_op jit(solution)/shard_map/other_rows/pallas_call | solution.py:402
  22.4 1.0 %collective-permute-start.6 = (s16[144,512]{1,0:T(8,128)(2,1)S(1)}, s16[144,512]{1,0:T(8,128)(2,1)S(1)}, u32[]{:S(2)}, u32[]{:S(2)}) collective-permute-start(s16[144,512]{1,0:T(8,128)(2,1)S(1)} %other_rows.1.first), channel_id=1, source_target_pairs={{0,2},{2,0},{1,3},{3,1},{4,6},{6,4},{5,7},{7,5},{8,10},{10,8},{9,1... | collective-permute-start | bytes 442376 | tf_op jit(solution)/shard_map/ppermute | solution.py:414
  23.4 0.0 collective-permute-start.8
  23.4 1.2 %collective-permute-done.7.refs_1_ = s16[128,512]{1,0:T(8,128)(2,1)S(1)} collective-permute-done((s16[128,512]{1,0:T(8,128)(2,1)S(1)}, s16[128,512]{1,0:T(8,128)(2,1)S(1)}, u32[]{:S(2)}, u32[]{:S(2)}) %collective-permute-start.7) | collective-permute-done | bytes 131104 | tf_op jit(solution)/shard_map/ppermute | solution.py:410
  24.6 0.2 collective-permute-done.8.refs_2_
  24.8 1.2 %collective-permute-done.9.refs_3_ = s16[128,512]{1,0:T(8,128)(2,1)S(1)} collective-permute-done((s16[128,512]{1,0:T(8,128)(2,1)S(1)}, s16[128,512]{1,0:T(8,128)(2,1)S(1)}, u32[]{:S(2)}, u32[]{:S(2)}) %collective-permute-start.9) | collective-permute-done | bytes 131104 | tf_op jit(solution)/shard_map/ppermute | solution.py:379
  25.9 1.9 %step.7.after.refs_4_ = f32[2,128,256]{2,1,0:T(8,128)S(1)} custom-call(s32[5,8]{1,0:T(8,128)S(1)} %get-tuple-element.23.plan, s16[128,512]{1,0:T(8,128)(2,1)S(1)} %get-tuple-element.35.refs_0_, s16[128,512]{1,0:T(8,128)(2,1)S(1)} %collective-permute-done.7.refs_1_, s16[128,512]{1,0:T(8,128)(2,1)S(1)} %collective-permute-done.8.refs_2_, ...), custom_call_target="tpu_custom_call" | custom-call | flops 1000000 | bytes 100000 | tf_op jit(solution)/shard_map/step/pallas_call | solution.py:348
  27.8 0.3 collective-permute-done.6.second
  28.1 0.1 collective-permute-start.10
  28.2 1.9 %step.8.refs_5_ = f32[2,128,256]{2,1,0:T(8,128)S(1)} custom-call(s32[5,8]{1,0:T(8,128)S(1)} %get-tuple-element.23.plan, s16[128,512]{1,0:T(8,128)(2,1)S(1)} %get-tuple-element.35.refs_0_, s16[128,512]{1,0:T(8,128)(2,1)S(1)} %collective-permute-done.7.refs_1_, s16[128,512]{1,0:T(8,128)(2,1)S(1)} %collective-permute-done.8.refs_2_, ...), custom_call_target="tpu_custom_call" | custom-call | flops 1000000 | bytes 100000 | tf_op jit(solution)/shard_map/step/pallas_call | solution.py:348
  30.1 2.8 %step.9 = (f32[128,512]{1,0:T(8,128)}, f32[128,512]{1,0:T(8,128)}) custom-call(s32[5,8]{1,0:T(8,128)S(1)} %get-tuple-element.23.plan, s16[2,128,512]{2,1,0:T(8,128)(2,1)S(1)} %join.3.refs_0_, s16[2,128,512]{2,1,0:T(8,128)(2,1)S(1)} %collective-permute-done.10.refs_1_, bf16[4,256,1152]{2,1,0:T(8,128)(2,1)S(1)} %get-tuple-element.27.refs_4_.refs_2_, ...), custom_call_target="tpu_custom_call" | custom-call | flops 1000000 | bytes 100000 | tf_op jit(solution)/shard_map/step/pallas_call | solution.py:348
  (15 shorter events, 0.1 us)
Async XLA Ops:
  0.6 5.9 %copy-start.3 = (f32[9]{0:T(128)S(1)}, f32[9]{0:T(128)}, u32[]{:S(2)}) copy-start(f32[9]{0:T(128)} %phonon.3) | copy-start | bytes 112
  0.6 5.9 %copy-start.2 = (s32[16]{0:T(128)S(1)}, s32[16]{0:T(128)}, u32[]{:S(2)}) copy-start(s32[16]{0:T(128)} %block_order.1) | copy-start | bytes 196
  0.7 5.9 %copy-start.1 = (s32[4]{0:T(128)S(1)}, s32[4]{0:T(128)}, u32[]{:S(2)}) copy-start(s32[4]{0:T(128)} %pair_count.1) | copy-start | bytes 52
  0.7 1.0 %copy-start.4 = (f32[128,512]{1,0:T(8,128)S(1)}, f32[128,512]{1,0:T(8,128)}, u32[]{:S(2)}) copy-start(f32[128,512]{1,0:T(8,128)} %gap.1) | copy-start | bytes 786436
  1.6 4.7 %copy-start.5 = (s32[4,2]{0,1:T(2,128)S(1)}, s32[4,2]{0,1:T(2,128)}, u32[]{:S(2)}) copy-start(s32[4,2]{0,1:T(2,128)} %param.8) | copy-start | bytes 100
  1.6 4.9 %copy-start = (bf16[4,2,9,128,128]{4,3,2,1,0:T(8,128)(2,1)S(1)}, bf16[4,2,9,128,128]{4,3,2,1,0:T(8,128)(2,1)}, u32[]{:S(2)}) copy-start(bf16[4,2,9,128,128]{4,3,2,1,0:T(8,128)(2,1)} %coupling.1) | copy-start | bytes 7077892
  1.8 7.0 %collective-permute-start = (s16[128,512]{1,0:T(8,128)(2,1)S(1)}, s16[128,512]{1,0:T(8,128)(2,1)S(1)}, u32[]{:S(2)}, u32[]{:S(2)}) collective-permute-start(s16[128,512]{1,0:T(8,128)(2,1)S(1)} %encode.1.refs_0_), channel_id=1, source_target_pairs={{0,2},{2,0},{1,3},{3,1},{4,6},{6,4},{5,7},{7,5},{8,10},{10,8},{9,1... | collective-permute-start | bytes 393224 | tf_op jit(solution)/shard_map/ppermute | solution.py:392
  4.8 5.0 %collective-permute-start.3 = (s16[128,512]{1,0:T(8,128)(2,1)S(1)}, s16[128,512]{1,0:T(8,128)(2,1)S(1)}, u32[]{:S(2)}, u32[]{:S(2)}) collective-permute-start(s16[128,512]{1,0:T(8,128)(2,1)S(1)} %encode.1.refs_0_), channel_id=1, source_target_pairs={{0,4},{4,0},{1,5},{5,1},{2,6},{6,2},{3,7},{7,3},{8,12},{12,8},{9,1... | collective-permute-start | bytes 393224 | tf_op jit(solution)/shard_map/ppermute | solution.py:393
  6.4 3.8 %collective-permute-start.1 = (s16[128,512]{1,0:T(8,128)(2,1)S(1)}, s16[128,512]{1,0:T(8,128)(2,1)S(1)}, u32[]{:S(2)}, u32[]{:S(2)}) collective-permute-start(s16[128,512]{1,0:T(8,128)(2,1)S(1)} %encode.1.refs_0_), channel_id=1, source_target_pairs={{0,1},{1,0},{2,3},{3,2},{4,5},{5,4},{6,7},{7,6},{8,9},{9,8},{10,11... | collective-permute-start | bytes 393224 | tf_op jit(solution)/shard_map/ppermute | solution.py:379
  8.8 1.6 %collective-permute-start.2 = (s16[128,512]{1,0:T(8,128)(2,1)S(1)}, s16[128,512]{1,0:T(8,128)(2,1)S(1)}, u32[]{:S(2)}, u32[]{:S(2)}) collective-permute-start(s16[128,512]{1,0:T(8,128)(2,1)S(1)} %collective-permute-done.refs_1_), channel_id=1, source_target_pairs={{0,1},{1,0},{2,3},{3,2},{4,5},{5,4},{6,7},{7,6},{8,9},{9,8},{10,11... | collective-permute-start | bytes 393224 | tf_op jit(solution)/shard_map/ppermute | solution.py:379
  9.8 5.1 %collective-permute-start.4 = (s16[128,512]{1,0:T(8,128)(2,1)S(1)}, s16[128,512]{1,0:T(8,128)(2,1)S(1)}, u32[]{:S(2)}, u32[]{:S(2)}) collective-permute-start(s16[128,512]{1,0:T(8,128)(2,1)S(1)} %collective-permute-done.3.first), channel_id=1, source_target_pairs={{0,2},{2,0},{1,3},{3,1},{4,6},{6,4},{5,7},{7,5},{8,10},{10,8},{9,1... | collective-permute-start | bytes 393224 | tf_op jit(solution)/shard_map/ppermute | solution.py:395
  14.9 1.6 %collective-permute-start.5 = (s16[2,128,512]{2,1,0:T(8,128)(2,1)S(1)}, s16[2,128,512]{2,1,0:T(8,128)(2,1)S(1)}, u32[]{:S(2)}, u32[]{:S(2)}) collective-permute-start(s16[2,128,512]{2,1,0:T(8,128)(2,1)S(1)} %join.2.refs_0_), channel_id=1, source_target_pairs={{0,1},{1,0},{2,3},{3,2},{4,5},{5,4},{6,7},{7,6},{8,9},{9,8},{10,11... | collective-permute-start | bytes 786440 | tf_op jit(solution)/shard_map/ppermute | solution.py:398
  19.0 5.6 %collective-permute-start.7 = (s16[128,512]{1,0:T(8,128)(2,1)S(1)}, s16[128,512]{1,0:T(8,128)(2,1)S(1)}, u32[]{:S(2)}, u32[]{:S(2)}) collective-permute-start(s16[128,512]{1,0:T(8,128)(2,1)S(1)} %get-tuple-element.35.refs_0_), channel_id=1, source_target_pairs={{0,2},{2,0},{1,3},{3,1},{4,6},{6,4},{5,7},{7,5},{8,10},{10,8},{9,1... | collective-permute-start | bytes 393224 | tf_op jit(solution)/shard_map/ppermute | solution.py:410
  22.4 5.7 %collective-permute-start.6 = (s16[144,512]{1,0:T(8,128)(2,1)S(1)}, s16[144,512]{1,0:T(8,128)(2,1)S(1)}, u32[]{:S(2)}, u32[]{:S(2)}) collective-permute-start(s16[144,512]{1,0:T(8,128)(2,1)S(1)} %other_rows.1.first), channel_id=1, source_target_pairs={{0,2},{2,0},{1,3},{3,1},{4,6},{6,4},{5,7},{7,5},{8,10},{10,8},{9,1... | collective-permute-start | bytes 442376 | tf_op jit(solution)/shard_map/ppermute | solution.py:414
  23.4 1.3 %collective-permute-start.8 = (s16[128,512]{1,0:T(8,128)(2,1)S(1)}, s16[128,512]{1,0:T(8,128)(2,1)S(1)}, u32[]{:S(2)}, u32[]{:S(2)}) collective-permute-start(s16[128,512]{1,0:T(8,128)(2,1)S(1)} %get-tuple-element.35.refs_0_), channel_id=1, source_target_pairs={{0,1},{1,0},{2,3},{3,2},{4,5},{5,4},{6,7},{7,6},{8,9},{9,8},{10,11... | collective-permute-start | bytes 393224 | tf_op jit(solution)/shard_map/ppermute | solution.py:379
  24.6 1.3 %collective-permute-start.9 = (s16[128,512]{1,0:T(8,128)(2,1)S(1)}, s16[128,512]{1,0:T(8,128)(2,1)S(1)}, u32[]{:S(2)}, u32[]{:S(2)}) collective-permute-start(s16[128,512]{1,0:T(8,128)(2,1)S(1)} %collective-permute-done.7.refs_1_), channel_id=1, source_target_pairs={{0,1},{1,0},{2,3},{3,2},{4,5},{5,4},{6,7},{7,6},{8,9},{9,8},{10,11... | collective-permute-start | bytes 393224 | tf_op jit(solution)/shard_map/ppermute | solution.py:379
  28.1 1.9 %collective-permute-start.10 = (s16[2,128,512]{2,1,0:T(8,128)(2,1)S(1)}, s16[2,128,512]{2,1,0:T(8,128)(2,1)S(1)}, u32[]{:S(2)}, u32[]{:S(2)}) collective-permute-start(s16[2,128,512]{2,1,0:T(8,128)(2,1)S(1)} %join.3.refs_0_), channel_id=1, source_target_pairs={{0,1},{1,0},{2,3},{3,2},{4,5},{5,4},{6,7},{7,6},{8,9},{9,8},{10,11... | collective-permute-start | bytes 786440 | tf_op jit(solution)/shard_map/ppermute | solution.py:416

commit v11 on v10

--- a/solution.py
+++ b/solution.py
@@ -106,6 +106,14 @@
                 ] = coupling[block, slot, mode].T
 
 
+def repeat(count, body):
+    lax.fori_loop(0, count, lambda at, none: body(at), None)
+
+
+def lanes_of(start, width):
+    return pl.ds(pl.multiple_of(start, LANES), width)
+
+
 def step_kernel(dims, segment, span, sides, coded, final, keep, parted, plan, *refs):
     freq_count, segments, segment_rows, padded_rows, modes = dims
     refs = list(refs)
@@ -114,6 +122,7 @@
     copied = last and final
     if copied:
         *held, sems = take(3)
+    sums = refs.pop()
     terms = [] if keep else take(2 if first else 1)
     ratios = refs.pop()
     terms = terms or take(2)
@@ -155,7 +164,7 @@
             ratios[block, segment_rows:, lanes] = (col_omega * inverse).astype(jnp.bfloat16)
 
     def find_terms(block):
-        lanes = slice(block * size, (block + 1) * size)
+        lanes = lanes_of(block * size, size)
         for start in range(0, modes, 2):
             stop = min(start + 2, modes)
             found = jnp.dot(
@@ -178,11 +187,12 @@
         return before[lanes.start // width][part, :, start : start + lanes.stop - lanes.start]
 
     def find_sums(lanes):
-        sums = []
-        for part in range(2):
+        def find(part):
             views = [held_terms.at[part, :, lanes] for held_terms in terms]
             total = table_sums(padded_rows, table.at[part], *views)
-            sums.append(total if first else total + earlier(part, lanes))
+            sums[part] = total if first else total + earlier(part, lanes)
+
+        repeat(2, find)
         if not last:
             for part in range(2):
                 outs[0][part, :, lanes] = sums[part]
@@ -209,13 +219,14 @@
         )
 
     halves = [slice(start * size, (start + 2) * size) for start in range(0, blocks, 2)]
-    for block in range(blocks):
+
+    def find_block(block):
         find_ratios(block)
-    for block in range(blocks):
         find_terms(block)
-        if block % 2 == 1 and block > 1:
-            find_sums(halves[block // 2 - 1])
-    find_sums(halves[-1])
+
+    repeat(blocks, find_block)
+    for lanes in halves:
+        find_sums(lanes)
     if copied:
         for lanes in halves:
             for at in range(2):
@@ -232,15 +243,17 @@
 
 def other_rows_kernel(dims, plan, *refs):
     freq_count, segments, segment_rows, padded_rows, modes = dims
-    tables, terms, code = refs[:segments], refs[segments:-1], refs[-1]
-    sums = []
-    for part in range(2):
+    tables, terms, code, sums = refs[:segments], refs[segments:-2], refs[-2], refs[-1]
+
+    def find(part):
         total = None
         for segment in range(segments):
             views = [terms[2 * segment + at].at[part] for at in range(2)]
             piece = table_sums(padded_rows, tables[segment].at[part], *views)
             total = piece if total is None else total + piece
-        sums.append(total)
+        sums[part] = total
+
+    repeat(2, find)
     row = lax.broadcasted_iota(jnp.int32, (padded_rows, code.shape[1]), 0) + plan[ROWS, 2]
     temperature = CUTOFF / freq_count
     renorm = 1.0 + temperature * sums[1] / omega_of(row, freq_count)
@@ -341,6 +354,7 @@
             out_specs += [vmem] * 2
         else:
             scratch += [pltpu.VMEM(terms_shape, jnp.bfloat16)] * (2 if segment == 0 else 1)
+        scratch += [pltpu.VMEM((2, padded_rows, 2 * size), jnp.float32)]
         if copied:
             scratch += [pltpu.VMEM(gap_in.shape, jnp.float32)] * 2
             scratch += [pltpu.SemaphoreType.DMA((2, blocks // 2))]
@@ -404,6 +418,7 @@
         out_shape=jax.ShapeDtypeStruct((own_rows + SPARE_ROWS, row_width), link_type),
         in_specs=[smem] + [vmem] * len(inputs),
         out_specs=vmem,
+        scratch_shapes=[pltpu.VMEM((2, padded_rows, row_width), jnp.float32)],
         name="other_rows",
         **step_params,
     )(plan, *inputs)

time: 33 us -> 36.4 us (1.10)
  Pallas kernels: 17.7 us -> 22.6 us
  waiting for transfers between devices: 5.32 us -> 3.72 us
    pallas_call x5, Pallas kernels: 11.9 us -> 16.5 us  [step(): pl.pallas_call(functools.partial(step_kernel, dims, segment, span, sides,...]
    ppermute x1, waiting for transfers between devices: 1.52 us -> 0.43 us  [on_device(): relayed = lax.ppermute(along_z, 'x', SWAP)]
  transfers between devices with their start and end apart: 11 -> 11, of which waited for: 8 -> 7; matrix products, arithmetic and copies ran while one was open for 1% -> 0% of each run, Pallas kernels for 38% -> 40%
where the time goes in v11:
time: 36.4 us; the launch traced here: 36.2 us
  Pallas kernels  22.6 us (62%)
  starting transfers between devices  7.96 us (22%)
  waiting for transfers between devices  3.72 us (10%)
  local copies, waits for them, and re-layouts  1.16 us (3%)
  between operations  0.78 us (2%)
    pallas_call x5, Pallas kernels, step(): pl.pallas_call(functools.partial(step_kernel, dims, segment, span, sides,...  16.5 us
    ppermute x1, starting transfers between devices, on_device(): along_x = lax.ppermute(passed, 'x', SWAP)  3 us
    pallas_call x1, Pallas kernels, on_device(): pl.pallas_call(functools.partial(other_rows_kernel, dims), out_shape=jax....  2.49 us
    pallas_call x1, Pallas kernels, on_device(): pl.pallas_call(functools.partial(tables_kernel, dims, sides), out_shape=[...  2.25 us
    ppermute x4, waiting for transfers between devices, with_core(): return near + [lax.ppermute(piece, 'core', SWAP) for piece in near]  1.62 us
    ppermute x1, starting transfers between devices, on_device(): along_z = lax.ppermute(passed, 'zlo', SWAP)  1.58 us
    pallas_call x1, Pallas kernels, on_device(): pl.pallas_call(functools.partial(other_tables_kernel, dims), out_shape=[f...  1.17 us
    ppermute x1, starting transfers between devices, on_device(): along_x = lax.ppermute(own, 'x', SWAP)  1.13 us
  transfers between devices with their start and end apart: 11, of which 7 were waited for; matrix products, arithmetic and copies ran while one was open for 0% of the time, Pallas kernels for 40%

profile of v11, /device:TPU:0, one launch (start us, length us, event | category | flops | bytes accessed | tf_op | source)
XLA Modules:
  0.0 36.2 jit_solution(10446578065842096221)
XLA Ops:
  0.7 1.0 %copy-done.4 = f32[128,512]{1,0:T(8,128)S(1)} copy-done((f32[128,512]{1,0:T(8,128)S(1)}, f32[128,512]{1,0:T(8,128)}, u32[]{:S(2)}) %copy-start.4) | copy-done | bytes 262168
  1.6 0.1 encode.1.refs_0_
  1.8 3.0 %collective-permute-start = (s16[128,512]{1,0:T(8,128)(2,1)S(1)}, s16[128,512]{1,0:T(8,128)(2,1)S(1)}, u32[]{:S(2)}, u32[]{:S(2)}) collective-permute-start(s16[128,512]{1,0:T(8,128)(2,1)S(1)} %encode.1.refs_0_), channel_id=1, source_target_pairs={{0,2},{2,0},{1,3},{3,1},{4,6},{6,4},{5,7},{7,5},{8,10},{10,8},{9,1... | collective-permute-start | bytes 393224 | tf_op jit(solution)/shard_map/ppermute | solution.py:406
  4.8 1.6 %collective-permute-start.3 = (s16[128,512]{1,0:T(8,128)(2,1)S(1)}, s16[128,512]{1,0:T(8,128)(2,1)S(1)}, u32[]{:S(2)}, u32[]{:S(2)}) collective-permute-start(s16[128,512]{1,0:T(8,128)(2,1)S(1)} %encode.1.refs_0_), channel_id=1, source_target_pairs={{0,4},{4,0},{1,5},{5,1},{2,6},{6,2},{3,7},{7,3},{8,12},{12,8},{9,1... | collective-permute-start | bytes 393224 | tf_op jit(solution)/shard_map/ppermute | solution.py:407
  6.4 0.0 collective-permute-start.1
  6.4 0.1 copy.8.pair_cols
  6.5 0.1 stack.20.meta
  6.6 2.2 %tables.1 = (s32[5,8]{1,0:T(8,128)S(1)}, bf16[4,256,1152]{2,1,0:T(8,128)(2,1)S(1)}, bf16[2,256,1152]{2,1,0:T(8,128)(2,1)S(1)}, bf16[2,128,1152]{2,1,0:T(8,128)(2,1)S(1)}) custom-call(s32[5]{0:T(128)S(1)} %stack.20.meta, f32[9]{0:T(128)S(1)} %copy-done.3, s32[4,2]{1,0:T(4,128)S(1)} %copy.8.pair_cols, s32[4]{0:T(128)S(1)} %copy-done.1, s32[16]{0:T(128)S(1)} %copy-done.2, ...), custom_call_target="tpu_custom_call" | custom-call | flops 10000000 | bytes 8000000 | tf_op jit(solution)/shard_map/tables/pallas_call | solution.py:317
  8.8 0.6 %collective-permute-start.2 = (s16[128,512]{1,0:T(8,128)(2,1)S(1)}, s16[128,512]{1,0:T(8,128)(2,1)S(1)}, u32[]{:S(2)}, u32[]{:S(2)}) collective-permute-start(s16[128,512]{1,0:T(8,128)(2,1)S(1)} %collective-permute-done.refs_1_), channel_id=1, source_target_pairs={{0,1},{1,0},{2,3},{3,2},{4,5},{5,4},{6,7},{7,6},{8,9},{9,8},{10,11... | collective-permute-start | bytes 393224 | tf_op jit(solution)/shard_map/ppermute | solution.py:393
  9.4 0.4 collective-permute-done.3.first
  9.8 0.4 collective-permute-start.4
  10.1 0.0 collective-permute-done.1.refs_2_
  10.1 0.3 collective-permute-done.2.refs_3_
  10.4 4.1 %step.5 = (f32[2,128,512]{2,1,0:T(8,128)S(1)}, bf16[2,1152,512]{2,1,0:T(8,128)(2,1)S(1)}, bf16[2,1152,512]{2,1,0:T(8,128)(2,1)S(1)}) custom-call(s32[5,8]{1,0:T(8,128)S(1)} %get-tuple-element.23.plan, s16[128,512]{1,0:T(8,128)(2,1)S(1)} %encode.1.refs_0_, s16[128,512]{1,0:T(8,128)(2,1)S(1)} %collective-permute-done.refs_1_, ...), custom_call_target="tpu_custom_call" | custom-call | flops 1000000 | bytes 100000 | tf_op jit(solution)/shard_map/step/pallas_call | solution.py:362
  14.5 0.4 %collective-permute-done.4.second = s16[128,512]{1,0:T(8,128)(2,1)S(1)} collective-permute-done((s16[128,512]{1,0:T(8,128)(2,1)S(1)}, s16[128,512]{1,0:T(8,128)(2,1)S(1)}, u32[]{:S(2)}, u32[]{:S(2)}) %collective-permute-start.4) | collective-permute-done | bytes 131104 | tf_op jit(solution)/shard_map/ppermute | solution.py:409
  14.9 0.1 collective-permute-start.5
  15.0 1.2 %other_tables.1 = (bf16[2,128,1152]{2,1,0:T(8,128)(2,1)S(1)}, bf16[2,256,1152]{2,1,0:T(8,128)(2,1)S(1)}) custom-call(s32[5]{0:T(128)S(1)} %stack.20.meta, f32[9]{0:T(128)S(1)} %copy-done.3), custom_call_target="tpu_custom_call" | custom-call | flops 10000000 | bytes 3000000 | tf_op jit(solution)/shard_map/other_tables/pallas_call | solution.py:395
  16.2 0.3 collective-permute-done.5.refs_1_
  16.5 3.6 %step.6 = (s16[128,512]{1,0:T(8,128)(2,1)S(1)}, bf16[2,1152,512]{2,1,0:T(8,128)(2,1)S(1)}, bf16[2,1152,512]{2,1,0:T(8,128)(2,1)S(1)}) custom-call(s32[5,8]{1,0:T(8,128)S(1)} %get-tuple-element.23.plan, s16[2,128,512]{2,1,0:T(8,128)(2,1)S(1)} %join.2.refs_0_, s16[2,128,512]{2,1,0:T(8,128)(2,1)S(1)} %collective-permute-done.5.refs_1_, ...), custom_call_target="tpu_custom_call" | custom-call | flops 1000000 | bytes 100000 | tf_op jit(solution)/shard_map/step/pallas_call | solution.py:362
  20.1 1.1 %collective-permute-start.7 = (s16[128,512]{1,0:T(8,128)(2,1)S(1)}, s16[128,512]{1,0:T(8,128)(2,1)S(1)}, u32[]{:S(2)}, u32[]{:S(2)}) collective-permute-start(s16[128,512]{1,0:T(8,128)(2,1)S(1)} %get-tuple-element.35.refs_0_), channel_id=1, source_target_pairs={{0,2},{2,0},{1,3},{3,1},{4,6},{6,4},{5,7},{7,5},{8,10},{10,8},{9,1... | collective-permute-start | bytes 393224 | tf_op jit(solution)/shard_map/ppermute | solution.py:425
  21.3 2.5 %other_rows.1.first = s16[144,512]{1,0:T(8,128)(2,1)S(1)} custom-call(s32[5,8]{1,0:T(8,128)S(1)} %get-tuple-element.23.plan, bf16[2,128,1152]{2,1,0:T(8,128)(2,1)S(1)} %get-tuple-element.24.refs_0_, bf16[2,256,1152]{2,1,0:T(8,128)(2,1)S(1)} %get-tuple-element.25.refs_1_, bf16[2,1152,512]{2,1,0:T(8,128)(2,1)S(1)} %get-tuple-element.29.refs_2_, ...), custom_call_target="tpu_custom_call" | custom-call | flops 1000000 | bytes 100000 | tf_op jit(solution)/shard_map/other_rows/pallas_call | solution.py:416
  23.8 1.0 %collective-permute-start.6 = (s16[144,512]{1,0:T(8,128)(2,1)S(1)}, s16[144,512]{1,0:T(8,128)(2,1)S(1)}, u32[]{:S(2)}, u32[]{:S(2)}) collective-permute-start(s16[144,512]{1,0:T(8,128)(2,1)S(1)} %other_rows.1.first), channel_id=1, source_target_pairs={{0,2},{2,0},{1,3},{3,1},{4,6},{6,4},{5,7},{7,5},{8,10},{10,8},{9,1... | collective-permute-start | bytes 442376 | tf_op jit(solution)/shard_map/ppermute | solution.py:429
  24.8 0.0 collective-permute-start.8
  24.8 1.0 %collective-permute-done.7.refs_1_ = s16[128,512]{1,0:T(8,128)(2,1)S(1)} collective-permute-done((s16[128,512]{1,0:T(8,128)(2,1)S(1)}, s16[128,512]{1,0:T(8,128)(2,1)S(1)}, u32[]{:S(2)}, u32[]{:S(2)}) %collective-permute-start.7) | collective-permute-done | bytes 131104 | tf_op jit(solution)/shard_map/ppermute | solution.py:425
  25.8 0.0 collective-permute-start.9
  25.8 0.4 %collective-permute-done.8.refs_2_ = s16[128,512]{1,0:T(8,128)(2,1)S(1)} collective-permute-done((s16[128,512]{1,0:T(8,128)(2,1)S(1)}, s16[128,512]{1,0:T(8,128)(2,1)S(1)}, u32[]{:S(2)}, u32[]{:S(2)}) %collective-permute-start.8) | collective-permute-done | bytes 131104 | tf_op jit(solution)/shard_map/ppermute | solution.py:393
  26.1 1.0 %collective-permute-done.9.refs_3_ = s16[128,512]{1,0:T(8,128)(2,1)S(1)} collective-permute-done((s16[128,512]{1,0:T(8,128)(2,1)S(1)}, s16[128,512]{1,0:T(8,128)(2,1)S(1)}, u32[]{:S(2)}, u32[]{:S(2)}) %collective-permute-start.9) | collective-permute-done | bytes 131104 | tf_op jit(solution)/shard_map/ppermute | solution.py:393
  27.1 2.4 %step.7.after.refs_4_ = f32[2,128,256]{2,1,0:T(8,128)S(1)} custom-call(s32[5,8]{1,0:T(8,128)S(1)} %get-tuple-element.23.plan, s16[128,512]{1,0:T(8,128)(2,1)S(1)} %get-tuple-element.35.refs_0_, s16[128,512]{1,0:T(8,128)(2,1)S(1)} %collective-permute-done.7.refs_1_, s16[128,512]{1,0:T(8,128)(2,1)S(1)} %collective-permute-done.8.refs_2_, ...), custom_call_target="tpu_custom_call" | custom-call | flops 1000000 | bytes 100000 | tf_op jit(solution)/shard_map/step/pallas_call | solution.py:362
  29.5 0.2 collective-permute-start.10
  29.7 2.3 %step.8.refs_5_ = f32[2,128,256]{2,1,0:T(8,128)S(1)} custom-call(s32[5,8]{1,0:T(8,128)S(1)} %get-tuple-element.23.plan, s16[128,512]{1,0:T(8,128)(2,1)S(1)} %get-tuple-element.35.refs_0_, s16[128,512]{1,0:T(8,128)(2,1)S(1)} %collective-permute-done.7.refs_1_, s16[128,512]{1,0:T(8,128)(2,1)S(1)} %collective-permute-done.8.refs_2_, ...), custom_call_target="tpu_custom_call" | custom-call | flops 1000000 | bytes 100000 | tf_op jit(solution)/shard_map/step/pallas_call | solution.py:362
  32.1 0.0 collective-permute-done.10.refs_1_
  32.1 4.2 %step.9 = (f32[128,512]{1,0:T(8,128)}, f32[128,512]{1,0:T(8,128)}) custom-call(s32[5,8]{1,0:T(8,128)S(1)} %get-tuple-element.23.plan, s16[2,128,512]{2,1,0:T(8,128)(2,1)S(1)} %join.3.refs_0_, s16[2,128,512]{2,1,0:T(8,128)(2,1)S(1)} %collective-permute-done.10.refs_1_, bf16[4,256,1152]{2,1,0:T(8,128)(2,1)S(1)} %get-tuple-element.27.refs_4_.refs_2_, ...), custom_call_target="tpu_custom_call" | custom-call | flops 1000000 | bytes 100000 | tf_op jit(solution)/shard_map/step/pallas_call | solution.py:362
  (15 shorter events, 0.1 us)
Async XLA Ops:
  0.6 5.9 %copy-start.3 = (f32[9]{0:T(128)S(1)}, f32[9]{0:T(128)}, u32[]{:S(2)}) copy-start(f32[9]{0:T(128)} %phonon.3) | copy-start | bytes 112
  0.6 5.9 %copy-start.2 = (s32[16]{0:T(128)S(1)}, s32[16]{0:T(128)}, u32[]{:S(2)}) copy-start(s32[16]{0:T(128)} %block_order.1) | copy-start | bytes 196
  0.7 5.9 %copy-start.1 = (s32[4]{0:T(128)S(1)}, s32[4]{0:T(128)}, u32[]{:S(2)}) copy-start(s32[4]{0:T(128)} %pair_count.1) | copy-start | bytes 52
  0.7 1.0 %copy-start.4 = (f32[128,512]{1,0:T(8,128)S(1)}, f32[128,512]{1,0:T(8,128)}, u32[]{:S(2)}) copy-start(f32[128,512]{1,0:T(8,128)} %gap.1) | copy-start | bytes 786436
  1.6 4.7 %copy-start.5 = (s32[4,2]{0,1:T(2,128)S(1)}, s32[4,2]{0,1:T(2,128)}, u32[]{:S(2)}) copy-start(s32[4,2]{0,1:T(2,128)} %param.8) | copy-start | bytes 100
  1.6 4.9 %copy-start = (bf16[4,2,9,128,128]{4,3,2,1,0:T(8,128)(2,1)S(1)}, bf16[4,2,9,128,128]{4,3,2,1,0:T(8,128)(2,1)}, u32[]{:S(2)}) copy-start(bf16[4,2,9,128,128]{4,3,2,1,0:T(8,128)(2,1)} %coupling.1) | copy-start | bytes 7077892
  1.8 7.0 %collective-permute-start = (s16[128,512]{1,0:T(8,128)(2,1)S(1)}, s16[128,512]{1,0:T(8,128)(2,1)S(1)}, u32[]{:S(2)}, u32[]{:S(2)}) collective-permute-start(s16[128,512]{1,0:T(8,128)(2,1)S(1)} %encode.1.refs_0_), channel_id=1, source_target_pairs={{0,2},{2,0},{1,3},{3,1},{4,6},{6,4},{5,7},{7,5},{8,10},{10,8},{9,1... | collective-permute-start | bytes 393224 | tf_op jit(solution)/shard_map/ppermute | solution.py:406
  4.8 5.0 %collective-permute-start.3 = (s16[128,512]{1,0:T(8,128)(2,1)S(1)}, s16[128,512]{1,0:T(8,128)(2,1)S(1)}, u32[]{:S(2)}, u32[]{:S(2)}) collective-permute-start(s16[128,512]{1,0:T(8,128)(2,1)S(1)} %encode.1.refs_0_), channel_id=1, source_target_pairs={{0,4},{4,0},{1,5},{5,1},{2,6},{6,2},{3,7},{7,3},{8,12},{12,8},{9,1... | collective-permute-start | bytes 393224 | tf_op jit(solution)/shard_map/ppermute | solution.py:407
  6.4 3.8 %collective-permute-start.1 = (s16[128,512]{1,0:T(8,128)(2,1)S(1)}, s16[128,512]{1,0:T(8,128)(2,1)S(1)}, u32[]{:S(2)}, u32[]{:S(2)}) collective-permute-start(s16[128,512]{1,0:T(8,128)(2,1)S(1)} %encode.1.refs_0_), channel_id=1, source_target_pairs={{0,1},{1,0},{2,3},{3,2},{4,5},{5,4},{6,7},{7,6},{8,9},{9,8},{10,11... | collective-permute-start | bytes 393224 | tf_op jit(solution)/shard_map/ppermute | solution.py:393
  8.8 1.6 %collective-permute-start.2 = (s16[128,512]{1,0:T(8,128)(2,1)S(1)}, s16[128,512]{1,0:T(8,128)(2,1)S(1)}, u32[]{:S(2)}, u32[]{:S(2)}) collective-permute-start(s16[128,512]{1,0:T(8,128)(2,1)S(1)} %collective-permute-done.refs_1_), channel_id=1, source_target_pairs={{0,1},{1,0},{2,3},{3,2},{4,5},{5,4},{6,7},{7,6},{8,9},{9,8},{10,11... | collective-permute-start | bytes 393224 | tf_op jit(solution)/shard_map/ppermute | solution.py:393
  9.8 5.1 %collective-permute-start.4 = (s16[128,512]{1,0:T(8,128)(2,1)S(1)}, s16[128,512]{1,0:T(8,128)(2,1)S(1)}, u32[]{:S(2)}, u32[]{:S(2)}) collective-permute-start(s16[128,512]{1,0:T(8,128)(2,1)S(1)} %collective-permute-done.3.first), channel_id=1, source_target_pairs={{0,2},{2,0},{1,3},{3,1},{4,6},{6,4},{5,7},{7,5},{8,10},{10,8},{9,1... | collective-permute-start | bytes 393224 | tf_op jit(solution)/shard_map/ppermute | solution.py:409
  14.9 1.6 %collective-permute-start.5 = (s16[2,128,512]{2,1,0:T(8,128)(2,1)S(1)}, s16[2,128,512]{2,1,0:T(8,128)(2,1)S(1)}, u32[]{:S(2)}, u32[]{:S(2)}) collective-permute-start(s16[2,128,512]{2,1,0:T(8,128)(2,1)S(1)} %join.2.refs_0_), channel_id=1, source_target_pairs={{0,1},{1,0},{2,3},{3,2},{4,5},{5,4},{6,7},{7,6},{8,9},{9,8},{10,11... | collective-permute-start | bytes 786440 | tf_op jit(solution)/shard_map/ppermute | solution.py:412
  20.1 5.6 %collective-permute-start.7 = (s16[128,512]{1,0:T(8,128)(2,1)S(1)}, s16[128,512]{1,0:T(8,128)(2,1)S(1)}, u32[]{:S(2)}, u32[]{:S(2)}) collective-permute-start(s16[128,512]{1,0:T(8,128)(2,1)S(1)} %get-tuple-element.35.refs_0_), channel_id=1, source_target_pairs={{0,2},{2,0},{1,3},{3,1},{4,6},{6,4},{5,7},{7,5},{8,10},{10,8},{9,1... | collective-permute-start | bytes 393224 | tf_op jit(solution)/shard_map/ppermute | solution.py:425
  23.8 5.7 %collective-permute-start.6 = (s16[144,512]{1,0:T(8,128)(2,1)S(1)}, s16[144,512]{1,0:T(8,128)(2,1)S(1)}, u32[]{:S(2)}, u32[]{:S(2)}) collective-permute-start(s16[144,512]{1,0:T(8,128)(2,1)S(1)} %other_rows.1.first), channel_id=1, source_target_pairs={{0,2},{2,0},{1,3},{3,1},{4,6},{6,4},{5,7},{7,5},{8,10},{10,8},{9,1... | collective-permute-start | bytes 442376 | tf_op jit(solution)/shard_map/ppermute | solution.py:429
  24.8 1.3 %collective-permute-start.8 = (s16[128,512]{1,0:T(8,128)(2,1)S(1)}, s16[128,512]{1,0:T(8,128)(2,1)S(1)}, u32[]{:S(2)}, u32[]{:S(2)}) collective-permute-start(s16[128,512]{1,0:T(8,128)(2,1)S(1)} %get-tuple-element.35.refs_0_), channel_id=1, source_target_pairs={{0,1},{1,0},{2,3},{3,2},{4,5},{5,4},{6,7},{7,6},{8,9},{9,8},{10,11... | collective-permute-start | bytes 393224 | tf_op jit(solution)/shard_map/ppermute | solution.py:393
  25.8 1.3 %collective-permute-start.9 = (s16[128,512]{1,0:T(8,128)(2,1)S(1)}, s16[128,512]{1,0:T(8,128)(2,1)S(1)}, u32[]{:S(2)}, u32[]{:S(2)}) collective-permute-start(s16[128,512]{1,0:T(8,128)(2,1)S(1)} %collective-permute-done.7.refs_1_), channel_id=1, source_target_pairs={{0,1},{1,0},{2,3},{3,2},{4,5},{5,4},{6,7},{7,6},{8,9},{9,8},{10,11... | collective-permute-start | bytes 393224 | tf_op jit(solution)/shard_map/ppermute | solution.py:393
  29.5 2.6 %collective-permute-start.10 = (s16[2,128,512]{2,1,0:T(8,128)(2,1)S(1)}, s16[2,128,512]{2,1,0:T(8,128)(2,1)S(1)}, u32[]{:S(2)}, u32[]{:S(2)}) collective-permute-start(s16[2,128,512]{2,1,0:T(8,128)(2,1)S(1)} %join.3.refs_0_), channel_id=1, source_target_pairs={{0,1},{1,0},{2,3},{3,2},{4,5},{5,4},{6,7},{7,6},{8,9},{9,8},{10,11... | collective-permute-start | bytes 786440 | tf_op jit(solution)/shard_map/ppermute | solution.py:431

commit v12 on v10

--- a/solution.py
+++ b/solution.py
@@ -178,27 +178,29 @@
         return before[lanes.start // width][part, :, start : start + lanes.stop - lanes.start]
 
     def find_sums(lanes):
-        sums = []
-        for part in range(2):
+        def total_of(part):
             views = [held_terms.at[part, :, lanes] for held_terms in terms]
             total = table_sums(padded_rows, table.at[part], *views)
-            sums.append(total if first else total + earlier(part, lanes))
+            return total if first else total + earlier(part, lanes)
+
         if not last:
             for part in range(2):
-                outs[0][part, :, lanes] = sums[part]
+                outs[0][part, :, lanes] = total_of(part)
             return
         own_rows = outs[0].shape[0]
         width = lanes.stop - lanes.start
         row = lax.broadcasted_iota(jnp.int32, (own_rows, width), 0) + plan[ROWS, 0]
         temperature = CUTOFF / freq_count
-        renorm = 1.0 + temperature * sums[1][:own_rows] / omega_of(row, freq_count)
-        gap = temperature * sums[0][:own_rows] / renorm
-        if not final:
+        renorm = 1.0 + temperature * total_of(1)[:own_rows] / omega_of(row, freq_count)
+        if final:
+            held[1][:, lanes] = renorm
+            copy_out(1, lanes).start()
+        gap = temperature * total_of(0)[:own_rows] / renorm
+        if final:
+            held[0][:, lanes] = gap
+            copy_out(0, lanes).start()
+        else:
             outs[0][:, lanes] = encoded(gap) if coded else gap
-            return
-        for at, value in enumerate((gap, renorm)):
-            held[at][:, lanes] = value
-            copy_out(at, lanes).start()
 
     def copy_out(at, lanes):
         width = lanes.stop - lanes.start
@@ -209,11 +211,12 @@
         )
 
     halves = [slice(start * size, (start + 2) * size) for start in range(0, blocks, 2)]
+    find_ratios(0)
     for block in range(blocks):
-        find_ratios(block)
-    for block in range(blocks):
+        if block + 1 < blocks:
+            find_ratios(block + 1)
         find_terms(block)
-        if block % 2 == 1 and block > 1:
+        if block % 2 == 0 and block > 1:
             find_sums(halves[block // 2 - 1])
     find_sums(halves[-1])
     if copied:
@@ -233,19 +236,24 @@
 def other_rows_kernel(dims, plan, *refs):
     freq_count, segments, segment_rows, padded_rows, modes = dims
     tables, terms, code = refs[:segments], refs[segments:-1], refs[-1]
-    sums = []
-    for part in range(2):
-        total = None
-        for segment in range(segments):
-            views = [terms[2 * segment + at].at[part] for at in range(2)]
-            piece = table_sums(padded_rows, tables[segment].at[part], *views)
-            total = piece if total is None else total + piece
-        sums.append(total)
-    row = lax.broadcasted_iota(jnp.int32, (padded_rows, code.shape[1]), 0) + plan[ROWS, 2]
+    states = code.shape[1]
     temperature = CUTOFF / freq_count
-    renorm = 1.0 + temperature * sums[1] / omega_of(row, freq_count)
-    code[:padded_rows] = encoded(temperature * sums[0] / renorm)
-    code[padded_rows:] = jnp.zeros((SPARE_ROWS, code.shape[1]), code.dtype)
+    for start in range(0, states, 2 * LANES):
+        lanes = slice(start, min(start + 2 * LANES, states))
+
+        def total_of(part):
+            total = None
+            for segment in range(segments):
+                views = [terms[2 * segment + at].at[part, :, lanes] for at in range(2)]
+                piece = table_sums(padded_rows, tables[segment].at[part], *views)
+                total = piece if total is None else total + piece
+            return total
+
+        row = lax.broadcasted_iota(jnp.int32, (padded_rows, lanes.stop - start), 0)
+        omega = omega_of(row + plan[ROWS, 2], freq_count)
+        renorm = 1.0 + temperature * total_of(1) / omega
+        code[:padded_rows, lanes] = encoded(temperature * total_of(0) / renorm)
+    code[padded_rows:] = jnp.zeros((SPARE_ROWS, states), code.dtype)
 
 
 SWAP = [(0, 1), (1, 0)]

time: 33 us -> 33 us (level)
  transfers between devices with their start and end apart: 11 -> 11, of which waited for: 8 -> 8; matrix products, arithmetic and copies ran while one was open for 1% -> 1% of each run, Pallas kernels for 38% -> 37%
where the time goes in v12:
time: 33 us; the launch traced here: 32.8 us
  Pallas kernels  17.6 us (53%)
  starting transfers between devices  7.81 us (24%)
  waiting for transfers between devices  5.4 us (16%)
  local copies, waits for them, and re-layouts  1.16 us (4%)
  between operations  0.77 us (2%)
    pallas_call x5, Pallas kernels, step(): pl.pallas_call(functools.partial(step_kernel, dims, segment, span, sides,...  11.9 us
    ppermute x1, starting transfers between devices, on_device(): along_x = lax.ppermute(passed, 'x', SWAP)  3 us
    pallas_call x1, Pallas kernels, on_device(): pl.pallas_call(functools.partial(tables_kernel, dims, sides), out_shape=[...  2.25 us
    pallas_call x1, Pallas kernels, on_device(): pl.pallas_call(functools.partial(other_rows_kernel, dims), out_shape=jax....  2.2 us
    ppermute x4, waiting for transfers between devices, with_core(): return near + [lax.ppermute(piece, 'core', SWAP) for piece in near]  1.62 us
    ppermute x1, waiting for transfers between devices, on_device(): relayed = lax.ppermute(along_z, 'x', SWAP)  1.59 us
    ppermute x1, starting transfers between devices, on_device(): along_z = lax.ppermute(passed, 'zlo', SWAP)  1.58 us
    ppermute x1, waiting for transfers between devices, on_device(): along_x = lax.ppermute(own, 'x', SWAP)  1.28 us
  transfers between devices with their start and end apart: 11, of which 8 were waited for; matrix products, arithmetic and copies ran while one was open for 1% of the time, Pallas kernels for 37%

profile of v12, /device:TPU:0, one launch (start us, length us, event | category | flops | bytes accessed | tf_op | source)
XLA Modules:
  0.0 32.8 jit_solution(18198062780659508989)
XLA Ops:
  0.7 1.0 %copy-done.4 = f32[128,512]{1,0:T(8,128)S(1)} copy-done((f32[128,512]{1,0:T(8,128)S(1)}, f32[128,512]{1,0:T(8,128)}, u32[]{:S(2)}) %copy-start.4) | copy-done | bytes 262168
  1.6 0.1 encode.1.refs_0_
  1.8 3.0 %collective-permute-start = (s16[128,512]{1,0:T(8,128)(2,1)S(1)}, s16[128,512]{1,0:T(8,128)(2,1)S(1)}, u32[]{:S(2)}, u32[]{:S(2)}) collective-permute-start(s16[128,512]{1,0:T(8,128)(2,1)S(1)} %encode.1.refs_0_), channel_id=1, source_target_pairs={{0,2},{2,0},{1,3},{3,1},{4,6},{6,4},{5,7},{7,5},{8,10},{10,8},{9,1... | collective-permute-start | bytes 393224 | tf_op jit(solution)/shard_map/ppermute | solution.py:400
  4.8 1.6 %collective-permute-start.3 = (s16[128,512]{1,0:T(8,128)(2,1)S(1)}, s16[128,512]{1,0:T(8,128)(2,1)S(1)}, u32[]{:S(2)}, u32[]{:S(2)}) collective-permute-start(s16[128,512]{1,0:T(8,128)(2,1)S(1)} %encode.1.refs_0_), channel_id=1, source_target_pairs={{0,4},{4,0},{1,5},{5,1},{2,6},{6,2},{3,7},{7,3},{8,12},{12,8},{9,1... | collective-permute-start | bytes 393224 | tf_op jit(solution)/shard_map/ppermute | solution.py:401
  6.4 0.1 copy.8.pair_cols
  6.5 0.1 stack.20.meta
  6.6 2.2 %tables.1 = (s32[5,8]{1,0:T(8,128)S(1)}, bf16[4,256,1152]{2,1,0:T(8,128)(2,1)S(1)}, bf16[2,256,1152]{2,1,0:T(8,128)(2,1)S(1)}, bf16[2,128,1152]{2,1,0:T(8,128)(2,1)S(1)}) custom-call(s32[5]{0:T(128)S(1)} %stack.20.meta, f32[9]{0:T(128)S(1)} %copy-done.3, s32[4,2]{1,0:T(4,128)S(1)} %copy.8.pair_cols, s32[4]{0:T(128)S(1)} %copy-done.1, s32[16]{0:T(128)S(1)} %copy-done.2, ...), custom_call_target="tpu_custom_call" | custom-call | flops 10000000 | bytes 8000000 | tf_op jit(solution)/shard_map/tables/pallas_call | solution.py:312
  8.8 0.6 %collective-permute-start.2 = (s16[128,512]{1,0:T(8,128)(2,1)S(1)}, s16[128,512]{1,0:T(8,128)(2,1)S(1)}, u32[]{:S(2)}, u32[]{:S(2)}) collective-permute-start(s16[128,512]{1,0:T(8,128)(2,1)S(1)} %collective-permute-done.refs_1_), channel_id=1, source_target_pairs={{0,1},{1,0},{2,3},{3,2},{4,5},{5,4},{6,7},{7,6},{8,9},{9,8},{10,11... | collective-permute-start | bytes 393224 | tf_op jit(solution)/shard_map/ppermute | solution.py:387
  9.4 0.4 %collective-permute-done.3.first = s16[128,512]{1,0:T(8,128)(2,1)S(1)} collective-permute-done((s16[128,512]{1,0:T(8,128)(2,1)S(1)}, s16[128,512]{1,0:T(8,128)(2,1)S(1)}, u32[]{:S(2)}, u32[]{:S(2)}) %collective-permute-start.3) | collective-permute-done | bytes 131104 | tf_op jit(solution)/shard_map/ppermute | solution.py:401
  9.8 0.4 %collective-permute-start.4 = (s16[128,512]{1,0:T(8,128)(2,1)S(1)}, s16[128,512]{1,0:T(8,128)(2,1)S(1)}, u32[]{:S(2)}, u32[]{:S(2)}) collective-permute-start(s16[128,512]{1,0:T(8,128)(2,1)S(1)} %collective-permute-done.3.first), channel_id=1, source_target_pairs={{0,2},{2,0},{1,3},{3,1},{4,6},{6,4},{5,7},{7,5},{8,10},{10,8},{9,1... | collective-permute-start | bytes 393224 | tf_op jit(solution)/shard_map/ppermute | solution.py:403
  10.1 0.0 collective-permute-done.1.refs_2_
  10.1 0.3 collective-permute-done.2.refs_3_
  10.4 2.9 %step.5 = (f32[2,128,512]{2,1,0:T(8,128)S(1)}, bf16[2,1152,512]{2,1,0:T(8,128)(2,1)S(1)}, bf16[2,1152,512]{2,1,0:T(8,128)(2,1)S(1)}) custom-call(s32[5,8]{1,0:T(8,128)S(1)} %get-tuple-element.23.plan, s16[128,512]{1,0:T(8,128)(2,1)S(1)} %encode.1.refs_0_, s16[128,512]{1,0:T(8,128)(2,1)S(1)} %collective-permute-done.refs_1_, ...), custom_call_target="tpu_custom_call" | custom-call | flops 1000000 | bytes 100000 | tf_op jit(solution)/shard_map/step/pallas_call | solution.py:356
  13.3 1.6 %collective-permute-done.4.second = s16[128,512]{1,0:T(8,128)(2,1)S(1)} collective-permute-done((s16[128,512]{1,0:T(8,128)(2,1)S(1)}, s16[128,512]{1,0:T(8,128)(2,1)S(1)}, u32[]{:S(2)}, u32[]{:S(2)}) %collective-permute-start.4) | collective-permute-done | bytes 131104 | tf_op jit(solution)/shard_map/ppermute | solution.py:403
  14.9 0.1 collective-permute-start.5
  15.0 1.2 %other_tables.1 = (bf16[2,128,1152]{2,1,0:T(8,128)(2,1)S(1)}, bf16[2,256,1152]{2,1,0:T(8,128)(2,1)S(1)}) custom-call(s32[5]{0:T(128)S(1)} %stack.20.meta, f32[9]{0:T(128)S(1)} %copy-done.3), custom_call_target="tpu_custom_call" | custom-call | flops 10000000 | bytes 3000000 | tf_op jit(solution)/shard_map/other_tables/pallas_call | solution.py:389
  16.2 0.3 %collective-permute-done.5.refs_1_ = s16[2,128,512]{2,1,0:T(8,128)(2,1)S(1)} collective-permute-done((s16[2,128,512]{2,1,0:T(8,128)(2,1)S(1)}, s16[2,128,512]{2,1,0:T(8,128)(2,1)S(1)}, u32[]{:S(2)}, u32[]{:S(2)}) %collective-permute-start.5) | collective-permute-done | bytes 262176 | tf_op jit(solution)/shard_map/ppermute | solution.py:406
  16.5 2.5 %step.6 = (s16[128,512]{1,0:T(8,128)(2,1)S(1)}, bf16[2,1152,512]{2,1,0:T(8,128)(2,1)S(1)}, bf16[2,1152,512]{2,1,0:T(8,128)(2,1)S(1)}) custom-call(s32[5,8]{1,0:T(8,128)S(1)} %get-tuple-element.23.plan, s16[2,128,512]{2,1,0:T(8,128)(2,1)S(1)} %join.2.refs_0_, s16[2,128,512]{2,1,0:T(8,128)(2,1)S(1)} %collective-permute-done.5.refs_1_, ...), custom_call_target="tpu_custom_call" | custom-call | flops 1000000 | bytes 100000 | tf_op jit(solution)/shard_map/step/pallas_call | solution.py:356
  19.0 1.1 %collective-permute-start.7 = (s16[128,512]{1,0:T(8,128)(2,1)S(1)}, s16[128,512]{1,0:T(8,128)(2,1)S(1)}, u32[]{:S(2)}, u32[]{:S(2)}) collective-permute-start(s16[128,512]{1,0:T(8,128)(2,1)S(1)} %get-tuple-element.35.refs_0_), channel_id=1, source_target_pairs={{0,2},{2,0},{1,3},{3,1},{4,6},{6,4},{5,7},{7,5},{8,10},{10,8},{9,1... | collective-permute-start | bytes 393224 | tf_op jit(solution)/shard_map/ppermute | solution.py:418
  20.1 2.2 %other_rows.1.first = s16[144,512]{1,0:T(8,128)(2,1)S(1)} custom-call(s32[5,8]{1,0:T(8,128)S(1)} %get-tuple-element.23.plan, bf16[2,128,1152]{2,1,0:T(8,128)(2,1)S(1)} %get-tuple-element.24.refs_0_, bf16[2,256,1152]{2,1,0:T(8,128)(2,1)S(1)} %get-tuple-element.25.refs_1_, bf16[2,1152,512]{2,1,0:T(8,128)(2,1)S(1)} %get-tuple-element.29.refs_2_, ...), custom_call_target="tpu_custom_call" | custom-call | flops 1000000 | bytes 100000 | tf_op jit(solution)/shard_map/other_rows/pallas_call | solution.py:410
  22.3 1.0 %collective-permute-start.6 = (s16[144,512]{1,0:T(8,128)(2,1)S(1)}, s16[144,512]{1,0:T(8,128)(2,1)S(1)}, u32[]{:S(2)}, u32[]{:S(2)}) collective-permute-start(s16[144,512]{1,0:T(8,128)(2,1)S(1)} %other_rows.1.first), channel_id=1, source_target_pairs={{0,2},{2,0},{1,3},{3,1},{4,6},{6,4},{5,7},{7,5},{8,10},{10,8},{9,1... | collective-permute-start | bytes 442376 | tf_op jit(solution)/shard_map/ppermute | solution.py:422
  23.3 0.0 collective-permute-start.8
  23.4 1.3 %collective-permute-done.7.refs_1_ = s16[128,512]{1,0:T(8,128)(2,1)S(1)} collective-permute-done((s16[128,512]{1,0:T(8,128)(2,1)S(1)}, s16[128,512]{1,0:T(8,128)(2,1)S(1)}, u32[]{:S(2)}, u32[]{:S(2)}) %collective-permute-start.7) | collective-permute-done | bytes 131104 | tf_op jit(solution)/shard_map/ppermute | solution.py:418
  24.6 0.0 collective-permute-start.9
  24.6 0.1 collective-permute-done.8.refs_2_
  24.7 1.3 %collective-permute-done.9.refs_3_ = s16[128,512]{1,0:T(8,128)(2,1)S(1)} collective-permute-done((s16[128,512]{1,0:T(8,128)(2,1)S(1)}, s16[128,512]{1,0:T(8,128)(2,1)S(1)}, u32[]{:S(2)}, u32[]{:S(2)}) %collective-permute-start.9) | collective-permute-done | bytes 131104 | tf_op jit(solution)/shard_map/ppermute | solution.py:387
  26.0 1.8 %step.7.after.refs_4_ = f32[2,128,256]{2,1,0:T(8,128)S(1)} custom-call(s32[5,8]{1,0:T(8,128)S(1)} %get-tuple-element.23.plan, s16[128,512]{1,0:T(8,128)(2,1)S(1)} %get-tuple-element.35.refs_0_, s16[128,512]{1,0:T(8,128)(2,1)S(1)} %collective-permute-done.7.refs_1_, s16[128,512]{1,0:T(8,128)(2,1)S(1)} %collective-permute-done.8.refs_2_, ...), custom_call_target="tpu_custom_call" | custom-call | flops 1000000 | bytes 100000 | tf_op jit(solution)/shard_map/step/pallas_call | solution.py:356
  27.8 0.2 collective-permute-done.6.second
  28.1 0.1 collective-permute-start.10
  28.1 1.8 %step.8.refs_5_ = f32[2,128,256]{2,1,0:T(8,128)S(1)} custom-call(s32[5,8]{1,0:T(8,128)S(1)} %get-tuple-element.23.plan, s16[128,512]{1,0:T(8,128)(2,1)S(1)} %get-tuple-element.35.refs_0_, s16[128,512]{1,0:T(8,128)(2,1)S(1)} %collective-permute-done.7.refs_1_, s16[128,512]{1,0:T(8,128)(2,1)S(1)} %collective-permute-done.8.refs_2_, ...), custom_call_target="tpu_custom_call" | custom-call | flops 1000000 | bytes 100000 | tf_op jit(solution)/shard_map/step/pallas_call | solution.py:356
  30.0 0.0 collective-permute-done.10.refs_1_
  30.0 2.8 %step.9 = (f32[128,512]{1,0:T(8,128)}, f32[128,512]{1,0:T(8,128)}) custom-call(s32[5,8]{1,0:T(8,128)S(1)} %get-tuple-element.23.plan, s16[2,128,512]{2,1,0:T(8,128)(2,1)S(1)} %join.3.refs_0_, s16[2,128,512]{2,1,0:T(8,128)(2,1)S(1)} %collective-permute-done.10.refs_1_, bf16[4,256,1152]{2,1,0:T(8,128)(2,1)S(1)} %get-tuple-element.27.refs_4_.refs_2_, ...), custom_call_target="tpu_custom_call" | custom-call | flops 1000000 | bytes 100000 | tf_op jit(solution)/shard_map/step/pallas_call | solution.py:356
  (15 shorter events, 0.1 us)
Async XLA Ops:
  0.6 5.9 %copy-start.3 = (f32[9]{0:T(128)S(1)}, f32[9]{0:T(128)}, u32[]{:S(2)}) copy-start(f32[9]{0:T(128)} %phonon.3) | copy-start | bytes 112
  0.6 5.9 %copy-start.2 = (s32[16]{0:T(128)S(1)}, s32[16]{0:T(128)}, u32[]{:S(2)}) copy-start(s32[16]{0:T(128)} %block_order.1) | copy-start | bytes 196
  0.7 5.9 %copy-start.1 = (s32[4]{0:T(128)S(1)}, s32[4]{0:T(128)}, u32[]{:S(2)}) copy-start(s32[4]{0:T(128)} %pair_count.1) | copy-start | bytes 52
  0.7 1.0 %copy-start.4 = (f32[128,512]{1,0:T(8,128)S(1)}, f32[128,512]{1,0:T(8,128)}, u32[]{:S(2)}) copy-start(f32[128,512]{1,0:T(8,128)} %gap.1) | copy-start | bytes 786436
  1.6 4.7 %copy-start.5 = (s32[4,2]{0,1:T(2,128)S(1)}, s32[4,2]{0,1:T(2,128)}, u32[]{:S(2)}) copy-start(s32[4,2]{0,1:T(2,128)} %param.8) | copy-start | bytes 100
  1.6 4.9 %copy-start = (bf16[4,2,9,128,128]{4,3,2,1,0:T(8,128)(2,1)S(1)}, bf16[4,2,9,128,128]{4,3,2,1,0:T(8,128)(2,1)}, u32[]{:S(2)}) copy-start(bf16[4,2,9,128,128]{4,3,2,1,0:T(8,128)(2,1)} %coupling.1) | copy-start | bytes 7077892
  1.8 7.0 %collective-permute-start = (s16[128,512]{1,0:T(8,128)(2,1)S(1)}, s16[128,512]{1,0:T(8,128)(2,1)S(1)}, u32[]{:S(2)}, u32[]{:S(2)}) collective-permute-start(s16[128,512]{1,0:T(8,128)(2,1)S(1)} %encode.1.refs_0_), channel_id=1, source_target_pairs={{0,2},{2,0},{1,3},{3,1},{4,6},{6,4},{5,7},{7,5},{8,10},{10,8},{9,1... | collective-permute-start | bytes 393224 | tf_op jit(solution)/shard_map/ppermute | solution.py:400
  4.8 5.0 %collective-permute-start.3 = (s16[128,512]{1,0:T(8,128)(2,1)S(1)}, s16[128,512]{1,0:T(8,128)(2,1)S(1)}, u32[]{:S(2)}, u32[]{:S(2)}) collective-permute-start(s16[128,512]{1,0:T(8,128)(2,1)S(1)} %encode.1.refs_0_), channel_id=1, source_target_pairs={{0,4},{4,0},{1,5},{5,1},{2,6},{6,2},{3,7},{7,3},{8,12},{12,8},{9,1... | collective-permute-start | bytes 393224 | tf_op jit(solution)/shard_map/ppermute | solution.py:401
  6.4 3.8 %collective-permute-start.1 = (s16[128,512]{1,0:T(8,128)(2,1)S(1)}, s16[128,512]{1,0:T(8,128)(2,1)S(1)}, u32[]{:S(2)}, u32[]{:S(2)}) collective-permute-start(s16[128,512]{1,0:T(8,128)(2,1)S(1)} %encode.1.refs_0_), channel_id=1, source_target_pairs={{0,1},{1,0},{2,3},{3,2},{4,5},{5,4},{6,7},{7,6},{8,9},{9,8},{10,11... | collective-permute-start | bytes 393224 | tf_op jit(solution)/shard_map/ppermute | solution.py:387
  8.8 1.6 %collective-permute-start.2 = (s16[128,512]{1,0:T(8,128)(2,1)S(1)}, s16[128,512]{1,0:T(8,128)(2,1)S(1)}, u32[]{:S(2)}, u32[]{:S(2)}) collective-permute-start(s16[128,512]{1,0:T(8,128)(2,1)S(1)} %collective-permute-done.refs_1_), channel_id=1, source_target_pairs={{0,1},{1,0},{2,3},{3,2},{4,5},{5,4},{6,7},{7,6},{8,9},{9,8},{10,11... | collective-permute-start | bytes 393224 | tf_op jit(solution)/shard_map/ppermute | solution.py:387
  9.8 5.1 %collective-permute-start.4 = (s16[128,512]{1,0:T(8,128)(2,1)S(1)}, s16[128,512]{1,0:T(8,128)(2,1)S(1)}, u32[]{:S(2)}, u32[]{:S(2)}) collective-permute-start(s16[128,512]{1,0:T(8,128)(2,1)S(1)} %collective-permute-done.3.first), channel_id=1, source_target_pairs={{0,2},{2,0},{1,3},{3,1},{4,6},{6,4},{5,7},{7,5},{8,10},{10,8},{9,1... | collective-permute-start | bytes 393224 | tf_op jit(solution)/shard_map/ppermute | solution.py:403
  14.9 1.6 %collective-permute-start.5 = (s16[2,128,512]{2,1,0:T(8,128)(2,1)S(1)}, s16[2,128,512]{2,1,0:T(8,128)(2,1)S(1)}, u32[]{:S(2)}, u32[]{:S(2)}) collective-permute-start(s16[2,128,512]{2,1,0:T(8,128)(2,1)S(1)} %join.2.refs_0_), channel_id=1, source_target_pairs={{0,1},{1,0},{2,3},{3,2},{4,5},{5,4},{6,7},{7,6},{8,9},{9,8},{10,11... | collective-permute-start | bytes 786440 | tf_op jit(solution)/shard_map/ppermute | solution.py:406
  19.0 5.6 %collective-permute-start.7 = (s16[128,512]{1,0:T(8,128)(2,1)S(1)}, s16[128,512]{1,0:T(8,128)(2,1)S(1)}, u32[]{:S(2)}, u32[]{:S(2)}) collective-permute-start(s16[128,512]{1,0:T(8,128)(2,1)S(1)} %get-tuple-element.35.refs_0_), channel_id=1, source_target_pairs={{0,2},{2,0},{1,3},{3,1},{4,6},{6,4},{5,7},{7,5},{8,10},{10,8},{9,1... | collective-permute-start | bytes 393224 | tf_op jit(solution)/shard_map/ppermute | solution.py:418
  22.3 5.7 %collective-permute-start.6 = (s16[144,512]{1,0:T(8,128)(2,1)S(1)}, s16[144,512]{1,0:T(8,128)(2,1)S(1)}, u32[]{:S(2)}, u32[]{:S(2)}) collective-permute-start(s16[144,512]{1,0:T(8,128)(2,1)S(1)} %other_rows.1.first), channel_id=1, source_target_pairs={{0,2},{2,0},{1,3},{3,1},{4,6},{6,4},{5,7},{7,5},{8,10},{10,8},{9,1... | collective-permute-start | bytes 442376 | tf_op jit(solution)/shard_map/ppermute | solution.py:422
  23.3 1.3 %collective-permute-start.8 = (s16[128,512]{1,0:T(8,128)(2,1)S(1)}, s16[128,512]{1,0:T(8,128)(2,1)S(1)}, u32[]{:S(2)}, u32[]{:S(2)}) collective-permute-start(s16[128,512]{1,0:T(8,128)(2,1)S(1)} %get-tuple-element.35.refs_0_), channel_id=1, source_target_pairs={{0,1},{1,0},{2,3},{3,2},{4,5},{5,4},{6,7},{7,6},{8,9},{9,8},{10,11... | collective-permute-start | bytes 393224 | tf_op jit(solution)/shard_map/ppermute | solution.py:387
  24.6 1.3 %collective-permute-start.9 = (s16[128,512]{1,0:T(8,128)(2,1)S(1)}, s16[128,512]{1,0:T(8,128)(2,1)S(1)}, u32[]{:S(2)}, u32[]{:S(2)}) collective-permute-start(s16[128,512]{1,0:T(8,128)(2,1)S(1)} %collective-permute-done.7.refs_1_), channel_id=1, source_target_pairs={{0,1},{1,0},{2,3},{3,2},{4,5},{5,4},{6,7},{7,6},{8,9},{9,8},{10,11... | collective-permute-start | bytes 393224 | tf_op jit(solution)/shard_map/ppermute | solution.py:387
  28.1 1.9 %collective-permute-start.10 = (s16[2,128,512]{2,1,0:T(8,128)(2,1)S(1)}, s16[2,128,512]{2,1,0:T(8,128)(2,1)S(1)}, u32[]{:S(2)}, u32[]{:S(2)}) collective-permute-start(s16[2,128,512]{2,1,0:T(8,128)(2,1)S(1)} %join.3.refs_0_), channel_id=1, source_target_pairs={{0,1},{1,0},{2,3},{3,2},{4,5},{5,4},{6,7},{7,6},{8,9},{9,8},{10,11... | collective-permute-start | bytes 786440 | tf_op jit(solution)/shard_map/ppermute | solution.py:424

commit v13 on v12

--- a/solution.py
+++ b/solution.py
@@ -14,7 +14,7 @@
 CODE_LIMIT = 32767.0
 CODE_POWER = 5
 STEP_FLOPS = 1_000_000
-SPARE_ROWS = 16
+SPARE_ROWS = 8
 HOLDER, PLACE, LIVE, SIDE, ROWS = 0, 1, 2, 3, 4
 
 
@@ -35,8 +35,9 @@
     return (root * GAP_LIMIT) * (square * square)
 
 
-def encode_kernel(gap, code):
+def encode_kernel(gap, code, longer):
     code[...] = encoded(gap[...])
+    longer[: code.shape[0]] = code[...]
 
 
 def join_kernel(first, second, after, joined):
@@ -253,7 +254,6 @@
         omega = omega_of(row + plan[ROWS, 2], freq_count)
         renorm = 1.0 + temperature * total_of(1) / omega
         code[:padded_rows, lanes] = encoded(temperature * total_of(0) / renorm)
-    code[padded_rows:] = jnp.zeros((SPARE_ROWS, states), code.dtype)
 
 
 SWAP = [(0, 1), (1, 0)]
@@ -293,11 +293,14 @@
 
     passed = gap_in
     if pairwise:
-        passed = pl.pallas_call(
+        passed, longer = pl.pallas_call(
             encode_kernel,
-            out_shape=jax.ShapeDtypeStruct(gap_in.shape, link_type),
+            out_shape=[
+                jax.ShapeDtypeStruct(gap_in.shape, link_type),
+                jax.ShapeDtypeStruct((own_rows + SPARE_ROWS, row_width), link_type),
+            ],
             in_specs=[vmem],
-            out_specs=vmem,
+            out_specs=[vmem, vmem],
             compiler_params=pltpu.CompilerParams(vmem_limit_bytes=8 << 20),
             cost_estimate=pl.CostEstimate(
                 flops=10_000_000_000, bytes_accessed=40_000_000, transcendentals=0
@@ -398,8 +401,8 @@
         name="other_tables",
     )(meta, phonon)
     along_x = lax.ppermute(passed, "x", SWAP)
-    along_z = lax.ppermute(passed, "zlo", SWAP)
-    along_x, plan = lax.optimization_barrier((along_x, plan))
+    along_z = lax.ppermute(longer, "zlo", SWAP)
+    along_z, plan = lax.optimization_barrier((along_z, plan))
     relayed = lax.ppermute(along_z, "x", SWAP)
     partial, *near_terms = step(plan, 0, False, with_core([passed, along_x]), [], keep=True)
     far = join(along_z, relayed, partial)

time: 33 us -> 32.9 us (level)
  waiting for transfers between devices: 5.4 us -> 3.84 us
  starting transfers between devices: 7.81 us -> 9.24 us
    ppermute x1, waiting for transfers between devices: 1.59 us -> 0.01 us  [on_device(): relayed = lax.ppermute(along_z, 'x', SWAP)]
    ppermute x1, starting transfers between devices: 1.58 us -> 3.09 us  [on_device(): along_z = lax.ppermute(longer, 'zlo', SWAP)]
    ppermute x1, starting transfers between devices: 3 us -> 1.49 us  [on_device(): along_x = lax.ppermute(passed, 'x', SWAP)]
    ppermute x1, starting transfers between devices: 0.36 us -> 1.38 us  [on_device(): relayed = lax.ppermute(along_z, 'x', SWAP)]
    ppermute x4, waiting for transfers between devices: 1.62 us -> 2.37 us  [with_core(): return near + [lax.ppermute(piece, 'core', SWAP) for piece in near]]
    ppermute x1, waiting for transfers between devices: 0.35 us -> 0.01 us  [on_device(): along_z = lax.ppermute(longer, 'zlo', SWAP)]
  transfers between devices with their start and end apart: 11 -> 11, of which waited for: 8 -> 4; matrix products, arithmetic and copies ran while one was open for 1% -> 1% of each run, Pallas kernels for 37% -> 37%
where the time goes in v13:
time: 32.9 us; the launch traced here: 32.8 us
  Pallas kernels  17.7 us (54%)
  starting transfers between devices  9.24 us (28%)
  waiting for transfers between devices  3.84 us (12%)
  local copies, waits for them, and re-layouts  1.16 us (4%)
  between operations  0.78 us (2%)
    pallas_call x5, Pallas kernels, step(): pl.pallas_call(functools.partial(step_kernel, dims, segment, span, sides,...  11.9 us
    ppermute x1, starting transfers between devices, on_device(): along_z = lax.ppermute(longer, 'zlo', SWAP)  3.09 us
    ppermute x4, waiting for transfers between devices, with_core(): return near + [lax.ppermute(piece, 'core', SWAP) for piece in near]  2.37 us
    pallas_call x1, Pallas kernels, on_device(): pl.pallas_call(functools.partial(tables_kernel, dims, sides), out_shape=[...  2.25 us
    pallas_call x1, Pallas kernels, on_device(): pl.pallas_call(functools.partial(other_rows_kernel, dims), out_shape=jax....  2.2 us
    ppermute x1, starting transfers between devices, on_device(): along_x = lax.ppermute(passed, 'x', SWAP)  1.49 us
    ppermute x1, waiting for transfers between devices, on_device(): along_x = lax.ppermute(own, 'x', SWAP)  1.42 us
    ppermute x1, starting transfers between devices, on_device(): relayed = lax.ppermute(along_z, 'x', SWAP)  1.38 us
  transfers between devices with their start and end apart: 11, of which 4 were waited for; matrix products, arithmetic and copies ran while one was open for 1% of the time, Pallas kernels for 37%

profile of v13, /device:TPU:0, one launch (start us, length us, event | category | flops | bytes accessed | tf_op | source)
XLA Modules:
  0.0 32.8 jit_solution(11124013999558172879)
XLA Ops:
  0.7 1.0 %copy-done.4 = f32[128,512]{1,0:T(8,128)S(1)} copy-done((f32[128,512]{1,0:T(8,128)S(1)}, f32[128,512]{1,0:T(8,128)}, u32[]{:S(2)}) %copy-start.4) | copy-done | bytes 262168
  1.6 0.2 encode.1
  1.8 3.1 %collective-permute-start = (s16[136,512]{1,0:T(8,128)(2,1)S(1)}, s16[136,512]{1,0:T(8,128)(2,1)S(1)}, u32[]{:S(2)}, u32[]{:S(2)}) collective-permute-start(s16[136,512]{1,0:T(8,128)(2,1)S(1)} %get-tuple-element.21), channel_id=1, source_target_pairs={{0,4},{4,0},{1,5},{5,1},{2,6},{6,2},{3,7},{7,3},{8,12},{12,8},{9,1... | collective-permute-start | bytes 417800 | tf_op jit(solution)/shard_map/ppermute | solution.py:404
  4.9 1.5 %collective-permute-start.1 = (s16[128,512]{1,0:T(8,128)(2,1)S(1)}, s16[128,512]{1,0:T(8,128)(2,1)S(1)}, u32[]{:S(2)}, u32[]{:S(2)}) collective-permute-start(s16[128,512]{1,0:T(8,128)(2,1)S(1)} %get-tuple-element.29.refs_0_), channel_id=1, source_target_pairs={{0,2},{2,0},{1,3},{3,1},{4,6},{6,4},{5,7},{7,5},{8,10},{10,8},{9,1... | collective-permute-start | bytes 393224 | tf_op jit(solution)/shard_map/ppermute | solution.py:403
  6.4 0.1 copy.8.pair_cols
  6.5 0.1 stack.20.meta
  6.6 2.2 %tables.1 = (s32[5,8]{1,0:T(8,128)S(1)}, bf16[4,256,1152]{2,1,0:T(8,128)(2,1)S(1)}, bf16[2,256,1152]{2,1,0:T(8,128)(2,1)S(1)}, bf16[2,128,1152]{2,1,0:T(8,128)(2,1)S(1)}) custom-call(s32[5]{0:T(128)S(1)} %stack.20.meta, f32[9]{0:T(128)S(1)} %copy-done.3, s32[4,2]{1,0:T(4,128)S(1)} %copy.8.pair_cols, s32[4]{0:T(128)S(1)} %copy-done.1, s32[16]{0:T(128)S(1)} %copy-done.2, ...), custom_call_target="tpu_custom_call" | custom-call | flops 10000000 | bytes 8000000 | tf_op jit(solution)/shard_map/tables/pallas_call | solution.py:315
  8.8 0.0 collective-permute-done.first
  8.9 1.4 %collective-permute-start.4 = (s16[136,512]{1,0:T(8,128)(2,1)S(1)}, s16[136,512]{1,0:T(8,128)(2,1)S(1)}, u32[]{:S(2)}, u32[]{:S(2)}) collective-permute-start(s16[136,512]{1,0:T(8,128)(2,1)S(1)} %collective-permute-done.first), channel_id=1, source_target_pairs={{0,2},{2,0},{1,3},{3,1},{4,6},{6,4},{5,7},{7,5},{8,10},{10,8},{9,1... | collective-permute-start | bytes 417800 | tf_op jit(solution)/shard_map/ppermute | solution.py:406
  10.2 0.0 collective-permute-start.2
  10.2 0.0 collective-permute-done.1.refs_1_
  10.2 0.5 %collective-permute-start.3 = (s16[128,512]{1,0:T(8,128)(2,1)S(1)}, s16[128,512]{1,0:T(8,128)(2,1)S(1)}, u32[]{:S(2)}, u32[]{:S(2)}) collective-permute-start(s16[128,512]{1,0:T(8,128)(2,1)S(1)} %collective-permute-done.1.refs_1_), channel_id=1, source_target_pairs={{0,1},{1,0},{2,3},{3,2},{4,5},{5,4},{6,7},{7,6},{8,9},{9,8},{10,11... | collective-permute-start | bytes 393224 | tf_op jit(solution)/shard_map/ppermute | solution.py:390
  10.8 0.8 %collective-permute-done.2.refs_2_ = s16[128,512]{1,0:T(8,128)(2,1)S(1)} collective-permute-done((s16[128,512]{1,0:T(8,128)(2,1)S(1)}, s16[128,512]{1,0:T(8,128)(2,1)S(1)}, u32[]{:S(2)}, u32[]{:S(2)}) %collective-permute-start.2) | collective-permute-done | bytes 131104 | tf_op jit(solution)/shard_map/ppermute | solution.py:390
  11.6 0.2 collective-permute-done.3.refs_3_
  11.8 2.9 %step.5 = (f32[2,128,512]{2,1,0:T(8,128)S(1)}, bf16[2,1152,512]{2,1,0:T(8,128)(2,1)S(1)}, bf16[2,1152,512]{2,1,0:T(8,128)(2,1)S(1)}) custom-call(s32[5,8]{1,0:T(8,128)S(1)} %get-tuple-element.26.plan, s16[128,512]{1,0:T(8,128)(2,1)S(1)} %get-tuple-element.29.refs_0_, s16[128,512]{1,0:T(8,128)(2,1)S(1)} %collective-permute-done.1.refs_1_, ...), custom_call_target="tpu_custom_call" | custom-call | flops 1000000 | bytes 100000 | tf_op jit(solution)/shard_map/step/pallas_call | solution.py:359
  14.7 0.0 collective-permute-done.4.second
  14.7 0.4 %collective-permute-start.5 = (s16[2,128,512]{2,1,0:T(8,128)(2,1)S(1)}, s16[2,128,512]{2,1,0:T(8,128)(2,1)S(1)}, u32[]{:S(2)}, u32[]{:S(2)}) collective-permute-start(s16[2,128,512]{2,1,0:T(8,128)(2,1)S(1)} %join.2.refs_0_), channel_id=1, source_target_pairs={{0,1},{1,0},{2,3},{3,2},{4,5},{5,4},{6,7},{7,6},{8,9},{9,8},{10,11... | collective-permute-start | bytes 786440 | tf_op jit(solution)/shard_map/ppermute | solution.py:409
  15.1 1.2 %other_tables.1 = (bf16[2,128,1152]{2,1,0:T(8,128)(2,1)S(1)}, bf16[2,256,1152]{2,1,0:T(8,128)(2,1)S(1)}) custom-call(s32[5]{0:T(128)S(1)} %stack.20.meta, f32[9]{0:T(128)S(1)} %copy-done.3), custom_call_target="tpu_custom_call" | custom-call | flops 10000000 | bytes 3000000 | tf_op jit(solution)/shard_map/other_tables/pallas_call | solution.py:392
  16.3 0.0 collective-permute-done.5.refs_1_
  16.3 2.5 %step.6 = (s16[128,512]{1,0:T(8,128)(2,1)S(1)}, bf16[2,1152,512]{2,1,0:T(8,128)(2,1)S(1)}, bf16[2,1152,512]{2,1,0:T(8,128)(2,1)S(1)}) custom-call(s32[5,8]{1,0:T(8,128)S(1)} %get-tuple-element.26.plan, s16[2,128,512]{2,1,0:T(8,128)(2,1)S(1)} %join.2.refs_0_, s16[2,128,512]{2,1,0:T(8,128)(2,1)S(1)} %collective-permute-done.5.refs_1_, ...), custom_call_target="tpu_custom_call" | custom-call | flops 1000000 | bytes 100000 | tf_op jit(solution)/shard_map/step/pallas_call | solution.py:359
  18.8 1.0 %collective-permute-start.7 = (s16[128,512]{1,0:T(8,128)(2,1)S(1)}, s16[128,512]{1,0:T(8,128)(2,1)S(1)}, u32[]{:S(2)}, u32[]{:S(2)}) collective-permute-start(s16[128,512]{1,0:T(8,128)(2,1)S(1)} %get-tuple-element.39.refs_0_), channel_id=1, source_target_pairs={{0,2},{2,0},{1,3},{3,1},{4,6},{6,4},{5,7},{7,5},{8,10},{10,8},{9,1... | collective-permute-start | bytes 393224 | tf_op jit(solution)/shard_map/ppermute | solution.py:421
  19.8 2.2 %other_rows.1.first = s16[136,512]{1,0:T(8,128)(2,1)S(1)} custom-call(s32[5,8]{1,0:T(8,128)S(1)} %get-tuple-element.26.plan, bf16[2,128,1152]{2,1,0:T(8,128)(2,1)S(1)} %get-tuple-element.27.refs_0_, bf16[2,256,1152]{2,1,0:T(8,128)(2,1)S(1)} %get-tuple-element.28.refs_1_, bf16[2,1152,512]{2,1,0:T(8,128)(2,1)S(1)} %get-tuple-element.32.refs_2_, ...), custom_call_target="tpu_custom_call" | custom-call | flops 1000000 | bytes 100000 | tf_op jit(solution)/shard_map/other_rows/pallas_call | solution.py:413
  22.0 1.1 %collective-permute-start.6 = (s16[136,512]{1,0:T(8,128)(2,1)S(1)}, s16[136,512]{1,0:T(8,128)(2,1)S(1)}, u32[]{:S(2)}, u32[]{:S(2)}) collective-permute-start(s16[136,512]{1,0:T(8,128)(2,1)S(1)} %other_rows.1.first), channel_id=1, source_target_pairs={{0,2},{2,0},{1,3},{3,1},{4,6},{6,4},{5,7},{7,5},{8,10},{10,8},{9,1... | collective-permute-start | bytes 417800 | tf_op jit(solution)/shard_map/ppermute | solution.py:425
  23.2 1.4 %collective-permute-done.7.refs_1_ = s16[128,512]{1,0:T(8,128)(2,1)S(1)} collective-permute-done((s16[128,512]{1,0:T(8,128)(2,1)S(1)}, s16[128,512]{1,0:T(8,128)(2,1)S(1)}, u32[]{:S(2)}, u32[]{:S(2)}) %collective-permute-start.7) | collective-permute-done | bytes 131104 | tf_op jit(solution)/shard_map/ppermute | solution.py:421
  24.6 0.0 collective-permute-start.9
  24.6 0.0 collective-permute-done.8.refs_2_
  24.6 1.3 %collective-permute-done.9.refs_3_ = s16[128,512]{1,0:T(8,128)(2,1)S(1)} collective-permute-done((s16[128,512]{1,0:T(8,128)(2,1)S(1)}, s16[128,512]{1,0:T(8,128)(2,1)S(1)}, u32[]{:S(2)}, u32[]{:S(2)}) %collective-permute-start.9) | collective-permute-done | bytes 131104 | tf_op jit(solution)/shard_map/ppermute | solution.py:390
  26.0 1.9 %step.7.after.refs_4_ = f32[2,128,256]{2,1,0:T(8,128)S(1)} custom-call(s32[5,8]{1,0:T(8,128)S(1)} %get-tuple-element.26.plan, s16[128,512]{1,0:T(8,128)(2,1)S(1)} %get-tuple-element.39.refs_0_, s16[128,512]{1,0:T(8,128)(2,1)S(1)} %collective-permute-done.7.refs_1_, s16[128,512]{1,0:T(8,128)(2,1)S(1)} %collective-permute-done.8.refs_2_, ...), custom_call_target="tpu_custom_call" | custom-call | flops 1000000 | bytes 100000 | tf_op jit(solution)/shard_map/step/pallas_call | solution.py:359
  27.8 0.0 collective-permute-done.6.second
  27.9 0.2 collective-permute-start.10
  28.1 1.9 %step.8.refs_5_ = f32[2,128,256]{2,1,0:T(8,128)S(1)} custom-call(s32[5,8]{1,0:T(8,128)S(1)} %get-tuple-element.26.plan, s16[128,512]{1,0:T(8,128)(2,1)S(1)} %get-tuple-element.39.refs_0_, s16[128,512]{1,0:T(8,128)(2,1)S(1)} %collective-permute-done.7.refs_1_, s16[128,512]{1,0:T(8,128)(2,1)S(1)} %collective-permute-done.8.refs_2_, ...), custom_call_target="tpu_custom_call" | custom-call | flops 1000000 | bytes 100000 | tf_op jit(solution)/shard_map/step/pallas_call | solution.py:359
  30.0 2.8 %step.9 = (f32[128,512]{1,0:T(8,128)}, f32[128,512]{1,0:T(8,128)}) custom-call(s32[5,8]{1,0:T(8,128)S(1)} %get-tuple-element.26.plan, s16[2,128,512]{2,1,0:T(8,128)(2,1)S(1)} %join.3.refs_0_, s16[2,128,512]{2,1,0:T(8,128)(2,1)S(1)} %collective-permute-done.10.refs_1_, bf16[4,256,1152]{2,1,0:T(8,128)(2,1)S(1)} %get-tuple-element.30.refs_4_.refs_2_, ...), custom_call_target="tpu_custom_call" | custom-call | flops 1000000 | bytes 100000 | tf_op jit(solution)/shard_map/step/pallas_call | solution.py:359
  (15 shorter events, 0.1 us)
Async XLA Ops:
  0.6 6.0 %copy-start.3 = (f32[9]{0:T(128)S(1)}, f32[9]{0:T(128)}, u32[]{:S(2)}) copy-start(f32[9]{0:T(128)} %phonon.3) | copy-start | bytes 112
  0.6 5.9 %copy-start.2 = (s32[16]{0:T(128)S(1)}, s32[16]{0:T(128)}, u32[]{:S(2)}) copy-start(s32[16]{0:T(128)} %block_order.1) | copy-start | bytes 196
  0.7 5.9 %copy-start.1 = (s32[4]{0:T(128)S(1)}, s32[4]{0:T(128)}, u32[]{:S(2)}) copy-start(s32[4]{0:T(128)} %pair_count.1) | copy-start | bytes 52
  0.7 1.0 %copy-start.4 = (f32[128,512]{1,0:T(8,128)S(1)}, f32[128,512]{1,0:T(8,128)}, u32[]{:S(2)}) copy-start(f32[128,512]{1,0:T(8,128)} %gap.1) | copy-start | bytes 786436
  1.6 4.8 %copy-start.5 = (s32[4,2]{0,1:T(2,128)S(1)}, s32[4,2]{0,1:T(2,128)}, u32[]{:S(2)}) copy-start(s32[4,2]{0,1:T(2,128)} %param.8) | copy-start | bytes 100
  1.6 5.0 %copy-start = (bf16[4,2,9,128,128]{4,3,2,1,0:T(8,128)(2,1)S(1)}, bf16[4,2,9,128,128]{4,3,2,1,0:T(8,128)(2,1)}, u32[]{:S(2)}) copy-start(bf16[4,2,9,128,128]{4,3,2,1,0:T(8,128)(2,1)} %coupling.1) | copy-start | bytes 7077892
  1.8 7.0 %collective-permute-start = (s16[136,512]{1,0:T(8,128)(2,1)S(1)}, s16[136,512]{1,0:T(8,128)(2,1)S(1)}, u32[]{:S(2)}, u32[]{:S(2)}) collective-permute-start(s16[136,512]{1,0:T(8,128)(2,1)S(1)} %get-tuple-element.21), channel_id=1, source_target_pairs={{0,4},{4,0},{1,5},{5,1},{2,6},{6,2},{3,7},{7,3},{8,12},{12,8},{9,1... | collective-permute-start | bytes 417800 | tf_op jit(solution)/shard_map/ppermute | solution.py:404
  4.9 5.3 %collective-permute-start.1 = (s16[128,512]{1,0:T(8,128)(2,1)S(1)}, s16[128,512]{1,0:T(8,128)(2,1)S(1)}, u32[]{:S(2)}, u32[]{:S(2)}) collective-permute-start(s16[128,512]{1,0:T(8,128)(2,1)S(1)} %get-tuple-element.29.refs_0_), channel_id=1, source_target_pairs={{0,2},{2,0},{1,3},{3,1},{4,6},{6,4},{5,7},{7,5},{8,10},{10,8},{9,1... | collective-permute-start | bytes 393224 | tf_op jit(solution)/shard_map/ppermute | solution.py:403
  8.9 5.8 %collective-permute-start.4 = (s16[136,512]{1,0:T(8,128)(2,1)S(1)}, s16[136,512]{1,0:T(8,128)(2,1)S(1)}, u32[]{:S(2)}, u32[]{:S(2)}) collective-permute-start(s16[136,512]{1,0:T(8,128)(2,1)S(1)} %collective-permute-done.first), channel_id=1, source_target_pairs={{0,2},{2,0},{1,3},{3,1},{4,6},{6,4},{5,7},{7,5},{8,10},{10,8},{9,1... | collective-permute-start | bytes 417800 | tf_op jit(solution)/shard_map/ppermute | solution.py:406
  10.2 1.3 %collective-permute-start.2 = (s16[128,512]{1,0:T(8,128)(2,1)S(1)}, s16[128,512]{1,0:T(8,128)(2,1)S(1)}, u32[]{:S(2)}, u32[]{:S(2)}) collective-permute-start(s16[128,512]{1,0:T(8,128)(2,1)S(1)} %get-tuple-element.29.refs_0_), channel_id=1, source_target_pairs={{0,1},{1,0},{2,3},{3,2},{4,5},{5,4},{6,7},{7,6},{8,9},{9,8},{10,11... | collective-permute-start | bytes 393224 | tf_op jit(solution)/shard_map/ppermute | solution.py:390
  10.2 1.5 %collective-permute-start.3 = (s16[128,512]{1,0:T(8,128)(2,1)S(1)}, s16[128,512]{1,0:T(8,128)(2,1)S(1)}, u32[]{:S(2)}, u32[]{:S(2)}) collective-permute-start(s16[128,512]{1,0:T(8,128)(2,1)S(1)} %collective-permute-done.1.refs_1_), channel_id=1, source_target_pairs={{0,1},{1,0},{2,3},{3,2},{4,5},{5,4},{6,7},{7,6},{8,9},{9,8},{10,11... | collective-permute-start | bytes 393224 | tf_op jit(solution)/shard_map/ppermute | solution.py:390
  14.7 1.6 %collective-permute-start.5 = (s16[2,128,512]{2,1,0:T(8,128)(2,1)S(1)}, s16[2,128,512]{2,1,0:T(8,128)(2,1)S(1)}, u32[]{:S(2)}, u32[]{:S(2)}) collective-permute-start(s16[2,128,512]{2,1,0:T(8,128)(2,1)S(1)} %join.2.refs_0_), channel_id=1, source_target_pairs={{0,1},{1,0},{2,3},{3,2},{4,5},{5,4},{6,7},{7,6},{8,9},{9,8},{10,11... | collective-permute-start | bytes 786440 | tf_op jit(solution)/shard_map/ppermute | solution.py:409
  18.8 5.8 %collective-permute-start.7 = (s16[128,512]{1,0:T(8,128)(2,1)S(1)}, s16[128,512]{1,0:T(8,128)(2,1)S(1)}, u32[]{:S(2)}, u32[]{:S(2)}) collective-permute-start(s16[128,512]{1,0:T(8,128)(2,1)S(1)} %get-tuple-element.39.refs_0_), channel_id=1, source_target_pairs={{0,2},{2,0},{1,3},{3,1},{4,6},{6,4},{5,7},{7,5},{8,10},{10,8},{9,1... | collective-permute-start | bytes 393224 | tf_op jit(solution)/shard_map/ppermute | solution.py:421
  22.0 5.8 %collective-permute-start.6 = (s16[136,512]{1,0:T(8,128)(2,1)S(1)}, s16[136,512]{1,0:T(8,128)(2,1)S(1)}, u32[]{:S(2)}, u32[]{:S(2)}) collective-permute-start(s16[136,512]{1,0:T(8,128)(2,1)S(1)} %other_rows.1.first), channel_id=1, source_target_pairs={{0,2},{2,0},{1,3},{3,1},{4,6},{6,4},{5,7},{7,5},{8,10},{10,8},{9,1... | collective-permute-start | bytes 417800 | tf_op jit(solution)/shard_map/ppermute | solution.py:425
  23.2 1.4 %collective-permute-start.8 = (s16[128,512]{1,0:T(8,128)(2,1)S(1)}, s16[128,512]{1,0:T(8,128)(2,1)S(1)}, u32[]{:S(2)}, u32[]{:S(2)}) collective-permute-start(s16[128,512]{1,0:T(8,128)(2,1)S(1)} %get-tuple-element.39.refs_0_), channel_id=1, source_target_pairs={{0,1},{1,0},{2,3},{3,2},{4,5},{5,4},{6,7},{7,6},{8,9},{9,8},{10,11... | collective-permute-start | bytes 393224 | tf_op jit(solution)/shard_map/ppermute | solution.py:390
  24.6 1.3 %collective-permute-start.9 = (s16[128,512]{1,0:T(8,128)(2,1)S(1)}, s16[128,512]{1,0:T(8,128)(2,1)S(1)}, u32[]{:S(2)}, u32[]{:S(2)}) collective-permute-start(s16[128,512]{1,0:T(8,128)(2,1)S(1)} %collective-permute-done.7.refs_1_), channel_id=1, source_target_pairs={{0,1},{1,0},{2,3},{3,2},{4,5},{5,4},{6,7},{7,6},{8,9},{9,8},{10,11... | collective-permute-start | bytes 393224 | tf_op jit(solution)/shard_map/ppermute | solution.py:390
  27.9 2.1 %collective-permute-start.10 = (s16[2,128,512]{2,1,0:T(8,128)(2,1)S(1)}, s16[2,128,512]{2,1,0:T(8,128)(2,1)S(1)}, u32[]{:S(2)}, u32[]{:S(2)}) collective-permute-start(s16[2,128,512]{2,1,0:T(8,128)(2,1)S(1)} %join.3.refs_0_), channel_id=1, source_target_pairs={{0,1},{1,0},{2,3},{3,2},{4,5},{5,4},{6,7},{7,6},{8,9},{9,8},{10,11... | collective-permute-start | bytes 786440 | tf_op jit(solution)/shard_map/ppermute | solution.py:427

commit v14 on v13

--- a/solution.py
+++ b/solution.py
@@ -402,9 +402,11 @@
     )(meta, phonon)
     along_x = lax.ppermute(passed, "x", SWAP)
     along_z = lax.ppermute(longer, "zlo", SWAP)
-    along_z, plan = lax.optimization_barrier((along_z, plan))
+    across = lax.ppermute(passed, "core", SWAP)
+    along_z, across, plan = lax.optimization_barrier((along_z, across, plan))
     relayed = lax.ppermute(along_z, "x", SWAP)
-    partial, *near_terms = step(plan, 0, False, with_core([passed, along_x]), [], keep=True)
+    near = [passed, along_x, across, lax.ppermute(along_x, "core", SWAP)]
+    partial, *near_terms = step(plan, 0, False, near, [], keep=True)
     far = join(along_z, relayed, partial)
     pieces = [far, lax.ppermute(far, "core", SWAP)]
     plan, *other_tables = lax.optimization_barrier((plan, *other_tables))

time: 32.9 us -> 33.5 us (1.018)
  waiting for transfers between devices: 3.84 us -> 5.21 us
  starting transfers between devices: 9.24 us -> 8.39 us
    ppermute x0 -> x2, waiting for transfers between devices: none -> 1.35 us  [the longest x1 1.35 us: on_device(): near = [passed, along_x, across, lax.ppermute(along_x, 'core', SWAP)]]
    ppermute x4 -> x2, waiting for transfers between devices: 2.37 us -> 1.34 us  [with_core(): return near + [lax.ppermute(piece, 'core', SWAP) for piece in near]]
    ppermute x1, waiting for transfers between devices: 0.01 us -> 0.58 us  [on_device(): along_x = lax.ppermute(passed, 'x', SWAP)]
    ppermute x1, starting transfers between devices: 1.15 us -> 0.6 us  [on_device(): far = join(other, lax.ppermute(other, 'x', SWAP), *partial)]
    ppermute x1, starting transfers between devices: 1.01 us -> 1.56 us  [on_device(): along_x = lax.ppermute(own, 'x', SWAP)]
    ppermute x4 -> x2, starting transfers between devices: 0.52 us -> 0.01 us  [with_core(): return near + [lax.ppermute(piece, 'core', SWAP) for piece in near]]
    ppermute x1, waiting for transfers between devices: 0.01 us -> 0.44 us  [on_device(): far = join(other, lax.ppermute(other, 'x', SWAP), *partial)]
  transfers between devices with their start and end apart: 11 -> 11, of which waited for: 4 -> 7; matrix products, arithmetic and copies ran while one was open for 1% -> 1% of each run, Pallas kernels for 37% -> 37%
where the time goes in v14:
time: 33.5 us; the launch traced here: 33.3 us
  Pallas kernels  17.7 us (53%)
  starting transfers between devices  8.39 us (25%)
  waiting for transfers between devices  5.21 us (16%)
  local copies, waits for them, and re-layouts  1.16 us (3%)
  between operations  0.78 us (2%)
    pallas_call x5, Pallas kernels, step(): pl.pallas_call(functools.partial(step_kernel, dims, segment, span, sides,...  11.9 us
    ppermute x1, starting transfers between devices, on_device(): along_z = lax.ppermute(longer, 'zlo', SWAP)  3.09 us
    pallas_call x1, Pallas kernels, on_device(): pl.pallas_call(functools.partial(tables_kernel, dims, sides), out_shape=[...  2.25 us
    pallas_call x1, Pallas kernels, on_device(): pl.pallas_call(functools.partial(other_rows_kernel, dims), out_shape=jax....  2.2 us
    ppermute x1, starting transfers between devices, on_device(): along_x = lax.ppermute(own, 'x', SWAP)  1.56 us
    ppermute x1, starting transfers between devices, on_device(): along_x = lax.ppermute(passed, 'x', SWAP)  1.49 us
    ppermute x1, starting transfers between devices, on_device(): relayed = lax.ppermute(along_z, 'x', SWAP)  1.36 us
    ppermute x1, waiting for transfers between devices, on_device(): near = [passed, along_x, across, lax.ppermute(along_x, 'core', SWAP)]  1.35 us
  transfers between devices with their start and end apart: 11, of which 7 were waited for; matrix products, arithmetic and copies ran while one was open for 1% of the time, Pallas kernels for 37%

profile of v14, /device:TPU:0, one launch (start us, length us, event | category | flops | bytes accessed | tf_op | source)
XLA Modules:
  0.0 33.3 jit_solution(2664974833155089696)
XLA Ops:
  0.7 1.0 %copy-done.4 = f32[128,512]{1,0:T(8,128)S(1)} copy-done((f32[128,512]{1,0:T(8,128)S(1)}, f32[128,512]{1,0:T(8,128)}, u32[]{:S(2)}) %copy-start.4) | copy-done | bytes 262168
  1.6 0.2 encode.1
  1.8 3.1 %collective-permute-start = (s16[136,512]{1,0:T(8,128)(2,1)S(1)}, s16[136,512]{1,0:T(8,128)(2,1)S(1)}, u32[]{:S(2)}, u32[]{:S(2)}) collective-permute-start(s16[136,512]{1,0:T(8,128)(2,1)S(1)} %get-tuple-element.22), channel_id=1, source_target_pairs={{0,4},{4,0},{1,5},{5,1},{2,6},{6,2},{3,7},{7,3},{8,12},{12,8},{9,1... | collective-permute-start | bytes 417800 | tf_op jit(solution)/shard_map/ppermute | solution.py:404
  4.9 0.0 collective-permute-start.1
  4.9 1.5 %collective-permute-start.2 = (s16[128,512]{1,0:T(8,128)(2,1)S(1)}, s16[128,512]{1,0:T(8,128)(2,1)S(1)}, u32[]{:S(2)}, u32[]{:S(2)}) collective-permute-start(s16[128,512]{1,0:T(8,128)(2,1)S(1)} %get-tuple-element.23.refs_0_), channel_id=1, source_target_pairs={{0,2},{2,0},{1,3},{3,1},{4,6},{6,4},{5,7},{7,5},{8,10},{10,8},{9,1... | collective-permute-start | bytes 393224 | tf_op jit(solution)/shard_map/ppermute | solution.py:403
  6.4 0.1 copy.8.pair_cols
  6.5 0.1 stack.20.meta
  6.6 2.2 %tables.1 = (s32[5,8]{1,0:T(8,128)S(1)}, bf16[4,256,1152]{2,1,0:T(8,128)(2,1)S(1)}, bf16[2,256,1152]{2,1,0:T(8,128)(2,1)S(1)}, bf16[2,128,1152]{2,1,0:T(8,128)(2,1)S(1)}) custom-call(s32[5]{0:T(128)S(1)} %stack.20.meta, f32[9]{0:T(128)S(1)} %copy-done.3, s32[4,2]{1,0:T(4,128)S(1)} %copy.8.pair_cols, s32[4]{0:T(128)S(1)} %copy-done.1, s32[16]{0:T(128)S(1)} %copy-done.2, ...), custom_call_target="tpu_custom_call" | custom-call | flops 10000000 | bytes 8000000 | tf_op jit(solution)/shard_map/tables/pallas_call | solution.py:315
  8.9 0.0 collective-permute-done.1.refs_2_
  8.9 0.0 collective-permute-done.first
  8.9 1.4 %collective-permute-start.4 = (s16[136,512]{1,0:T(8,128)(2,1)S(1)}, s16[136,512]{1,0:T(8,128)(2,1)S(1)}, u32[]{:S(2)}, u32[]{:S(2)}) collective-permute-start(s16[136,512]{1,0:T(8,128)(2,1)S(1)} %collective-permute-done.first), channel_id=1, source_target_pairs={{0,2},{2,0},{1,3},{3,1},{4,6},{6,4},{5,7},{7,5},{8,10},{10,8},{9,1... | collective-permute-start | bytes 417800 | tf_op jit(solution)/shard_map/ppermute | solution.py:407
  10.2 0.6 %collective-permute-done.2.refs_1_ = s16[128,512]{1,0:T(8,128)(2,1)S(1)} collective-permute-done((s16[128,512]{1,0:T(8,128)(2,1)S(1)}, s16[128,512]{1,0:T(8,128)(2,1)S(1)}, u32[]{:S(2)}, u32[]{:S(2)}) %collective-permute-start.2) | collective-permute-done | bytes 131104 | tf_op jit(solution)/shard_map/ppermute | solution.py:403
  10.8 0.0 collective-permute-start.3
  10.8 1.3 %collective-permute-done.3.refs_3_ = s16[128,512]{1,0:T(8,128)(2,1)S(1)} collective-permute-done((s16[128,512]{1,0:T(8,128)(2,1)S(1)}, s16[128,512]{1,0:T(8,128)(2,1)S(1)}, u32[]{:S(2)}, u32[]{:S(2)}) %collective-permute-start.3) | collective-permute-done | bytes 131104 | tf_op jit(solution)/shard_map/ppermute | solution.py:408
  12.2 2.9 %step.5 = (f32[2,128,512]{2,1,0:T(8,128)S(1)}, bf16[2,1152,512]{2,1,0:T(8,128)(2,1)S(1)}, bf16[2,1152,512]{2,1,0:T(8,128)(2,1)S(1)}) custom-call(s32[5,8]{1,0:T(8,128)S(1)} %get-tuple-element.28.plan, s16[128,512]{1,0:T(8,128)(2,1)S(1)} %get-tuple-element.23.refs_0_, s16[128,512]{1,0:T(8,128)(2,1)S(1)} %collective-permute-done.2.refs_1_, ...), custom_call_target="tpu_custom_call" | custom-call | flops 1000000 | bytes 100000 | tf_op jit(solution)/shard_map/step/pallas_call | solution.py:359
  15.1 0.0 collective-permute-done.4.second
  15.1 0.2 collective-permute-start.5
  15.3 1.2 %other_tables.1 = (bf16[2,128,1152]{2,1,0:T(8,128)(2,1)S(1)}, bf16[2,256,1152]{2,1,0:T(8,128)(2,1)S(1)}) custom-call(s32[5]{0:T(128)S(1)} %stack.20.meta, f32[9]{0:T(128)S(1)} %copy-done.3), custom_call_target="tpu_custom_call" | custom-call | flops 10000000 | bytes 3000000 | tf_op jit(solution)/shard_map/other_tables/pallas_call | solution.py:392
  16.5 0.2 collective-permute-done.5.refs_1_
  16.7 2.5 %step.6 = (s16[128,512]{1,0:T(8,128)(2,1)S(1)}, bf16[2,1152,512]{2,1,0:T(8,128)(2,1)S(1)}, bf16[2,1152,512]{2,1,0:T(8,128)(2,1)S(1)}) custom-call(s32[5,8]{1,0:T(8,128)S(1)} %get-tuple-element.28.plan, s16[2,128,512]{2,1,0:T(8,128)(2,1)S(1)} %join.2.refs_0_, s16[2,128,512]{2,1,0:T(8,128)(2,1)S(1)} %collective-permute-done.5.refs_1_, ...), custom_call_target="tpu_custom_call" | custom-call | flops 1000000 | bytes 100000 | tf_op jit(solution)/shard_map/step/pallas_call | solution.py:359
  19.2 1.6 %collective-permute-start.7 = (s16[128,512]{1,0:T(8,128)(2,1)S(1)}, s16[128,512]{1,0:T(8,128)(2,1)S(1)}, u32[]{:S(2)}, u32[]{:S(2)}) collective-permute-start(s16[128,512]{1,0:T(8,128)(2,1)S(1)} %get-tuple-element.41.refs_0_), channel_id=1, source_target_pairs={{0,2},{2,0},{1,3},{3,1},{4,6},{6,4},{5,7},{7,5},{8,10},{10,8},{9,1... | collective-permute-start | bytes 393224 | tf_op jit(solution)/shard_map/ppermute | solution.py:423
  20.8 2.2 %other_rows.1.first = s16[136,512]{1,0:T(8,128)(2,1)S(1)} custom-call(s32[5,8]{1,0:T(8,128)S(1)} %get-tuple-element.28.plan, bf16[2,128,1152]{2,1,0:T(8,128)(2,1)S(1)} %get-tuple-element.29.refs_0_, bf16[2,256,1152]{2,1,0:T(8,128)(2,1)S(1)} %get-tuple-element.30.refs_1_, bf16[2,1152,512]{2,1,0:T(8,128)(2,1)S(1)} %get-tuple-element.34.refs_2_, ...), custom_call_target="tpu_custom_call" | custom-call | flops 1000000 | bytes 100000 | tf_op jit(solution)/shard_map/other_rows/pallas_call | solution.py:415
  23.0 0.6 %collective-permute-start.6 = (s16[136,512]{1,0:T(8,128)(2,1)S(1)}, s16[136,512]{1,0:T(8,128)(2,1)S(1)}, u32[]{:S(2)}, u32[]{:S(2)}) collective-permute-start(s16[136,512]{1,0:T(8,128)(2,1)S(1)} %other_rows.1.first), channel_id=1, source_target_pairs={{0,2},{2,0},{1,3},{3,1},{4,6},{6,4},{5,7},{7,5},{8,10},{10,8},{9,1... | collective-permute-start | bytes 417800 | tf_op jit(solution)/shard_map/ppermute | solution.py:427
  23.6 1.3 %collective-permute-done.7.refs_1_ = s16[128,512]{1,0:T(8,128)(2,1)S(1)} collective-permute-done((s16[128,512]{1,0:T(8,128)(2,1)S(1)}, s16[128,512]{1,0:T(8,128)(2,1)S(1)}, u32[]{:S(2)}, u32[]{:S(2)}) %collective-permute-start.7) | collective-permute-done | bytes 131104 | tf_op jit(solution)/shard_map/ppermute | solution.py:423
  24.9 0.1 collective-permute-done.8.refs_2_
  24.9 1.3 %collective-permute-done.9.refs_3_ = s16[128,512]{1,0:T(8,128)(2,1)S(1)} collective-permute-done((s16[128,512]{1,0:T(8,128)(2,1)S(1)}, s16[128,512]{1,0:T(8,128)(2,1)S(1)}, u32[]{:S(2)}, u32[]{:S(2)}) %collective-permute-start.9) | collective-permute-done | bytes 131104 | tf_op jit(solution)/shard_map/ppermute | solution.py:390
  26.2 1.9 %step.7.after.refs_4_ = f32[2,128,256]{2,1,0:T(8,128)S(1)} custom-call(s32[5,8]{1,0:T(8,128)S(1)} %get-tuple-element.28.plan, s16[128,512]{1,0:T(8,128)(2,1)S(1)} %get-tuple-element.41.refs_0_, s16[128,512]{1,0:T(8,128)(2,1)S(1)} %collective-permute-done.7.refs_1_, s16[128,512]{1,0:T(8,128)(2,1)S(1)} %collective-permute-done.8.refs_2_, ...), custom_call_target="tpu_custom_call" | custom-call | flops 1000000 | bytes 100000 | tf_op jit(solution)/shard_map/step/pallas_call | solution.py:359
  28.1 0.4 %collective-permute-done.6.second = s16[136,512]{1,0:T(8,128)(2,1)S(1)} collective-permute-done((s16[136,512]{1,0:T(8,128)(2,1)S(1)}, s16[136,512]{1,0:T(8,128)(2,1)S(1)}, u32[]{:S(2)}, u32[]{:S(2)}) %collective-permute-start.6) | collective-permute-done | bytes 139296 | tf_op jit(solution)/shard_map/ppermute | solution.py:427
  28.5 0.1 collective-permute-start.10
  28.6 1.9 %step.8.refs_5_ = f32[2,128,256]{2,1,0:T(8,128)S(1)} custom-call(s32[5,8]{1,0:T(8,128)S(1)} %get-tuple-element.28.plan, s16[128,512]{1,0:T(8,128)(2,1)S(1)} %get-tuple-element.41.refs_0_, s16[128,512]{1,0:T(8,128)(2,1)S(1)} %collective-permute-done.7.refs_1_, s16[128,512]{1,0:T(8,128)(2,1)S(1)} %collective-permute-done.8.refs_2_, ...), custom_call_target="tpu_custom_call" | custom-call | flops 1000000 | bytes 100000 | tf_op jit(solution)/shard_map/step/pallas_call | solution.py:359
  30.5 0.0 collective-permute-done.10.refs_1_
  30.5 2.8 %step.9 = (f32[128,512]{1,0:T(8,128)}, f32[128,512]{1,0:T(8,128)}) custom-call(s32[5,8]{1,0:T(8,128)S(1)} %get-tuple-element.28.plan, s16[2,128,512]{2,1,0:T(8,128)(2,1)S(1)} %join.3.refs_0_, s16[2,128,512]{2,1,0:T(8,128)(2,1)S(1)} %collective-permute-done.10.refs_1_, bf16[4,256,1152]{2,1,0:T(8,128)(2,1)S(1)} %get-tuple-element.32.refs_4_.refs_2_, ...), custom_call_target="tpu_custom_call" | custom-call | flops 1000000 | bytes 100000 | tf_op jit(solution)/shard_map/step/pallas_call | solution.py:359
  (15 shorter events, 0.1 us)
Async XLA Ops:
  0.6 6.0 %copy-start.3 = (f32[9]{0:T(128)S(1)}, f32[9]{0:T(128)}, u32[]{:S(2)}) copy-start(f32[9]{0:T(128)} %phonon.3) | copy-start | bytes 112
  0.6 5.9 %copy-start.2 = (s32[16]{0:T(128)S(1)}, s32[16]{0:T(128)}, u32[]{:S(2)}) copy-start(s32[16]{0:T(128)} %block_order.1) | copy-start | bytes 196
  0.7 5.9 %copy-start.1 = (s32[4]{0:T(128)S(1)}, s32[4]{0:T(128)}, u32[]{:S(2)}) copy-start(s32[4]{0:T(128)} %pair_count.1) | copy-start | bytes 52
  0.7 1.0 %copy-start.4 = (f32[128,512]{1,0:T(8,128)S(1)}, f32[128,512]{1,0:T(8,128)}, u32[]{:S(2)}) copy-start(f32[128,512]{1,0:T(8,128)} %gap.1) | copy-start | bytes 786436
  1.6 4.8 %copy-start.5 = (s32[4,2]{0,1:T(2,128)S(1)}, s32[4,2]{0,1:T(2,128)}, u32[]{:S(2)}) copy-start(s32[4,2]{0,1:T(2,128)} %param.8) | copy-start | bytes 100
  1.6 5.0 %copy-start = (bf16[4,2,9,128,128]{4,3,2,1,0:T(8,128)(2,1)S(1)}, bf16[4,2,9,128,128]{4,3,2,1,0:T(8,128)(2,1)}, u32[]{:S(2)}) copy-start(bf16[4,2,9,128,128]{4,3,2,1,0:T(8,128)(2,1)} %coupling.1) | copy-start | bytes 7077892
  1.8 7.0 %collective-permute-start = (s16[136,512]{1,0:T(8,128)(2,1)S(1)}, s16[136,512]{1,0:T(8,128)(2,1)S(1)}, u32[]{:S(2)}, u32[]{:S(2)}) collective-permute-start(s16[136,512]{1,0:T(8,128)(2,1)S(1)} %get-tuple-element.22), channel_id=1, source_target_pairs={{0,4},{4,0},{1,5},{5,1},{2,6},{6,2},{3,7},{7,3},{8,12},{12,8},{9,1... | collective-permute-start | bytes 417800 | tf_op jit(solution)/shard_map/ppermute | solution.py:404
  4.9 3.9 %collective-permute-start.1 = (s16[128,512]{1,0:T(8,128)(2,1)S(1)}, s16[128,512]{1,0:T(8,128)(2,1)S(1)}, u32[]{:S(2)}, u32[]{:S(2)}) collective-permute-start(s16[128,512]{1,0:T(8,128)(2,1)S(1)} %get-tuple-element.23.refs_0_), channel_id=1, source_target_pairs={{0,1},{1,0},{2,3},{3,2},{4,5},{5,4},{6,7},{7,6},{8,9},{9,8},{10,11... | collective-permute-start | bytes 393224 | tf_op jit(solution)/shard_map/ppermute | solution.py:405
  4.9 5.9 %collective-permute-start.2 = (s16[128,512]{1,0:T(8,128)(2,1)S(1)}, s16[128,512]{1,0:T(8,128)(2,1)S(1)}, u32[]{:S(2)}, u32[]{:S(2)}) collective-permute-start(s16[128,512]{1,0:T(8,128)(2,1)S(1)} %get-tuple-element.23.refs_0_), channel_id=1, source_target_pairs={{0,2},{2,0},{1,3},{3,1},{4,6},{6,4},{5,7},{7,5},{8,10},{10,8},{9,1... | collective-permute-start | bytes 393224 | tf_op jit(solution)/shard_map/ppermute | solution.py:403
  8.9 6.2 %collective-permute-start.4 = (s16[136,512]{1,0:T(8,128)(2,1)S(1)}, s16[136,512]{1,0:T(8,128)(2,1)S(1)}, u32[]{:S(2)}, u32[]{:S(2)}) collective-permute-start(s16[136,512]{1,0:T(8,128)(2,1)S(1)} %collective-permute-done.first), channel_id=1, source_target_pairs={{0,2},{2,0},{1,3},{3,1},{4,6},{6,4},{5,7},{7,5},{8,10},{10,8},{9,1... | collective-permute-start | bytes 417800 | tf_op jit(solution)/shard_map/ppermute | solution.py:407
  10.8 1.3 %collective-permute-start.3 = (s16[128,512]{1,0:T(8,128)(2,1)S(1)}, s16[128,512]{1,0:T(8,128)(2,1)S(1)}, u32[]{:S(2)}, u32[]{:S(2)}) collective-permute-start(s16[128,512]{1,0:T(8,128)(2,1)S(1)} %collective-permute-done.2.refs_1_), channel_id=1, source_target_pairs={{0,1},{1,0},{2,3},{3,2},{4,5},{5,4},{6,7},{7,6},{8,9},{9,8},{10,11... | collective-permute-start | bytes 393224 | tf_op jit(solution)/shard_map/ppermute | solution.py:408
  15.1 1.6 %collective-permute-start.5 = (s16[2,128,512]{2,1,0:T(8,128)(2,1)S(1)}, s16[2,128,512]{2,1,0:T(8,128)(2,1)S(1)}, u32[]{:S(2)}, u32[]{:S(2)}) collective-permute-start(s16[2,128,512]{2,1,0:T(8,128)(2,1)S(1)} %join.2.refs_0_), channel_id=1, source_target_pairs={{0,1},{1,0},{2,3},{3,2},{4,5},{5,4},{6,7},{7,6},{8,9},{9,8},{10,11... | collective-permute-start | bytes 786440 | tf_op jit(solution)/shard_map/ppermute | solution.py:411
  19.2 5.6 %collective-permute-start.7 = (s16[128,512]{1,0:T(8,128)(2,1)S(1)}, s16[128,512]{1,0:T(8,128)(2,1)S(1)}, u32[]{:S(2)}, u32[]{:S(2)}) collective-permute-start(s16[128,512]{1,0:T(8,128)(2,1)S(1)} %get-tuple-element.41.refs_0_), channel_id=1, source_target_pairs={{0,2},{2,0},{1,3},{3,1},{4,6},{6,4},{5,7},{7,5},{8,10},{10,8},{9,1... | collective-permute-start | bytes 393224 | tf_op jit(solution)/shard_map/ppermute | solution.py:423
  23.0 5.5 %collective-permute-start.6 = (s16[136,512]{1,0:T(8,128)(2,1)S(1)}, s16[136,512]{1,0:T(8,128)(2,1)S(1)}, u32[]{:S(2)}, u32[]{:S(2)}) collective-permute-start(s16[136,512]{1,0:T(8,128)(2,1)S(1)} %other_rows.1.first), channel_id=1, source_target_pairs={{0,2},{2,0},{1,3},{3,1},{4,6},{6,4},{5,7},{7,5},{8,10},{10,8},{9,1... | collective-permute-start | bytes 417800 | tf_op jit(solution)/shard_map/ppermute | solution.py:427
  23.6 1.3 %collective-permute-start.8 = (s16[128,512]{1,0:T(8,128)(2,1)S(1)}, s16[128,512]{1,0:T(8,128)(2,1)S(1)}, u32[]{:S(2)}, u32[]{:S(2)}) collective-permute-start(s16[128,512]{1,0:T(8,128)(2,1)S(1)} %get-tuple-element.41.refs_0_), channel_id=1, source_target_pairs={{0,1},{1,0},{2,3},{3,2},{4,5},{5,4},{6,7},{7,6},{8,9},{9,8},{10,11... | collective-permute-start | bytes 393224 | tf_op jit(solution)/shard_map/ppermute | solution.py:390
  24.9 1.3 %collective-permute-start.9 = (s16[128,512]{1,0:T(8,128)(2,1)S(1)}, s16[128,512]{1,0:T(8,128)(2,1)S(1)}, u32[]{:S(2)}, u32[]{:S(2)}) collective-permute-start(s16[128,512]{1,0:T(8,128)(2,1)S(1)} %collective-permute-done.7.refs_1_), channel_id=1, source_target_pairs={{0,1},{1,0},{2,3},{3,2},{4,5},{5,4},{6,7},{7,6},{8,9},{9,8},{10,11... | collective-permute-start | bytes 393224 | tf_op jit(solution)/shard_map/ppermute | solution.py:390
  28.5 1.9 %collective-permute-start.10 = (s16[2,128,512]{2,1,0:T(8,128)(2,1)S(1)}, s16[2,128,512]{2,1,0:T(8,128)(2,1)S(1)}, u32[]{:S(2)}, u32[]{:S(2)}) collective-permute-start(s16[2,128,512]{2,1,0:T(8,128)(2,1)S(1)} %join.3.refs_0_), channel_id=1, source_target_pairs={{0,1},{1,0},{2,3},{3,2},{4,5},{5,4},{6,7},{7,6},{8,9},{9,8},{10,11... | collective-permute-start | bytes 786440 | tf_op jit(solution)/shard_map/ppermute | solution.py:429

commit v15 on v12

--- a/solution.py
+++ b/solution.py
@@ -139,9 +139,9 @@
     def fetch(pair):
         column = pl.multiple_of(plan[PLACE, pair] * size, size)
         wanted = plan[SIDE, pair] * holders + plan[HOLDER, pair]
-        value = pieces[0][:, pl.ds(column, size)]
+        value = pieces[0][:segment_rows, pl.ds(column, size)]
         for at in range(1, len(pieces)):
-            value = lax.select(wanted == at, pieces[at][:, pl.ds(column, size)], value)
+            value = lax.select(wanted == at, pieces[at][:segment_rows, pl.ds(column, size)], value)
         return decoded(value) if coded else value
 
     def find_ratios(block):
@@ -417,11 +417,11 @@
     )(plan, *inputs)
     along_x = lax.ppermute(own, "x", SWAP)
     near = with_core([own, along_x])
-    middle = blocks // 2
-    partial = step(plan, 0, True, near, [], span=(0, middle))
-    far = join(other, lax.ppermute(other, "x", SWAP), *partial)
-    partial += step(plan, 0, True, near, [], span=(middle, blocks))
-    return tuple(step(plan, 1, True, [far, lax.ppermute(far, "core", SWAP)], partial))
+    across = lax.ppermute(other, "core", SWAP)
+    partial = step(plan, 0, True, near, [])
+    along_x, *partial = lax.optimization_barrier((lax.ppermute(other, "x", SWAP), *partial))
+    far = [other, along_x, across, lax.ppermute(along_x, "core", SWAP)]
+    return tuple(step(plan, 1, True, far, partial))
 
 
 def solution(mesh):

time: 33 us -> 33.4 us (1.012)
  starting transfers between devices: 7.81 us -> 8.46 us
  Pallas kernels: 17.6 us -> 17 us
  waiting for transfers between devices: 5.4 us -> 5.88 us
    ppermute x2 -> x3, waiting for transfers between devices: 0.21 us -> 1.23 us  [the longest x1 1.23 us: on_device(): far = [other, along_x, across, lax.ppermute(along_x, 'core', SWAP)]]
    ppermute x2 -> x3, starting transfers between devices: 1.09 us -> 1.75 us  [the longest x1 1.04 us: on_device(): lax.ppermute(other, 'x', SWAP)]
    pallas_call x5 -> x4, Pallas kernels: 11.9 us -> 11.2 us  [step(): pl.pallas_call(functools.partial(step_kernel, dims, segment, span, sides,...]
    ppermute x4, waiting for transfers between devices: 1.62 us -> 1.11 us  [with_core(): return near + [lax.ppermute(piece, 'core', SWAP) for piece in near]]
  transfers between devices with their start and end apart: 11 -> 12, of which waited for: 8 -> 7; matrix products, arithmetic and copies ran while one was open for 1% -> 1% of each run, Pallas kernels for 37% -> 35%
where the time goes in v15:
time: 33.4 us; the launch traced here: 33.2 us
  Pallas kernels  17 us (51%)
  starting transfers between devices  8.46 us (25%)
  waiting for transfers between devices  5.88 us (18%)
  local copies, waits for them, and re-layouts  1.16 us (3%)
  between operations  0.76 us (2%)
    pallas_call x4, Pallas kernels, step(): pl.pallas_call(functools.partial(step_kernel, dims, segment, span, sides,...  11.2 us
    ppermute x1, starting transfers between devices, on_device(): along_x = lax.ppermute(passed, 'x', SWAP)  3 us
    pallas_call x1, Pallas kernels, on_device(): pl.pallas_call(functools.partial(tables_kernel, dims, sides), out_shape=[...  2.25 us
    pallas_call x1, Pallas kernels, on_device(): pl.pallas_call(functools.partial(other_rows_kernel, dims), out_shape=jax....  2.2 us
    ppermute x1, starting transfers between devices, on_device(): along_z = lax.ppermute(passed, 'zlo', SWAP)  1.58 us
    ppermute x1, waiting for transfers between devices, on_device(): relayed = lax.ppermute(along_z, 'x', SWAP)  1.57 us
    ppermute x1, waiting for transfers between devices, on_device(): along_x = lax.ppermute(own, 'x', SWAP)  1.27 us
    ppermute x1, waiting for transfers between devices, on_device(): far = [other, along_x, across, lax.ppermute(along_x, 'core', SWAP)]  1.23 us
  transfers between devices with their start and end apart: 12, of which 7 were waited for; matrix products, arithmetic and copies ran while one was open for 1% of the time, Pallas kernels for 35%

profile of v15, /device:TPU:0, one launch (start us, length us, event | category | flops | bytes accessed | tf_op | source)
XLA Modules:
  0.0 33.2 jit_solution(4332817245039226130)
XLA Ops:
  0.7 1.0 %copy-done.4 = f32[128,512]{1,0:T(8,128)S(1)} copy-done((f32[128,512]{1,0:T(8,128)S(1)}, f32[128,512]{1,0:T(8,128)}, u32[]{:S(2)}) %copy-start.4) | copy-done | bytes 262168
  1.6 0.1 encode.1.refs_0_
  1.8 3.0 %collective-permute-start = (s16[128,512]{1,0:T(8,128)(2,1)S(1)}, s16[128,512]{1,0:T(8,128)(2,1)S(1)}, u32[]{:S(2)}, u32[]{:S(2)}) collective-permute-start(s16[128,512]{1,0:T(8,128)(2,1)S(1)} %encode.1.refs_0_), channel_id=1, source_target_pairs={{0,2},{2,0},{1,3},{3,1},{4,6},{6,4},{5,7},{7,5},{8,10},{10,8},{9,1... | collective-permute-start | bytes 393224 | tf_op jit(solution)/shard_map/ppermute | solution.py:400
  4.8 1.6 %collective-permute-start.3 = (s16[128,512]{1,0:T(8,128)(2,1)S(1)}, s16[128,512]{1,0:T(8,128)(2,1)S(1)}, u32[]{:S(2)}, u32[]{:S(2)}) collective-permute-start(s16[128,512]{1,0:T(8,128)(2,1)S(1)} %encode.1.refs_0_), channel_id=1, source_target_pairs={{0,4},{4,0},{1,5},{5,1},{2,6},{6,2},{3,7},{7,3},{8,12},{12,8},{9,1... | collective-permute-start | bytes 393224 | tf_op jit(solution)/shard_map/ppermute | solution.py:401
  6.4 0.0 collective-permute-start.1
  6.4 0.1 copy.8.pair_cols
  6.5 0.1 stack.20.meta
  6.6 2.2 %tables.1 = (s32[5,8]{1,0:T(8,128)S(1)}, bf16[4,256,1152]{2,1,0:T(8,128)(2,1)S(1)}, bf16[2,256,1152]{2,1,0:T(8,128)(2,1)S(1)}, bf16[2,128,1152]{2,1,0:T(8,128)(2,1)S(1)}) custom-call(s32[5]{0:T(128)S(1)} %stack.20.meta, f32[9]{0:T(128)S(1)} %copy-done.3, s32[4,2]{1,0:T(4,128)S(1)} %copy.8.pair_cols, s32[4]{0:T(128)S(1)} %copy-done.1, s32[16]{0:T(128)S(1)} %copy-done.2, ...), custom_call_target="tpu_custom_call" | custom-call | flops 10000000 | bytes 8000000 | tf_op jit(solution)/shard_map/tables/pallas_call | solution.py:312
  8.8 0.0 collective-permute-done.refs_1_
  8.8 0.6 %collective-permute-start.2 = (s16[128,512]{1,0:T(8,128)(2,1)S(1)}, s16[128,512]{1,0:T(8,128)(2,1)S(1)}, u32[]{:S(2)}, u32[]{:S(2)}) collective-permute-start(s16[128,512]{1,0:T(8,128)(2,1)S(1)} %collective-permute-done.refs_1_), channel_id=1, source_target_pairs={{0,1},{1,0},{2,3},{3,2},{4,5},{5,4},{6,7},{7,6},{8,9},{9,8},{10,11... | collective-permute-start | bytes 393224 | tf_op jit(solution)/shard_map/ppermute | solution.py:387
  9.4 0.4 %collective-permute-done.3.first = s16[128,512]{1,0:T(8,128)(2,1)S(1)} collective-permute-done((s16[128,512]{1,0:T(8,128)(2,1)S(1)}, s16[128,512]{1,0:T(8,128)(2,1)S(1)}, u32[]{:S(2)}, u32[]{:S(2)}) %collective-permute-start.3) | collective-permute-done | bytes 131104 | tf_op jit(solution)/shard_map/ppermute | solution.py:401
  9.8 0.4 %collective-permute-start.4 = (s16[128,512]{1,0:T(8,128)(2,1)S(1)}, s16[128,512]{1,0:T(8,128)(2,1)S(1)}, u32[]{:S(2)}, u32[]{:S(2)}) collective-permute-start(s16[128,512]{1,0:T(8,128)(2,1)S(1)} %collective-permute-done.3.first), channel_id=1, source_target_pairs={{0,2},{2,0},{1,3},{3,1},{4,6},{6,4},{5,7},{7,5},{8,10},{10,8},{9,1... | collective-permute-start | bytes 393224 | tf_op jit(solution)/shard_map/ppermute | solution.py:403
  10.1 0.3 collective-permute-done.2.refs_3_
  10.4 2.9 %step.4 = (f32[2,128,512]{2,1,0:T(8,128)S(1)}, bf16[2,1152,512]{2,1,0:T(8,128)(2,1)S(1)}, bf16[2,1152,512]{2,1,0:T(8,128)(2,1)S(1)}) custom-call(s32[5,8]{1,0:T(8,128)S(1)} %get-tuple-element.25.plan, s16[128,512]{1,0:T(8,128)(2,1)S(1)} %encode.1.refs_0_, s16[128,512]{1,0:T(8,128)(2,1)S(1)} %collective-permute-done.refs_1_, ...), custom_call_target="tpu_custom_call" | custom-call | flops 1000000 | bytes 100000 | tf_op jit(solution)/shard_map/step/pallas_call | solution.py:356
  13.3 1.6 %collective-permute-done.4.second = s16[128,512]{1,0:T(8,128)(2,1)S(1)} collective-permute-done((s16[128,512]{1,0:T(8,128)(2,1)S(1)}, s16[128,512]{1,0:T(8,128)(2,1)S(1)}, u32[]{:S(2)}, u32[]{:S(2)}) %collective-permute-start.4) | collective-permute-done | bytes 131104 | tf_op jit(solution)/shard_map/ppermute | solution.py:403
  14.9 0.1 collective-permute-start.5
  15.0 1.2 %other_tables.1 = (bf16[2,128,1152]{2,1,0:T(8,128)(2,1)S(1)}, bf16[2,256,1152]{2,1,0:T(8,128)(2,1)S(1)}) custom-call(s32[5]{0:T(128)S(1)} %stack.20.meta, f32[9]{0:T(128)S(1)} %copy-done.3), custom_call_target="tpu_custom_call" | custom-call | flops 10000000 | bytes 3000000 | tf_op jit(solution)/shard_map/other_tables/pallas_call | solution.py:389
  16.2 0.3 %collective-permute-done.5.refs_1_ = s16[2,128,512]{2,1,0:T(8,128)(2,1)S(1)} collective-permute-done((s16[2,128,512]{2,1,0:T(8,128)(2,1)S(1)}, s16[2,128,512]{2,1,0:T(8,128)(2,1)S(1)}, u32[]{:S(2)}, u32[]{:S(2)}) %collective-permute-start.5) | collective-permute-done | bytes 262176 | tf_op jit(solution)/shard_map/ppermute | solution.py:406
  16.5 2.5 %step.5 = (s16[128,512]{1,0:T(8,128)(2,1)S(1)}, bf16[2,1152,512]{2,1,0:T(8,128)(2,1)S(1)}, bf16[2,1152,512]{2,1,0:T(8,128)(2,1)S(1)}) custom-call(s32[5,8]{1,0:T(8,128)S(1)} %get-tuple-element.25.plan, s16[2,128,512]{2,1,0:T(8,128)(2,1)S(1)} %join.1.refs_0_, s16[2,128,512]{2,1,0:T(8,128)(2,1)S(1)} %collective-permute-done.5.refs_1_, ...), custom_call_target="tpu_custom_call" | custom-call | flops 1000000 | bytes 100000 | tf_op jit(solution)/shard_map/step/pallas_call | solution.py:356
  19.0 1.1 %collective-permute-start.7 = (s16[128,512]{1,0:T(8,128)(2,1)S(1)}, s16[128,512]{1,0:T(8,128)(2,1)S(1)}, u32[]{:S(2)}, u32[]{:S(2)}) collective-permute-start(s16[128,512]{1,0:T(8,128)(2,1)S(1)} %get-tuple-element.37.refs_0_), channel_id=1, source_target_pairs={{0,2},{2,0},{1,3},{3,1},{4,6},{6,4},{5,7},{7,5},{8,10},{10,8},{9,1... | collective-permute-start | bytes 393224 | tf_op jit(solution)/shard_map/ppermute | solution.py:418
  20.1 2.2 %other_rows.1.refs_0_ = s16[144,512]{1,0:T(8,128)(2,1)S(1)} custom-call(s32[5,8]{1,0:T(8,128)S(1)} %get-tuple-element.25.plan, bf16[2,128,1152]{2,1,0:T(8,128)(2,1)S(1)} %get-tuple-element.26.refs_0_, bf16[2,256,1152]{2,1,0:T(8,128)(2,1)S(1)} %get-tuple-element.27.refs_1_, bf16[2,1152,512]{2,1,0:T(8,128)(2,1)S(1)} %get-tuple-element.31.refs_2_, ...), custom_call_target="tpu_custom_call" | custom-call | flops 1000000 | bytes 100000 | tf_op jit(solution)/shard_map/other_rows/pallas_call | solution.py:410
  22.3 1.0 %collective-permute-start.6 = (s16[144,512]{1,0:T(8,128)(2,1)S(1)}, s16[144,512]{1,0:T(8,128)(2,1)S(1)}, u32[]{:S(2)}, u32[]{:S(2)}) collective-permute-start(s16[144,512]{1,0:T(8,128)(2,1)S(1)} %other_rows.1.refs_0_), channel_id=1, source_target_pairs={{0,2},{2,0},{1,3},{3,1},{4,6},{6,4},{5,7},{7,5},{8,10},{10,8},{9,1... | collective-permute-start | bytes 442376 | tf_op jit(solution)/shard_map/ppermute | solution.py:422
  23.4 1.3 %collective-permute-done.7.refs_1_ = s16[128,512]{1,0:T(8,128)(2,1)S(1)} collective-permute-done((s16[128,512]{1,0:T(8,128)(2,1)S(1)}, s16[128,512]{1,0:T(8,128)(2,1)S(1)}, u32[]{:S(2)}, u32[]{:S(2)}) %collective-permute-start.7) | collective-permute-done | bytes 131104 | tf_op jit(solution)/shard_map/ppermute | solution.py:418
  24.6 0.0 collective-permute-start.9
  24.6 0.5 %collective-permute-start.10 = (s16[144,512]{1,0:T(8,128)(2,1)S(1)}, s16[144,512]{1,0:T(8,128)(2,1)S(1)}, u32[]{:S(2)}, u32[]{:S(2)}) collective-permute-start(s16[144,512]{1,0:T(8,128)(2,1)S(1)} %other_rows.1.refs_0_), channel_id=1, source_target_pairs={{0,1},{1,0},{2,3},{3,2},{4,5},{5,4},{6,7},{7,6},{8,9},{9,8},{10,11... | collective-permute-start | bytes 442376 | tf_op jit(solution)/shard_map/ppermute | solution.py:420
  25.1 0.0 collective-permute-done.8.refs_2_
  25.1 0.8 %collective-permute-done.9.refs_3_ = s16[128,512]{1,0:T(8,128)(2,1)S(1)} collective-permute-done((s16[128,512]{1,0:T(8,128)(2,1)S(1)}, s16[128,512]{1,0:T(8,128)(2,1)S(1)}, u32[]{:S(2)}, u32[]{:S(2)}) %collective-permute-start.9) | collective-permute-done | bytes 131104 | tf_op jit(solution)/shard_map/ppermute | solution.py:387
  26.0 3.0 %step.6.refs_6_ = f32[2,128,512]{2,1,0:T(8,128)S(1)} custom-call(s32[5,8]{1,0:T(8,128)S(1)} %get-tuple-element.25.plan, s16[128,512]{1,0:T(8,128)(2,1)S(1)} %get-tuple-element.37.refs_0_, s16[128,512]{1,0:T(8,128)(2,1)S(1)} %collective-permute-done.7.refs_1_, s16[128,512]{1,0:T(8,128)(2,1)S(1)} %collective-permute-done.8.refs_2_, ...), custom_call_target="tpu_custom_call" | custom-call | flops 1000000 | bytes 100000 | tf_op jit(solution)/shard_map/step/pallas_call | solution.py:356
  29.0 0.0 collective-permute-done.6.refs_1_
  29.0 0.2 collective-permute-start.11
  29.2 1.2 %collective-permute-done.11.refs_3_ = s16[144,512]{1,0:T(8,128)(2,1)S(1)} collective-permute-done((s16[144,512]{1,0:T(8,128)(2,1)S(1)}, s16[144,512]{1,0:T(8,128)(2,1)S(1)}, u32[]{:S(2)}, u32[]{:S(2)}) %collective-permute-start.11) | collective-permute-done | bytes 147488 | tf_op jit(solution)/shard_map/ppermute | solution.py:423
  30.4 2.8 %step.7 = (f32[128,512]{1,0:T(8,128)}, f32[128,512]{1,0:T(8,128)}) custom-call(s32[5,8]{1,0:T(8,128)S(1)} %get-tuple-element.25.plan, s16[144,512]{1,0:T(8,128)(2,1)S(1)} %other_rows.1.refs_0_, s16[144,512]{1,0:T(8,128)(2,1)S(1)} %collective-permute-done.6.refs_1_, s16[144,512]{1,0:T(8,128)(2,1)S(1)} %collective-permute-done.10.refs_2_, ...), custom_call_target="tpu_custom_call" | custom-call | flops 1000000 | bytes 100000 | tf_op jit(solution)/shard_map/step/pallas_call | solution.py:356
  (15 shorter events, 0.0 us)
Async XLA Ops:
  0.6 5.9 %copy-start.3 = (f32[9]{0:T(128)S(1)}, f32[9]{0:T(128)}, u32[]{:S(2)}) copy-start(f32[9]{0:T(128)} %phonon.3) | copy-start | bytes 112
  0.6 5.9 %copy-start.2 = (s32[16]{0:T(128)S(1)}, s32[16]{0:T(128)}, u32[]{:S(2)}) copy-start(s32[16]{0:T(128)} %block_order.1) | copy-start | bytes 196
  0.7 5.9 %copy-start.1 = (s32[4]{0:T(128)S(1)}, s32[4]{0:T(128)}, u32[]{:S(2)}) copy-start(s32[4]{0:T(128)} %pair_count.1) | copy-start | bytes 52
  0.7 1.0 %copy-start.4 = (f32[128,512]{1,0:T(8,128)S(1)}, f32[128,512]{1,0:T(8,128)}, u32[]{:S(2)}) copy-start(f32[128,512]{1,0:T(8,128)} %gap.1) | copy-start | bytes 786436
  1.6 4.7 %copy-start.5 = (s32[4,2]{0,1:T(2,128)S(1)}, s32[4,2]{0,1:T(2,128)}, u32[]{:S(2)}) copy-start(s32[4,2]{0,1:T(2,128)} %param.8) | copy-start | bytes 100
  1.6 4.9 %copy-start = (bf16[4,2,9,128,128]{4,3,2,1,0:T(8,128)(2,1)S(1)}, bf16[4,2,9,128,128]{4,3,2,1,0:T(8,128)(2,1)}, u32[]{:S(2)}) copy-start(bf16[4,2,9,128,128]{4,3,2,1,0:T(8,128)(2,1)} %coupling.1) | copy-start | bytes 7077892
  1.8 7.0 %collective-permute-start = (s16[128,512]{1,0:T(8,128)(2,1)S(1)}, s16[128,512]{1,0:T(8,128)(2,1)S(1)}, u32[]{:S(2)}, u32[]{:S(2)}) collective-permute-start(s16[128,512]{1,0:T(8,128)(2,1)S(1)} %encode.1.refs_0_), channel_id=1, source_target_pairs={{0,2},{2,0},{1,3},{3,1},{4,6},{6,4},{5,7},{7,5},{8,10},{10,8},{9,1... | collective-permute-start | bytes 393224 | tf_op jit(solution)/shard_map/ppermute | solution.py:400
  4.8 5.0 %collective-permute-start.3 = (s16[128,512]{1,0:T(8,128)(2,1)S(1)}, s16[128,512]{1,0:T(8,128)(2,1)S(1)}, u32[]{:S(2)}, u32[]{:S(2)}) collective-permute-start(s16[128,512]{1,0:T(8,128)(2,1)S(1)} %encode.1.refs_0_), channel_id=1, source_target_pairs={{0,4},{4,0},{1,5},{5,1},{2,6},{6,2},{3,7},{7,3},{8,12},{12,8},{9,1... | collective-permute-start | bytes 393224 | tf_op jit(solution)/shard_map/ppermute | solution.py:401
  6.4 3.8 %collective-permute-start.1 = (s16[128,512]{1,0:T(8,128)(2,1)S(1)}, s16[128,512]{1,0:T(8,128)(2,1)S(1)}, u32[]{:S(2)}, u32[]{:S(2)}) collective-permute-start(s16[128,512]{1,0:T(8,128)(2,1)S(1)} %encode.1.refs_0_), channel_id=1, source_target_pairs={{0,1},{1,0},{2,3},{3,2},{4,5},{5,4},{6,7},{7,6},{8,9},{9,8},{10,11... | collective-permute-start | bytes 393224 | tf_op jit(solution)/shard_map/ppermute | solution.py:387
  8.8 1.6 %collective-permute-start.2 = (s16[128,512]{1,0:T(8,128)(2,1)S(1)}, s16[128,512]{1,0:T(8,128)(2,1)S(1)}, u32[]{:S(2)}, u32[]{:S(2)}) collective-permute-start(s16[128,512]{1,0:T(8,128)(2,1)S(1)} %collective-permute-done.refs_1_), channel_id=1, source_target_pairs={{0,1},{1,0},{2,3},{3,2},{4,5},{5,4},{6,7},{7,6},{8,9},{9,8},{10,11... | collective-permute-start | bytes 393224 | tf_op jit(solution)/shard_map/ppermute | solution.py:387
  9.8 5.1 %collective-permute-start.4 = (s16[128,512]{1,0:T(8,128)(2,1)S(1)}, s16[128,512]{1,0:T(8,128)(2,1)S(1)}, u32[]{:S(2)}, u32[]{:S(2)}) collective-permute-start(s16[128,512]{1,0:T(8,128)(2,1)S(1)} %collective-permute-done.3.first), channel_id=1, source_target_pairs={{0,2},{2,0},{1,3},{3,1},{4,6},{6,4},{5,7},{7,5},{8,10},{10,8},{9,1... | collective-permute-start | bytes 393224 | tf_op jit(solution)/shard_map/ppermute | solution.py:403
  14.9 1.6 %collective-permute-start.5 = (s16[2,128,512]{2,1,0:T(8,128)(2,1)S(1)}, s16[2,128,512]{2,1,0:T(8,128)(2,1)S(1)}, u32[]{:S(2)}, u32[]{:S(2)}) collective-permute-start(s16[2,128,512]{2,1,0:T(8,128)(2,1)S(1)} %join.1.refs_0_), channel_id=1, source_target_pairs={{0,1},{1,0},{2,3},{3,2},{4,5},{5,4},{6,7},{7,6},{8,9},{9,8},{10,11... | collective-permute-start | bytes 786440 | tf_op jit(solution)/shard_map/ppermute | solution.py:406
  19.0 5.6 %collective-permute-start.7 = (s16[128,512]{1,0:T(8,128)(2,1)S(1)}, s16[128,512]{1,0:T(8,128)(2,1)S(1)}, u32[]{:S(2)}, u32[]{:S(2)}) collective-permute-start(s16[128,512]{1,0:T(8,128)(2,1)S(1)} %get-tuple-element.37.refs_0_), channel_id=1, source_target_pairs={{0,2},{2,0},{1,3},{3,1},{4,6},{6,4},{5,7},{7,5},{8,10},{10,8},{9,1... | collective-permute-start | bytes 393224 | tf_op jit(solution)/shard_map/ppermute | solution.py:418
  22.3 6.7 %collective-permute-start.6 = (s16[144,512]{1,0:T(8,128)(2,1)S(1)}, s16[144,512]{1,0:T(8,128)(2,1)S(1)}, u32[]{:S(2)}, u32[]{:S(2)}) collective-permute-start(s16[144,512]{1,0:T(8,128)(2,1)S(1)} %other_rows.1.refs_0_), channel_id=1, source_target_pairs={{0,2},{2,0},{1,3},{3,1},{4,6},{6,4},{5,7},{7,5},{8,10},{10,8},{9,1... | collective-permute-start | bytes 442376 | tf_op jit(solution)/shard_map/ppermute | solution.py:422
  23.4 1.8 %collective-permute-start.8 = (s16[128,512]{1,0:T(8,128)(2,1)S(1)}, s16[128,512]{1,0:T(8,128)(2,1)S(1)}, u32[]{:S(2)}, u32[]{:S(2)}) collective-permute-start(s16[128,512]{1,0:T(8,128)(2,1)S(1)} %get-tuple-element.37.refs_0_), channel_id=1, source_target_pairs={{0,1},{1,0},{2,3},{3,2},{4,5},{5,4},{6,7},{7,6},{8,9},{9,8},{10,11... | collective-permute-start | bytes 393224 | tf_op jit(solution)/shard_map/ppermute | solution.py:387
  24.6 1.3 %collective-permute-start.9 = (s16[128,512]{1,0:T(8,128)(2,1)S(1)}, s16[128,512]{1,0:T(8,128)(2,1)S(1)}, u32[]{:S(2)}, u32[]{:S(2)}) collective-permute-start(s16[128,512]{1,0:T(8,128)(2,1)S(1)} %collective-permute-done.7.refs_1_), channel_id=1, source_target_pairs={{0,1},{1,0},{2,3},{3,2},{4,5},{5,4},{6,7},{7,6},{8,9},{9,8},{10,11... | collective-permute-start | bytes 393224 | tf_op jit(solution)/shard_map/ppermute | solution.py:387
  24.6 4.6 %collective-permute-start.10 = (s16[144,512]{1,0:T(8,128)(2,1)S(1)}, s16[144,512]{1,0:T(8,128)(2,1)S(1)}, u32[]{:S(2)}, u32[]{:S(2)}) collective-permute-start(s16[144,512]{1,0:T(8,128)(2,1)S(1)} %other_rows.1.refs_0_), channel_id=1, source_target_pairs={{0,1},{1,0},{2,3},{3,2},{4,5},{5,4},{6,7},{7,6},{8,9},{9,8},{10,11... | collective-permute-start | bytes 442376 | tf_op jit(solution)/shard_map/ppermute | solution.py:420
  29.0 1.4 %collective-permute-start.11 = (s16[144,512]{1,0:T(8,128)(2,1)S(1)}, s16[144,512]{1,0:T(8,128)(2,1)S(1)}, u32[]{:S(2)}, u32[]{:S(2)}) collective-permute-start(s16[144,512]{1,0:T(8,128)(2,1)S(1)} %collective-permute-done.6.refs_1_), channel_id=1, source_target_pairs={{0,1},{1,0},{2,3},{3,2},{4,5},{5,4},{6,7},{7,6},{8,9},{9,8},{10,11... | collective-permute-start | bytes 442376 | tf_op jit(solution)/shard_map/ppermute | solution.py:423

commit v16 on v12

--- a/solution.py
+++ b/solution.py
@@ -402,8 +402,9 @@
     along_x, plan = lax.optimization_barrier((along_x, plan))
     relayed = lax.ppermute(along_z, "x", SWAP)
     partial, *near_terms = step(plan, 0, False, with_core([passed, along_x]), [], keep=True)
-    far = join(along_z, relayed, partial)
-    pieces = [far, lax.ppermute(far, "core", SWAP)]
+    across = lax.ppermute(along_z, "core", SWAP)
+    relayed, partial = lax.optimization_barrier((relayed, partial))
+    pieces = [along_z, relayed, across, lax.ppermute(relayed, "core", SWAP)]
     plan, *other_tables = lax.optimization_barrier((plan, *other_tables))
     own, *far_terms = step(plan, 1, False, pieces, [partial], keep=True)
     inputs = [*other_tables, *near_terms, *far_terms]

time: 33 us -> 32.9 us (level)
  transfers between devices with their start and end apart: 11 -> 12, of which waited for: 8 -> 7; matrix products, arithmetic and copies ran while one was open for 1% -> 1% of each run, Pallas kernels for 37% -> 37%
where the time goes in v16:
time: 32.9 us; the launch traced here: 32.7 us
  Pallas kernels  17.7 us (54%)
  starting transfers between devices  7.92 us (24%)
  waiting for transfers between devices  5.22 us (16%)
  local copies, waits for them, and re-layouts  1.16 us (4%)
  between operations  0.76 us (2%)
    pallas_call x5, Pallas kernels, step(): pl.pallas_call(functools.partial(step_kernel, dims, segment, span, sides,...  11.9 us
    ppermute x1, starting transfers between devices, on_device(): along_x = lax.ppermute(passed, 'x', SWAP)  3 us
    pallas_call x1, Pallas kernels, on_device(): pl.pallas_call(functools.partial(tables_kernel, dims, sides), out_shape=[...  2.25 us
    pallas_call x1, Pallas kernels, on_device(): pl.pallas_call(functools.partial(other_rows_kernel, dims), out_shape=jax....  2.2 us
    ppermute x1, waiting for transfers between devices, on_device(): relayed = lax.ppermute(along_z, 'x', SWAP)  1.59 us
    ppermute x1, starting transfers between devices, on_device(): along_z = lax.ppermute(passed, 'zlo', SWAP)  1.58 us
    ppermute x4, waiting for transfers between devices, with_core(): return near + [lax.ppermute(piece, 'core', SWAP) for piece in near]  1.46 us
    ppermute x1, waiting for transfers between devices, on_device(): along_x = lax.ppermute(own, 'x', SWAP)  1.45 us
  transfers between devices with their start and end apart: 12, of which 7 were waited for; matrix products, arithmetic and copies ran while one was open for 1% of the time, Pallas kernels for 37%

profile of v16, /device:TPU:0, one launch (start us, length us, event | category | flops | bytes accessed | tf_op | source)
XLA Modules:
  0.0 32.7 jit_solution(5824577267717926900)
XLA Ops:
  0.7 1.0 %copy-done.4 = f32[128,512]{1,0:T(8,128)S(1)} copy-done((f32[128,512]{1,0:T(8,128)S(1)}, f32[128,512]{1,0:T(8,128)}, u32[]{:S(2)}) %copy-start.4) | copy-done | bytes 262168
  1.6 0.1 encode.1.refs_0_
  1.8 3.0 %collective-permute-start = (s16[128,512]{1,0:T(8,128)(2,1)S(1)}, s16[128,512]{1,0:T(8,128)(2,1)S(1)}, u32[]{:S(2)}, u32[]{:S(2)}) collective-permute-start(s16[128,512]{1,0:T(8,128)(2,1)S(1)} %encode.1.refs_0_), channel_id=1, source_target_pairs={{0,2},{2,0},{1,3},{3,1},{4,6},{6,4},{5,7},{7,5},{8,10},{10,8},{9,1... | collective-permute-start | bytes 393224 | tf_op jit(solution)/shard_map/ppermute | solution.py:400
  4.8 1.6 %collective-permute-start.3 = (s16[128,512]{1,0:T(8,128)(2,1)S(1)}, s16[128,512]{1,0:T(8,128)(2,1)S(1)}, u32[]{:S(2)}, u32[]{:S(2)}) collective-permute-start(s16[128,512]{1,0:T(8,128)(2,1)S(1)} %encode.1.refs_0_), channel_id=1, source_target_pairs={{0,4},{4,0},{1,5},{5,1},{2,6},{6,2},{3,7},{7,3},{8,12},{12,8},{9,1... | collective-permute-start | bytes 393224 | tf_op jit(solution)/shard_map/ppermute | solution.py:401
  6.4 0.0 collective-permute-start.1
  6.4 0.1 copy.8.pair_cols
  6.5 0.1 stack.20.meta
  6.6 2.2 %tables.1 = (s32[5,8]{1,0:T(8,128)S(1)}, bf16[4,256,1152]{2,1,0:T(8,128)(2,1)S(1)}, bf16[2,256,1152]{2,1,0:T(8,128)(2,1)S(1)}, bf16[2,128,1152]{2,1,0:T(8,128)(2,1)S(1)}) custom-call(s32[5]{0:T(128)S(1)} %stack.20.meta, f32[9]{0:T(128)S(1)} %copy-done.3, s32[4,2]{1,0:T(4,128)S(1)} %copy.8.pair_cols, s32[4]{0:T(128)S(1)} %copy-done.1, s32[16]{0:T(128)S(1)} %copy-done.2, ...), custom_call_target="tpu_custom_call" | custom-call | flops 10000000 | bytes 8000000 | tf_op jit(solution)/shard_map/tables/pallas_call | solution.py:312
  8.8 0.0 collective-permute-done.refs_1_
  8.8 0.6 %collective-permute-start.2 = (s16[128,512]{1,0:T(8,128)(2,1)S(1)}, s16[128,512]{1,0:T(8,128)(2,1)S(1)}, u32[]{:S(2)}, u32[]{:S(2)}) collective-permute-start(s16[128,512]{1,0:T(8,128)(2,1)S(1)} %collective-permute-done.refs_1_), channel_id=1, source_target_pairs={{0,1},{1,0},{2,3},{3,2},{4,5},{5,4},{6,7},{7,6},{8,9},{9,8},{10,11... | collective-permute-start | bytes 393224 | tf_op jit(solution)/shard_map/ppermute | solution.py:387
  9.4 0.4 %collective-permute-done.3.refs_0_ = s16[128,512]{1,0:T(8,128)(2,1)S(1)} collective-permute-done((s16[128,512]{1,0:T(8,128)(2,1)S(1)}, s16[128,512]{1,0:T(8,128)(2,1)S(1)}, u32[]{:S(2)}, u32[]{:S(2)}) %collective-permute-start.3) | collective-permute-done | bytes 131104 | tf_op jit(solution)/shard_map/ppermute | solution.py:401
  9.8 0.4 %collective-permute-start.4 = (s16[128,512]{1,0:T(8,128)(2,1)S(1)}, s16[128,512]{1,0:T(8,128)(2,1)S(1)}, u32[]{:S(2)}, u32[]{:S(2)}) collective-permute-start(s16[128,512]{1,0:T(8,128)(2,1)S(1)} %collective-permute-done.3.refs_0_), channel_id=1, source_target_pairs={{0,2},{2,0},{1,3},{3,1},{4,6},{6,4},{5,7},{7,5},{8,10},{10,8},{9,1... | collective-permute-start | bytes 393224 | tf_op jit(solution)/shard_map/ppermute | solution.py:403
  10.1 0.2 collective-permute-start.5
  10.3 0.0 collective-permute-done.1.refs_2_
  10.3 0.1 collective-permute-done.2.refs_3_
  10.4 2.9 %step.5 = (f32[2,128,512]{2,1,0:T(8,128)S(1)}, bf16[2,1152,512]{2,1,0:T(8,128)(2,1)S(1)}, bf16[2,1152,512]{2,1,0:T(8,128)(2,1)S(1)}) custom-call(s32[5,8]{1,0:T(8,128)S(1)} %get-tuple-element.25.plan, s16[128,512]{1,0:T(8,128)(2,1)S(1)} %encode.1.refs_0_, s16[128,512]{1,0:T(8,128)(2,1)S(1)} %collective-permute-done.refs_1_, ...), custom_call_target="tpu_custom_call" | custom-call | flops 1000000 | bytes 100000 | tf_op jit(solution)/shard_map/step/pallas_call | solution.py:356
  13.3 1.6 %collective-permute-done.4.refs_1_ = s16[128,512]{1,0:T(8,128)(2,1)S(1)} collective-permute-done((s16[128,512]{1,0:T(8,128)(2,1)S(1)}, s16[128,512]{1,0:T(8,128)(2,1)S(1)}, u32[]{:S(2)}, u32[]{:S(2)}) %collective-permute-start.4) | collective-permute-done | bytes 131104 | tf_op jit(solution)/shard_map/ppermute | solution.py:403
  14.9 0.0 collective-permute-start.6
  14.9 1.2 %other_tables.1 = (bf16[2,128,1152]{2,1,0:T(8,128)(2,1)S(1)}, bf16[2,256,1152]{2,1,0:T(8,128)(2,1)S(1)}) custom-call(s32[5]{0:T(128)S(1)} %stack.20.meta, f32[9]{0:T(128)S(1)} %copy-done.3), custom_call_target="tpu_custom_call" | custom-call | flops 10000000 | bytes 3000000 | tf_op jit(solution)/shard_map/other_tables/pallas_call | solution.py:389
  16.1 0.0 collective-permute-done.5.refs_2_
  16.1 0.2 collective-permute-done.6.refs_3_
  16.2 2.5 %step.6 = (s16[128,512]{1,0:T(8,128)(2,1)S(1)}, bf16[2,1152,512]{2,1,0:T(8,128)(2,1)S(1)}, bf16[2,1152,512]{2,1,0:T(8,128)(2,1)S(1)}) custom-call(s32[5,8]{1,0:T(8,128)S(1)} %get-tuple-element.25.plan, s16[128,512]{1,0:T(8,128)(2,1)S(1)} %collective-permute-done.3.refs_0_, s16[128,512]{1,0:T(8,128)(2,1)S(1)} %collective-permute-done.4.refs_1_, ...), custom_call_target="tpu_custom_call" | custom-call | flops 1000000 | bytes 100000 | tf_op jit(solution)/shard_map/step/pallas_call | solution.py:356
  18.7 1.1 %collective-permute-start.8 = (s16[128,512]{1,0:T(8,128)(2,1)S(1)}, s16[128,512]{1,0:T(8,128)(2,1)S(1)}, u32[]{:S(2)}, u32[]{:S(2)}) collective-permute-start(s16[128,512]{1,0:T(8,128)(2,1)S(1)} %get-tuple-element.39.refs_0_), channel_id=1, source_target_pairs={{0,2},{2,0},{1,3},{3,1},{4,6},{6,4},{5,7},{7,5},{8,10},{10,8},{9,1... | collective-permute-start | bytes 393224 | tf_op jit(solution)/shard_map/ppermute | solution.py:419
  19.9 2.2 %other_rows.1.first = s16[144,512]{1,0:T(8,128)(2,1)S(1)} custom-call(s32[5,8]{1,0:T(8,128)S(1)} %get-tuple-element.25.plan, bf16[2,128,1152]{2,1,0:T(8,128)(2,1)S(1)} %get-tuple-element.26.refs_0_, bf16[2,256,1152]{2,1,0:T(8,128)(2,1)S(1)} %get-tuple-element.27.refs_1_, bf16[2,1152,512]{2,1,0:T(8,128)(2,1)S(1)} %get-tuple-element.31.refs_2_, ...), custom_call_target="tpu_custom_call" | custom-call | flops 1000000 | bytes 100000 | tf_op jit(solution)/shard_map/other_rows/pallas_call | solution.py:411
  22.1 1.0 %collective-permute-start.7 = (s16[144,512]{1,0:T(8,128)(2,1)S(1)}, s16[144,512]{1,0:T(8,128)(2,1)S(1)}, u32[]{:S(2)}, u32[]{:S(2)}) collective-permute-start(s16[144,512]{1,0:T(8,128)(2,1)S(1)} %other_rows.1.first), channel_id=1, source_target_pairs={{0,2},{2,0},{1,3},{3,1},{4,6},{6,4},{5,7},{7,5},{8,10},{10,8},{9,1... | collective-permute-start | bytes 442376 | tf_op jit(solution)/shard_map/ppermute | solution.py:423
  23.1 1.5 %collective-permute-done.8.refs_1_ = s16[128,512]{1,0:T(8,128)(2,1)S(1)} collective-permute-done((s16[128,512]{1,0:T(8,128)(2,1)S(1)}, s16[128,512]{1,0:T(8,128)(2,1)S(1)}, u32[]{:S(2)}, u32[]{:S(2)}) %collective-permute-start.8) | collective-permute-done | bytes 131104 | tf_op jit(solution)/shard_map/ppermute | solution.py:419
  24.6 1.3 %collective-permute-done.10.refs_3_ = s16[128,512]{1,0:T(8,128)(2,1)S(1)} collective-permute-done((s16[128,512]{1,0:T(8,128)(2,1)S(1)}, s16[128,512]{1,0:T(8,128)(2,1)S(1)}, u32[]{:S(2)}, u32[]{:S(2)}) %collective-permute-start.10) | collective-permute-done | bytes 131104 | tf_op jit(solution)/shard_map/ppermute | solution.py:387
  25.9 1.9 %step.7.after.refs_4_ = f32[2,128,256]{2,1,0:T(8,128)S(1)} custom-call(s32[5,8]{1,0:T(8,128)S(1)} %get-tuple-element.25.plan, s16[128,512]{1,0:T(8,128)(2,1)S(1)} %get-tuple-element.39.refs_0_, s16[128,512]{1,0:T(8,128)(2,1)S(1)} %collective-permute-done.8.refs_1_, s16[128,512]{1,0:T(8,128)(2,1)S(1)} %collective-permute-done.9.refs_2_, ...), custom_call_target="tpu_custom_call" | custom-call | flops 1000000 | bytes 100000 | tf_op jit(solution)/shard_map/step/pallas_call | solution.py:356
  27.8 0.2 collective-permute-done.7.second
  28.0 0.1 collective-permute-start.11
  28.1 1.8 %step.8.refs_5_ = f32[2,128,256]{2,1,0:T(8,128)S(1)} custom-call(s32[5,8]{1,0:T(8,128)S(1)} %get-tuple-element.25.plan, s16[128,512]{1,0:T(8,128)(2,1)S(1)} %get-tuple-element.39.refs_0_, s16[128,512]{1,0:T(8,128)(2,1)S(1)} %collective-permute-done.8.refs_1_, s16[128,512]{1,0:T(8,128)(2,1)S(1)} %collective-permute-done.9.refs_2_, ...), custom_call_target="tpu_custom_call" | custom-call | flops 1000000 | bytes 100000 | tf_op jit(solution)/shard_map/step/pallas_call | solution.py:356
  29.9 2.8 %step.9 = (f32[128,512]{1,0:T(8,128)}, f32[128,512]{1,0:T(8,128)}) custom-call(s32[5,8]{1,0:T(8,128)S(1)} %get-tuple-element.25.plan, s16[2,128,512]{2,1,0:T(8,128)(2,1)S(1)} %join.1.refs_0_, s16[2,128,512]{2,1,0:T(8,128)(2,1)S(1)} %collective-permute-done.11.refs_1_, bf16[4,256,1152]{2,1,0:T(8,128)(2,1)S(1)} %get-tuple-element.29.refs_4_.refs_2_, ...), custom_call_target="tpu_custom_call" | custom-call | flops 1000000 | bytes 100000 | tf_op jit(solution)/shard_map/step/pallas_call | solution.py:356
  (16 shorter events, 0.1 us)
Async XLA Ops:
  0.6 5.9 %copy-start.3 = (f32[9]{0:T(128)S(1)}, f32[9]{0:T(128)}, u32[]{:S(2)}) copy-start(f32[9]{0:T(128)} %phonon.3) | copy-start | bytes 112
  0.6 5.9 %copy-start.2 = (s32[16]{0:T(128)S(1)}, s32[16]{0:T(128)}, u32[]{:S(2)}) copy-start(s32[16]{0:T(128)} %block_order.1) | copy-start | bytes 196
  0.7 5.9 %copy-start.1 = (s32[4]{0:T(128)S(1)}, s32[4]{0:T(128)}, u32[]{:S(2)}) copy-start(s32[4]{0:T(128)} %pair_count.1) | copy-start | bytes 52
  0.7 1.0 %copy-start.4 = (f32[128,512]{1,0:T(8,128)S(1)}, f32[128,512]{1,0:T(8,128)}, u32[]{:S(2)}) copy-start(f32[128,512]{1,0:T(8,128)} %gap.1) | copy-start | bytes 786436
  1.6 4.7 %copy-start.5 = (s32[4,2]{0,1:T(2,128)S(1)}, s32[4,2]{0,1:T(2,128)}, u32[]{:S(2)}) copy-start(s32[4,2]{0,1:T(2,128)} %param.8) | copy-start | bytes 100
  1.6 4.9 %copy-start = (bf16[4,2,9,128,128]{4,3,2,1,0:T(8,128)(2,1)S(1)}, bf16[4,2,9,128,128]{4,3,2,1,0:T(8,128)(2,1)}, u32[]{:S(2)}) copy-start(bf16[4,2,9,128,128]{4,3,2,1,0:T(8,128)(2,1)} %coupling.1) | copy-start | bytes 7077892
  1.8 7.0 %collective-permute-start = (s16[128,512]{1,0:T(8,128)(2,1)S(1)}, s16[128,512]{1,0:T(8,128)(2,1)S(1)}, u32[]{:S(2)}, u32[]{:S(2)}) collective-permute-start(s16[128,512]{1,0:T(8,128)(2,1)S(1)} %encode.1.refs_0_), channel_id=1, source_target_pairs={{0,2},{2,0},{1,3},{3,1},{4,6},{6,4},{5,7},{7,5},{8,10},{10,8},{9,1... | collective-permute-start | bytes 393224 | tf_op jit(solution)/shard_map/ppermute | solution.py:400
  4.8 5.0 %collective-permute-start.3 = (s16[128,512]{1,0:T(8,128)(2,1)S(1)}, s16[128,512]{1,0:T(8,128)(2,1)S(1)}, u32[]{:S(2)}, u32[]{:S(2)}) collective-permute-start(s16[128,512]{1,0:T(8,128)(2,1)S(1)} %encode.1.refs_0_), channel_id=1, source_target_pairs={{0,4},{4,0},{1,5},{5,1},{2,6},{6,2},{3,7},{7,3},{8,12},{12,8},{9,1... | collective-permute-start | bytes 393224 | tf_op jit(solution)/shard_map/ppermute | solution.py:401
  6.4 3.9 %collective-permute-start.1 = (s16[128,512]{1,0:T(8,128)(2,1)S(1)}, s16[128,512]{1,0:T(8,128)(2,1)S(1)}, u32[]{:S(2)}, u32[]{:S(2)}) collective-permute-start(s16[128,512]{1,0:T(8,128)(2,1)S(1)} %encode.1.refs_0_), channel_id=1, source_target_pairs={{0,1},{1,0},{2,3},{3,2},{4,5},{5,4},{6,7},{7,6},{8,9},{9,8},{10,11... | collective-permute-start | bytes 393224 | tf_op jit(solution)/shard_map/ppermute | solution.py:387
  8.8 1.6 %collective-permute-start.2 = (s16[128,512]{1,0:T(8,128)(2,1)S(1)}, s16[128,512]{1,0:T(8,128)(2,1)S(1)}, u32[]{:S(2)}, u32[]{:S(2)}) collective-permute-start(s16[128,512]{1,0:T(8,128)(2,1)S(1)} %collective-permute-done.refs_1_), channel_id=1, source_target_pairs={{0,1},{1,0},{2,3},{3,2},{4,5},{5,4},{6,7},{7,6},{8,9},{9,8},{10,11... | collective-permute-start | bytes 393224 | tf_op jit(solution)/shard_map/ppermute | solution.py:387
  9.8 5.1 %collective-permute-start.4 = (s16[128,512]{1,0:T(8,128)(2,1)S(1)}, s16[128,512]{1,0:T(8,128)(2,1)S(1)}, u32[]{:S(2)}, u32[]{:S(2)}) collective-permute-start(s16[128,512]{1,0:T(8,128)(2,1)S(1)} %collective-permute-done.3.refs_0_), channel_id=1, source_target_pairs={{0,2},{2,0},{1,3},{3,1},{4,6},{6,4},{5,7},{7,5},{8,10},{10,8},{9,1... | collective-permute-start | bytes 393224 | tf_op jit(solution)/shard_map/ppermute | solution.py:403
  10.1 6.0 %collective-permute-start.5 = (s16[128,512]{1,0:T(8,128)(2,1)S(1)}, s16[128,512]{1,0:T(8,128)(2,1)S(1)}, u32[]{:S(2)}, u32[]{:S(2)}) collective-permute-start(s16[128,512]{1,0:T(8,128)(2,1)S(1)} %collective-permute-done.3.refs_0_), channel_id=1, source_target_pairs={{0,1},{1,0},{2,3},{3,2},{4,5},{5,4},{6,7},{7,6},{8,9},{9,8},{10,11... | collective-permute-start | bytes 393224 | tf_op jit(solution)/shard_map/ppermute | solution.py:405
  14.9 1.3 %collective-permute-start.6 = (s16[128,512]{1,0:T(8,128)(2,1)S(1)}, s16[128,512]{1,0:T(8,128)(2,1)S(1)}, u32[]{:S(2)}, u32[]{:S(2)}) collective-permute-start(s16[128,512]{1,0:T(8,128)(2,1)S(1)} %collective-permute-done.4.refs_1_), channel_id=1, source_target_pairs={{0,1},{1,0},{2,3},{3,2},{4,5},{5,4},{6,7},{7,6},{8,9},{9,8},{10,11... | collective-permute-start | bytes 393224 | tf_op jit(solution)/shard_map/ppermute | solution.py:407
  18.7 5.8 %collective-permute-start.8 = (s16[128,512]{1,0:T(8,128)(2,1)S(1)}, s16[128,512]{1,0:T(8,128)(2,1)S(1)}, u32[]{:S(2)}, u32[]{:S(2)}) collective-permute-start(s16[128,512]{1,0:T(8,128)(2,1)S(1)} %get-tuple-element.39.refs_0_), channel_id=1, source_target_pairs={{0,2},{2,0},{1,3},{3,1},{4,6},{6,4},{5,7},{7,5},{8,10},{10,8},{9,1... | collective-permute-start | bytes 393224 | tf_op jit(solution)/shard_map/ppermute | solution.py:419
  22.1 5.9 %collective-permute-start.7 = (s16[144,512]{1,0:T(8,128)(2,1)S(1)}, s16[144,512]{1,0:T(8,128)(2,1)S(1)}, u32[]{:S(2)}, u32[]{:S(2)}) collective-permute-start(s16[144,512]{1,0:T(8,128)(2,1)S(1)} %other_rows.1.first), channel_id=1, source_target_pairs={{0,2},{2,0},{1,3},{3,1},{4,6},{6,4},{5,7},{7,5},{8,10},{10,8},{9,1... | collective-permute-start | bytes 442376 | tf_op jit(solution)/shard_map/ppermute | solution.py:423
  23.1 1.5 %collective-permute-start.9 = (s16[128,512]{1,0:T(8,128)(2,1)S(1)}, s16[128,512]{1,0:T(8,128)(2,1)S(1)}, u32[]{:S(2)}, u32[]{:S(2)}) collective-permute-start(s16[128,512]{1,0:T(8,128)(2,1)S(1)} %get-tuple-element.39.refs_0_), channel_id=1, source_target_pairs={{0,1},{1,0},{2,3},{3,2},{4,5},{5,4},{6,7},{7,6},{8,9},{9,8},{10,11... | collective-permute-start | bytes 393224 | tf_op jit(solution)/shard_map/ppermute | solution.py:387
  24.6 1.3 %collective-permute-start.10 = (s16[128,512]{1,0:T(8,128)(2,1)S(1)}, s16[128,512]{1,0:T(8,128)(2,1)S(1)}, u32[]{:S(2)}, u32[]{:S(2)}) collective-permute-start(s16[128,512]{1,0:T(8,128)(2,1)S(1)} %collective-permute-done.8.refs_1_), channel_id=1, source_target_pairs={{0,1},{1,0},{2,3},{3,2},{4,5},{5,4},{6,7},{7,6},{8,9},{9,8},{10,11... | collective-permute-start | bytes 393224 | tf_op jit(solution)/shard_map/ppermute | solution.py:387
  28.0 1.9 %collective-permute-start.11 = (s16[2,128,512]{2,1,0:T(8,128)(2,1)S(1)}, s16[2,128,512]{2,1,0:T(8,128)(2,1)S(1)}, u32[]{:S(2)}, u32[]{:S(2)}) collective-permute-start(s16[2,128,512]{2,1,0:T(8,128)(2,1)S(1)} %join.1.refs_0_), channel_id=1, source_target_pairs={{0,1},{1,0},{2,3},{3,2},{4,5},{5,4},{6,7},{7,6},{8,9},{9,8},{10,11... | collective-permute-start | bytes 786440 | tf_op jit(solution)/shard_map/ppermute | solution.py:425
